TPU v7x, 32 devices: a whole 2x2x4 slice. The times are simulated.
32 devices in a mesh: gx: 8 (over z, x), gy: 4 (over y, core).
Axes of the slice: x: 2, y: 2, z: 4, core: 2. Of those that a mesh axis runs over, the one named last changes fastest.
Arguments:
- old_states: float32 [8192, 12, 512], P(('gx', 'gy')), may hold values from -6 to 6
- new_place: int32 [8192], P(('gx', 'gy')), may hold values from -1 to 4095, as said below
- vectors_x: float32 [10, 10], replicated, may hold values from -2 to 2
- vectors_s: float32 [10, 10], replicated, may hold values from -2 to 2
- vectors_w: float32 [16, 10, 10], replicated, may hold values from -2 to 2
- values_x: float32 [10], replicated, may hold values from 0.2 to 5
- values_s: float32 [10], replicated, may hold values from 0.2 to 5
- values_w: float32 [16, 10], replicated, may hold values from 0.2 to 5
Outputs:
- new_states: float32 [32, 8, 16, 12, 512], P('gx', 'gy')
- correction: float32 [256, 64, 128], P('gx', 'gy')
Inputs may be any that keep to these rules, and one draw needn't show every extreme that they name: `new_place`: every element number appears in exactly one slot; the other slots hold -1. One device's slots send at most 8 elements to any one device, and some pairs reach 8; some devices have all 256 slots filled.
All inputs are finite; a program needn't handle non-finite values.
Results may differ from a plain program's by a relative error of at most 0.00007.
Values sent between devices are 32-bit elements; how exact they have to be, the bound alone decides.
No kernel may reach another device: no remote copies, remote signals or barrier semaphores. Data moves between devices by JAX's collectives and lax.ppermute only.
A program may use at most 128 MiB of HBM per device.

v0:
```python
import jax
import jax.numpy as jnp
from jax import lax
from jax.sharding import PartitionSpec as P

BX = 4
BS = 2


def shifted(value, axis, steps):
    count = lax.axis_size(axis)
    pairs = [(source, (source + steps) % count) for source in range(count)]
    return lax.ppermute(value, axis, pairs)


def rim_mask(extent):
    offset = jnp.arange(extent)
    on_rim = ((offset == 0) | (offset == extent - 1)).astype(jnp.int32)
    rim_count = on_rim[:, None, None] + on_rim[None, :, None] + on_rim[None, None, :]
    return (rim_count <= 1).astype(jnp.float32)[..., None]


def diag_solve(extended, vectors_x, vectors_s, stacked_w, values_x, values_s, stacked_values):
    highest = lax.Precision.HIGHEST
    section = jnp.einsum("ui,uvwn->ivwn", vectors_x, extended, precision=highest)
    section = jnp.einsum("vj,ivwn->ijwn", vectors_s, section, precision=highest)
    section = jnp.einsum("wkn,ijwn->ijkn", stacked_w, section, precision=highest)
    denom = (
        values_x[:, None, None, None]
        + values_s[None, :, None, None]
        + stacked_values[None, None, :, :]
    )
    modal = section / denom
    section = jnp.einsum("ui,ijkn->ujkn", vectors_x, modal, precision=highest)
    section = jnp.einsum("vj,ujkn->uvkn", vectors_s, section, precision=highest)
    return jnp.einsum("wkn,uvkn->uvwn", stacked_w, section, precision=highest)


def leading_product(left, right):
    return lax.dot_general(
        left,
        right,
        (((0,), (0,)), ((), ())),
        precision=lax.Precision.HIGHEST,
        preferred_element_type=jnp.float32,
    )


def relocate(payload, slot_marks):
    arrived, arrived_marks = (
        lax.all_to_all(payload, ("gx", "gy"), split_axis=0, concat_axis=0, tiled=True),
        lax.all_to_all(slot_marks, ("gx", "gy"), split_axis=0, concat_axis=0, tiled=True),
    )
    return (arrived, arrived_marks)


def placement(arrived_marks, per_dev):
    return (arrived_marks[:, None] == jnp.arange(per_dev, dtype=jnp.float32)[None, :]).astype(
        jnp.float32
    )


def settle(arrived, selector):
    rows = arrived.shape[0]
    placed = leading_product(selector, arrived.reshape(rows, -1))
    return placed.reshape((selector.shape[1],) + arrived.shape[1:])


def pressure_points(arrived, selector):
    pressure_rows = 3.0 * arrived[:, 0] - 3.0 * arrived[:, 1] + arrived[:, 2]
    return leading_product(pressure_rows, selector)


def send_x(plane, by):
    return shifted(plane, "gx", by)


def send_y(plane, by):
    return shifted(plane, "gy", by)


def back_x(plane, by):
    return shifted(plane, "gx", by)


def back_y(plane, by):
    return shifted(plane, "gy", by)


def shards(old_states, new_place, vectors_x, vectors_s, vectors_w, values_x, values_s, values_w):
    count_x = lax.axis_size("gx")
    count_y = lax.axis_size("gy")
    devices = count_x * count_y
    slot_count = old_states.shape[0]
    fields = old_states.shape[1]
    points = old_states.shape[2]
    extent = vectors_x.shape[0]
    per_side = extent - 2
    layers = vectors_w.shape[0]
    per_dev = BX * BS * layers
    capacity = 2 * per_dev // devices
    send_rows = devices * capacity
    span_total = BS * count_y
    is_live = new_place >= 0
    placed = jnp.maximum(new_place, 0)
    column = placed // layers
    layer_pos = placed % layers
    elem_x = column // span_total
    elem_s = column % span_total
    target = elem_x // BX * count_y + elem_s // BS
    local_row = (elem_x % BX * BS + elem_s % BS) * layers + layer_pos
    onehot = (
        (target[:, None] == jnp.arange(devices, dtype=jnp.int32)[None, :]) & is_live[:, None]
    ).astype(jnp.int32)
    bucket_rank = jnp.sum((jnp.cumsum(onehot, axis=0) - onehot) * onehot, axis=1)
    slot_pos = jnp.where(is_live, target * capacity + bucket_rank, send_rows)
    chooser = (jnp.arange(send_rows, dtype=jnp.int32)[:, None] == slot_pos[None, :]).astype(
        jnp.float32
    )
    packed = jnp.dot(
        chooser,
        old_states.reshape(slot_count, fields * points),
        precision=lax.Precision.HIGHEST,
        preferred_element_type=jnp.float32,
    ).reshape(send_rows, fields, points)
    row_plus = jnp.where(is_live, local_row + 1, 0).astype(jnp.float32)
    slot_marks = (
        jnp.dot(
            chooser, row_plus, precision=lax.Precision.HIGHEST, preferred_element_type=jnp.float32
        )
        - 1.0
    )
    arrived, arrived_marks = relocate(packed, slot_marks)
    selector = placement(arrived_marks, per_dev)
    new_flat = settle(arrived, selector)
    field_points = pressure_points(arrived, selector)
    new_states = new_flat.reshape(BX, BS, layers, fields, points)
    cells = field_points.reshape(per_side, per_side, per_side, BX, BS, layers)
    top_x = cells[per_side - 1]
    low_x = cells[0]
    face_xlow = jnp.concatenate(
        [send_x(top_x[:, :, BX - 1], 1)[:, :, None], top_x[:, :, : BX - 1]], axis=2
    )
    face_xup = jnp.concatenate([low_x[:, :, 1:], send_x(low_x[:, :, 0], -1)[:, :, None]], axis=2)
    top_s = cells[:, per_side - 1]
    low_s = cells[:, 0]
    face_slow = jnp.concatenate(
        [send_y(top_s[:, :, :, BS - 1], 1)[:, :, :, None], top_s[:, :, :, : BS - 1]], axis=3
    )
    face_sup = jnp.concatenate(
        [low_s[:, :, :, 1:], send_y(low_s[:, :, :, 0], -1)[:, :, :, None]], axis=3
    )
    top_w = cells[:, :, per_side - 1]
    low_w = cells[:, :, 0]
    zero_layer = jnp.zeros(top_w.shape[:4] + (1,), jnp.float32)
    face_wlow = jnp.concatenate([zero_layer, top_w[..., : layers - 1]], axis=4)
    face_wup = jnp.concatenate([low_w[..., 1:], zero_layer], axis=4)
    boxes = jnp.zeros((extent, extent, extent, BX, BS, layers), jnp.float32)
    boxes = boxes.at[1:-1, 1:-1, 1:-1].set(cells)
    boxes = boxes.at[0, 1:-1, 1:-1].set(face_xlow).at[-1, 1:-1, 1:-1].set(face_xup)
    boxes = boxes.at[1:-1, 0, 1:-1].set(face_slow).at[1:-1, -1, 1:-1].set(face_sup)
    boxes = boxes.at[1:-1, 1:-1, 0].set(face_wlow).at[1:-1, 1:-1, -1].set(face_wup)
    box_mask = rim_mask(extent)
    extended = boxes.reshape(extent, extent, extent, per_dev) * box_mask
    repeat = BX * BS
    stacked_w = jnp.transpose(jnp.tile(vectors_w, (repeat, 1, 1)), (1, 2, 0))
    stacked_values = jnp.tile(values_w, (repeat, 1)).T
    local_fix = (
        diag_solve(extended, vectors_x, vectors_s, stacked_w, values_x, values_s, stacked_values)
        * box_mask
    )
    fixed = local_fix.reshape(extent, extent, extent, BX, BS, layers)
    total = fixed[1:-1, 1:-1, 1:-1]
    out_xlow = fixed[0, 1:-1, 1:-1]
    out_xup = fixed[-1, 1:-1, 1:-1]
    to_last_x = jnp.concatenate(
        [out_xlow[:, :, 1:], back_x(out_xlow[:, :, 0], -1)[:, :, None]], axis=2
    )
    to_first_x = jnp.concatenate(
        [back_x(out_xup[:, :, BX - 1], 1)[:, :, None], out_xup[:, :, : BX - 1]], axis=2
    )
    total = total.at[per_side - 1].add(to_last_x).at[0].add(to_first_x)
    out_slow = fixed[1:-1, 0, 1:-1]
    out_sup = fixed[1:-1, -1, 1:-1]
    to_last_s = jnp.concatenate(
        [out_slow[:, :, :, 1:], back_y(out_slow[:, :, :, 0], -1)[:, :, :, None]], axis=3
    )
    to_first_s = jnp.concatenate(
        [back_y(out_sup[:, :, :, BS - 1], 1)[:, :, :, None], out_sup[:, :, :, : BS - 1]], axis=3
    )
    total = total.at[:, per_side - 1].add(to_last_s).at[:, 0].add(to_first_s)
    out_wlow = fixed[1:-1, 1:-1, 0]
    out_wup = fixed[1:-1, 1:-1, -1]
    to_last_w = jnp.concatenate([out_wlow[..., 1:], zero_layer], axis=4)
    to_first_w = jnp.concatenate([zero_layer, out_wup[..., : layers - 1]], axis=4)
    total = total.at[:, :, per_side - 1].add(to_last_w).at[:, :, 0].add(to_first_w)
    correction = jnp.transpose(total, (3, 0, 4, 1, 5, 2)).reshape(
        BX * per_side, BS * per_side, layers * per_side
    )
    return (new_states, correction)


def solution(mesh):
    placed = (P(("gx", "gy"), None, None), P(("gx", "gy")), P(), P(), P(), P(), P(), P())
    return jax.shard_map(
        shards,
        mesh=mesh,
        in_specs=placed,
        out_specs=(P("gx", "gy", None, None, None), P("gx", "gy", None)),
        check_vma=False,
    )
```

profile of v0, /device:TPU:1, one launch (start us, length us, event | category | flops | bytes accessed | tf_op | source)
XLA Modules:
  0.0 409.8 jit_solution(3927925091096390708)
XLA Ops:
  0.6 0.7 select_convert_fusion
  1.4 0.6 reduce-window.6
  2.5 0.8 all_to_all.9
  3.3 7.1 %all-to-all-start = ((f32[32,8,1]{1,2,0:T(1,128)}), f32[32,8,1]{1,2,0:T(1,128)S(1)}, u32[]{:S(2)}, u32[]{:S(2)}) async-start(f32[32,8,1]{1,2,0:T(1,128)} %bitcast.5), calls=%async_computation | async-start | bytes 32768 | tf_op jit(solution)/shard_map/all_to_all | solution.py:52
  10.4 6.6 %copy.59 = f32[256,12,512]{0,2,1:T(8,128)} copy(f32[256,12,512]{2,0,1:T(8,128)} %param.34) | data formatting | bytes 12582912 | tf_op args[0]
  17.0 9.4 %fusion.2 = f32[256,12,512]{2,0,1:T(8,128)S(1)} fusion(f32[256,12,512]{0,2,1:T(8,128)} %copy.59, s32[256]{0:T(256)S(1)} %add_select_fusion), kind=kOutput, calls=%fused_computation.3 | convolution fusion | flops 4831903744 | bytes 12583936 | tf_op jit(solution)/shard_map/dot_general | solution.py:120
  26.3 7.0 %copy.60 = f32[256,12,512]{2,1,0:T(8,128)} copy(f32[256,12,512]{2,0,1:T(8,128)S(1)} %fusion.2) | data formatting | bytes 12582912 | tf_op jit(solution)/shard_map/dot_general | solution.py:120
  33.3 6.5 %all-to-all-start.1 = ((f32[256,12,512]{2,1,0:T(8,128)}), f32[256,12,512]{2,1,0:T(8,128)}, u32[]{:S(2)}, u32[]{:S(2)}) async-start(f32[256,12,512]{2,1,0:T(8,128)} %copy.60), calls=%async_computation.1 | async-start | bytes 16777216 | tf_op jit(solution)/shard_map/all_to_all | solution.py:51
  40.9 0.7 reduce.31
  41.6 182.7 %all-to-all-done.1 = f32[256,12,512]{2,1,0:T(8,128)} async-done(((f32[256,12,512]{2,1,0:T(8,128)}), f32[256,12,512]{2,1,0:T(8,128)}, u32[]{:S(2)}, u32[]{:S(2)}) %all-to-all-start.1) | async-done | bytes 6291488 | tf_op jit(solution)/shard_map/all_to_all | solution.py:51
  224.4 6.4 %slice_add_fusion = f32[256,1,512]{2,1,0:T(1,128)S(1)} fusion(f32[256,12,512]{2,1,0:T(8,128)} %all-to-all-done.1), kind=kLoop, calls=%fused_computation.13 | loop fusion | flops 524288 | bytes 2097152 | tf_op jit(solution)/shard_map/add | solution.py:70
  230.8 0.7 fusion.7
  231.5 2.7 reshape.807
  234.6 1.1 collective-permute-start
  236.1 0.7 slice_bitcast_fusion.9
  236.8 3.1 collective-permute-start.1
  240.2 3.8 collective-permute-start.2
  244.1 0.9 fusion.47
  245.1 9.2 %copy.61 = f32[256,12,512]{0,2,1:T(8,128)} copy(f32[256,12,512]{2,1,0:T(8,128)} %all-to-all-done.1) | data formatting | bytes 12582912 | tf_op jit(solution)/shard_map/all_to_all | solution.py:51
  254.3 8.0 %fusion = f32[4,2,16,12,512]{4,2,3,1,0:T(8,128)} fusion(f32[256,12,512]{0,2,1:T(8,128)} %copy.61, f32[4,2,16]{2,1,0:T(2,128)S(1)} %multiply_add_fusion, f32[256]{0:T(256)S(1)} %eq.130), kind=kOutput, calls=%fused_computation.1 | convolution fusion | flops 2415951872 | bytes 9438720 | tf_op jit(solution)/shard_map/dot_general | solution.py:40
  262.5 3.5 scatter.24
  266.3 1.7 fusion.14
  268.1 1.7 fusion.15
  269.7 1.0 maximum_bitcast_fusion.3
  270.7 1.0 fusion.16
  271.7 0.9 copy_dynamic-update-slice_fusion
  272.6 1.1 bitcast_dynamic-update-slice_fusion.1
  273.7 0.9 bitcast_dynamic-update-slice_fusion
  274.6 6.6 %reshape.833 = f32[10,10,10,128]{3,2,1,0:T(8,128)S(1)} reshape(f32[10,10,10,4,2,16]{5,4,3,2,1,0:T(2,128)} %bitcast_dynamic-update-slice_fusion) | data formatting | bytes 1024000 | tf_op jit(solution)/shard_map/reshape | solution.py:164
  281.1 1.1 convolution_bitcast_fusion.3
  282.3 1.2 convolution_bitcast_fusion.2
  283.5 5.8 %copy.76 = f32[10,10,10,128]{2,1,0,3:T(8,128)} copy(f32[10,10,10,128]{3,1,2,0:T(8,128)S(1)} %convolution_bitcast_fusion.2) | data formatting | bytes 1024000 | tf_op jit(solution)/shard_map/vj,ivwn->ijwn/transpose | solution.py:26
  289.4 13.5 %bitcast_divide_fusion = f32[10,10,10,128]{2,1,0,3:T(8,128)} fusion(f32[10,128]{0,1:T(8,128)S(1)} %bitcast.218, f32[10,10]{1,0:T(8,128)S(1)} %broadcast_add_fusion, f32[10,10,10,128]{2,1,0,3:T(8,128)} %copy.76, f32[10,10,128,1]{1,0,3,2:T(8,128)S(1)} %bitcast.202), kind=kOutput, calls=%fused_computation | convolution fusion | flops 15616000 | bytes 1080720 | tf_op jit(solution)/shard_map/wkn,ijwn->ijkn/dot_general | solution.py:27
  302.9 11.1 %copy.77 = f32[10,10,10,128]{3,0,2,1:T(8,128)S(1)} copy(f32[10,10,10,128]{2,1,0,3:T(8,128)} %bitcast_divide_fusion) | data formatting | bytes 1024000 | tf_op jit(solution)/shard_map/div | solution.py:33
  314.0 0.8 convolution_bitcast_fusion.1
  314.9 1.2 convolution_bitcast_fusion
  316.0 5.6 %copy.79 = f32[10,10,10,128]{2,1,0,3:T(8,128)} copy(f32[10,10,10,128]{3,1,2,0:T(8,128)S(1)} %convolution_bitcast_fusion) | data formatting | bytes 1024000 | tf_op jit(solution)/shard_map/vj,ujkn->uvkn/transpose | solution.py:35
  321.6 12.3 %broadcast_multiply_fusion = f32[128,10,10,10]{3,2,1,0:T(8,128)S(1)} fusion(f32[10,10,10]{2,1,0:T(8,128)S(1)} %fusion.26, f32[10,10,10,128]{2,1,0,3:T(8,128)} %copy.79, f32[10,10,128,1]{1,0,3,2:T(8,128)S(1)} %bitcast.203), kind=kOutput, calls=%fused_computation.5 | convolution fusion | flops 15488000 | bytes 1079200 | tf_op jit(solution)/shard_map/wkn,uvkn->uvwn/dot_general | solution.py:36
  333.9 3.8 slice.727
  337.7 1.6 copy-done.1
  339.3 1.4 fusion.46
  341.0 0.7 slice.735
  341.7 0.6 slice_bitcast_fusion.7
  342.3 5.7 %fusion.45 = (f32[8,1,8,4,2,16]{2,1,0,5,4,3:T(1,128)S(1)}, f32[8,1,8,4,2,16]{2,1,0,5,4,3:T(1,128)S(1)}) fusion(f32[10,10,10,4,2,16]{2,1,0,5,4,3:T(8,128)} %bitcast.199), kind=kLoop, calls=%fused_computation.121 | loop fusion | bytes 131072 | tf_op jit(solution)/shard_map/slice | solution.py:184
  348.1 10.5 %fusion.44 = (f32[8,8,1,4,2,16]{2,1,0,5,4,3:T(8,128)}, f32[8,8,1,4,2,16]{2,1,0,5,4,3:T(8,128)}) fusion(f32[10,10,10,4,2,16]{2,1,0,5,4,3:T(8,128)} %bitcast.200), kind=kLoop, calls=%fused_computation.120 | loop fusion | bytes 131072 | tf_op jit(solution)/shard_map/slice | solution.py:193
  358.6 5.1 %copy.108 = f32[8,8,8,4,2,16]{5,2,4,3,1,0:T(8,128)S(1)} copy(f32[8,8,8,4,2,16]{2,1,0,5,4,3:T(8,128)} %slice.727) | data formatting | bytes 524288
  363.7 1.2 copy.109
  364.9 1.9 copy.110
  366.9 1.5 slice_bitcast_fusion.8
  368.3 1.7 collective-permute-start.4
  370.1 1.0 copy.112
  371.1 1.6 slice_bitcast_fusion.6
  373.1 0.7 slice_bitcast_fusion.4
  373.9 1.9 collective-permute-start.7
  375.8 5.7 %copy.114 = f32[8,8,1,4,2,16]{5,4,3,1,0,2:T(2,128)S(1)} copy(f32[8,8,1,4,2,16]{2,1,0,5,4,3:T(8,128)} %get-tuple-element.163) | data formatting | bytes 65536
  382.0 4.8 %copy.115 = f32[8,8,1,4,2,16]{5,1,4,3,2,0:T(8,128)S(1)} copy(f32[8,8,1,4,2,16]{2,1,0,5,4,3:T(8,128)} %get-tuple-element.162) | data formatting | bytes 65536
  387.2 0.9 fusion.18
  388.1 1.0 fusion.13
  389.2 1.0 fusion.12
  390.2 1.0 fusion.11
  391.6 5.4 %scatter-add.26 = f32[8,8,8,4,2,16]{5,2,4,3,1,0:T(8,128)S(1)} dynamic-update-slice(f32[8,8,8,4,2,16]{5,2,4,3,1,0:T(8,128)S(1)} %fusion.11, f32[8,8,1,4,2,16]{5,2,4,3,1,0:T(1,128)S(1)} %slice_add_fusion.2, s32[]{:T(128)} %constant.480.clone.1, s32[]{:T(128)} %constant.480.clone.1, s32[]{:T(128)} %constant.485.clone.1, s32[]{:T(128)} %constant.480.clone.1, s32[]{:T(128)} %constant.480.clone.1, ...) | dynamic-update-slice | bytes 65540 | tf_op jit(solution)/shard_map/scatter-add | solution.py:196
  397.2 5.4 %scatter-add.29 = f32[8,8,8,4,2,16]{5,2,4,3,1,0:T(8,128)S(1)} dynamic-update-slice(f32[8,8,8,4,2,16]{5,2,4,3,1,0:T(8,128)S(1)} %scatter-add.26, f32[8,8,1,4,2,16]{5,2,4,3,1,0:T(1,128)S(1)} %slice_add_fusion.1, s32[]{:T(128)} %constant.480.clone.1, s32[]{:T(128)} %constant.480.clone.1, s32[]{:T(128)} %constant.480.clone.1, s32[]{:T(128)} %constant.480.clone.1, s32[]{:T(128)} %constant.480.clone.1, ...) | dynamic-update-slice | bytes 65540 | tf_op jit(solution)/shard_map/scatter-add | solution.py:196
  402.6 2.8 copy.93
  405.3 4.3 %reshape.822 = f32[32,16,128]{2,1,0:T(8,128)} reshape(f32[4,8,2,8,16,8]{5,4,3,2,1,0:T(8,128)} %copy.93) | data formatting | bytes 524288 | tf_op jit(solution)/shard_map/reshape | solution.py:197
  (71 shorter events, 5.5 us)
Async XLA Ops:
  0.6 280.5 %copy-start = (f32[10,10]{1,0:T(8,128)S(1)}, f32[10,10]{1,0:T(8,128)}, u32[]{:S(2)}) copy-start(f32[10,10]{1,0:T(8,128)} %param.36) | copy-start | bytes 1204
  3.3 30.0 %all-to-all-start = ((f32[32,8,1]{1,2,0:T(1,128)}), f32[32,8,1]{1,2,0:T(1,128)S(1)}, u32[]{:S(2)}, u32[]{:S(2)}) async-start(f32[32,8,1]{1,2,0:T(1,128)} %bitcast.5), calls=%async_computation | async-start | bytes 32768 | tf_op jit(solution)/shard_map/all_to_all | solution.py:52
  33.3 6.9 %copy-start.5 = (f32[16,10,10]{2,0,1:T(8,128)S(1)}, f32[16,10,10]{2,0,1:T(8,128)}, u32[]{:S(2)}) copy-start(f32[16,10,10]{2,0,1:T(8,128)} %param.38) | copy-start | bytes 19204
  33.3 6.9 %copy-start.8 = (f32[10]{0:T(128)S(1)}, f32[10]{0:T(128)}, u32[]{:S(2)}) copy-start(f32[10]{0:T(128)} %param.40) | copy-start | bytes 124
  33.3 7.0 %copy-start.9 = (f32[10]{0:T(128)S(1)}, f32[10]{0:T(128)}, u32[]{:S(2)}) copy-start(f32[10]{0:T(128)} %param.39) | copy-start | bytes 124
  33.3 191.1 %all-to-all-start.1 = ((f32[256,12,512]{2,1,0:T(8,128)}), f32[256,12,512]{2,1,0:T(8,128)}, u32[]{:S(2)}, u32[]{:S(2)}) async-start(f32[256,12,512]{2,1,0:T(8,128)} %copy.60), calls=%async_computation.1 | async-start | bytes 16777216 | tf_op jit(solution)/shard_map/all_to_all | solution.py:51
  234.6 27.9 %copy-start.4 = (f32[8,8,4,2,16]{4,3,2,1,0:T(2,128)}, f32[8,8,4,2,16]{4,3,2,1,0:T(2,128)S(1)}, u32[]{:S(2)}) copy-start(f32[8,8,4,2,16]{4,3,2,1,0:T(2,128)S(1)} %squeeze.63) | copy-start | bytes 98308
  234.6 31.7 %collective-permute-start = (f32[8,8,2,16]{3,2,1,0:T(2,128)S(1)}, f32[8,8,2,16]{3,2,1,0:T(2,128)}, u32[]{:S(2)}, u32[]{:S(2)}) collective-permute-start(f32[8,8,2,16]{3,2,1,0:T(2,128)S(1)} %slice_bitcast_fusion.10), channel_id=1, source_target_pairs={{0,4},{4,8},{8,12},{12,16},{16,20},{20,24},{24,28},{28,0},{1,5},{5... | collective-permute-start | bytes 24584 | tf_op jit(solution)/shard_map/ppermute | solution.py:13
  236.1 26.3 %copy-start.3 = (f32[8,8,4,2,16]{4,3,2,1,0:T(2,128)}, f32[8,8,4,2,16]{4,3,2,1,0:T(2,128)S(1)}, u32[]{:S(2)}) copy-start(f32[8,8,4,2,16]{4,3,2,1,0:T(2,128)S(1)} %squeeze.65) | copy-start | bytes 98308
  236.8 31.2 %collective-permute-start.1 = (f32[8,8,2,16]{3,2,1,0:T(2,128)}, f32[8,8,2,16]{3,2,1,0:T(2,128)}, u32[]{:S(2)}, u32[]{:S(2)}) collective-permute-start(f32[8,8,2,16]{3,2,1,0:T(2,128)} %slice_bitcast_fusion.9), channel_id=1, source_target_pairs={{0,28},{4,0},{8,4},{12,8},{16,12},{20,16},{24,20},{28,24},{1,29},{... | collective-permute-start | bytes 24584 | tf_op jit(solution)/shard_map/ppermute | solution.py:13
  240.2 30.5 %collective-permute-start.2 = (f32[8,8,4,16]{3,2,1,0:T(4,128)S(1)}, f32[8,8,4,16]{3,2,1,0:T(4,128)S(1)}, u32[]{:S(2)}, u32[]{:S(2)}) collective-permute-start(f32[8,8,4,16]{3,2,1,0:T(4,128)S(1)} %bitcast.216), channel_id=1, source_target_pairs={{0,1},{1,2},{2,3},{3,0},{4,5},{5,6},{6,7},{7,4},{8,9},{9,10},{10,1... | collective-permute-start | bytes 49160 | tf_op jit(solution)/shard_map/ppermute | solution.py:13
  245.0 24.8 %collective-permute-start.3 = (f32[8,8,4,16]{3,2,1,0:T(4,128)}, f32[8,8,4,16]{3,2,1,0:T(4,128)}, u32[]{:S(2)}, u32[]{:S(2)}) collective-permute-start(f32[8,8,4,16]{3,2,1,0:T(4,128)} %bitcast.30), channel_id=1, source_target_pairs={{0,3},{1,0},{2,1},{3,2},{4,7},{5,4},{6,5},{7,6},{8,11},{9,8},{10,9... | collective-permute-start | bytes 49160 | tf_op jit(solution)/shard_map/ppermute | solution.py:13
  262.5 3.9 slice-start.1
  262.5 5.6 %slice-start = ((f32[8,8,4,2,16]{4,3,2,1,0:T(2,128)}), f32[8,8,3,2,16]{4,3,2,1,0:T(2,128)S(1)}, s32[]{:S(2)}) async-start(f32[8,8,4,2,16]{4,3,2,1,0:T(2,128)} %copy-done.3), calls=%async_computation.2 | async-start | bytes 393216 | tf_op jit(solution)/shard_map/slice | solution.py:144
  271.7 10.5 %copy-start.6 = (f32[10,10]{1,0:T(8,128)S(1)}, f32[10,10]{1,0:T(8,128)}, u32[]{:S(2)}) copy-start(f32[10,10]{1,0:T(8,128)} %param.37) | copy-start | bytes 1204
  283.5 5.8 %copy-start.7 = (f32[16,10]{1,0:T(8,128)S(1)}, f32[16,10]{1,0:T(8,128)}, u32[]{:S(2)}) copy-start(f32[16,10]{1,0:T(8,128)} %param.41) | copy-start | bytes 1924
  333.9 5.4 %copy-start.1 = (f32[128,10,10,10]{3,2,1,0:T(8,128)}, f32[128,10,10,10]{3,2,1,0:T(8,128)S(1)}, u32[]{:S(2)}) copy-start(f32[128,10,10,10]{3,2,1,0:T(8,128)S(1)} %broadcast_multiply_fusion) | copy-start | bytes 1536004
  368.3 18.9 %collective-permute-start.4 = (f32[8,8,2,16]{3,1,2,0:T(8,128)}, f32[8,8,2,16]{3,1,2,0:T(8,128)}, u32[]{:S(2)}, u32[]{:S(2)}) collective-permute-start(f32[8,8,2,16]{3,1,2,0:T(8,128)} %slice_bitcast_fusion.8), channel_id=1, source_target_pairs={{0,28},{4,0},{8,4},{12,8},{16,12},{20,16},{24,20},{28,24},{1,29},{... | collective-permute-start | bytes 24584 | tf_op jit(solution)/shard_map/ppermute | solution.py:13
  370.1 18.1 %collective-permute-start.5 = (f32[8,8,2,16]{3,1,2,0:T(8,128)}, f32[8,8,2,16]{3,1,2,0:T(8,128)}, u32[]{:S(2)}, u32[]{:S(2)}) collective-permute-start(f32[8,8,2,16]{3,1,2,0:T(8,128)} %slice_bitcast_fusion.7), channel_id=1, source_target_pairs={{0,4},{4,8},{8,12},{12,16},{16,20},{20,24},{24,28},{28,0},{1,5},{5... | collective-permute-start | bytes 24584 | tf_op jit(solution)/shard_map/ppermute | solution.py:13
  372.7 16.5 %collective-permute-start.6 = (f32[8,8,4,16]{3,1,2,0:T(8,128)}, f32[8,8,4,16]{3,1,2,0:T(8,128)}, u32[]{:S(2)}, u32[]{:S(2)}) collective-permute-start(f32[8,8,4,16]{3,1,2,0:T(8,128)} %get-tuple-element.176), channel_id=1, source_target_pairs={{0,3},{1,0},{2,1},{3,2},{4,7},{5,4},{6,5},{7,6},{8,11},{9,8},{10,9... | collective-permute-start | bytes 49160 | tf_op jit(solution)/shard_map/ppermute | solution.py:13
  373.9 16.3 %collective-permute-start.7 = (f32[8,8,4,16]{3,1,2,0:T(8,128)}, f32[8,8,4,16]{3,1,2,0:T(8,128)}, u32[]{:S(2)}, u32[]{:S(2)}) collective-permute-start(f32[8,8,4,16]{3,1,2,0:T(8,128)} %get-tuple-element.173), channel_id=1, source_target_pairs={{0,1},{1,2},{2,3},{3,0},{4,5},{5,6},{6,7},{7,4},{8,9},{9,10},{10,1... | collective-permute-start | bytes 49160 | tf_op jit(solution)/shard_map/ppermute | solution.py:13
  381.5 5.7 %copy-start.2 = (f32[1,8,8,4,2,16]{5,2,4,1,3,0:T(8,128)S(1)}, f32[1,8,8,4,2,16]{5,2,4,1,3,0:T(8,128)}, u32[]{:S(2)}) copy-start(f32[1,8,8,4,2,16]{5,2,4,1,3,0:T(8,128)} %copy.110) | copy-start | bytes 98308
where the time goes:
time: 417 us; the launch traced here: 410 us
  waiting for transfers between devices  183 us (44%)
  local copies, waits for them, and re-layouts  133 us (32%)
  matrix products  48.3 us (12%)
  starting transfers between devices  25.6 us (6%)
  other arithmetic  18.7 us (4%)
    all_to_all x1, waiting for transfers between devices, relocate(): lax.all_to_all(payload, ('gx', 'gy'), split_axis=0, concat_axis=0, tiled=...  183 us
    unnamed x31, local copies, waits for them, and re-layouts  28.7 us
    dot_general x1, matrix products, diag_solve(): jnp.einsum('wkn,ijwn->ijkn', stacked_w, section, precision=highest)  13.5 us
    dot_general x1, matrix products, diag_solve(): return jnp.einsum('wkn,uvkn->uvwn', stacked_w, section, precision=highest)  12.3 us
    ppermute x8, starting transfers between devices, shifted(): return lax.ppermute(value, axis, pairs)  12 us
    div x1, local copies, waits for them, and re-layouts, diag_solve(): modal = section / denom  11.1 us
    scatter-add x2, local copies, waits for them, and re-layouts, shards(): total.at[:, :, per_side - 1].add(to_last_w).at[:, :, 0].add(to_first_w)  10.7 us
    slice x1, local copies, waits for them, and re-layouts, shards(): out_wup = fixed[1:-1, 1:-1, -1]  10.5 us
  transfers between devices with their start and end apart: 10, of which 1 were waited for; matrix products, arithmetic and copies ran while one was open for 17% of the time, Pallas kernels for 0%

commit v1 on v0

v1 whole, which is shorter than its diff:
```python
import functools

import jax
import jax.numpy as jnp
import numpy as np
from jax import lax
from jax.experimental import pallas as pl
from jax.experimental.pallas import tpu as pltpu
from jax.sharding import PartitionSpec as P

BX = 4
BS = 2
FACE = 8
VMEM_LIMIT = 40 * 1024 * 1024
PARAMS = pltpu.CompilerParams(vmem_limit_bytes=VMEM_LIMIT)
HIGHEST = lax.Precision.HIGHEST
F32 = jnp.float32
BF16 = jnp.bfloat16


class Plan:
    def __init__(self, n_x, n_y, slots, fields, points, layers, extent):
        self.n_x, self.n_y = n_x, n_y
        self.devices = n_x * n_y
        self.lines = n_x // 2
        self.plane = self.devices // self.lines
        self.slots, self.fields, self.points = slots, fields, points
        self.layers, self.extent, self.side = layers, extent, extent - 2
        self.per_dev = BX * BS * layers
        self.cap = 2 * self.per_dev // self.devices
        self.msg_rows = self.lines * self.cap
        self.rows = self.plane * self.msg_rows
        full = self.plane * self.cap
        self.kept = [full] * self.lines
        self.offset = [sum(self.kept[:m]) for m in range(self.lines)]
        self.relay_rows = sum(self.kept) - full
        self.groups = [(0, 3), (3, 4), (7, 5)]


def halves(value, count):
    if count & (count - 1) == 0:
        return lax.shift_right_logical(value, int(count).bit_length() - 1)
    return value // count


def rest(value, count):
    if count & (count - 1) == 0:
        return value & (count - 1)
    return value % count


def three_terms(value):
    high = value.astype(BF16)
    left = value - high.astype(F32)
    middle = left.astype(BF16)
    low = (left - middle.astype(F32)).astype(BF16)
    return high, middle, low


def pick(chooser, value, contract=((1,), (0,))):
    high, middle, low = three_terms(value)
    dims = (contract, ((), ()))
    product = functools.partial(lax.dot_general, dimension_numbers=dims, preferred_element_type=F32)
    return (product(chooser, high) + product(chooser, middle)) + product(chooser, low)


def iota(shape, dim):
    return lax.broadcasted_iota(jnp.int32, shape, dim)


def before(count):
    return (iota((count, count), 0) < iota((count, count), 1)).astype(BF16)


def pack_kernel(plan, fields, marked, me_ref, place_ref, states_ref, *refs):
    outs, chooser_ref = refs[: plan.plane], refs[plan.plane]
    field = pl.program_id(0)
    rows = plan.msg_rows

    @pl.when(field == 0)
    def _():
        me = me_ref[0]
        new_place = place_ref[...]
        live = new_place >= 0
        placed = jnp.maximum(new_place, 0)
        column = halves(placed, plan.layers)
        layer_pos = rest(placed, plan.layers)
        span = BS * plan.n_y
        elem_x = halves(column, span)
        elem_s = rest(column, span)
        target = halves(elem_x, BX) * plan.n_y + halves(elem_s, BS)
        local_row = (rest(elem_x, BX) * BS + rest(elem_s, BS)) * plan.layers + layer_pos
        target = jnp.where(live, target, -1)
        hot = iota((plan.devices, plan.slots), 0) == target
        earlier = jnp.dot(hot.astype(BF16), before(plan.slots), preferred_element_type=F32)
        rank = jnp.sum(jnp.where(hot, earlier, 0.0), axis=0, keepdims=True).astype(jnp.int32)
        across = target ^ me
        row = rest(across, plan.plane) * rows + halves(across, plan.plane) * plan.cap + rank
        row = jnp.where(live, row, -1)
        chooser = (iota((plan.rows, plan.slots), 0) == row).astype(F32)
        chooser_ref[...] = chooser.astype(BF16)
        if marked:
            marks = lax.dot_general(
                jnp.broadcast_to((local_row + 1).astype(F32), (8, plan.slots)),
                chooser,
                (((1,), (1,)), ((), ())),
                precision=HIGHEST,
                preferred_element_type=F32,
            )
            for out in outs:
                out[fields * rows : fields * rows + 8, :] = jnp.zeros((8, plan.points), F32)
                out[fields * rows : fields * rows + 8, : plan.rows] = marks

    moved = pick(chooser_ref[...], states_ref[0])
    start = pl.multiple_of(field * rows, rows)
    for j, out in enumerate(outs):
        out[pl.ds(start, rows), :] = moved[j * rows : (j + 1) * rows]


def whole(shape):
    return pl.BlockSpec(shape, lambda *_: (0,) * len(shape))


def pack(plan, group, me, place_row, states, marked):
    first, fields = group
    shape = (fields * plan.msg_rows + (8 if marked else 0), plan.points)
    return pl.pallas_call(
        functools.partial(pack_kernel, plan, fields, marked),
        grid=(fields,),
        in_specs=[
            pl.BlockSpec(memory_space=pltpu.SMEM),
            whole((1, plan.slots)),
            pl.BlockSpec((1, plan.slots, plan.points), lambda f: (first + f, 0, 0)),
        ],
        out_specs=[whole(shape)] * plan.plane,
        out_shape=[jax.ShapeDtypeStruct(shape, F32)] * plan.plane,
        scratch_shapes=[pltpu.VMEM((plan.rows, plan.slots), BF16)],
        compiler_params=PARAMS,
    )(me, place_row, states)


def route_rows(plan, marks):
    lane = iota((1, plan.rows), 1)
    step = rest(halves(lane, plan.cap), plan.lines)
    filled = marks[:1] > 0.0
    valid = (iota((plan.lines, plan.rows), 0) == step) & filled
    earlier = jnp.dot(valid.astype(BF16), before(plan.rows), preferred_element_type=F32)
    earlier = earlier.astype(jnp.int32)
    row = halves(lane, plan.msg_rows) * plan.cap + rest(lane, plan.cap)
    for m in range(1, plan.lines):
        place = jnp.where(earlier[m : m + 1] < plan.kept[m], earlier[m : m + 1] + plan.offset[m], -1)
        row = jnp.where(step == m, place, row)
    return jnp.where(filled, row, -1)


def gather_marks(plan, fields, messages):
    lane = iota((8, plan.rows), 1)
    marks = jnp.zeros((8, plan.rows), F32)
    base = fields * plan.msg_rows
    for j, message in enumerate(messages):
        part = message[base : base + 8, : plan.rows]
        marks = jnp.where(halves(lane, plan.msg_rows) == j, part, marks)
    return marks


def relay_kernel(plan, fields, marked, *refs):
    messages = refs[: plan.plane]
    refs = refs[plan.plane :]
    if not marked:
        marks_ref, refs = refs[0], refs[1:]
    outs, refs = refs[: plan.lines - 1], refs[plan.lines - 1 :]
    if marked:
        marks = gather_marks(plan, fields, messages)
        marks_out, own_out = refs[:2]
        refs = refs[2:]
        marks_out[...] = marks
    else:
        marks = marks_ref[...]
    (held,) = refs
    row = route_rows(plan, marks)
    spread = (iota((plan.rows, plan.rows), 0) == row).astype(F32)
    if marked:
        landed = lax.dot_general(
            marks, spread, (((1,), (1,)), ((), ())), precision=HIGHEST, preferred_element_type=F32
        )
        own_out[...] = landed
        for m, out in enumerate(outs, 1):
            base = fields * plan.kept[m]
            out[base : base + 8, :] = jnp.zeros((8, plan.points), F32)
            out[base : base + 8, : plan.rows] = landed
    first = plan.offset[1]
    chooser = spread[first : first + plan.relay_rows].astype(BF16)
    for field in range(fields):
        for j, message in enumerate(messages):
            held[j * plan.msg_rows : (j + 1) * plan.msg_rows, :] = message[
                field * plan.msg_rows : (field + 1) * plan.msg_rows, :
            ]
        moved = pick(chooser, held[...])
        for m, out in enumerate(outs, 1):
            at = plan.offset[m] - first
            out[field * plan.kept[m] : (field + 1) * plan.kept[m], :] = moved[at : at + plan.kept[m]]


def relay(plan, group, messages, marks):
    _, fields = group
    marked = marks is None
    extra = 8 if marked else 0
    out_shape = [
        jax.ShapeDtypeStruct((fields * plan.kept[m] + extra, plan.points), F32) for m in range(1, plan.lines)
    ]
    if marked:
        out_shape += [jax.ShapeDtypeStruct((8, plan.rows), F32)] * 2
    operands = list(messages) + ([] if marked else [marks])
    result = pl.pallas_call(
        functools.partial(relay_kernel, plan, fields, marked),
        in_specs=[pl.BlockSpec(memory_space=pltpu.VMEM)] * len(operands),
        out_specs=[pl.BlockSpec(memory_space=pltpu.VMEM)] * len(out_shape),
        out_shape=out_shape,
        scratch_shapes=[pltpu.VMEM((plan.rows, plan.points), F32)],
        compiler_params=PARAMS,
    )(*operands)
    return result[: plan.lines - 1], result[plan.lines - 1 :]


def settle_kernel(plan, fields, marked, *refs):
    messages, refs = refs[: plan.plane], refs[plan.plane :]
    relays, refs = refs[: plan.lines - 1], refs[plan.lines - 1 :]
    if marked:
        own_ref, order_ref = refs[:2]
        out, marks_out, cells_out = refs[2:5]
        refs = refs[5:]
    else:
        marks_ref = refs[0]
        out = refs[2]
        refs = refs[3:]
    chooser_ref, held = refs[:2]
    field = pl.program_id(0)
    full = plan.kept[0]

    @pl.when(field == 0)
    def _():
        if marked:
            lane = iota((8, plan.rows), 1)
            marks = jnp.where(lane < full, own_ref[...], 0.0)
            for m in range(1, plan.lines):
                base = fields * plan.kept[m]
                part = relays[m - 1][base : base + 8, : plan.rows]
                inside = (lane >= plan.offset[m]) & (lane < plan.offset[m] + plan.kept[m])
                marks = jnp.where(inside, part, marks)
            marks_out[...] = marks
        else:
            marks = marks_ref[...]
        element = iota((plan.per_dev, plan.rows), 0).astype(F32) + 1.0
        chooser_ref[...] = (element == marks[:1]).astype(F32).astype(BF16)
        used = plan.offset[-1] + plan.kept[-1]
        if used < plan.rows:
            held[used:, :] = jnp.zeros((plan.rows - used, plan.points), F32)

    start = field * plan.msg_rows
    for j, message in enumerate(messages):
        held[j * plan.cap : (j + 1) * plan.cap, :] = message[pl.ds(start, plan.msg_rows), :][: plan.cap]
    for m, part in enumerate(relays, 1):
        kept = plan.kept[m]
        held[plan.offset[m] : plan.offset[m] + kept, :] = part[pl.ds(pl.multiple_of(field * kept, 8), kept), :]
    placed = pick(chooser_ref[...], held[...])
    out[...] = placed.reshape(out.shape)

    if marked:
        pressure_ref = refs[2]

        @pl.when(field == 0)
        def _():
            pressure_ref[...] = 3.0 * placed

        @pl.when(field == 1)
        def _():
            pressure_ref[...] = pressure_ref[...] - 3.0 * placed

        @pl.when(field == 2)
        def _():
            cells_out[...] = pick(order_ref[...], pressure_ref[...] + placed, ((1,), (1,)))


def cell_order(side):
    rows = []
    for k in range(side):
        rows += [(i * side + j) * side + k for i in range(side) for j in range(side)]
        rows += [(i * side + side - 1) * side + k for i in range(side)]
        rows += [(i * side) * side + k for i in range(side)]
    order = np.zeros((len(rows), side**3), np.float32)
    order[np.arange(len(rows)), rows] = 1.0
    return order


def settle(plan, group, messages, relays, marks, buffer, own, order):
    first, fields = group
    marked = marks is None
    columns = BX * BS
    states_shape = (columns, plan.fields, plan.layers, plan.points)
    out_specs = [pl.BlockSpec((columns, 1, plan.layers, plan.points), lambda f: (0, first + f, 0, 0))]
    out_shape = [jax.ShapeDtypeStruct(states_shape, F32)]
    scratch = [pltpu.VMEM((plan.per_dev, plan.rows), BF16), pltpu.VMEM((plan.rows, plan.points), F32)]
    operands = list(messages) + list(relays)
    aliases = {}
    if marked:
        operands += [own, order]
        cells = (order.shape[0], plan.per_dev)
        out_specs += [whole((8, plan.rows)), whole(cells)]
        out_shape += [jax.ShapeDtypeStruct((8, plan.rows), F32), jax.ShapeDtypeStruct(cells, F32)]
        scratch += [pltpu.VMEM((plan.per_dev, plan.points), F32)]
        in_specs = [whole(o.shape) for o in operands]
    else:
        operands += [marks, buffer]
        in_specs = [whole(o.shape) for o in operands[:-1]] + [pl.BlockSpec(memory_space=pl.ANY)]
        aliases = {len(operands) - 1: 0}
    return pl.pallas_call(
        functools.partial(settle_kernel, plan, fields, marked),
        grid=(fields,),
        in_specs=in_specs,
        out_specs=out_specs,
        out_shape=out_shape,
        scratch_shapes=scratch,
        input_output_aliases=aliases,
        compiler_params=PARAMS,
    )(*operands)


def lane_steps(plan):
    lane = iota((FACE, plan.per_dev), 1)
    layer = rest(lane, plan.layers)
    row_s = rest(halves(lane, plan.layers), BS)
    row_x = halves(lane, plan.layers * BS)
    return layer, row_s, row_x


def roll(value, steps):
    return pltpu.roll(value, steps % value.shape[1], 1)


def solve_kernel(plan, cells, from_xlow, from_xup, from_slow, from_sup, mix, mix_t, weights, sum_xs, values_w, *refs):
    total, out_xlow, out_xup, out_slow, out_sup, box, section, modal = refs
    side, extent = plan.side, plan.extent
    layer, row_s, row_x = lane_steps(plan)
    points = side * side
    stride = points + 2 * FACE
    width = plan.layers
    wide = width * BS
    box_rows = points + 4 * FACE

    def cell(k, start):
        return cells[k * stride + start : k * stride + start + FACE, :]

    def piece(ref, k):
        return ref[k * FACE : (k + 1) * FACE, :]

    for k in range(side):
        w = k + 1
        for i in range(side):
            box[w * box_rows + i * FACE : w * box_rows + (i + 1) * FACE, :] = cell(k, i * FACE)
        at = w * box_rows + points
        low = jnp.where(row_x == 0, roll(piece(from_xlow, k), wide), roll(cell(k, points - FACE), wide))
        up = jnp.where(row_x == BX - 1, roll(piece(from_xup, k), -wide), roll(cell(k, 0), -wide))
        box[at : at + FACE, :] = low
        box[at + FACE : at + 2 * FACE, :] = up
        top, bottom = cell(k, points), cell(k, points + FACE)
        back = (BS - 1) * width
        low = jnp.where(row_s == 0, roll(piece(from_slow, k), -back), roll(top, width))
        up = jnp.where(row_s == BS - 1, roll(piece(from_sup, k), back), roll(bottom, -width))
        box[at + 2 * FACE : at + 3 * FACE, :] = low
        box[at + 3 * FACE : at + 4 * FACE, :] = up
    last = (extent - 1) * box_rows
    for i in range(side):
        below = jnp.where(layer == 0, 0.0, roll(cell(side - 1, i * FACE), 1))
        above = jnp.where(layer == width - 1, 0.0, roll(cell(0, i * FACE), -1))
        box[i * FACE : (i + 1) * FACE, :] = below
        box[last + i * FACE : last + (i + 1) * FACE, :] = above

    modal_rows = mix.shape[0]
    lanes = plan.per_dev
    for w in range(extent):
        rows = points if w in (0, extent - 1) else box_rows
        section[w] = jnp.dot(
            mix[:, :rows], box[w * box_rows : w * box_rows + rows, :], precision=HIGHEST, preferred_element_type=F32
        )
    for block in range(0, modal_rows, FACE):
        held = [section[w, block : block + FACE, :] for w in range(extent)]
        out = [None] * extent
        base = jnp.broadcast_to(sum_xs[block : block + FACE, :], (FACE, lanes))
        for k in range(extent):
            value = None
            for w in range(extent):
                term = weights[w, k : k + 1, :] * held[w]
                value = term if value is None else value + term
            value = value / (base + values_w[k : k + 1, :])
            for w in range(extent):
                term = weights[w, k : k + 1, :] * value
                out[w] = term if out[w] is None else out[w] + term
        for w in range(extent):
            modal[w, block : block + FACE, :] = out[w]
    for w in range(extent):
        rows = points if w in (0, extent - 1) else box_rows
        box[w * box_rows : w * box_rows + rows, :] = jnp.dot(
            mix_t[:rows, :], modal[w], precision=HIGHEST, preferred_element_type=F32
        )

    for k in range(side):
        at = (k + 1) * box_rows
        total[k * points : (k + 1) * points, :] = box[at : at + points, :]
        for out, shift in ((out_xlow, 0), (out_xup, 1), (out_slow, 2), (out_sup, 3)):
            start = at + points + shift * FACE
            out[k * FACE : (k + 1) * FACE, :] = box[start : start + FACE, :]
    for i in range(side):
        below = jnp.where(layer == width - 1, 0.0, roll(box[i * FACE : (i + 1) * FACE, :], -1))
        above = jnp.where(layer == 0, 0.0, roll(box[last + i * FACE : last + (i + 1) * FACE, :], 1))
        top = (side - 1) * points + i * FACE
        total[top : top + FACE, :] += below
        total[i * FACE : (i + 1) * FACE, :] += above


def finish_kernel(plan, total, xlow, xup, slow, sup, from_x_up, from_x_low, from_s_up, from_s_low, out, held):
    side = plan.side
    points = side * side
    layer, row_s, row_x = lane_steps(plan)
    width = plan.layers
    wide = width * BS
    back = (BS - 1) * width
    sub = iota((FACE, plan.per_dev), 0)
    for k in range(side):
        part = slice(k * FACE, (k + 1) * FACE)
        rows = [total[k * points + i * FACE : k * points + (i + 1) * FACE, :] for i in range(side)]
        rows[side - 1] = rows[side - 1] + jnp.where(
            row_x == BX - 1, roll(from_x_up[part, :], -wide), roll(xlow[part, :], -wide)
        )
        rows[0] = rows[0] + jnp.where(row_x == 0, roll(from_x_low[part, :], wide), roll(xup[part, :], wide))
        to_last = jnp.where(row_s == BS - 1, roll(from_s_up[part, :], back), roll(slow[part, :], -width))
        to_first = jnp.where(row_s == 0, roll(from_s_low[part, :], -back), roll(sup[part, :], width))
        for i in range(side):
            last = jnp.broadcast_to(to_last[i : i + 1, :], sub.shape)
            first = jnp.broadcast_to(to_first[i : i + 1, :], sub.shape)
            value = rows[i] + jnp.where(sub == side - 1, last, 0.0) + jnp.where(sub == 0, first, 0.0)
            held[k * points + i * FACE : k * points + (i + 1) * FACE, :] = value
    lanes = plan.layers * side
    source = iota((plan.per_dev, lanes), 0)
    lane = iota((plan.per_dev, lanes), 1)
    terms = three_terms(held[...])
    kept = rest(iota((points, lanes), 1), side)
    for column in range(BX * BS):
        chooser = (source == halves(lane, side) + column * plan.layers).astype(F32).astype(BF16)
        high, middle, low = [jnp.dot(t, chooser, preferred_element_type=F32) for t in terms]
        spread = (high + middle) + low
        value = jnp.zeros((points, lanes), F32)
        for k in range(side):
            value = jnp.where(kept == k, spread[k * points : (k + 1) * points], value)
        b, s = column // BS, column % BS
        for i in range(side):
            out[b * side + i, s * side : (s + 1) * side, :] = value[i * side : (i + 1) * side]


def simple_call(kernel, operands, out_shape, scratch):
    return pl.pallas_call(
        kernel,
        in_specs=[pl.BlockSpec(memory_space=pltpu.VMEM)] * len(operands),
        out_specs=[pl.BlockSpec(memory_space=pltpu.VMEM)] * len(out_shape),
        out_shape=out_shape,
        scratch_shapes=scratch,
        compiler_params=PARAMS,
    )(*operands)


def box_tables(plan, vectors_x, vectors_s, vectors_w, values_x, values_s, values_w):
    extent = plan.extent
    rim = [0, extent - 1]
    inside = slice(1, extent - 1)

    def kron(left, right):
        return (left[:, None, :, None] * right[None, :, None, :]).reshape(
            left.shape[0] * right.shape[0], extent * extent
        )

    ends_x = jnp.stack([vectors_x[r] for r in rim])
    ends_s = jnp.stack([vectors_s[r] for r in rim])
    mix_t = jnp.concatenate(
        [
            kron(vectors_x[inside], vectors_s[inside]),
            kron(ends_x, vectors_s[inside]),
            kron(ends_s, vectors_x[inside]).reshape(-1, extent, extent).swapaxes(1, 2).reshape(-1, extent * extent),
        ]
    )
    modal_rows = -(-extent * extent // FACE) * FACE
    more = modal_rows - extent * extent
    mix_t = jnp.pad(mix_t, ((0, 0), (0, more)))
    sum_xs = (values_x[:, None] + values_s[None, :]).reshape(-1, 1)
    sum_xs = jnp.pad(sum_xs, ((0, more), (0, 0)), constant_values=1.0)
    columns = BX * BS
    weights = jnp.tile(jnp.transpose(vectors_w, (1, 2, 0)), (1, 1, columns))
    lane_values = jnp.tile(values_w.T, (1, columns))
    return mix_t.T, mix_t, weights, sum_xs, lane_values


def shards(old_states, new_place, vectors_x, vectors_s, vectors_w, values_x, values_s, values_w):
    n_x, n_y = lax.axis_size("gx"), lax.axis_size("gy")
    slots, fields, points = old_states.shape
    plan = Plan(n_x, n_y, slots, fields, points, vectors_w.shape[0], vectors_x.shape[0])
    place = lax.axis_index("gx") * n_y + lax.axis_index("gy")
    me = place.astype(jnp.int32).reshape(1)
    states = jnp.transpose(old_states, (1, 0, 2))
    place_row = new_place.reshape(1, slots)
    both = ("gx", "gy")

    def across(value, flip):
        return lax.ppermute(value, both, [(d, d ^ flip) for d in range(plan.devices)])

    def shifted(value, axis, steps):
        count = lax.axis_size(axis)
        return lax.ppermute(value, axis, [(s, (s + steps) % count) for s in range(count)])

    order = jnp.asarray(cell_order(plan.side), BF16)
    tables = box_tables(plan, vectors_x, vectors_s, vectors_w, values_x, values_s, values_w)

    packed = [pack(plan, group, me, place_row, states, g == 0) for g, group in enumerate(plan.groups)]
    marks = None
    held = []
    for group, sent in zip(plan.groups, packed):
        messages = [sent[0]] + [across(sent[j], j) for j in range(1, plan.plane)]
        relays, more = relay(plan, group, messages, marks)
        if marks is None:
            marks, own = more
        arrived = [across(relays[m - 1], m * plan.plane) for m in range(1, plan.lines)]
        held.append((messages, arrived))

    buffer, row_marks, cells = settle(plan, plan.groups[0], *held[0], None, None, own, order)
    side = plan.side
    face = jax.ShapeDtypeStruct((side * FACE, plan.per_dev), F32)
    layered = cells.reshape(side, side * side + 2 * FACE, plan.per_dev)

    def rows(start):
        return layered[:, start : start + FACE].reshape(side * FACE, plan.per_dev)

    inner = side * side
    halo = [
        shifted(rows(inner - FACE), "gx", 1),
        shifted(rows(0), "gx", -1),
        shifted(rows(inner), "gy", 1),
        shifted(rows(inner + FACE), "gy", -1),
    ]
    modal_rows = tables[0].shape[0]
    total, xlow, xup, slow, sup = simple_call(
        functools.partial(solve_kernel, plan),
        [cells, *halo, *tables],
        [jax.ShapeDtypeStruct((side * inner, plan.per_dev), F32)] + [face] * 4,
        [pltpu.VMEM((plan.extent * (inner + 4 * FACE), plan.per_dev), F32)]
        + [pltpu.VMEM((plan.extent, modal_rows, plan.per_dev), F32)] * 2,
    )
    returned = [shifted(xlow, "gx", -1), shifted(xup, "gx", 1), shifted(slow, "gy", -1), shifted(sup, "gy", 1)]
    (correction,) = simple_call(
        functools.partial(finish_kernel, plan),
        [total, xlow, xup, slow, sup, *returned],
        [jax.ShapeDtypeStruct((BX * side, BS * side, plan.layers * side), F32)],
        [pltpu.VMEM((side * inner, plan.per_dev), F32)],
    )
    for group, (messages, arrived) in zip(plan.groups[1:], held[1:]):
        (buffer,) = settle(plan, group, messages, arrived, row_marks, buffer, None, None)
    new_states = buffer.reshape(BX, BS, fields, plan.layers, points).transpose(0, 1, 3, 2, 4)
    return new_states, correction


def solution(mesh):
    placed = (P(("gx", "gy"), None, None), P(("gx", "gy")), P(), P(), P(), P(), P(), P())
    return jax.shard_map(
        shards,
        mesh=mesh,
        in_specs=placed,
        out_specs=(P("gx", "gy", None, None, None), P("gx", "gy", None)),
        check_vma=False,
    )
```

time: 417 us -> 266 us (0.64)
  the two profiles are of different devices: /device:TPU:1 before, /device:TPU:11 now
where the time goes in v1:
time: 266 us; the launch traced here: 262 us
  waiting for transfers between devices  168 us (63%)
  local copies, waits for them, and re-layouts  32.4 us (12%)
  starting transfers between devices  28.7 us (11%)
  Pallas kernels  27.7 us (10%)
  other arithmetic  4.43 us (2%)
    ppermute x30, waiting for transfers between devices, across(): lax.ppermute(value, both, [(d, d ^ flip) for d in range(plan.devices)])  98.2 us
    ppermute x8, waiting for transfers between devices, shifted(): lax.ppermute(value, axis, [(s, (s + steps) % count) for s in range(count)])  69.7 us
    ppermute x30, starting transfers between devices, across(): lax.ppermute(value, both, [(d, d ^ flip) for d in range(plan.devices)])  21.4 us
    unnamed x110, local copies, waits for them, and re-layouts  21.4 us
    pallas_call x3, Pallas kernels, settle(): pl.pallas_call(functools.partial(settle_kernel, plan, fields, marked), gr...  10.4 us
    pallas_call x3, Pallas kernels, pack(): pl.pallas_call(functools.partial(pack_kernel, plan, fields, marked), grid...  7.51 us
    ppermute x8, starting transfers between devices, shifted(): lax.ppermute(value, axis, [(s, (s + steps) % count) for s in range(count)])  7.29 us
  transfers between devices with their start and end apart: 38, of which 16 were waited for; matrix products, arithmetic and copies ran while one was open for 6% of the time, Pallas kernels for 9%

profile of v1, /device:TPU:11, one launch (start us, length us, event | category | flops | bytes accessed | tf_op | source)
XLA Modules:
  0.0 262.2 jit_solution(15749776660706425201)
XLA Ops:
  0.6 2.8 %copy-done = f32[256,12,512]{2,0,1:T(8,128)S(1)} copy-done((f32[256,12,512]{2,0,1:T(8,128)S(1)}, f32[256,12,512]{2,0,1:T(8,128)}, u32[]{:S(2)}) %copy-start) | copy-done | bytes 6291480
  4.1 1.8 shard_map.105
  6.7 1.3 collective-permute-start.8
  8.6 1.5 collective-permute-start.11
  10.2 2.6 shard_map.109
  13.5 1.2 collective-permute-start.12
  14.7 3.8 %collective-permute-done.9.refs_3_ = f32[104,512]{1,0:T(8,128)S(1)} collective-permute-done((f32[104,512]{1,0:T(8,128)S(1)}, f32[104,512]{1,0:T(8,128)S(1)}, u32[]{:S(2)}, u32[]{:S(2)}) %collective-permute-start.9) | collective-permute-done | bytes 213024 | tf_op jit(solution)/shard_map/ppermute | solution.py:511
  18.5 1.0 collective-permute-start.13
  20.5 1.3 collective-permute-start.22
  21.8 3.4 %collective-permute-done.12.refs_6_ = f32[104,512]{1,0:T(8,128)S(1)} collective-permute-done((f32[104,512]{1,0:T(8,128)S(1)}, f32[104,512]{1,0:T(8,128)S(1)}, u32[]{:S(2)}, u32[]{:S(2)}) %collective-permute-start.12) | collective-permute-done | bytes 213024 | tf_op jit(solution)/shard_map/ppermute | solution.py:511
  25.4 5.2 %collective-permute-done.13.refs_7_ = f32[104,512]{1,0:T(8,128)S(1)} collective-permute-done((f32[104,512]{1,0:T(8,128)S(1)}, f32[104,512]{1,0:T(8,128)S(1)}, u32[]{:S(2)}, u32[]{:S(2)}) %collective-permute-start.13) | collective-permute-done | bytes 213024 | tf_op jit(solution)/shard_map/ppermute | solution.py:511
  30.6 2.0 shard_map.106
  32.8 3.0 %collective-permute-done.21.refs_2_ = f32[128,512]{1,0:T(8,128)S(1)} collective-permute-done((f32[128,512]{1,0:T(8,128)S(1)}, f32[128,512]{1,0:T(8,128)S(1)}, u32[]{:S(2)}, u32[]{:S(2)}) %collective-permute-start.21) | collective-permute-done | bytes 262176 | tf_op jit(solution)/shard_map/ppermute | solution.py:511
  36.0 6.1 %collective-permute-done.22.refs_3_ = f32[128,512]{1,0:T(8,128)S(1)} collective-permute-done((f32[128,512]{1,0:T(8,128)S(1)}, f32[128,512]{1,0:T(8,128)S(1)}, u32[]{:S(2)}, u32[]{:S(2)}) %collective-permute-start.22) | collective-permute-done | bytes 262176 | tf_op jit(solution)/shard_map/ppermute | solution.py:511
  42.7 3.1 %shard_map.104 = (f32[160,512]{1,0:T(8,128)S(1)}, f32[160,512]{1,0:T(8,128)}, f32[160,512]{1,0:T(8,128)}, f32[160,512]{1,0:T(8,128)S(1)}, f32[160,512]{1,0:T(8,1...) custom-call(s32[1]{0:T(128)} %bitcast.me_ref, s32[1,256]{1,0:T(1,128)S(1)} %bitcast.39, ...), custom_call_target="tpu_custom_call" | custom-call | tf_op jit(solution)/shard_map/pallas_call | solution.py:127
  49.7 2.4 collective-permute-start.18
  52.1 0.8 broadcast_multiply_fusion.1
  53.6 1.0 collective-permute-start.1
  54.5 0.8 collective-permute-start.2
  55.9 1.8 shard_map.110
  57.8 0.8 copy-done.38
  58.6 0.8 copy-done.40
  59.4 19.7 %collective-permute-done.18.refs_9_ = f32[200,512]{1,0:T(8,128)S(1)} collective-permute-done((f32[200,512]{1,0:T(8,128)}, f32[200,512]{1,0:T(8,128)S(1)}, u32[]{:S(2)}, u32[]{:S(2)}) %collective-permute-start.18) | collective-permute-done | bytes 409632 | tf_op jit(solution)/shard_map/ppermute | solution.py:511
  79.2 8.6 %collective-permute-done.19.refs_10_ = f32[200,512]{1,0:T(8,128)S(1)} collective-permute-done((f32[200,512]{1,0:T(8,128)}, f32[200,512]{1,0:T(8,128)S(1)}, u32[]{:S(2)}, u32[]{:S(2)}) %collective-permute-start.19) | collective-permute-done | bytes 409632 | tf_op jit(solution)/shard_map/ppermute | solution.py:511
  87.8 0.9 copy-done.12
  88.8 0.9 copy-done.14
  89.7 0.9 copy-done.16
  90.6 0.9 copy-done.18
  91.6 0.9 copy-done.20
  92.5 0.9 copy-done.22
  93.4 0.9 copy-done.24
  94.4 0.9 copy-done.26
  95.3 1.1 copy-done.27
  96.4 3.8 %shard_map.108 = (f32[8,12,16,512]{3,2,1,0:T(8,128)}, f32[8,256]{1,0:T(8,128)S(1)}, f32[640,128]{1,0:T(8,128)S(1)}) custom-call(f32[104,512]{1,0:T(8,128)S(1)} %copy-done.12, f32[104,512]{1,0:T(8,128)S(1)} %copy-done.14, f32[104,512]{1,0:T(8,128)S(1)} %copy-done.16, f32[104,512]{1,0:T(8,128)S(1)} %copy-done.18, f32[104,512]{1,0:T(8,128)S(1)} %copy-done.20, ...), custom_call_target="tpu_custom_call" | custom-call | tf_op jit(solution)/shard_map/pallas_call | solution.py:316
  102.1 1.3 collective-permute-start.32
  103.3 1.2 collective-permute-start.31
  104.6 2.0 collective-permute-start.30
  109.5 1.0 copy.33
  110.5 1.0 mul.72
  111.9 1.5 collective-permute-start.4
  114.0 2.2 collective-permute-start.6
  116.2 1.6 broadcast_multiply_fusion
  117.8 1.8 mul.68
  119.6 1.5 copy.31
  121.1 1.4 select_maximum_fusion
  122.5 0.9 copy.36.mix
  123.4 0.9 pad.9.sum_xs
  124.4 1.0 copy-done.29
  125.3 0.8 copy-done.30
  126.8 0.8 copy-done.33
  127.6 3.0 %shard_map.113 = (f32[512,128]{1,0:T(8,128)S(1)}, f32[64,128]{1,0:T(8,128)S(1)}, f32[64,128]{1,0:T(8,128)S(1)}, f32[64,128]{1,0:T(8,128)S(1)}, f32[64,128]{1,0:T(8,128)S(1)}) custom-call(f32[640,128]{1,0:T(8,128)S(1)} %copy-done.29, f32[64,128]{1,0:T(8,128)} %collective-permute-done.30.from_xlow, f32[64,128]{1,0:T(8,128)} %collective-permute-done.31.from_xup, ...), custom_call_target="tpu_custom_call" | custom-call | tf_op jit(solution)/shard_map/pallas_call | solution.py:460
  130.7 6.5 %collective-permute-done.5.refs_6_ = f32[160,512]{1,0:T(8,128)S(1)} collective-permute-done((f32[160,512]{1,0:T(8,128)}, f32[160,512]{1,0:T(8,128)S(1)}, u32[]{:S(2)}, u32[]{:S(2)}) %collective-permute-start.5) | collective-permute-done | bytes 327712 | tf_op jit(solution)/shard_map/ppermute | solution.py:511
  137.2 7.0 %collective-permute-done.6.refs_7_ = f32[160,512]{1,0:T(8,128)S(1)} collective-permute-done((f32[160,512]{1,0:T(8,128)}, f32[160,512]{1,0:T(8,128)S(1)}, u32[]{:S(2)}, u32[]{:S(2)}) %collective-permute-start.6) | collective-permute-done | bytes 327712 | tf_op jit(solution)/shard_map/ppermute | solution.py:511
  144.2 1.3 shard_map.107
  145.5 2.3 collective-permute-start.15
  148.9 66.5 %collective-permute-done.35.from_x_low = f32[64,128]{1,0:T(8,128)S(1)} collective-permute-done((f32[64,128]{1,0:T(8,128)S(1)}, f32[64,128]{1,0:T(8,128)S(1)}, u32[]{:S(2)}, u32[]{:S(2)}) %collective-permute-start.35) | collective-permute-done | bytes 32800 | tf_op jit(solution)/shard_map/ppermute | solution.py:515
  215.4 1.5 collective-permute-start.36
  216.9 2.0 collective-permute-done.36.from_s_up
  218.9 1.2 collective-permute-done.37.from_s_low
  220.2 1.8 shard_map.114
  221.9 19.1 %collective-permute-done.28.refs_9_ = f32[256,512]{1,0:T(8,128)S(1)} collective-permute-done((f32[256,512]{1,0:T(8,128)S(1)}, f32[256,512]{1,0:T(8,128)S(1)}, u32[]{:S(2)}, u32[]{:S(2)}) %collective-permute-start.28) | collective-permute-done | bytes 524320 | tf_op jit(solution)/shard_map/ppermute | solution.py:511
  241.0 14.6 %collective-permute-done.29.refs_10_ = f32[256,512]{1,0:T(8,128)S(1)} collective-permute-done((f32[256,512]{1,0:T(8,128)S(1)}, f32[256,512]{1,0:T(8,128)S(1)}, u32[]{:S(2)}, u32[]{:S(2)}) %collective-permute-start.29) | collective-permute-done | bytes 524320 | tf_op jit(solution)/shard_map/ppermute | solution.py:511
  255.6 3.5 %shard_map.111.refs_12_ = f32[8,12,16,512]{3,2,1,0:T(8,128)} custom-call(f32[128,512]{1,0:T(8,128)S(1)} %get-tuple-element.70.refs_0_, f32[128,512]{1,0:T(8,128)S(1)} %collective-permute-done.20.refs_1_, f32[128,512]{1,0:T(8,128)S(1)} %collective-permute-done.21.refs_2_, f32[128,512]{1,0:T(8,128)S(1)} %copy-done.2, ...), custom_call_target="tpu_custom_call", output_to_operand_aliasing={{}: (12, {})} | custom-call | tf_op jit(solution)/shard_map/pallas_call | solution.py:316
  259.1 3.1 %shard_map.112 = f32[8,12,16,512]{3,2,1,0:T(8,128)} custom-call(f32[160,512]{1,0:T(8,128)S(1)} %get-tuple-element.45.refs_0_, f32[160,512]{1,0:T(8,128)S(1)} %collective-permute-done.refs_1_, f32[160,512]{1,0:T(8,128)S(1)} %collective-permute-done.1.refs_2_, f32[160,512]{1,0:T(8,128)S(1)} %collective-permute-done.2.refs_3_, ...), custom_call_target="tpu_custom_call", output_to_operand_aliasing={{}: (12, {})} | custom-call | tf_op jit(solution)/shard_map/pallas_call | solution.py:316
  (166 shorter events, 18.1 us)
Async XLA Ops:
  4.1 38.6 %slice-start = ((s8[6291456]{0:T(1024)(128)(4,1)}), s8[4194304]{0:T(1024)(128)(4,1)S(1)}, s32[]{:S(2)}) async-start(s8[6291456]{0:T(1024)(128)(4,1)} %bitcast.33), calls=%async_computation | async-start | bytes 8388608
  5.9 24.7 %copy-start.11 = (f32[104,512]{1,0:T(8,128)}, f32[104,512]{1,0:T(8,128)S(1)}, u32[]{:S(2)}) copy-start(f32[104,512]{1,0:T(8,128)S(1)} %get-tuple-element.53.refs_0_) | copy-start | bytes 638980
  5.9 6.9 %collective-permute-start.7 = (f32[104,512]{1,0:T(8,128)S(1)}, f32[104,512]{1,0:T(8,128)S(1)}, u32[]{:S(2)}, u32[]{:S(2)}) collective-permute-start(f32[104,512]{1,0:T(8,128)S(1)} %get-tuple-element.54), channel_id=1, source_target_pairs={{0,1},{1,0},{2,3},{3,2},{4,5},{5,4},{6,7},{7,6},{8,9},{9,8},{10,11... | collective-permute-start | bytes 638984 | tf_op jit(solution)/shard_map/ppermute | solution.py:511
  6.7 6.8 %collective-permute-start.8 = (f32[104,512]{1,0:T(8,128)S(1)}, f32[104,512]{1,0:T(8,128)S(1)}, u32[]{:S(2)}, u32[]{:S(2)}) collective-permute-start(f32[104,512]{1,0:T(8,128)S(1)} %get-tuple-element.55), channel_id=1, source_target_pairs={{0,2},{1,3},{2,0},{3,1},{4,6},{5,7},{6,4},{7,5},{8,10},{9,11},{10,... | collective-permute-start | bytes 638984 | tf_op jit(solution)/shard_map/ppermute | solution.py:511
  7.9 10.6 %collective-permute-start.9 = (f32[104,512]{1,0:T(8,128)S(1)}, f32[104,512]{1,0:T(8,128)S(1)}, u32[]{:S(2)}, u32[]{:S(2)}) collective-permute-start(f32[104,512]{1,0:T(8,128)S(1)} %get-tuple-element.56), channel_id=1, source_target_pairs={{0,3},{1,2},{2,1},{3,0},{4,7},{5,6},{6,5},{7,4},{8,11},{9,10},{10,... | collective-permute-start | bytes 638984 | tf_op jit(solution)/shard_map/ppermute | solution.py:511
  8.4 11.2 %collective-permute-start.10 = (f32[104,512]{1,0:T(8,128)S(1)}, f32[104,512]{1,0:T(8,128)S(1)}, u32[]{:S(2)}, u32[]{:S(2)}) collective-permute-start(f32[104,512]{1,0:T(8,128)S(1)} %get-tuple-element.57), channel_id=1, source_target_pairs={{0,4},{1,5},{2,6},{3,7},{4,0},{5,1},{6,2},{7,3},{8,12},{9,13},{10,... | collective-permute-start | bytes 638984 | tf_op jit(solution)/shard_map/ppermute | solution.py:511
  8.6 11.9 %collective-permute-start.11 = (f32[104,512]{1,0:T(8,128)S(1)}, f32[104,512]{1,0:T(8,128)S(1)}, u32[]{:S(2)}, u32[]{:S(2)}) collective-permute-start(f32[104,512]{1,0:T(8,128)S(1)} %get-tuple-element.58), channel_id=1, source_target_pairs={{0,5},{1,4},{2,7},{3,6},{4,1},{5,0},{6,3},{7,2},{8,13},{9,12},{10,... | collective-permute-start | bytes 638984 | tf_op jit(solution)/shard_map/ppermute | solution.py:511
  10.2 32.5 %slice-start.1 = ((s8[6291456]{0:T(1024)(128)(4,1)}), s8[2097152]{0:T(1024)(128)(4,1)S(1)}, s32[]{:S(2)}) async-start(s8[6291456]{0:T(1024)(128)(4,1)} %bitcast.33), calls=%async_computation.1 | async-start | bytes 4194304
  10.2 32.5 %copy-start.37 = (s32[256]{0:T(256)S(1)}, s32[256]{0:T(256)}, u32[]{:S(2)}) copy-start(s32[256]{0:T(256)} %param.10) | copy-start | bytes 3076
  12.8 29.8 %copy-start.13 = (f32[104,512]{1,0:T(8,128)}, f32[104,512]{1,0:T(8,128)S(1)}, u32[]{:S(2)}) copy-start(f32[104,512]{1,0:T(8,128)S(1)} %collective-permute-done.7.refs_1_) | copy-start | bytes 638980
  12.8 19.8 %collective-permute-start.20 = (f32[128,512]{1,0:T(8,128)S(1)}, f32[128,512]{1,0:T(8,128)S(1)}, u32[]{:S(2)}, u32[]{:S(2)}) collective-permute-start(f32[128,512]{1,0:T(8,128)S(1)} %get-tuple-element.71), channel_id=1, source_target_pairs={{0,1},{1,0},{2,3},{3,2},{4,5},{5,4},{6,7},{7,6},{8,9},{9,8},{10,11... | collective-permute-start | bytes 786440 | tf_op jit(solution)/shard_map/ppermute | solution.py:511
  13.5 29.1 %copy-start.15 = (f32[104,512]{1,0:T(8,128)}, f32[104,512]{1,0:T(8,128)S(1)}, u32[]{:S(2)}) copy-start(f32[104,512]{1,0:T(8,128)S(1)} %collective-permute-done.8.refs_2_) | copy-start | bytes 638980
  13.5 11.7 %collective-permute-start.12 = (f32[104,512]{1,0:T(8,128)S(1)}, f32[104,512]{1,0:T(8,128)S(1)}, u32[]{:S(2)}, u32[]{:S(2)}) collective-permute-start(f32[104,512]{1,0:T(8,128)S(1)} %get-tuple-element.59), channel_id=1, source_target_pairs={{0,6},{1,7},{2,4},{3,5},{4,2},{5,3},{6,0},{7,1},{8,14},{9,15},{10,... | collective-permute-start | bytes 638984 | tf_op jit(solution)/shard_map/ppermute | solution.py:511
  18.5 17.3 %copy-start.17 = (f32[104,512]{1,0:T(8,128)}, f32[104,512]{1,0:T(8,128)S(1)}, u32[]{:S(2)}) copy-start(f32[104,512]{1,0:T(8,128)S(1)} %collective-permute-done.9.refs_3_) | copy-start | bytes 638980
  18.5 12.1 %collective-permute-start.13 = (f32[104,512]{1,0:T(8,128)S(1)}, f32[104,512]{1,0:T(8,128)S(1)}, u32[]{:S(2)}, u32[]{:S(2)}) collective-permute-start(f32[104,512]{1,0:T(8,128)S(1)} %get-tuple-element.60), channel_id=1, source_target_pairs={{0,7},{1,6},{2,5},{3,4},{4,3},{5,2},{6,1},{7,0},{8,15},{9,14},{10,... | collective-permute-start | bytes 638984 | tf_op jit(solution)/shard_map/ppermute | solution.py:511
  19.5 16.3 %copy-start.19 = (f32[104,512]{1,0:T(8,128)}, f32[104,512]{1,0:T(8,128)S(1)}, u32[]{:S(2)}) copy-start(f32[104,512]{1,0:T(8,128)S(1)} %collective-permute-done.10.refs_4_) | copy-start | bytes 638980
  19.5 16.3 %collective-permute-start.21 = (f32[128,512]{1,0:T(8,128)S(1)}, f32[128,512]{1,0:T(8,128)S(1)}, u32[]{:S(2)}, u32[]{:S(2)}) collective-permute-start(f32[128,512]{1,0:T(8,128)S(1)} %get-tuple-element.72), channel_id=1, source_target_pairs={{0,2},{1,3},{2,0},{3,1},{4,6},{5,7},{6,4},{7,5},{8,10},{9,11},{10,... | collective-permute-start | bytes 786440 | tf_op jit(solution)/shard_map/ppermute | solution.py:511
  20.5 22.2 %copy-start.21 = (f32[104,512]{1,0:T(8,128)}, f32[104,512]{1,0:T(8,128)S(1)}, u32[]{:S(2)}) copy-start(f32[104,512]{1,0:T(8,128)S(1)} %collective-permute-done.11.refs_5_) | copy-start | bytes 638980
  20.5 21.7 %collective-permute-start.22 = (f32[128,512]{1,0:T(8,128)S(1)}, f32[128,512]{1,0:T(8,128)S(1)}, u32[]{:S(2)}, u32[]{:S(2)}) collective-permute-start(f32[128,512]{1,0:T(8,128)S(1)} %get-tuple-element.73), channel_id=1, source_target_pairs={{0,3},{1,2},{2,1},{3,0},{4,7},{5,6},{6,5},{7,4},{8,11},{9,10},{10,... | collective-permute-start | bytes 786440 | tf_op jit(solution)/shard_map/ppermute | solution.py:511
  25.2 17.4 %copy-start.23 = (f32[104,512]{1,0:T(8,128)}, f32[104,512]{1,0:T(8,128)S(1)}, u32[]{:S(2)}) copy-start(f32[104,512]{1,0:T(8,128)S(1)} %collective-permute-done.12.refs_6_) | copy-start | bytes 638980
  25.2 24.5 %collective-permute-start.23 = (f32[128,512]{1,0:T(8,128)}, f32[128,512]{1,0:T(8,128)S(1)}, u32[]{:S(2)}, u32[]{:S(2)}) collective-permute-start(f32[128,512]{1,0:T(8,128)} %get-tuple-element.74), channel_id=1, source_target_pairs={{0,4},{1,5},{2,6},{3,7},{4,0},{5,1},{6,2},{7,3},{8,12},{9,13},{10,... | collective-permute-start | bytes 786440 | tf_op jit(solution)/shard_map/ppermute | solution.py:511
  30.6 21.5 %collective-permute-start.24 = (f32[128,512]{1,0:T(8,128)S(1)}, f32[128,512]{1,0:T(8,128)S(1)}, u32[]{:S(2)}, u32[]{:S(2)}) collective-permute-start(f32[128,512]{1,0:T(8,128)S(1)} %get-tuple-element.75), channel_id=1, source_target_pairs={{0,5},{1,4},{2,7},{3,6},{4,1},{5,0},{6,3},{7,2},{8,13},{9,12},{10,... | collective-permute-start | bytes 786440 | tf_op jit(solution)/shard_map/ppermute | solution.py:511
  32.6 21.9 %collective-permute-start.17 = (f32[200,512]{1,0:T(8,128)}, f32[200,512]{1,0:T(8,128)}, u32[]{:S(2)}, u32[]{:S(2)}) collective-permute-start(f32[200,512]{1,0:T(8,128)} %get-tuple-element.65), channel_id=1, source_target_pairs={{0,8},{1,9},{2,10},{3,11},{4,12},{5,13},{6,14},{7,15},{8,0},{9,1},... | collective-permute-start | bytes 1228808 | tf_op jit(solution)/shard_map/ppermute | solution.py:511
  35.8 17.0 %collective-permute-start.25 = (f32[128,512]{1,0:T(8,128)S(1)}, f32[128,512]{1,0:T(8,128)S(1)}, u32[]{:S(2)}, u32[]{:S(2)}) collective-permute-start(f32[128,512]{1,0:T(8,128)S(1)} %get-tuple-element.76), channel_id=1, source_target_pairs={{0,6},{1,7},{2,4},{3,5},{4,2},{5,3},{6,0},{7,1},{8,14},{9,15},{10,... | collective-permute-start | bytes 786440 | tf_op jit(solution)/shard_map/ppermute | solution.py:511
  42.1 13.8 %copy-start.1 = (f32[128,512]{1,0:T(8,128)}, f32[128,512]{1,0:T(8,128)S(1)}, u32[]{:S(2)}) copy-start(f32[128,512]{1,0:T(8,128)S(1)} %collective-permute-done.22.refs_3_) | copy-start | bytes 786436
  42.1 11.4 %collective-permute-start.26 = (f32[128,512]{1,0:T(8,128)S(1)}, f32[128,512]{1,0:T(8,128)S(1)}, u32[]{:S(2)}, u32[]{:S(2)}) collective-permute-start(f32[128,512]{1,0:T(8,128)S(1)} %get-tuple-element.77), channel_id=1, source_target_pairs={{0,7},{1,6},{2,5},{3,4},{4,3},{5,2},{6,1},{7,0},{8,15},{9,14},{10,... | collective-permute-start | bytes 786440 | tf_op jit(solution)/shard_map/ppermute | solution.py:511
  49.6 57.0 %copy-start.51 = (f32[10]{0:T(128)S(1)}, f32[10]{0:T(128)}, u32[]{:S(2)}) copy-start(f32[10]{0:T(128)} %param.15) | copy-start | bytes 124
  49.6 57.0 %copy-start.52 = (f32[10]{0:T(128)S(1)}, f32[10]{0:T(128)}, u32[]{:S(2)}) copy-start(f32[10]{0:T(128)} %param.14) | copy-start | bytes 124
  49.6 58.4 %copy-start.48 = (f32[16,10]{1,0:T(8,128)S(1)}, f32[16,10]{1,0:T(8,128)}, u32[]{:S(2)}) copy-start(f32[16,10]{1,0:T(8,128)} %param.16) | copy-start | bytes 1924
  49.7 58.3 %copy-start.3 = (f32[128,512]{1,0:T(8,128)}, f32[128,512]{1,0:T(8,128)S(1)}, u32[]{:S(2)}) copy-start(f32[128,512]{1,0:T(8,128)S(1)} %collective-permute-done.23.refs_4_) | copy-start | bytes 786436
  49.7 29.3 %collective-permute-start.18 = (f32[200,512]{1,0:T(8,128)}, f32[200,512]{1,0:T(8,128)S(1)}, u32[]{:S(2)}, u32[]{:S(2)}) collective-permute-start(f32[200,512]{1,0:T(8,128)} %get-tuple-element.66), channel_id=1, source_target_pairs={{0,16},{1,17},{2,18},{3,19},{4,20},{5,21},{6,22},{7,23},{8,24},{9,... | collective-permute-start | bytes 1228808 | tf_op jit(solution)/shard_map/ppermute | solution.py:511
  52.1 56.0 %copy-start.5 = (f32[128,512]{1,0:T(8,128)}, f32[128,512]{1,0:T(8,128)S(1)}, u32[]{:S(2)}) copy-start(f32[128,512]{1,0:T(8,128)S(1)} %collective-permute-done.24.refs_5_) | copy-start | bytes 786436
  52.1 35.7 %collective-permute-start.19 = (f32[200,512]{1,0:T(8,128)}, f32[200,512]{1,0:T(8,128)S(1)}, u32[]{:S(2)}, u32[]{:S(2)}) collective-permute-start(f32[200,512]{1,0:T(8,128)} %get-tuple-element.67), channel_id=1, source_target_pairs={{0,24},{1,25},{2,26},{3,27},{4,28},{5,29},{6,30},{7,31},{8,16},{9,... | collective-permute-start | bytes 1228808 | tf_op jit(solution)/shard_map/ppermute | solution.py:511
  52.9 56.6 %copy-start.7 = (f32[128,512]{1,0:T(8,128)}, f32[128,512]{1,0:T(8,128)S(1)}, u32[]{:S(2)}) copy-start(f32[128,512]{1,0:T(8,128)S(1)} %collective-permute-done.25.refs_6_) | copy-start | bytes 786436
  52.9 49.2 %collective-permute-start = (f32[160,512]{1,0:T(8,128)}, f32[160,512]{1,0:T(8,128)S(1)}, u32[]{:S(2)}, u32[]{:S(2)}) collective-permute-start(f32[160,512]{1,0:T(8,128)} %get-tuple-element.46), channel_id=1, source_target_pairs={{0,1},{1,0},{2,3},{3,2},{4,5},{5,4},{6,7},{7,6},{8,9},{9,8},{10,11... | collective-permute-start | bytes 983048 | tf_op jit(solution)/shard_map/ppermute | solution.py:511
  53.6 55.9 %copy-start.9 = (f32[128,512]{1,0:T(8,128)}, f32[128,512]{1,0:T(8,128)S(1)}, u32[]{:S(2)}) copy-start(f32[128,512]{1,0:T(8,128)S(1)} %collective-permute-done.26.refs_7_) | copy-start | bytes 786436
  53.6 49.7 %collective-permute-start.1 = (f32[160,512]{1,0:T(8,128)}, f32[160,512]{1,0:T(8,128)S(1)}, u32[]{:S(2)}, u32[]{:S(2)}) collective-permute-start(f32[160,512]{1,0:T(8,128)} %get-tuple-element.47), channel_id=1, source_target_pairs={{0,2},{1,3},{2,0},{3,1},{4,6},{5,7},{6,4},{7,5},{8,10},{9,11},{10,... | collective-permute-start | bytes 983048 | tf_op jit(solution)/shard_map/ppermute | solution.py:511
  54.5 50.0 %collective-permute-start.2 = (f32[160,512]{1,0:T(8,128)}, f32[160,512]{1,0:T(8,128)S(1)}, u32[]{:S(2)}, u32[]{:S(2)}) collective-permute-start(f32[160,512]{1,0:T(8,128)} %copy-done.46), channel_id=1, source_target_pairs={{0,3},{1,2},{2,1},{3,0},{4,7},{5,6},{6,5},{7,4},{8,11},{9,10},{10,... | collective-permute-start | bytes 983048 | tf_op jit(solution)/shard_map/ppermute | solution.py:511
  79.0 141.0 %collective-permute-start.27 = (f32[256,512]{1,0:T(8,128)}, f32[256,512]{1,0:T(8,128)}, u32[]{:S(2)}, u32[]{:S(2)}) collective-permute-start(f32[256,512]{1,0:T(8,128)} %get-tuple-element.78), channel_id=1, source_target_pairs={{0,8},{1,9},{2,10},{3,11},{4,12},{5,13},{6,14},{7,15},{8,0},{9,1},... | collective-permute-start | bytes 1572872 | tf_op jit(solution)/shard_map/ppermute | solution.py:511
  101.6 10.2 %collective-permute-start.33 = (f32[64,128]{1,0:T(8,128)}, f32[64,128]{1,0:T(8,128)S(1)}, u32[]{:S(2)}, u32[]{:S(2)}) collective-permute-start(f32[64,128]{1,0:T(8,128)} %get-tuple-element.88), channel_id=1, source_target_pairs={{0,3},{1,0},{2,1},{3,2},{4,7},{5,4},{6,5},{7,6},{8,11},{9,8},{10,9... | collective-permute-start | bytes 98312 | tf_op jit(solution)/shard_map/ppermute | solution.py:515
  102.1 9.8 %collective-permute-start.32 = (f32[64,128]{1,0:T(8,128)}, f32[64,128]{1,0:T(8,128)}, u32[]{:S(2)}, u32[]{:S(2)}) collective-permute-start(f32[64,128]{1,0:T(8,128)} %get-tuple-element.89), channel_id=1, source_target_pairs={{0,1},{1,2},{2,3},{3,0},{4,5},{5,6},{6,7},{7,4},{8,9},{9,10},{10,1... | collective-permute-start | bytes 98312 | tf_op jit(solution)/shard_map/ppermute | solution.py:515
  103.3 10.1 %collective-permute-start.31 = (f32[64,128]{1,0:T(8,128)}, f32[64,128]{1,0:T(8,128)}, u32[]{:S(2)}, u32[]{:S(2)}) collective-permute-start(f32[64,128]{1,0:T(8,128)} %get-tuple-element.90), channel_id=1, source_target_pairs={{0,28},{4,0},{8,4},{12,8},{16,12},{20,16},{24,20},{28,24},{1,29},{... | collective-permute-start | bytes 98312 | tf_op jit(solution)/shard_map/ppermute | solution.py:515
  104.6 9.5 %collective-permute-start.30 = (f32[64,128]{1,0:T(8,128)}, f32[64,128]{1,0:T(8,128)}, u32[]{:S(2)}, u32[]{:S(2)}) collective-permute-start(f32[64,128]{1,0:T(8,128)} %get-tuple-element.91), channel_id=1, source_target_pairs={{0,4},{4,8},{8,12},{12,16},{16,20},{20,24},{24,28},{28,0},{1,5},{5... | collective-permute-start | bytes 98312 | tf_op jit(solution)/shard_map/ppermute | solution.py:515
  111.8 18.8 %collective-permute-start.3 = (f32[160,512]{1,0:T(8,128)}, f32[160,512]{1,0:T(8,128)S(1)}, u32[]{:S(2)}, u32[]{:S(2)}) collective-permute-start(f32[160,512]{1,0:T(8,128)} %copy-done.45), channel_id=1, source_target_pairs={{0,4},{1,5},{2,6},{3,7},{4,0},{5,1},{6,2},{7,3},{8,12},{9,13},{10,... | collective-permute-start | bytes 983048 | tf_op jit(solution)/shard_map/ppermute | solution.py:511
  111.9 18.8 %collective-permute-start.4 = (f32[160,512]{1,0:T(8,128)}, f32[160,512]{1,0:T(8,128)S(1)}, u32[]{:S(2)}, u32[]{:S(2)}) collective-permute-start(f32[160,512]{1,0:T(8,128)} %copy-done.44), channel_id=1, source_target_pairs={{0,5},{1,4},{2,7},{3,6},{4,1},{5,0},{6,3},{7,2},{8,13},{9,12},{10,... | collective-permute-start | bytes 983048 | tf_op jit(solution)/shard_map/ppermute | solution.py:511
  113.4 23.8 %collective-permute-start.5 = (f32[160,512]{1,0:T(8,128)}, f32[160,512]{1,0:T(8,128)S(1)}, u32[]{:S(2)}, u32[]{:S(2)}) collective-permute-start(f32[160,512]{1,0:T(8,128)} %copy-done.43), channel_id=1, source_target_pairs={{0,6},{1,7},{2,4},{3,5},{4,2},{5,3},{6,0},{7,1},{8,14},{9,15},{10,... | collective-permute-start | bytes 983048 | tf_op jit(solution)/shard_map/ppermute | solution.py:511
  114.0 30.2 %collective-permute-start.6 = (f32[160,512]{1,0:T(8,128)}, f32[160,512]{1,0:T(8,128)S(1)}, u32[]{:S(2)}, u32[]{:S(2)}) collective-permute-start(f32[160,512]{1,0:T(8,128)} %copy-done.42), channel_id=1, source_target_pairs={{0,7},{1,6},{2,5},{3,4},{4,3},{5,2},{6,1},{7,0},{8,15},{9,14},{10,... | collective-permute-start | bytes 983048 | tf_op jit(solution)/shard_map/ppermute | solution.py:511
  123.4 132.2 %copy-start.2 = (f32[128,512]{1,0:T(8,128)S(1)}, f32[128,512]{1,0:T(8,128)}, u32[]{:S(2)}) copy-start(f32[128,512]{1,0:T(8,128)} %copy-done.1) | copy-start | bytes 786436
  123.4 132.2 %copy-start.4 = (f32[128,512]{1,0:T(8,128)S(1)}, f32[128,512]{1,0:T(8,128)}, u32[]{:S(2)}) copy-start(f32[128,512]{1,0:T(8,128)} %copy-done.3) | copy-start | bytes 786436
  123.4 132.2 %copy-start.6 = (f32[128,512]{1,0:T(8,128)S(1)}, f32[128,512]{1,0:T(8,128)}, u32[]{:S(2)}) copy-start(f32[128,512]{1,0:T(8,128)} %copy-done.5) | copy-start | bytes 786436
  123.4 132.2 %copy-start.8 = (f32[128,512]{1,0:T(8,128)S(1)}, f32[128,512]{1,0:T(8,128)}, u32[]{:S(2)}) copy-start(f32[128,512]{1,0:T(8,128)} %copy-done.7) | copy-start | bytes 786436
  123.4 132.2 %copy-start.10 = (f32[128,512]{1,0:T(8,128)S(1)}, f32[128,512]{1,0:T(8,128)}, u32[]{:S(2)}) copy-start(f32[128,512]{1,0:T(8,128)} %copy-done.9) | copy-start | bytes 786436
  127.6 92.5 %copy-start.41 = (f32[256,512]{1,0:T(8,128)S(1)}, f32[256,512]{1,0:T(8,128)}, u32[]{:S(2)}) copy-start(f32[256,512]{1,0:T(8,128)} %copy-done.40) | copy-start | bytes 1572868
  127.6 92.5 %copy-start.39 = (f32[256,512]{1,0:T(8,128)S(1)}, f32[256,512]{1,0:T(8,128)}, u32[]{:S(2)}) copy-start(f32[256,512]{1,0:T(8,128)} %copy-done.38) | copy-start | bytes 1572868
  127.6 128.1 %copy-start.35 = (f32[8,256]{1,0:T(8,128)S(1)}, f32[8,256]{1,0:T(8,128)}, u32[]{:S(2)}) copy-start(f32[8,256]{1,0:T(8,128)} %copy-done.34) | copy-start | bytes 24580
  130.6 17.6 %collective-permute-start.34 = (f32[64,128]{1,0:T(8,128)S(1)}, f32[64,128]{1,0:T(8,128)S(1)}, u32[]{:S(2)}, u32[]{:S(2)}) collective-permute-start(f32[64,128]{1,0:T(8,128)S(1)} %get-tuple-element.84.xlow), channel_id=1, source_target_pairs={{0,28},{4,0},{8,4},{12,8},{16,12},{20,16},{24,20},{28,24},{1,29},{... | collective-permute-start | bytes 98312 | tf_op jit(solution)/shard_map/ppermute | solution.py:515
  145.5 113.7 %collective-permute-start.14 = (f32[320,512]{1,0:T(8,128)S(1)}, f32[320,512]{1,0:T(8,128)S(1)}, u32[]{:S(2)}, u32[]{:S(2)}) collective-permute-start(f32[320,512]{1,0:T(8,128)S(1)} %get-tuple-element.62), channel_id=1, source_target_pairs={{0,8},{1,9},{2,10},{3,11},{4,12},{5,13},{6,14},{7,15},{8,0},{9,1},... | collective-permute-start | bytes 1966088 | tf_op jit(solution)/shard_map/ppermute | solution.py:511
  145.5 113.6 %collective-permute-start.15 = (f32[320,512]{1,0:T(8,128)S(1)}, f32[320,512]{1,0:T(8,128)S(1)}, u32[]{:S(2)}, u32[]{:S(2)}) collective-permute-start(f32[320,512]{1,0:T(8,128)S(1)} %get-tuple-element.63), channel_id=1, source_target_pairs={{0,16},{1,17},{2,18},{3,19},{4,20},{5,21},{6,22},{7,23},{8,24},{9,... | collective-permute-start | bytes 1966088 | tf_op jit(solution)/shard_map/ppermute | solution.py:511
  147.9 111.3 %collective-permute-start.16 = (f32[320,512]{1,0:T(8,128)S(1)}, f32[320,512]{1,0:T(8,128)S(1)}, u32[]{:S(2)}, u32[]{:S(2)}) collective-permute-start(f32[320,512]{1,0:T(8,128)S(1)} %get-tuple-element.64), channel_id=1, source_target_pairs={{0,24},{1,25},{2,26},{3,27},{4,28},{5,29},{6,30},{7,31},{8,16},{9,... | collective-permute-start | bytes 1966088 | tf_op jit(solution)/shard_map/ppermute | solution.py:511
  148.2 67.2 %collective-permute-start.35 = (f32[64,128]{1,0:T(8,128)S(1)}, f32[64,128]{1,0:T(8,128)S(1)}, u32[]{:S(2)}, u32[]{:S(2)}) collective-permute-start(f32[64,128]{1,0:T(8,128)S(1)} %get-tuple-element.85.xup), channel_id=1, source_target_pairs={{0,4},{4,8},{8,12},{12,16},{16,20},{20,24},{24,28},{28,0},{1,5},{5... | collective-permute-start | bytes 98312 | tf_op jit(solution)/shard_map/ppermute | solution.py:515
  215.4 3.5 %collective-permute-start.36 = (f32[64,128]{1,0:T(8,128)S(1)}, f32[64,128]{1,0:T(8,128)S(1)}, u32[]{:S(2)}, u32[]{:S(2)}) collective-permute-start(f32[64,128]{1,0:T(8,128)S(1)} %get-tuple-element.86.slow), channel_id=1, source_target_pairs={{0,3},{1,0},{2,1},{3,2},{4,7},{5,4},{6,5},{7,6},{8,11},{9,8},{10,9... | collective-permute-start | bytes 98312 | tf_op jit(solution)/shard_map/ppermute | solution.py:515
  218.9 1.2 collective-permute-start.37
  220.1 21.0 %collective-permute-start.28 = (f32[256,512]{1,0:T(8,128)S(1)}, f32[256,512]{1,0:T(8,128)S(1)}, u32[]{:S(2)}, u32[]{:S(2)}) collective-permute-start(f32[256,512]{1,0:T(8,128)S(1)} %copy-done.41), channel_id=1, source_target_pairs={{0,16},{1,17},{2,18},{3,19},{4,20},{5,21},{6,22},{7,23},{8,24},{9,... | collective-permute-start | bytes 1572872 | tf_op jit(solution)/shard_map/ppermute | solution.py:511
  220.1 35.5 %collective-permute-start.29 = (f32[256,512]{1,0:T(8,128)S(1)}, f32[256,512]{1,0:T(8,128)S(1)}, u32[]{:S(2)}, u32[]{:S(2)}) collective-permute-start(f32[256,512]{1,0:T(8,128)S(1)} %copy-done.39), channel_id=1, source_target_pairs={{0,24},{1,25},{2,26},{3,27},{4,28},{5,29},{6,30},{7,31},{8,16},{9,... | collective-permute-start | bytes 1572872 | tf_op jit(solution)/shard_map/ppermute | solution.py:511
  (29 other events, 73.6 us)

commit v2 on v1

--- a/solution.py
+++ b/solution.py
@@ -11,7 +11,8 @@
 BX = 4
 BS = 2
 FACE = 8
-VMEM_LIMIT = 40 * 1024 * 1024
+MERGE_FLOPS = 40_000_000_000
+VMEM_LIMIT = 12 * 1024 * 1024
 PARAMS = pltpu.CompilerParams(vmem_limit_bytes=VMEM_LIMIT)
 HIGHEST = lax.Precision.HIGHEST
 F32 = jnp.float32
@@ -29,6 +30,8 @@
         self.per_dev = BX * BS * layers
         self.cap = 2 * self.per_dev // self.devices
         self.msg_rows = self.lines * self.cap
+        self.pairs = self.plane // 2
+        self.pair_rows = 2 * self.msg_rows
         self.rows = self.plane * self.msg_rows
         full = self.plane * self.cap
         self.kept = [full] * self.lines
@@ -73,7 +76,7 @@
 
 
 def pack_kernel(plan, fields, marked, me_ref, place_ref, states_ref, *refs):
-    outs, chooser_ref = refs[: plan.plane], refs[plan.plane]
+    outs, chooser_ref = refs[:-1], refs[-1]
     field = pl.program_id(0)
     rows = plan.msg_rows
 
@@ -107,14 +110,16 @@
                 precision=HIGHEST,
                 preferred_element_type=F32,
             )
-            for out in outs:
-                out[fields * rows : fields * rows + 8, :] = jnp.zeros((8, plan.points), F32)
-                out[fields * rows : fields * rows + 8, : plan.rows] = marks
+            for out, held in zip(outs, [rows] * (len(outs) - 1) + [rows * plan.pairs]):
+                out[fields * held : fields * held + 8, :] = jnp.zeros((8, plan.points), F32)
+                out[fields * held : fields * held + 8, : plan.rows] = marks
 
     moved = pick(chooser_ref[...], states_ref[0])
     start = pl.multiple_of(field * rows, rows)
-    for j, out in enumerate(outs):
-        out[pl.ds(start, rows), :] = moved[j * rows : (j + 1) * rows]
+    aside = pl.multiple_of(field * rows * plan.pairs, rows)
+    for b in range(plan.pairs):
+        outs[b][pl.ds(start, rows), :] = moved[2 * b * rows : (2 * b + 1) * rows]
+        outs[-1][pl.ds(aside + b * rows, rows), :] = moved[(2 * b + 1) * rows : (2 * b + 2) * rows]
 
 
 def whole(shape):
@@ -123,7 +128,9 @@
 
 def pack(plan, group, me, place_row, states, marked):
     first, fields = group
-    shape = (fields * plan.msg_rows + (8 if marked else 0), plan.points)
+    extra = 8 if marked else 0
+    shapes = [(fields * plan.msg_rows + extra, plan.points)] * plan.pairs
+    shapes.append((fields * plan.msg_rows * plan.pairs + extra, plan.points))
     return pl.pallas_call(
         functools.partial(pack_kernel, plan, fields, marked),
         grid=(fields,),
@@ -132,11 +139,44 @@
             whole((1, plan.slots)),
             pl.BlockSpec((1, plan.slots, plan.points), lambda f: (first + f, 0, 0)),
         ],
-        out_specs=[whole(shape)] * plan.plane,
-        out_shape=[jax.ShapeDtypeStruct(shape, F32)] * plan.plane,
+        out_specs=[pl.BlockSpec(memory_space=pltpu.VMEM)] * len(shapes),
+        out_shape=[jax.ShapeDtypeStruct(shape, F32) for shape in shapes],
         scratch_shapes=[pltpu.VMEM((plan.rows, plan.slots), BF16)],
         compiler_params=PARAMS,
     )(me, place_row, states)
+
+
+def merge_kernel(plan, fields, marked, *refs):
+    near, refs = refs[: plan.pairs], refs[plan.pairs :]
+    aside, outs = refs[0], refs[1:]
+    rows = plan.msg_rows
+    for b, out in enumerate(outs):
+        for field in range(fields):
+            start = field * plan.pair_rows
+            other = (field * plan.pairs + b) * rows
+            out[start : start + rows, :] = near[b][field * rows : (field + 1) * rows, :]
+            out[start + rows : start + 2 * rows, :] = aside[other : other + rows, :]
+        if marked:
+            lane = iota((8, plan.rows), 1)
+            mine = near[0][fields * rows : fields * rows + 8, : plan.rows]
+            base = fields * rows * plan.pairs
+            other = aside[base : base + 8, : plan.rows]
+            marks = jnp.where(rest(halves(lane, rows), 2) == 0, mine, other)
+            base = fields * plan.pair_rows
+            out[base : base + 8, :] = jnp.zeros((8, plan.points), F32)
+            out[base : base + 8, : plan.rows] = marks
+
+
+def merge(plan, group, near, aside, marked, cost):
+    _, fields = group
+    shape = (fields * plan.pair_rows + (8 if marked else 0), plan.points)
+    return simple_call(
+        functools.partial(merge_kernel, plan, fields, marked),
+        [*near, aside],
+        [jax.ShapeDtypeStruct(shape, F32)] * plan.pairs,
+        [],
+        cost,
+    )
 
 
 def route_rows(plan, marks):
@@ -156,16 +196,15 @@
 def gather_marks(plan, fields, messages):
     lane = iota((8, plan.rows), 1)
     marks = jnp.zeros((8, plan.rows), F32)
-    base = fields * plan.msg_rows
-    for j, message in enumerate(messages):
+    base = fields * plan.pair_rows
+    for b, message in enumerate(messages):
         part = message[base : base + 8, : plan.rows]
-        marks = jnp.where(halves(lane, plan.msg_rows) == j, part, marks)
+        marks = jnp.where(halves(lane, plan.pair_rows) == b, part, marks)
     return marks
 
 
 def relay_kernel(plan, fields, marked, *refs):
-    messages = refs[: plan.plane]
-    refs = refs[plan.plane :]
+    messages, refs = refs[: plan.pairs], refs[plan.pairs :]
     if not marked:
         marks_ref, refs = refs[0], refs[1:]
     outs, refs = refs[: plan.lines - 1], refs[plan.lines - 1 :]
@@ -191,9 +230,9 @@
     first = plan.offset[1]
     chooser = spread[first : first + plan.relay_rows].astype(BF16)
     for field in range(fields):
-        for j, message in enumerate(messages):
-            held[j * plan.msg_rows : (j + 1) * plan.msg_rows, :] = message[
-                field * plan.msg_rows : (field + 1) * plan.msg_rows, :
+        for b, message in enumerate(messages):
+            held[b * plan.pair_rows : (b + 1) * plan.pair_rows, :] = message[
+                field * plan.pair_rows : (field + 1) * plan.pair_rows, :
             ]
         moved = pick(chooser, held[...])
         for m, out in enumerate(outs, 1):
@@ -223,7 +262,7 @@
 
 
 def settle_kernel(plan, fields, marked, *refs):
-    messages, refs = refs[: plan.plane], refs[plan.plane :]
+    messages, refs = refs[: plan.pairs], refs[plan.pairs :]
     relays, refs = refs[: plan.lines - 1], refs[plan.lines - 1 :]
     if marked:
         own_ref, order_ref = refs[:2]
@@ -256,9 +295,10 @@
         if used < plan.rows:
             held[used:, :] = jnp.zeros((plan.rows - used, plan.points), F32)
 
-    start = field * plan.msg_rows
-    for j, message in enumerate(messages):
-        held[j * plan.cap : (j + 1) * plan.cap, :] = message[pl.ds(start, plan.msg_rows), :][: plan.cap]
+    for j in range(plan.plane):
+        start = pl.multiple_of((field * 2 + j % 2) * plan.msg_rows, plan.msg_rows)
+        part = messages[j // 2][pl.ds(start, plan.msg_rows), :]
+        held[j * plan.cap : (j + 1) * plan.cap, :] = part[: plan.cap]
     for m, part in enumerate(relays, 1):
         kept = plan.kept[m]
         held[plan.offset[m] : plan.offset[m] + kept, :] = part[pl.ds(pl.multiple_of(field * kept, 8), kept), :]
@@ -305,13 +345,13 @@
     if marked:
         operands += [own, order]
         cells = (order.shape[0], plan.per_dev)
-        out_specs += [whole((8, plan.rows)), whole(cells)]
+        out_specs += [pl.BlockSpec(memory_space=pltpu.VMEM)] * 2
         out_shape += [jax.ShapeDtypeStruct((8, plan.rows), F32), jax.ShapeDtypeStruct(cells, F32)]
         scratch += [pltpu.VMEM((plan.per_dev, plan.points), F32)]
-        in_specs = [whole(o.shape) for o in operands]
+        in_specs = [pl.BlockSpec(memory_space=pltpu.VMEM)] * len(operands)
     else:
         operands += [marks, buffer]
-        in_specs = [whole(o.shape) for o in operands[:-1]] + [pl.BlockSpec(memory_space=pl.ANY)]
+        in_specs = [pl.BlockSpec(memory_space=pltpu.VMEM)] * (len(operands) - 1) + [pl.BlockSpec(memory_space=pl.ANY)]
         aliases = {len(operands) - 1: 0}
     return pl.pallas_call(
         functools.partial(settle_kernel, plan, fields, marked),
@@ -456,7 +496,7 @@
             out[b * side + i, s * side : (s + 1) * side, :] = value[i * side : (i + 1) * side]
 
 
-def simple_call(kernel, operands, out_shape, scratch):
+def simple_call(kernel, operands, out_shape, scratch, cost=None):
     return pl.pallas_call(
         kernel,
         in_specs=[pl.BlockSpec(memory_space=pltpu.VMEM)] * len(operands),
@@ -464,6 +504,7 @@
         out_shape=out_shape,
         scratch_shapes=scratch,
         compiler_params=PARAMS,
+        cost_estimate=cost,
     )(*operands)
 
 
@@ -497,6 +538,10 @@
     return mix_t.T, mix_t, weights, sum_xs, lane_values
 
 
+def after(value, earlier):
+    return lax.optimization_barrier((value, earlier))[0]
+
+
 def shards(old_states, new_place, vectors_x, vectors_s, vectors_w, values_x, values_s, values_w):
     n_x, n_y = lax.axis_size("gx"), lax.axis_size("gy")
     slots, fields, points = old_states.shape
@@ -517,16 +562,33 @@
     order = jnp.asarray(cell_order(plan.side), BF16)
     tables = box_tables(plan, vectors_x, vectors_s, vectors_w, values_x, values_s, values_w)
 
-    packed = [pack(plan, group, me, place_row, states, g == 0) for g, group in enumerate(plan.groups)]
+    merged = []
+    for g, group in enumerate(plan.groups):
+        *near, aside = pack(plan, group, me, place_row, states, g == 0)
+        cost = pl.CostEstimate(flops=MERGE_FLOPS if g else 0, bytes_accessed=0, transcendentals=0)
+        merged.append(functools.partial(merge, plan, group, near, across(aside, 1), g == 0, cost))
     marks = None
     held = []
-    for group, sent in zip(plan.groups, packed):
-        messages = [sent[0]] + [across(sent[j], j) for j in range(1, plan.plane)]
+    gate = None
+    arrived = [None] * (plan.lines - 1)
+    for g, group in enumerate(plan.groups):
+        if g:
+            near = merged[g].args[2]
+            merged[g] = functools.partial(
+                merge, plan, group, [after(near[0], gate)] + near[1:], *merged[g].args[3:]
+            )
+        sent = merged[g]()
+        messages = [sent[0]] + [across(sent[b], 2 * b) for b in range(1, plan.pairs)]
         relays, more = relay(plan, group, messages, marks)
         if marks is None:
             marks, own = more
-        arrived = [across(relays[m - 1], m * plan.plane) for m in range(1, plan.lines)]
-        held.append((messages, arrived))
+        gate = relays[0]
+        for m in reversed(range(1, plan.lines)):
+            ready = relays[m - 1]
+            if g:
+                ready = after(ready, arrived[m - 1])
+            arrived[m - 1] = across(ready, m * plan.plane)
+        held.append((messages, list(arrived)))
 
     buffer, row_marks, cells = settle(plan, plan.groups[0], *held[0], None, None, own, order)
     side = plan.side

time: 266 us -> 213 us (0.80)
  waiting for transfers between devices: 168 us -> 83 us
  starting transfers between devices: 28.7 us -> 58.8 us
    ppermute x8, waiting for transfers between devices: 69.7 us -> 17.9 us  [shifted(): lax.ppermute(value, axis, [(s, (s + steps) % count) for s in range(count)])]
    ppermute x30 -> x21, waiting for transfers between devices: 98.2 us -> 65.1 us  [across(): lax.ppermute(value, both, [(d, d ^ flip) for d in range(plan.devices)])]
    ppermute x8, starting transfers between devices: 7.29 us -> 30 us  [shifted(): lax.ppermute(value, axis, [(s, (s + steps) % count) for s in range(count)])]
    ppermute x30 -> x21, starting transfers between devices: 21.4 us -> 28.7 us  [across(): lax.ppermute(value, both, [(d, d ^ flip) for d in range(plan.devices)])]
    unnamed x110 -> x82, local copies, waits for them, and re-layouts: 21.4 us -> 16.9 us
    pallas_call x2 -> x5, Pallas kernels: 4.73 us -> 5.64 us  [simple_call(): pl.pallas_call(kernel, in_specs=[pl.BlockSpec(memory_space=pltpu.VMEM)] *...]
  transfers between devices with their start and end apart: 38 -> 29, of which waited for: 16 -> 11; matrix products, arithmetic and copies ran while one was open for 6% -> 11% of each run, Pallas kernels for 9% -> 10%
where the time goes in v2:
time: 213 us; the launch traced here: 210 us
  waiting for transfers between devices  83 us (39%)
  starting transfers between devices  58.8 us (28%)
  local copies, waits for them, and re-layouts  33.3 us (16%)
  Pallas kernels  27.9 us (13%)
  other arithmetic  5.67 us (3%)
    ppermute x21, waiting for transfers between devices, across(): lax.ppermute(value, both, [(d, d ^ flip) for d in range(plan.devices)])  65.1 us
    ppermute x8, starting transfers between devices, shifted(): lax.ppermute(value, axis, [(s, (s + steps) % count) for s in range(count)])  30 us
    ppermute x21, starting transfers between devices, across(): lax.ppermute(value, both, [(d, d ^ flip) for d in range(plan.devices)])  28.7 us
    ppermute x8, waiting for transfers between devices, shifted(): lax.ppermute(value, axis, [(s, (s + steps) % count) for s in range(count)])  17.9 us
    unnamed x82, local copies, waits for them, and re-layouts  16.9 us
    pallas_call x3, Pallas kernels, settle(): pl.pallas_call(functools.partial(settle_kernel, plan, fields, marked), gr...  10.9 us
    mul x9, local copies, waits for them, and re-layouts, kron(): left[:, None, :, None] * right[None, :, None, :]  7.12 us
    pallas_call x3, Pallas kernels, pack(): pl.pallas_call(functools.partial(pack_kernel, plan, fields, marked), grid...  6.01 us
  transfers between devices with their start and end apart: 29, of which 11 were waited for; matrix products, arithmetic and copies ran while one was open for 11% of the time, Pallas kernels for 10%

profile of v2, /device:TPU:11, one launch (start us, length us, event | category | flops | bytes accessed | tf_op | source)
XLA Modules:
  0.0 209.7 jit_solution(11008629579858401226)
XLA Ops:
  0.6 2.8 %copy-done = f32[256,12,512]{2,0,1:T(8,128)S(1)} copy-done((f32[256,12,512]{2,0,1:T(8,128)S(1)}, f32[256,12,512]{2,0,1:T(8,128)}, u32[]{:S(2)}) %copy-start) | copy-done | bytes 6291480
  4.1 1.8 shard_map.106
  6.6 1.9 shard_map.105
  8.8 1.3 collective-permute-start.1
  10.3 1.2 collective-permute-start.3
  11.5 2.3 %shard_map.104 = (f32[160,512]{1,0:T(8,128)S(1)}, f32[160,512]{1,0:T(8,128)S(1)}, f32[160,512]{1,0:T(8,128)S(1)}, f32[160,512]{1,0:T(8,128)S(1)}, f32[640,512]{1,0:T(8,128)S(1)}) custom-call(s32[1]{0:T(128)} %bitcast.me_ref, s32[1,256]{1,0:T(1,128)S(1)} %bitcast.39, f32[12,256,512]{2,1,0:T(8,128)S(1)} %bitcast.35), custom_call_target="tpu_custom_call" | custom-call | tf_op jit(solution)/shard_map/pallas_call | solution.py:134
  13.8 1.4 collective-permute-start.8
  15.2 4.2 %collective-permute-done.1.refs_1_ = f32[200,512]{1,0:T(8,128)S(1)} collective-permute-done((f32[200,512]{1,0:T(8,128)S(1)}, f32[200,512]{1,0:T(8,128)S(1)}, u32[]{:S(2)}, u32[]{:S(2)}) %collective-permute-start.1) | collective-permute-done | bytes 409632 | tf_op jit(solution)/shard_map/ppermute | solution.py:556
  19.4 0.9 collective-permute-done.2.refs_2_
  20.3 8.7 %collective-permute-done.3.refs_3_ = f32[200,512]{1,0:T(8,128)S(1)} collective-permute-done((f32[200,512]{1,0:T(8,128)S(1)}, f32[200,512]{1,0:T(8,128)S(1)}, u32[]{:S(2)}, u32[]{:S(2)}) %collective-permute-start.3) | collective-permute-done | bytes 409632 | tf_op jit(solution)/shard_map/ppermute | solution.py:556
  29.1 1.9 shard_map.108
  31.7 1.3 collective-permute-start.5
  33.3 1.2 collective-permute-start.7
  34.5 2.4 %collective-permute-start.15 = (f32[200,512]{1,0:T(8,128)S(1)}, f32[200,512]{1,0:T(8,128)S(1)}, u32[]{:S(2)}, u32[]{:S(2)}) collective-permute-start(f32[200,512]{1,0:T(8,128)S(1)} %get-tuple-element.93), channel_id=1, source_target_pairs={{0,16},{1,17},{2,18},{3,19},{4,20},{5,21},{6,22},{7,23},{8,24},{9,... | collective-permute-start | bytes 1228808 | tf_op jit(solution)/shard_map/ppermute | solution.py:556
  36.8 6.7 %collective-permute-done.5.refs_1_ = f32[256,512]{1,0:T(8,128)S(1)} collective-permute-done((f32[256,512]{1,0:T(8,128)S(1)}, f32[256,512]{1,0:T(8,128)S(1)}, u32[]{:S(2)}, u32[]{:S(2)}) %collective-permute-start.5) | collective-permute-done | bytes 524320 | tf_op jit(solution)/shard_map/ppermute | solution.py:556
  43.6 1.0 collective-permute-done.6.refs_2_
  44.5 11.2 %collective-permute-done.7.refs_3_ = f32[256,512]{1,0:T(8,128)S(1)} collective-permute-done((f32[256,512]{1,0:T(8,128)S(1)}, f32[256,512]{1,0:T(8,128)S(1)}, u32[]{:S(2)}, u32[]{:S(2)}) %collective-permute-start.7) | collective-permute-done | bytes 524320 | tf_op jit(solution)/shard_map/ppermute | solution.py:556
  55.7 1.1 shard_map.110
  56.9 1.6 shard_map.111
  58.6 1.2 collective-permute-start.9
  60.6 2.4 %collective-permute-start.18 = (f32[200,512]{1,0:T(8,128)}, f32[200,512]{1,0:T(8,128)}, u32[]{:S(2)}, u32[]{:S(2)}) collective-permute-start(f32[200,512]{1,0:T(8,128)} %get-tuple-element.98), channel_id=1, source_target_pairs={{0,24},{1,25},{2,26},{3,27},{4,28},{5,29},{6,30},{7,31},{8,16},{9,... | collective-permute-start | bytes 1228808 | tf_op jit(solution)/shard_map/ppermute | solution.py:556
  64.7 1.1 collective-permute-start.11
  66.9 1.3 copy.27
  68.3 1.4 copy.29
  69.6 1.4 copy.28
  71.0 1.4 copy.30
  72.4 7.2 %collective-permute-start.13 = (f32[256,512]{1,0:T(8,128)}, f32[256,512]{1,0:T(8,128)S(1)}, u32[]{:S(2)}, u32[]{:S(2)}) collective-permute-start(f32[256,512]{1,0:T(8,128)} %copy-done.33), channel_id=1, source_target_pairs={{0,8},{1,9},{2,10},{3,11},{4,12},{5,13},{6,14},{7,15},{8,0},{9,1},... | collective-permute-start | bytes 1572872 | tf_op jit(solution)/shard_map/ppermute | solution.py:556
  79.8 1.9 collective-permute-start.16
  82.3 1.4 broadcast_multiply_fusion.1
  83.7 1.6 broadcast_multiply_fusion
  85.3 5.0 %collective-permute-done.11.refs_3_ = f32[320,512]{1,0:T(8,128)S(1)} collective-permute-done((f32[320,512]{1,0:T(8,128)}, f32[320,512]{1,0:T(8,128)S(1)}, u32[]{:S(2)}, u32[]{:S(2)}) %collective-permute-start.11) | collective-permute-done | bytes 655392 | tf_op jit(solution)/shard_map/ppermute | solution.py:556
  91.1 2.4 %shard_map.112 = (f32[320,512]{1,0:T(8,128)}, f32[320,512]{1,0:T(8,128)}, f32[320,512]{1,0:T(8,128)}) custom-call(f32[320,512]{1,0:T(8,128)S(1)} %get-tuple-element.84.refs_0_, f32[320,512]{1,0:T(8,128)S(1)} %collective-permute-done.9.refs_1_, f32[320,512]{1,0:T(8,128)S(1)} %collective-permute-done.10.refs_2_, ...), custom_call_target="tpu_custom_call" | custom-call | tf_op jit(solution)/shard_map/pallas_call | solution.py:253
  93.5 0.8 copy-done.16
  94.3 27.4 %collective-permute-done.16.refs_5_ = f32[256,512]{1,0:T(8,128)S(1)} collective-permute-done((f32[256,512]{1,0:T(8,128)}, f32[256,512]{1,0:T(8,128)S(1)}, u32[]{:S(2)}, u32[]{:S(2)}) %collective-permute-start.16) | collective-permute-done | bytes 524320 | tf_op jit(solution)/shard_map/ppermute | solution.py:556
  121.7 0.8 copy-done.20
  122.5 0.8 copy-done.18
  123.5 3.9 %collective-permute-start.17 = (f32[320,512]{1,0:T(8,128)}, f32[320,512]{1,0:T(8,128)}, u32[]{:S(2)}, u32[]{:S(2)}) collective-permute-start(f32[320,512]{1,0:T(8,128)} %get-tuple-element.95), channel_id=1, source_target_pairs={{0,16},{1,17},{2,18},{3,19},{4,20},{5,21},{6,22},{7,23},{8,24},{9,... | collective-permute-start | bytes 1966088 | tf_op jit(solution)/shard_map/ppermute | solution.py:556
  127.5 1.4 broadcast_multiply_fusion.2
  129.6 3.9 %shard_map.113 = (f32[8,12,16,512]{3,2,1,0:T(8,128)}, f32[8,256]{1,0:T(8,128)S(1)}, f32[640,128]{1,0:T(8,128)S(1)}) custom-call(f32[200,512]{1,0:T(8,128)S(1)} %get-tuple-element.63.refs_0_, f32[200,512]{1,0:T(8,128)S(1)} %copy-done.8, f32[200,512]{1,0:T(8,128)S(1)} %copy-done.10, f32[200,512]{1,0:T(8,128)S(1)} %copy-done.12, ...), custom_call_target="tpu_custom_call" | custom-call | tf_op jit(solution)/shard_map/pallas_call | solution.py:356
  134.8 21.6 %collective-permute-start.24 = (f32[64,128]{1,0:T(8,128)S(1)}, f32[64,128]{1,0:T(8,128)S(1)}, u32[]{:S(2)}, u32[]{:S(2)}) collective-permute-start(f32[64,128]{1,0:T(8,128)S(1)} %get-tuple-element.110), channel_id=1, source_target_pairs={{0,3},{1,0},{2,1},{3,2},{4,7},{5,4},{6,5},{7,6},{8,11},{9,8},{10,9... | collective-permute-start | bytes 98312 | tf_op jit(solution)/shard_map/ppermute | solution.py:560
  156.7 0.9 mul.80
  157.7 1.0 mul.72
  158.7 1.2 mul.68
  160.2 2.2 %collective-permute-start.21 = (f32[64,128]{1,0:T(8,128)}, f32[64,128]{1,0:T(8,128)S(1)}, u32[]{:S(2)}, u32[]{:S(2)}) collective-permute-start(f32[64,128]{1,0:T(8,128)} %get-tuple-element.113), channel_id=1, source_target_pairs={{0,4},{4,8},{8,12},{12,16},{16,20},{20,24},{24,28},{28,0},{1,5},{5... | collective-permute-start | bytes 98312 | tf_op jit(solution)/shard_map/ppermute | solution.py:560
  164.0 1.0 copy.33
  165.0 0.8 tile.8
  165.8 1.2 tile.9.weights
  167.0 0.9 copy.36.mix
  167.9 15.0 %collective-permute-done.22.from_xup = f32[64,128]{1,0:T(8,128)S(1)} collective-permute-done((f32[64,128]{1,0:T(8,128)}, f32[64,128]{1,0:T(8,128)S(1)}, u32[]{:S(2)}, u32[]{:S(2)}) %collective-permute-start.22) | collective-permute-done | bytes 32800 | tf_op jit(solution)/shard_map/ppermute | solution.py:560
  182.9 1.0 copy-done.15
  183.9 2.1 shard_map.116
  186.0 2.4 %collective-permute-start.26 = (f32[64,128]{1,0:T(8,128)S(1)}, f32[64,128]{1,0:T(8,128)S(1)}, u32[]{:S(2)}, u32[]{:S(2)}) collective-permute-start(f32[64,128]{1,0:T(8,128)S(1)} %get-tuple-element.107.xup), channel_id=1, source_target_pairs={{0,4},{4,8},{8,12},{12,16},{16,20},{20,24},{24,28},{28,0},{1,5},{5... | collective-permute-start | bytes 98312 | tf_op jit(solution)/shard_map/ppermute | solution.py:560
  188.4 1.3 collective-permute-done.25.from_x_up
  189.7 3.2 %collective-permute-start.27 = (f32[64,128]{1,0:T(8,128)S(1)}, f32[64,128]{1,0:T(8,128)S(1)}, u32[]{:S(2)}, u32[]{:S(2)}) collective-permute-start(f32[64,128]{1,0:T(8,128)S(1)} %get-tuple-element.108.slow), channel_id=1, source_target_pairs={{0,3},{1,0},{2,1},{3,2},{4,7},{5,4},{6,5},{7,6},{8,11},{9,8},{10,9... | collective-permute-start | bytes 98312 | tf_op jit(solution)/shard_map/ppermute | solution.py:560
  193.1 1.6 collective-permute-done.27.from_s_up
  194.7 1.8 shard_map.117
  196.4 1.0 copy-done.2
  197.5 1.0 copy-done.4
  198.5 1.0 copy-done.6
  199.5 1.0 copy-done.17
  200.6 1.0 copy-done.19
  201.6 1.0 copy-done.21
  202.7 2.4 %shard_map.114.refs_8_ = f32[8,12,16,512]{3,2,1,0:T(8,128)} custom-call(f32[256,512]{1,0:T(8,128)S(1)} %get-tuple-element.73.refs_0_, f32[256,512]{1,0:T(8,128)S(1)} %copy-done.2, f32[256,512]{1,0:T(8,128)S(1)} %copy-done.4, f32[256,512]{1,0:T(8,128)S(1)} %copy-done.6, f32[256,512]{1,0:T(8,128)S(1)} %copy-done.17, ...), custom_call_target="tpu_custom_call", output_to_operand_aliasing={{}: (8, {})} | custom-call | tf_op jit(solution)/shard_map/pallas_call | solution.py:356
  205.1 4.6 %shard_map.115 = f32[8,12,16,512]{3,2,1,0:T(8,128)} custom-call(f32[320,512]{1,0:T(8,128)S(1)} %get-tuple-element.84.refs_0_, f32[320,512]{1,0:T(8,128)S(1)} %collective-permute-done.9.refs_1_, f32[320,512]{1,0:T(8,128)S(1)} %collective-permute-done.10.refs_2_, f32[320,512]{1,0:T(8,128)S(1)} %collective-permute-done.11.refs_3_, ...), custom_call_target="tpu_custom_call", output_to_operand_aliasing={{}: (8, {})} | custom-call | tf_op jit(solution)/shard_map/pallas_call | solution.py:356
  (123 shorter events, 13.0 us)
Async XLA Ops:
  0.6 2.8 %copy-start = (f32[256,12,512]{2,0,1:T(8,128)S(1)}, f32[256,12,512]{2,0,1:T(8,128)}, u32[]{:S(2)}) copy-start(f32[256,12,512]{2,0,1:T(8,128)} %param.9) | copy-start | bytes 18874372
  4.1 7.4 %slice-start = ((s8[6291456]{0:T(1024)(128)(4,1)}), s8[4194304]{0:T(1024)(128)(4,1)S(1)}, s32[]{:S(2)}) async-start(s8[6291456]{0:T(1024)(128)(4,1)} %bitcast.33), calls=%async_computation | async-start | bytes 8388608
  5.9 5.6 %slice-start.1 = ((s8[6291456]{0:T(1024)(128)(4,1)}), s8[2097152]{0:T(1024)(128)(4,1)S(1)}, s32[]{:S(2)}) async-start(s8[6291456]{0:T(1024)(128)(4,1)} %bitcast.33), calls=%async_computation.1 | async-start | bytes 4194304
  5.9 2.8 %collective-permute-start = (f32[392,512]{1,0:T(8,128)S(1)}, f32[392,512]{1,0:T(8,128)S(1)}, u32[]{:S(2)}, u32[]{:S(2)}) collective-permute-start(f32[392,512]{1,0:T(8,128)S(1)} %get-tuple-element.62), channel_id=1, source_target_pairs={{0,1},{1,0},{2,3},{3,2},{4,5},{5,4},{6,7},{7,6},{8,9},{9,8},{10,11... | collective-permute-start | bytes 2408456 | tf_op jit(solution)/shard_map/ppermute | solution.py:556
  8.6 23.0 %collective-permute-start.4 = (f32[512,512]{1,0:T(8,128)S(1)}, f32[512,512]{1,0:T(8,128)S(1)}, u32[]{:S(2)}, u32[]{:S(2)}) collective-permute-start(f32[512,512]{1,0:T(8,128)S(1)} %get-tuple-element.72), channel_id=1, source_target_pairs={{0,1},{1,0},{2,3},{3,2},{4,5},{5,4},{6,7},{7,6},{8,9},{9,8},{10,11... | collective-permute-start | bytes 3145736 | tf_op jit(solution)/shard_map/ppermute | solution.py:556
  8.8 10.6 %collective-permute-start.1 = (f32[200,512]{1,0:T(8,128)S(1)}, f32[200,512]{1,0:T(8,128)S(1)}, u32[]{:S(2)}, u32[]{:S(2)}) collective-permute-start(f32[200,512]{1,0:T(8,128)S(1)} %get-tuple-element.64), channel_id=1, source_target_pairs={{0,2},{1,3},{2,0},{3,1},{4,6},{5,7},{6,4},{7,5},{8,10},{9,11},{10,... | collective-permute-start | bytes 1228808 | tf_op jit(solution)/shard_map/ppermute | solution.py:556
  10.1 10.3 %collective-permute-start.2 = (f32[200,512]{1,0:T(8,128)S(1)}, f32[200,512]{1,0:T(8,128)S(1)}, u32[]{:S(2)}, u32[]{:S(2)}) collective-permute-start(f32[200,512]{1,0:T(8,128)S(1)} %get-tuple-element.65), channel_id=1, source_target_pairs={{0,4},{1,5},{2,6},{3,7},{4,0},{5,1},{6,2},{7,3},{8,12},{9,13},{10,... | collective-permute-start | bytes 1228808 | tf_op jit(solution)/shard_map/ppermute | solution.py:556
  10.3 18.7 %collective-permute-start.3 = (f32[200,512]{1,0:T(8,128)S(1)}, f32[200,512]{1,0:T(8,128)S(1)}, u32[]{:S(2)}, u32[]{:S(2)}) collective-permute-start(f32[200,512]{1,0:T(8,128)S(1)} %get-tuple-element.66), channel_id=1, source_target_pairs={{0,6},{1,7},{2,4},{3,5},{4,2},{5,3},{6,0},{7,1},{8,14},{9,15},{10,... | collective-permute-start | bytes 1228808 | tf_op jit(solution)/shard_map/ppermute | solution.py:556
  13.8 43.0 %collective-permute-start.8 = (f32[640,512]{1,0:T(8,128)S(1)}, f32[640,512]{1,0:T(8,128)S(1)}, u32[]{:S(2)}, u32[]{:S(2)}) collective-permute-start(f32[640,512]{1,0:T(8,128)S(1)} %get-tuple-element.83), channel_id=1, source_target_pairs={{0,1},{1,0},{2,3},{3,2},{4,5},{5,4},{6,7},{7,6},{8,9},{9,8},{10,11... | collective-permute-start | bytes 3932168 | tf_op jit(solution)/shard_map/ppermute | solution.py:556
  19.4 12.1 %copy-start.7 = (f32[200,512]{1,0:T(8,128)}, f32[200,512]{1,0:T(8,128)S(1)}, u32[]{:S(2)}) copy-start(f32[200,512]{1,0:T(8,128)S(1)} %collective-permute-done.1.refs_1_) | copy-start | bytes 1228804
  20.3 11.2 %copy-start.9 = (f32[200,512]{1,0:T(8,128)}, f32[200,512]{1,0:T(8,128)S(1)}, u32[]{:S(2)}) copy-start(f32[200,512]{1,0:T(8,128)S(1)} %collective-permute-done.2.refs_2_) | copy-start | bytes 1228804
  29.1 2.5 %copy-start.11 = (f32[200,512]{1,0:T(8,128)}, f32[200,512]{1,0:T(8,128)S(1)}, u32[]{:S(2)}) copy-start(f32[200,512]{1,0:T(8,128)S(1)} %collective-permute-done.3.refs_3_) | copy-start | bytes 1228804
  31.5 24.2 %copy-start.24 = (f32[8,256]{1,0:T(8,128)}, f32[8,256]{1,0:T(8,128)S(1)}, u32[]{:S(2)}) copy-start(f32[8,256]{1,0:T(8,128)S(1)} %get-tuple-element.77.refs_4_) | copy-start | bytes 24580
  31.5 2.9 %copy-start.35 = (f32[10,10]{1,0:T(8,128)S(1)}, f32[10,10]{1,0:T(8,128)}, u32[]{:S(2)}) copy-start(f32[10,10]{1,0:T(8,128)} %param.11) | copy-start | bytes 1204
  31.6 2.9 %copy-start.36 = (f32[10,10]{1,0:T(8,128)S(1)}, f32[10,10]{1,0:T(8,128)}, u32[]{:S(2)}) copy-start(f32[10,10]{1,0:T(8,128)} %param.12) | copy-start | bytes 1204
  31.7 11.9 %collective-permute-start.5 = (f32[256,512]{1,0:T(8,128)S(1)}, f32[256,512]{1,0:T(8,128)S(1)}, u32[]{:S(2)}, u32[]{:S(2)}) collective-permute-start(f32[256,512]{1,0:T(8,128)S(1)} %get-tuple-element.74), channel_id=1, source_target_pairs={{0,2},{1,3},{2,0},{3,1},{4,6},{5,7},{6,4},{7,5},{8,10},{9,11},{10,... | collective-permute-start | bytes 1572872 | tf_op jit(solution)/shard_map/ppermute | solution.py:556
  33.0 11.5 %collective-permute-start.6 = (f32[256,512]{1,0:T(8,128)S(1)}, f32[256,512]{1,0:T(8,128)S(1)}, u32[]{:S(2)}, u32[]{:S(2)}) collective-permute-start(f32[256,512]{1,0:T(8,128)S(1)} %get-tuple-element.75), channel_id=1, source_target_pairs={{0,4},{1,5},{2,6},{3,7},{4,0},{5,1},{6,2},{7,3},{8,12},{9,13},{10,... | collective-permute-start | bytes 1572872 | tf_op jit(solution)/shard_map/ppermute | solution.py:556
  33.3 22.5 %collective-permute-start.7 = (f32[256,512]{1,0:T(8,128)S(1)}, f32[256,512]{1,0:T(8,128)S(1)}, u32[]{:S(2)}, u32[]{:S(2)}) collective-permute-start(f32[256,512]{1,0:T(8,128)S(1)} %get-tuple-element.76), channel_id=1, source_target_pairs={{0,6},{1,7},{2,4},{3,5},{4,2},{5,3},{6,0},{7,1},{8,14},{9,15},{10,... | collective-permute-start | bytes 1572872 | tf_op jit(solution)/shard_map/ppermute | solution.py:556
  34.4 25.4 %copy-start.34 = (f32[8,10]{1,0:T(8,128)}, f32[8,10]{1,0:T(8,128)S(1)}, u32[]{:S(2)}) copy-start(f32[8,10]{1,0:T(8,128)S(1)} %slice.36) | copy-start | bytes 964
  34.5 29.4 %collective-permute-start.15 = (f32[200,512]{1,0:T(8,128)S(1)}, f32[200,512]{1,0:T(8,128)S(1)}, u32[]{:S(2)}, u32[]{:S(2)}) collective-permute-start(f32[200,512]{1,0:T(8,128)S(1)} %get-tuple-element.93), channel_id=1, source_target_pairs={{0,16},{1,17},{2,18},{3,19},{4,20},{5,21},{6,22},{7,23},{8,24},{9,... | collective-permute-start | bytes 1228808 | tf_op jit(solution)/shard_map/ppermute | solution.py:556
  43.6 13.3 %copy-start.1 = (f32[256,512]{1,0:T(8,128)}, f32[256,512]{1,0:T(8,128)S(1)}, u32[]{:S(2)}) copy-start(f32[256,512]{1,0:T(8,128)S(1)} %collective-permute-done.5.refs_1_) | copy-start | bytes 1572868
  44.5 12.3 %copy-start.3 = (f32[256,512]{1,0:T(8,128)}, f32[256,512]{1,0:T(8,128)S(1)}, u32[]{:S(2)}) copy-start(f32[256,512]{1,0:T(8,128)S(1)} %collective-permute-done.6.refs_2_) | copy-start | bytes 1572868
  55.7 1.2 copy-start.5
  56.8 1.6 copy-start.31
  56.8 1.6 copy-start.32
  56.8 1.8 copy-start.33
  58.6 21.2 %collective-permute-start.9 = (f32[320,512]{1,0:T(8,128)}, f32[320,512]{1,0:T(8,128)S(1)}, u32[]{:S(2)}, u32[]{:S(2)}) collective-permute-start(f32[320,512]{1,0:T(8,128)} %get-tuple-element.85), channel_id=1, source_target_pairs={{0,2},{1,3},{2,0},{3,1},{4,6},{5,7},{6,4},{7,5},{8,10},{9,11},{10,... | collective-permute-start | bytes 1966088 | tf_op jit(solution)/shard_map/ppermute | solution.py:556
  60.4 11.9 %collective-permute-start.12 = (f32[200,512]{1,0:T(8,128)}, f32[200,512]{1,0:T(8,128)}, u32[]{:S(2)}, u32[]{:S(2)}) collective-permute-start(f32[200,512]{1,0:T(8,128)} %get-tuple-element.67), channel_id=1, source_target_pairs={{0,8},{1,9},{2,10},{3,11},{4,12},{5,13},{6,14},{7,15},{8,0},{9,1},... | collective-permute-start | bytes 1228808 | tf_op jit(solution)/shard_map/ppermute | solution.py:556
  60.6 11.8 %collective-permute-start.18 = (f32[200,512]{1,0:T(8,128)}, f32[200,512]{1,0:T(8,128)}, u32[]{:S(2)}, u32[]{:S(2)}) collective-permute-start(f32[200,512]{1,0:T(8,128)} %get-tuple-element.98), channel_id=1, source_target_pairs={{0,24},{1,25},{2,26},{3,27},{4,28},{5,29},{6,30},{7,31},{8,16},{9,... | collective-permute-start | bytes 1228808 | tf_op jit(solution)/shard_map/ppermute | solution.py:556
  63.6 21.7 %collective-permute-start.10 = (f32[320,512]{1,0:T(8,128)}, f32[320,512]{1,0:T(8,128)S(1)}, u32[]{:S(2)}, u32[]{:S(2)}) collective-permute-start(f32[320,512]{1,0:T(8,128)} %get-tuple-element.86), channel_id=1, source_target_pairs={{0,4},{1,5},{2,6},{3,7},{4,0},{5,1},{6,2},{7,3},{8,12},{9,13},{10,... | collective-permute-start | bytes 1966088 | tf_op jit(solution)/shard_map/ppermute | solution.py:556
  64.7 25.7 %collective-permute-start.11 = (f32[320,512]{1,0:T(8,128)}, f32[320,512]{1,0:T(8,128)S(1)}, u32[]{:S(2)}, u32[]{:S(2)}) collective-permute-start(f32[320,512]{1,0:T(8,128)} %get-tuple-element.87), channel_id=1, source_target_pairs={{0,6},{1,7},{2,4},{3,5},{4,2},{5,3},{6,0},{7,1},{8,14},{9,15},{10,... | collective-permute-start | bytes 1966088 | tf_op jit(solution)/shard_map/ppermute | solution.py:556
  72.3 56.5 %copy-start.8 = (f32[200,512]{1,0:T(8,128)S(1)}, f32[200,512]{1,0:T(8,128)}, u32[]{:S(2)}) copy-start(f32[200,512]{1,0:T(8,128)} %copy-done.7) | copy-start | bytes 1228804
  72.3 56.5 %copy-start.10 = (f32[200,512]{1,0:T(8,128)S(1)}, f32[200,512]{1,0:T(8,128)}, u32[]{:S(2)}) copy-start(f32[200,512]{1,0:T(8,128)} %copy-done.9) | copy-start | bytes 1228804
  72.3 56.5 %copy-start.12 = (f32[200,512]{1,0:T(8,128)S(1)}, f32[200,512]{1,0:T(8,128)}, u32[]{:S(2)}) copy-start(f32[200,512]{1,0:T(8,128)} %copy-done.11) | copy-start | bytes 1228804
  72.3 56.5 %copy-start.13 = (bf16[640,512]{1,0:T(8,128)(2,1)S(1)}, bf16[640,512]{1,0:T(8,128)(2,1)}, u32[]{:S(2)}) copy-start(bf16[640,512]{1,0:T(8,128)(2,1)} %constant.18.clone.refs_8_) | copy-start | bytes 1966084
  72.4 56.5 %copy-start.23 = (f32[200,512]{1,0:T(8,128)S(1)}, f32[200,512]{1,0:T(8,128)}, u32[]{:S(2)}) copy-start(f32[200,512]{1,0:T(8,128)} %copy-done.22) | copy-start | bytes 1228804
  72.4 21.1 %collective-permute-start.13 = (f32[256,512]{1,0:T(8,128)}, f32[256,512]{1,0:T(8,128)S(1)}, u32[]{:S(2)}, u32[]{:S(2)}) collective-permute-start(f32[256,512]{1,0:T(8,128)} %copy-done.33), channel_id=1, source_target_pairs={{0,8},{1,9},{2,10},{3,11},{4,12},{5,13},{6,14},{7,15},{8,0},{9,1},... | collective-permute-start | bytes 1572872 | tf_op jit(solution)/shard_map/ppermute | solution.py:556
  79.6 42.8 %collective-permute-start.19 = (f32[256,512]{1,0:T(8,128)}, f32[256,512]{1,0:T(8,128)S(1)}, u32[]{:S(2)}, u32[]{:S(2)}) collective-permute-start(f32[256,512]{1,0:T(8,128)} %copy-done.31), channel_id=1, source_target_pairs={{0,24},{1,25},{2,26},{3,27},{4,28},{5,29},{6,30},{7,31},{8,16},{9,... | collective-permute-start | bytes 1572872 | tf_op jit(solution)/shard_map/ppermute | solution.py:556
  79.8 41.9 %collective-permute-start.16 = (f32[256,512]{1,0:T(8,128)}, f32[256,512]{1,0:T(8,128)S(1)}, u32[]{:S(2)}, u32[]{:S(2)}) collective-permute-start(f32[256,512]{1,0:T(8,128)} %copy-done.32), channel_id=1, source_target_pairs={{0,16},{1,17},{2,18},{3,19},{4,20},{5,21},{6,22},{7,23},{8,24},{9,... | collective-permute-start | bytes 1572872 | tf_op jit(solution)/shard_map/ppermute | solution.py:556
  91.0 65.6 %copy-start.37 = (f32[10]{0:T(128)S(1)}, f32[10]{0:T(128)}, u32[]{:S(2)}) copy-start(f32[10]{0:T(128)} %param.15) | copy-start | bytes 124
  91.0 65.6 %copy-start.38 = (f32[10]{0:T(128)S(1)}, f32[10]{0:T(128)}, u32[]{:S(2)}) copy-start(f32[10]{0:T(128)} %param.14) | copy-start | bytes 124
  93.5 0.8 copy-start.16
  121.7 0.8 copy-start.20
  122.5 0.8 copy-start.18
  123.3 81.8 %collective-permute-start.20 = (f32[320,512]{1,0:T(8,128)}, f32[320,512]{1,0:T(8,128)}, u32[]{:S(2)}, u32[]{:S(2)}) collective-permute-start(f32[320,512]{1,0:T(8,128)} %get-tuple-element.100), channel_id=1, source_target_pairs={{0,24},{1,25},{2,26},{3,27},{4,28},{5,29},{6,30},{7,31},{8,16},{9,... | collective-permute-start | bytes 1966088 | tf_op jit(solution)/shard_map/ppermute | solution.py:556
  123.5 81.5 %collective-permute-start.17 = (f32[320,512]{1,0:T(8,128)}, f32[320,512]{1,0:T(8,128)}, u32[]{:S(2)}, u32[]{:S(2)}) collective-permute-start(f32[320,512]{1,0:T(8,128)} %get-tuple-element.95), channel_id=1, source_target_pairs={{0,16},{1,17},{2,18},{3,19},{4,20},{5,21},{6,22},{7,23},{8,24},{9,... | collective-permute-start | bytes 1966088 | tf_op jit(solution)/shard_map/ppermute | solution.py:556
  127.4 77.7 %collective-permute-start.14 = (f32[320,512]{1,0:T(8,128)}, f32[320,512]{1,0:T(8,128)}, u32[]{:S(2)}, u32[]{:S(2)}) collective-permute-start(f32[320,512]{1,0:T(8,128)} %get-tuple-element.90), channel_id=1, source_target_pairs={{0,8},{1,9},{2,10},{3,11},{4,12},{5,13},{6,14},{7,15},{8,0},{9,1},... | collective-permute-start | bytes 1966088 | tf_op jit(solution)/shard_map/ppermute | solution.py:556
  133.5 23.0 %copy-start.26 = (f32[8,256]{1,0:T(8,128)}, f32[8,256]{1,0:T(8,128)S(1)}, u32[]{:S(2)}) copy-start(f32[8,256]{1,0:T(8,128)S(1)} %get-tuple-element.102.refs_7_) | copy-start | bytes 24580
  134.8 25.1 %collective-permute-start.24 = (f32[64,128]{1,0:T(8,128)S(1)}, f32[64,128]{1,0:T(8,128)S(1)}, u32[]{:S(2)}, u32[]{:S(2)}) collective-permute-start(f32[64,128]{1,0:T(8,128)S(1)} %get-tuple-element.110), channel_id=1, source_target_pairs={{0,3},{1,0},{2,1},{3,2},{4,7},{5,4},{6,5},{7,6},{8,11},{9,8},{10,9... | collective-permute-start | bytes 98312 | tf_op jit(solution)/shard_map/ppermute | solution.py:560
  156.4 40.0 %copy-start.27 = (f32[8,256]{1,0:T(8,128)S(1)}, f32[8,256]{1,0:T(8,128)}, u32[]{:S(2)}) copy-start(f32[8,256]{1,0:T(8,128)} %copy-done.26) | copy-start | bytes 24580
  156.4 3.8 %collective-permute-start.23 = (f32[64,128]{1,0:T(8,128)S(1)}, f32[64,128]{1,0:T(8,128)S(1)}, u32[]{:S(2)}, u32[]{:S(2)}) collective-permute-start(f32[64,128]{1,0:T(8,128)S(1)} %get-tuple-element.111), channel_id=1, source_target_pairs={{0,1},{1,2},{2,3},{3,0},{4,5},{5,6},{6,7},{7,4},{8,9},{9,10},{10,1... | collective-permute-start | bytes 98312 | tf_op jit(solution)/shard_map/ppermute | solution.py:560
  160.0 22.9 %collective-permute-start.22 = (f32[64,128]{1,0:T(8,128)}, f32[64,128]{1,0:T(8,128)S(1)}, u32[]{:S(2)}, u32[]{:S(2)}) collective-permute-start(f32[64,128]{1,0:T(8,128)} %get-tuple-element.112), channel_id=1, source_target_pairs={{0,28},{4,0},{8,4},{12,8},{16,12},{20,16},{24,20},{28,24},{1,29},{... | collective-permute-start | bytes 98312 | tf_op jit(solution)/shard_map/ppermute | solution.py:560
  160.2 22.7 %collective-permute-start.21 = (f32[64,128]{1,0:T(8,128)}, f32[64,128]{1,0:T(8,128)S(1)}, u32[]{:S(2)}, u32[]{:S(2)}) collective-permute-start(f32[64,128]{1,0:T(8,128)} %get-tuple-element.113), channel_id=1, source_target_pairs={{0,4},{4,8},{8,12},{12,16},{16,20},{20,24},{24,28},{28,0},{1,5},{5... | collective-permute-start | bytes 98312 | tf_op jit(solution)/shard_map/ppermute | solution.py:560
  182.9 1.0 copy-start.15
  186.0 3.7 %collective-permute-start.25 = (f32[64,128]{1,0:T(8,128)S(1)}, f32[64,128]{1,0:T(8,128)S(1)}, u32[]{:S(2)}, u32[]{:S(2)}) collective-permute-start(f32[64,128]{1,0:T(8,128)S(1)} %get-tuple-element.106.xlow), channel_id=1, source_target_pairs={{0,28},{4,0},{8,4},{12,8},{16,12},{20,16},{24,20},{28,24},{1,29},{... | collective-permute-start | bytes 98312 | tf_op jit(solution)/shard_map/ppermute | solution.py:560
  186.0 6.9 %collective-permute-start.26 = (f32[64,128]{1,0:T(8,128)S(1)}, f32[64,128]{1,0:T(8,128)S(1)}, u32[]{:S(2)}, u32[]{:S(2)}) collective-permute-start(f32[64,128]{1,0:T(8,128)S(1)} %get-tuple-element.107.xup), channel_id=1, source_target_pairs={{0,4},{4,8},{8,12},{12,16},{16,20},{20,24},{24,28},{28,0},{1,5},{5... | collective-permute-start | bytes 98312 | tf_op jit(solution)/shard_map/ppermute | solution.py:560
  189.7 5.0 %collective-permute-start.27 = (f32[64,128]{1,0:T(8,128)S(1)}, f32[64,128]{1,0:T(8,128)S(1)}, u32[]{:S(2)}, u32[]{:S(2)}) collective-permute-start(f32[64,128]{1,0:T(8,128)S(1)} %get-tuple-element.108.slow), channel_id=1, source_target_pairs={{0,3},{1,0},{2,1},{3,2},{4,7},{5,4},{6,5},{7,6},{8,11},{9,8},{10,9... | collective-permute-start | bytes 98312 | tf_op jit(solution)/shard_map/ppermute | solution.py:560
  192.9 1.7 collective-permute-start.28
  196.4 1.0 copy-start.2
  197.5 1.0 copy-start.4
  198.5 1.0 copy-start.6
  199.5 1.0 copy-start.17
  200.6 1.0 copy-start.19
  201.6 1.0 copy-start.21
  (6 other events, 4.2 us)

commit v3 on v2

--- a/solution.py
+++ b/solution.py
@@ -33,11 +33,11 @@
         self.pairs = self.plane // 2
         self.pair_rows = 2 * self.msg_rows
         self.rows = self.plane * self.msg_rows
-        full = self.plane * self.cap
-        self.kept = [full] * self.lines
-        self.offset = [sum(self.kept[:m]) for m in range(self.lines)]
-        self.relay_rows = sum(self.kept) - full
-        self.groups = [(0, 3), (3, 4), (7, 5)]
+        self.full = self.plane * self.cap
+        self.kept = [self.full] * 2 + [self.full * 3 // 4] * (self.lines - 2)
+        self.spill = [m for m in range(self.lines) if self.kept[m] < self.full]
+        second = (fields - 3) * 4 // 9
+        self.groups = [(0, 3), (3, second), (3 + second, fields - 3 - second)]
 
 
 def halves(value, count):
@@ -146,9 +146,9 @@
     )(me, place_row, states)
 
 
-def merge_kernel(plan, fields, marked, *refs):
+def merge_kernel(plan, fields, marked, flagged, *refs):
     near, refs = refs[: plan.pairs], refs[plan.pairs :]
-    aside, outs = refs[0], refs[1:]
+    aside, outs = refs[0], refs[-plan.pairs :]
     rows = plan.msg_rows
     for b, out in enumerate(outs):
         for field in range(fields):
@@ -165,14 +165,18 @@
             base = fields * plan.pair_rows
             out[base : base + 8, :] = jnp.zeros((8, plan.points), F32)
             out[base : base + 8, : plan.rows] = marks
-
-
-def merge(plan, group, near, aside, marked, cost):
+        if flagged:
+            base = fields * plan.pair_rows
+            out[base : base + 8, :] = jnp.zeros((8, plan.points), F32)
+            out[base : base + 8, : plan.rows] = jnp.maximum(refs[1][...], refs[2][...])
+
+
+def merge(plan, group, near, aside, marked, flags, cost):
     _, fields = group
-    shape = (fields * plan.pair_rows + (8 if marked else 0), plan.points)
+    shape = (fields * plan.pair_rows + (8 if marked or flags else 0), plan.points)
     return simple_call(
-        functools.partial(merge_kernel, plan, fields, marked),
-        [*near, aside],
+        functools.partial(merge_kernel, plan, fields, marked, bool(flags)),
+        [*near, aside, *flags],
         [jax.ShapeDtypeStruct(shape, F32)] * plan.pairs,
         [],
         cost,
@@ -187,10 +191,12 @@
     earlier = jnp.dot(valid.astype(BF16), before(plan.rows), preferred_element_type=F32)
     earlier = earlier.astype(jnp.int32)
     row = halves(lane, plan.msg_rows) * plan.cap + rest(lane, plan.cap)
+    over = jnp.zeros((1, plan.rows), F32)
     for m in range(1, plan.lines):
-        place = jnp.where(earlier[m : m + 1] < plan.kept[m], earlier[m : m + 1] + plan.offset[m], -1)
-        row = jnp.where(step == m, place, row)
-    return jnp.where(filled, row, -1)
+        number = earlier[m : m + 1]
+        row = jnp.where(step == m, number + m * plan.full, row)
+        over = jnp.maximum(over, jnp.where((step == m) & filled & (number >= plan.kept[m]), 1.0, 0.0))
+    return jnp.where(filled, row, -1), jnp.max(over, axis=1, keepdims=True)
 
 
 def gather_marks(plan, fields, messages):
@@ -203,32 +209,40 @@
     return marks
 
 
-def relay_kernel(plan, fields, marked, *refs):
+def put_tail(plan, out, value):
+    base = out.shape[0] - 8
+    out[base:, :] = jnp.zeros((8, plan.points), F32)
+    out[base:, : plan.rows] = value
+
+
+def relay_kernel(plan, fields, marked, flagged, *refs):
     messages, refs = refs[: plan.pairs], refs[plan.pairs :]
     if not marked:
         marks_ref, refs = refs[0], refs[1:]
     outs, refs = refs[: plan.lines - 1], refs[plan.lines - 1 :]
-    if marked:
-        marks = gather_marks(plan, fields, messages)
-        marks_out, own_out = refs[:2]
-        refs = refs[2:]
-        marks_out[...] = marks
-    else:
-        marks = marks_ref[...]
-    (held,) = refs
-    row = route_rows(plan, marks)
+    late, refs = refs[: len(plan.spill)], refs[len(plan.spill) :]
+    held = refs[-1]
+    marks = gather_marks(plan, fields, messages) if marked else marks_ref[...]
+    row, over = route_rows(plan, marks)
     spread = (iota((plan.rows, plan.rows), 0) == row).astype(F32)
     if marked:
+        marks_out, own_out, flag_out = refs[:3]
         landed = lax.dot_general(
             marks, spread, (((1,), (1,)), ((), ())), precision=HIGHEST, preferred_element_type=F32
         )
+        marks_out[...] = marks
         own_out[...] = landed
-        for m, out in enumerate(outs, 1):
-            base = fields * plan.kept[m]
-            out[base : base + 8, :] = jnp.zeros((8, plan.points), F32)
-            out[base : base + 8, : plan.rows] = landed
-    first = plan.offset[1]
-    chooser = spread[first : first + plan.relay_rows].astype(BF16)
+        flag_out[...] = jnp.broadcast_to(over, (8, plan.rows))
+        for out in outs:
+            put_tail(plan, out, landed)
+    if flagged:
+        flag = messages[0][fields * plan.pair_rows :, : plan.rows]
+        for message in messages[1:]:
+            flag = jnp.maximum(flag, message[fields * plan.pair_rows :, : plan.rows])
+        refs[0][...] = flag
+        for out in outs:
+            put_tail(plan, out, flag)
+    chooser = spread[plan.full :].astype(BF16)
     for field in range(fields):
         for b, message in enumerate(messages):
             held[b * plan.pair_rows : (b + 1) * plan.pair_rows, :] = message[
@@ -236,77 +250,78 @@
             ]
         moved = pick(chooser, held[...])
         for m, out in enumerate(outs, 1):
-            at = plan.offset[m] - first
-            out[field * plan.kept[m] : (field + 1) * plan.kept[m], :] = moved[at : at + plan.kept[m]]
-
-
-def relay(plan, group, messages, marks):
+            at, kept = (m - 1) * plan.full, plan.kept[m]
+            out[field * kept : (field + 1) * kept, :] = moved[at : at + kept]
+        for m, out in zip(plan.spill, late):
+            at, kept = (m - 1) * plan.full, plan.kept[m]
+            left = plan.full - kept
+            out[field * left : (field + 1) * left, :] = moved[at + kept : at + plan.full]
+
+
+def relay(plan, group, messages, marks, flagged):
     _, fields = group
     marked = marks is None
-    extra = 8 if marked else 0
-    out_shape = [
-        jax.ShapeDtypeStruct((fields * plan.kept[m] + extra, plan.points), F32) for m in range(1, plan.lines)
-    ]
-    if marked:
-        out_shape += [jax.ShapeDtypeStruct((8, plan.rows), F32)] * 2
-    operands = list(messages) + ([] if marked else [marks])
-    result = pl.pallas_call(
-        functools.partial(relay_kernel, plan, fields, marked),
-        in_specs=[pl.BlockSpec(memory_space=pltpu.VMEM)] * len(operands),
-        out_specs=[pl.BlockSpec(memory_space=pltpu.VMEM)] * len(out_shape),
-        out_shape=out_shape,
-        scratch_shapes=[pltpu.VMEM((plan.rows, plan.points), F32)],
-        compiler_params=PARAMS,
-    )(*operands)
-    return result[: plan.lines - 1], result[plan.lines - 1 :]
-
-
-def settle_kernel(plan, fields, marked, *refs):
+    extra = 8 if marked or flagged else 0
+    shapes = [(fields * kept + extra, plan.points) for kept in plan.kept[1:]]
+    shapes += [(fields * (plan.full - plan.kept[m]), plan.points) for m in plan.spill]
+    shapes += [(8, plan.rows)] * (3 if marked else 1 if flagged else 0)
+    result = simple_call(
+        functools.partial(relay_kernel, plan, fields, marked, flagged),
+        list(messages) + ([] if marked else [marks]),
+        [jax.ShapeDtypeStruct(shape, F32) for shape in shapes],
+        [pltpu.VMEM((plan.rows, plan.points), F32)],
+    )
+    split = plan.lines - 1
+    return result[:split], result[split : split + len(plan.spill)], result[split + len(plan.spill) :]
+
+
+def element_chooser(plan, marks):
+    element = iota((plan.per_dev, plan.rows), 0).astype(F32) + 1.0
+    return (element == marks[:1]).astype(F32).astype(BF16)
+
+
+def settle_kernel(plan, fields, marked, flagged, *refs):
     messages, refs = refs[: plan.pairs], refs[plan.pairs :]
     relays, refs = refs[: plan.lines - 1], refs[plan.lines - 1 :]
+    if marked or flagged:
+        tails, refs = refs[: plan.lines - 1], refs[plan.lines - 1 :]
     if marked:
-        own_ref, order_ref = refs[:2]
-        out, marks_out, cells_out = refs[2:5]
-        refs = refs[5:]
+        own_ref, order_ref, out, marks_out, cells_out, chooser_ref, held, pressure_ref = refs
+    elif flagged:
+        marks_ref, flag_ref, _, out, flag_out, chooser_ref, held = refs
     else:
-        marks_ref = refs[0]
-        out = refs[2]
-        refs = refs[3:]
-    chooser_ref, held = refs[:2]
+        marks_ref, _, out, chooser_ref, held = refs
     field = pl.program_id(0)
-    full = plan.kept[0]
 
     @pl.when(field == 0)
     def _():
         if marked:
             lane = iota((8, plan.rows), 1)
-            marks = jnp.where(lane < full, own_ref[...], 0.0)
+            marks = own_ref[...]
             for m in range(1, plan.lines):
-                base = fields * plan.kept[m]
-                part = relays[m - 1][base : base + 8, : plan.rows]
-                inside = (lane >= plan.offset[m]) & (lane < plan.offset[m] + plan.kept[m])
-                marks = jnp.where(inside, part, marks)
+                marks = jnp.where(halves(lane, plan.full) == m, tails[m - 1][:, : plan.rows], marks)
             marks_out[...] = marks
         else:
             marks = marks_ref[...]
-        element = iota((plan.per_dev, plan.rows), 0).astype(F32) + 1.0
-        chooser_ref[...] = (element == marks[:1]).astype(F32).astype(BF16)
-        used = plan.offset[-1] + plan.kept[-1]
-        if used < plan.rows:
-            held[used:, :] = jnp.zeros((plan.rows - used, plan.points), F32)
+        if flagged:
+            flag = flag_ref[...]
+            for tail in tails:
+                flag = jnp.maximum(flag, tail[:, : plan.rows])
+            flag_out[...] = flag
+        chooser_ref[...] = element_chooser(plan, marks)
+        for m in plan.spill:
+            start = m * plan.full + plan.kept[m]
+            held[start : (m + 1) * plan.full, :] = jnp.zeros((plan.full - plan.kept[m], plan.points), F32)
 
     for j in range(plan.plane):
-        start = pl.multiple_of((field * 2 + j % 2) * plan.msg_rows, plan.msg_rows)
-        part = messages[j // 2][pl.ds(start, plan.msg_rows), :]
-        held[j * plan.cap : (j + 1) * plan.cap, :] = part[: plan.cap]
+        start = j % 2 * plan.msg_rows
+        held[j * plan.cap : (j + 1) * plan.cap, :] = messages[j // 2][start : start + plan.cap, :]
     for m, part in enumerate(relays, 1):
-        kept = plan.kept[m]
-        held[plan.offset[m] : plan.offset[m] + kept, :] = part[pl.ds(pl.multiple_of(field * kept, 8), kept), :]
+        held[m * plan.full : m * plan.full + plan.kept[m], :] = part[...]
     placed = pick(chooser_ref[...], held[...])
     out[...] = placed.reshape(out.shape)
 
     if marked:
-        pressure_ref = refs[2]
 
         @pl.when(field == 0)
         def _():
@@ -332,29 +347,45 @@
     return order
 
 
-def settle(plan, group, messages, relays, marks, buffer, own, order):
+def states_block(plan, first):
+    columns = BX * BS
+    block = pl.BlockSpec((columns, 1, plan.layers, plan.points), lambda f: (0, first + f, 0, 0))
+    return block, jax.ShapeDtypeStruct((columns, plan.fields, plan.layers, plan.points), F32)
+
+
+def settle(plan, group, messages, relays, marks, buffer, own, order, flag):
     first, fields = group
-    marked = marks is None
-    columns = BX * BS
-    states_shape = (columns, plan.fields, plan.layers, plan.points)
-    out_specs = [pl.BlockSpec((columns, 1, plan.layers, plan.points), lambda f: (0, first + f, 0, 0))]
-    out_shape = [jax.ShapeDtypeStruct(states_shape, F32)]
+    marked, flagged = marks is None, flag is not None
+    in_vmem = pl.BlockSpec(memory_space=pltpu.VMEM)
+    block, states = states_block(plan, first)
+    out_specs, out_shape = [block], [states]
     scratch = [pltpu.VMEM((plan.per_dev, plan.rows), BF16), pltpu.VMEM((plan.rows, plan.points), F32)]
     operands = list(messages) + list(relays)
+    in_specs = [pl.BlockSpec((plan.pair_rows, plan.points), lambda f: (f, 0))] * plan.pairs
+    in_specs += [pl.BlockSpec((kept, plan.points), lambda f: (f, 0)) for kept in plan.kept[1:]]
+    if marked or flagged:
+        operands += list(relays)
+        in_specs += [
+            pl.BlockSpec((8, plan.points), lambda f, at=fields * kept // 8: (at, 0)) for kept in plan.kept[1:]
+        ]
+    known = [own, order] if marked else [marks, flag] if flagged else [marks]
+    operands += known
+    in_specs += [in_vmem] * len(known)
     aliases = {}
+    row = jax.ShapeDtypeStruct((8, plan.rows), F32)
     if marked:
-        operands += [own, order]
-        cells = (order.shape[0], plan.per_dev)
-        out_specs += [pl.BlockSpec(memory_space=pltpu.VMEM)] * 2
-        out_shape += [jax.ShapeDtypeStruct((8, plan.rows), F32), jax.ShapeDtypeStruct(cells, F32)]
+        out_shape += [row, jax.ShapeDtypeStruct((order.shape[0], plan.per_dev), F32)]
+        out_specs += [in_vmem] * 2
         scratch += [pltpu.VMEM((plan.per_dev, plan.points), F32)]
-        in_specs = [pl.BlockSpec(memory_space=pltpu.VMEM)] * len(operands)
     else:
-        operands += [marks, buffer]
-        in_specs = [pl.BlockSpec(memory_space=pltpu.VMEM)] * (len(operands) - 1) + [pl.BlockSpec(memory_space=pl.ANY)]
-        aliases = {len(operands) - 1: 0}
+        aliases = {len(operands): 0}
+        operands += [buffer]
+        in_specs += [pl.BlockSpec(memory_space=pl.ANY)]
+        if flagged:
+            out_shape += [row]
+            out_specs += [in_vmem]
     return pl.pallas_call(
-        functools.partial(settle_kernel, plan, fields, marked),
+        functools.partial(settle_kernel, plan, fields, marked, flagged),
         grid=(fields,),
         in_specs=in_specs,
         out_specs=out_specs,
@@ -363,6 +394,51 @@
         input_output_aliases=aliases,
         compiler_params=PARAMS,
     )(*operands)
+
+
+def add_late_kernel(plan, *refs):
+    parts, (marks_ref, states_ref, out, held) = refs[: len(plan.spill)], refs[len(plan.spill) :]
+    held[...] = jnp.zeros(held.shape, F32)
+    for m, part in zip(plan.spill, parts):
+        held[m * plan.full + plan.kept[m] : (m + 1) * plan.full, :] = part[...]
+    placed = pick(element_chooser(plan, marks_ref[...]), held[...])
+    out[...] = states_ref[...] + placed.reshape(out.shape)
+
+
+def add_late(plan, group, parts, marks, buffer):
+    first, fields = group
+    block, states = states_block(plan, first)
+    return pl.pallas_call(
+        functools.partial(add_late_kernel, plan),
+        grid=(fields,),
+        in_specs=[pl.BlockSpec((plan.full - plan.kept[m], plan.points), lambda f: (f, 0)) for m in plan.spill]
+        + [pl.BlockSpec(memory_space=pltpu.VMEM), block],
+        out_specs=block,
+        out_shape=states,
+        scratch_shapes=[pltpu.VMEM((plan.rows, plan.points), F32)],
+        input_output_aliases={len(parts) + 1: 0},
+        compiler_params=PARAMS,
+    )(*parts, marks, buffer)
+
+
+def cells_kernel(plan, states_ref, order_ref, out):
+    held = states_ref[...]
+    pressure = 3.0 * held[:, 0] - 3.0 * held[:, 1] + held[:, 2]
+    out[...] = pick(order_ref[...], pressure.reshape(plan.per_dev, plan.points), ((1,), (1,)))
+
+
+def cells_of(plan, buffer, order):
+    return pl.pallas_call(
+        functools.partial(cells_kernel, plan),
+        grid=(1,),
+        in_specs=[
+            pl.BlockSpec((BX * BS, 3, plan.layers, plan.points), lambda f: (0, 0, 0, 0)),
+            whole(order.shape),
+        ],
+        out_specs=whole((order.shape[0], plan.per_dev)),
+        out_shape=jax.ShapeDtypeStruct((order.shape[0], plan.per_dev), F32),
+        compiler_params=PARAMS,
+    )(buffer, order)
 
 
 def lane_steps(plan):
@@ -562,66 +638,86 @@
     order = jnp.asarray(cell_order(plan.side), BF16)
     tables = box_tables(plan, vectors_x, vectors_s, vectors_w, values_x, values_s, values_w)
 
-    merged = []
+    side = plan.side
+    inner = side * side
+
+    def solve(cells, earlier):
+        layered = cells.reshape(side, inner + 2 * FACE, plan.per_dev)
+
+        def rows(start):
+            return layered[:, start : start + FACE].reshape(side * FACE, plan.per_dev)
+
+        halo = [
+            shifted(rows(inner - FACE), "gx", 1),
+            shifted(rows(0), "gx", -1),
+            shifted(rows(inner), "gy", 1),
+            shifted(rows(inner + FACE), "gy", -1),
+        ]
+        if earlier is not None:
+            cells = after(cells, earlier)
+        face = jax.ShapeDtypeStruct((side * FACE, plan.per_dev), F32)
+        sections = (plan.extent, tables[0].shape[0], plan.per_dev)
+        total, xlow, xup, slow, sup = simple_call(
+            functools.partial(solve_kernel, plan),
+            [cells, *halo, *tables],
+            [jax.ShapeDtypeStruct((side * inner, plan.per_dev), F32)] + [face] * 4,
+            [pltpu.VMEM((plan.extent * (inner + 4 * FACE), plan.per_dev), F32)] + [pltpu.VMEM(sections, F32)] * 2,
+        )
+        returned = [shifted(xlow, "gx", -1), shifted(xup, "gx", 1), shifted(slow, "gy", -1), shifted(sup, "gy", 1)]
+        (correction,) = simple_call(
+            functools.partial(finish_kernel, plan),
+            [total, xlow, xup, slow, sup, *returned],
+            [jax.ShapeDtypeStruct((BX * side, BS * side, plan.layers * side), F32)],
+            [pltpu.VMEM((side * inner, plan.per_dev), F32)],
+        )
+        return correction
+
+    packed = []
     for g, group in enumerate(plan.groups):
         *near, aside = pack(plan, group, me, place_row, states, g == 0)
-        cost = pl.CostEstimate(flops=MERGE_FLOPS if g else 0, bytes_accessed=0, transcendentals=0)
-        merged.append(functools.partial(merge, plan, group, near, across(aside, 1), g == 0, cost))
-    marks = None
-    held = []
-    gate = None
-    arrived = [None] * (plan.lines - 1)
-    for g, group in enumerate(plan.groups):
-        if g:
-            near = merged[g].args[2]
-            merged[g] = functools.partial(
-                merge, plan, group, [after(near[0], gate)] + near[1:], *merged[g].args[3:]
-            )
-        sent = merged[g]()
+        packed.append((near, across(aside, 1)))
+
+    marks = gate = None
+    flags, arrived, held = [], [], []
+    for g, (group, (near, aside)) in enumerate(zip(plan.groups, packed)):
+        first, flagged = g == 0, g == 1
+        if not first:
+            near[0] = after(near[0], gate)
+        cost = pl.CostEstimate(flops=0 if first else MERGE_FLOPS, bytes_accessed=0, transcendentals=0)
+        sent = merge(plan, group, near, aside, first, flags if flagged else [], cost)
         messages = [sent[0]] + [across(sent[b], 2 * b) for b in range(1, plan.pairs)]
-        relays, more = relay(plan, group, messages, marks)
-        if marks is None:
-            marks, own = more
+        if not first:
+            messages[0] = after(messages[0], arrived[1:])
+        relays, late, more = relay(plan, group, messages, marks, flagged)
+        if first:
+            marks, own, over = more
+            flags = [over, across(over, 1)]
+        if flagged:
+            (flag,) = more
         gate = relays[0]
-        for m in reversed(range(1, plan.lines)):
-            ready = relays[m - 1]
-            if g:
-                ready = after(ready, arrived[m - 1])
-            arrived[m - 1] = across(ready, m * plan.plane)
-        held.append((messages, list(arrived)))
-
-    buffer, row_marks, cells = settle(plan, plan.groups[0], *held[0], None, None, own, order)
-    side = plan.side
-    face = jax.ShapeDtypeStruct((side * FACE, plan.per_dev), F32)
-    layered = cells.reshape(side, side * side + 2 * FACE, plan.per_dev)
-
-    def rows(start):
-        return layered[:, start : start + FACE].reshape(side * FACE, plan.per_dev)
-
-    inner = side * side
-    halo = [
-        shifted(rows(inner - FACE), "gx", 1),
-        shifted(rows(0), "gx", -1),
-        shifted(rows(inner), "gy", 1),
-        shifted(rows(inner + FACE), "gy", -1),
-    ]
-    modal_rows = tables[0].shape[0]
-    total, xlow, xup, slow, sup = simple_call(
-        functools.partial(solve_kernel, plan),
-        [cells, *halo, *tables],
-        [jax.ShapeDtypeStruct((side * inner, plan.per_dev), F32)] + [face] * 4,
-        [pltpu.VMEM((plan.extent * (inner + 4 * FACE), plan.per_dev), F32)]
-        + [pltpu.VMEM((plan.extent, modal_rows, plan.per_dev), F32)] * 2,
-    )
-    returned = [shifted(xlow, "gx", -1), shifted(xup, "gx", 1), shifted(slow, "gy", -1), shifted(sup, "gy", 1)]
-    (correction,) = simple_call(
-        functools.partial(finish_kernel, plan),
-        [total, xlow, xup, slow, sup, *returned],
-        [jax.ShapeDtypeStruct((BX * side, BS * side, plan.layers * side), F32)],
-        [pltpu.VMEM((side * inner, plan.per_dev), F32)],
-    )
-    for group, (messages, arrived) in zip(plan.groups[1:], held[1:]):
-        (buffer,) = settle(plan, group, messages, arrived, row_marks, buffer, None, None)
+        ready = list(relays)
+        ready[0] = after(ready[0], messages[1:] if first else [messages[1], arrived[0]])
+        arrived = [across(r, m * plan.plane) for m, r in enumerate(ready, 1)]
+        held.append((messages, arrived, late))
+
+    buffer, row_marks, cells = settle(plan, plan.groups[0], *held[0][:2], None, None, own, order, None)
+    buffer, flag = settle(plan, plan.groups[1], *held[1][:2], row_marks, buffer, None, None, flag)
+    correction = solve(after(cells, gate), buffer)
+    for group, (messages, arrived, _) in zip(plan.groups[2:], held[2:]):
+        (buffer,) = settle(plan, group, messages, arrived, row_marks, buffer, None, None, None)
+
+    def send_rest(buffer, correction, late):
+        for group, parts in zip(plan.groups, late):
+            parts = [across(part, m * plan.plane) for m, part in zip(plan.spill, parts)]
+            buffer = add_late(plan, group, parts, row_marks, buffer)
+        return buffer, solve(cells_of(plan, buffer, order), None)
+
+    def keep(buffer, correction, late):
+        return buffer, correction
+
+    late = [rows_left for _, _, rows_left in held]
+    if plan.spill:
+        buffer, correction = lax.cond(flag[0, 0] > 0.0, send_rest, keep, buffer, correction, late)
     new_states = buffer.reshape(BX, BS, fields, plan.layers, points).transpose(0, 1, 3, 2, 4)
     return new_states, correction
 

time: 213 us -> 194 us (0.911)
  starting transfers between devices: 58.8 us -> 39.2 us
  waiting for transfers between devices: 83 us -> 95.6 us
  local copies, waits for them, and re-layouts: 33.3 us -> 22.8 us
  other arithmetic: 5.67 us -> 2.93 us
  Pallas kernels: 27.9 us -> 30.2 us
    ppermute x8, starting transfers between devices: 30 us -> 12.3 us  [shifted(): lax.ppermute(value, axis, [(s, (s + steps) % count) for s in range(count)])]
    ppermute x8, waiting for transfers between devices: 17.9 us -> 35.4 us  [shifted(): lax.ppermute(value, axis, [(s, (s + steps) % count) for s in range(count)])]
    pallas_call x5 -> x8, Pallas kernels: 5.64 us -> 11.1 us  [simple_call(): pl.pallas_call(kernel, in_specs=[pl.BlockSpec(memory_space=pltpu.VMEM)] *...]
    ppermute x21 -> x22, waiting for transfers between devices: 65.1 us -> 60.2 us  [across(): lax.ppermute(value, both, [(d, d ^ flip) for d in range(plan.devices)])]
    mul x9, local copies, waits for them, and re-layouts: 7.12 us -> 3.37 us  [kron(): left[:, None, :, None] * right[None, :, None, :]]
    unnamed x82 -> x78, local copies, waits for them, and re-layouts: 16.9 us -> 13.3 us
    pallas_call x6 -> x3, Pallas kernels: 16.3 us -> 13.1 us  [settle(): pl.pallas_call(functools.partial(settle_kernel, plan, fields, marked, fla...]
    ppermute x21 -> x22, starting transfers between devices: 28.7 us -> 26.9 us  [across(): lax.ppermute(value, both, [(d, d ^ flip) for d in range(plan.devices)])]
  transfers between devices with their start and end apart: 29 -> 30, of which waited for: 11 -> 12; matrix products, arithmetic and copies ran while one was open for 11% -> 6% of each run, Pallas kernels for 10% -> 12%
where the time goes in v3:
time: 194 us; the launch traced here: 192 us
  waiting for transfers between devices  95.6 us (49%)
  starting transfers between devices  39.2 us (20%)
  Pallas kernels  30.2 us (16%)
  local copies, waits for them, and re-layouts  22.8 us (12%)
  other arithmetic  2.93 us (2%)
    ppermute x22, waiting for transfers between devices, across(): lax.ppermute(value, both, [(d, d ^ flip) for d in range(plan.devices)])  60.2 us
    ppermute x8, waiting for transfers between devices, shifted(): lax.ppermute(value, axis, [(s, (s + steps) % count) for s in range(count)])  35.4 us
    ppermute x22, starting transfers between devices, across(): lax.ppermute(value, both, [(d, d ^ flip) for d in range(plan.devices)])  26.9 us
    unnamed x78, local copies, waits for them, and re-layouts  13.3 us
    pallas_call x3, Pallas kernels, settle(): pl.pallas_call(functools.partial(settle_kernel, plan, fields, marked, fla...  13.1 us
    ppermute x8, starting transfers between devices, shifted(): lax.ppermute(value, axis, [(s, (s + steps) % count) for s in range(count)])  12.3 us
    pallas_call x8, Pallas kernels, simple_call(): pl.pallas_call(kernel, in_specs=[pl.BlockSpec(memory_space=pltpu.VMEM)] *...  11.1 us
    pallas_call x3, Pallas kernels, pack(): pl.pallas_call(functools.partial(pack_kernel, plan, fields, marked), grid...  6.01 us
  transfers between devices with their start and end apart: 30, of which 12 were waited for; matrix products, arithmetic and copies ran while one was open for 6% of the time, Pallas kernels for 12%

profile of v3, /device:TPU:11, one launch (start us, length us, event | category | flops | bytes accessed | tf_op | source)
XLA Modules:
  0.0 192.5 jit_solution(7971373577665001207)
XLA Ops:
  0.6 2.8 %copy-done = f32[256,12,512]{2,0,1:T(8,128)S(1)} copy-done((f32[256,12,512]{2,0,1:T(8,128)S(1)}, f32[256,12,512]{2,0,1:T(8,128)}, u32[]{:S(2)}) %copy-start) | copy-done | bytes 6291480
  4.1 1.8 shard_map.105
  5.9 0.7 collective-permute-start.14
  6.6 1.9 shard_map.104
  8.8 1.3 collective-permute-start.15
  10.4 1.1 collective-permute-start.17
  11.5 2.3 %shard_map.112 = (f32[160,512]{1,0:T(8,128)S(1)}, f32[160,512]{1,0:T(8,128)S(1)}, f32[160,512]{1,0:T(8,128)S(1)}, f32[160,512]{1,0:T(8,128)S(1)}, f32[640,512]{1,0:T(8,128)S(1)}) custom-call(s32[1]{0:T(128)} %bitcast.5.me_ref, s32[1,256]{1,0:T(1,128)S(1)} %bitcast.50, f32[12,256,512]{2,1,0:T(8,128)S(1)} %bitcast.45), custom_call_target="tpu_custom_call" | custom-call | tf_op jit(solution)/shard_map/pallas_call | solution.py:134
  13.9 1.4 collective-permute-start.29
  15.2 4.2 %collective-permute-done.15.refs_1_ = f32[200,512]{1,0:T(8,128)S(1)} collective-permute-done((f32[200,512]{1,0:T(8,128)S(1)}, f32[200,512]{1,0:T(8,128)S(1)}, u32[]{:S(2)}, u32[]{:S(2)}) %collective-permute-start.15) | collective-permute-done | bytes 409632 | tf_op jit(solution)/shard_map/ppermute | solution.py:632
  19.4 0.9 collective-permute-done.16.refs_2_
  20.3 8.7 %collective-permute-done.17.refs_3_ = f32[200,512]{1,0:T(8,128)S(1)} collective-permute-done((f32[200,512]{1,0:T(8,128)S(1)}, f32[200,512]{1,0:T(8,128)S(1)}, u32[]{:S(2)}, u32[]{:S(2)}) %collective-permute-start.17) | collective-permute-done | bytes 409632 | tf_op jit(solution)/shard_map/ppermute | solution.py:632
  29.1 1.9 shard_map.107
  30.9 1.6 collective-permute-start.19
  32.6 2.3 %collective-permute-start.20 = (f32[152,512]{1,0:T(8,128)S(1)}, f32[152,512]{1,0:T(8,128)S(1)}, u32[]{:S(2)}, u32[]{:S(2)}) collective-permute-start(f32[152,512]{1,0:T(8,128)S(1)} %get-tuple-element.138), channel_id=1, source_target_pairs={{0,16},{1,17},{2,18},{3,19},{4,20},{5,21},{6,22},{7,23},{8,24},{9,... | collective-permute-start | bytes 933896 | tf_op jit(solution)/shard_map/ppermute | solution.py:632
  35.1 1.3 collective-permute-start.22
  36.6 1.2 collective-permute-start.24
  37.8 10.8 %collective-permute-done.20.refs_5_.refs_8_ = f32[152,512]{1,0:T(8,128)S(1)} collective-permute-done((f32[152,512]{1,0:T(8,128)S(1)}, f32[152,512]{1,0:T(8,128)S(1)}, u32[]{:S(2)}, u32[]{:S(2)}) %collective-permute-start.20) | collective-permute-done | bytes 311328 | tf_op jit(solution)/shard_map/ppermute | solution.py:632
  48.6 15.1 %collective-permute-done.21.refs_6_.refs_9_ = f32[152,512]{1,0:T(8,128)S(1)} collective-permute-done((f32[152,512]{1,0:T(8,128)S(1)}, f32[152,512]{1,0:T(8,128)S(1)}, u32[]{:S(2)}, u32[]{:S(2)}) %collective-permute-start.21) | collective-permute-done | bytes 311328 | tf_op jit(solution)/shard_map/ppermute | solution.py:632
  63.7 0.7 copy-done.19
  64.5 1.9 shard_map.109
  66.4 0.8 copy-done.24
  67.2 1.5 collective-permute-start.27
  68.7 1.4 shard_map.113
  70.2 1.2 collective-permute-start.30
  71.7 1.2 collective-permute-start.32
  73.2 4.1 %collective-permute-done.25.refs_4_.refs_7_ = f32[200,512]{1,0:T(8,128)} collective-permute-done((f32[200,512]{1,0:T(8,128)}, f32[200,512]{1,0:T(8,128)}, u32[]{:S(2)}, u32[]{:S(2)}) %collective-permute-start.25) | collective-permute-done | bytes 409632 | tf_op jit(solution)/shard_map/ppermute | solution.py:632
  77.3 2.3 %collective-permute-start.26 = (f32[264,512]{1,0:T(8,128)}, f32[264,512]{1,0:T(8,128)S(1)}, u32[]{:S(2)}, u32[]{:S(2)}) collective-permute-start(f32[264,512]{1,0:T(8,128)} %copy-done.24), channel_id=1, source_target_pairs={{0,8},{1,9},{2,10},{3,11},{4,12},{5,13},{6,14},{7,15},{8,0},{9,1},... | collective-permute-start | bytes 1622024 | tf_op jit(solution)/shard_map/ppermute | solution.py:632
  79.7 4.7 %collective-permute-done.27.refs_5_.refs_8_ = f32[200,512]{1,0:T(8,128)} collective-permute-done((f32[200,512]{1,0:T(8,128)}, f32[200,512]{1,0:T(8,128)}, u32[]{:S(2)}, u32[]{:S(2)}) %collective-permute-start.27) | collective-permute-done | bytes 409632 | tf_op jit(solution)/shard_map/ppermute | solution.py:632
  84.4 1.7 collective-permute-start.28
  86.1 0.7 broadcast_multiply_fusion.1
  86.8 0.8 broadcast_multiply_fusion
  87.6 7.3 %collective-permute-done.28.refs_6_.refs_9_ = f32[200,512]{1,0:T(8,128)S(1)} collective-permute-done((f32[200,512]{1,0:T(8,128)}, f32[200,512]{1,0:T(8,128)S(1)}, u32[]{:S(2)}, u32[]{:S(2)}) %collective-permute-start.28) | collective-permute-done | bytes 409632 | tf_op jit(solution)/shard_map/ppermute | solution.py:632
  94.9 0.8 copy-done.17
  95.7 4.3 %collective-permute-done.32.refs_3_ = f32[320,512]{1,0:T(8,128)S(1)} collective-permute-done((f32[320,512]{1,0:T(8,128)}, f32[320,512]{1,0:T(8,128)S(1)}, u32[]{:S(2)}, u32[]{:S(2)}) %collective-permute-start.32) | collective-permute-done | bytes 655392 | tf_op jit(solution)/shard_map/ppermute | solution.py:632
  100.0 2.5 %shard_map.114 = (f32[320,512]{1,0:T(8,128)}, f32[240,512]{1,0:T(8,128)}, f32[240,512]{1,0:T(8,128)}, f32[80,512]{1,0:T(8,128)}, f32[80,512]{1,0:T(8,128)}) custom-call(f32[320,512]{1,0:T(8,128)S(1)} %get-tuple-element.162.refs_0_, f32[320,512]{1,0:T(8,128)S(1)} %collective-permute-done.30.refs_1_, f32[320,512]{1,0:T(8,128)S(1)} %collective-permute-done.31.refs_2_, ...), custom_call_target="tpu_custom_call" | custom-call | tf_op jit(solution)/shard_map/pallas_call | solution.py:576
  102.5 0.8 copy-done.7
  103.3 5.9 %collective-permute-start.33 = (f32[320,512]{1,0:T(8,128)}, f32[320,512]{1,0:T(8,128)}, u32[]{:S(2)}, u32[]{:S(2)}) collective-permute-start(f32[320,512]{1,0:T(8,128)} %get-tuple-element.167), channel_id=1, source_target_pairs={{0,8},{1,9},{2,10},{3,11},{4,12},{5,13},{6,14},{7,15},{8,0},{9,1},... | collective-permute-start | bytes 1966088 | tf_op jit(solution)/shard_map/ppermute | solution.py:632
  109.9 4.1 %shard_map.110 = (f32[8,12,16,512]{3,2,1,0:T(8,128)}, f32[8,256]{1,0:T(8,128)S(1)}, f32[640,128]{1,0:T(8,128)S(1)}) custom-call(f32[200,512]{1,0:T(8,128)S(1)} %copy-done.10, f32[200,512]{1,0:T(8,128)S(1)} %copy-done.12, f32[200,512]{1,0:T(8,128)S(1)} %copy-done.14, f32[200,512]{1,0:T(8,128)S(1)} %copy-done.16, ...), custom_call_target="tpu_custom_call" | custom-call | tf_op jit(solution)/shard_map/pallas_call | solution.py:387
  115.8 0.7 copy-done.21
  116.5 0.8 collective-permute-start.36
  117.2 0.7 collective-permute-start.37
  118.0 0.9 mul.80
  119.0 1.0 mul.72
  120.0 1.2 mul.68
  121.2 33.3 %collective-permute-done.36.from_xlow = f32[64,128]{1,0:T(8,128)S(1)} collective-permute-done((f32[64,128]{1,0:T(8,128)S(1)}, f32[64,128]{1,0:T(8,128)S(1)}, u32[]{:S(2)}, u32[]{:S(2)}) %collective-permute-start.36) | collective-permute-done | bytes 32800 | tf_op jit(solution)/shard_map/ppermute | solution.py:636
  154.5 5.0 %collective-permute-start.38 = (f32[64,128]{1,0:T(8,128)}, f32[64,128]{1,0:T(8,128)S(1)}, u32[]{:S(2)}, u32[]{:S(2)}) collective-permute-start(f32[64,128]{1,0:T(8,128)} %get-tuple-element.234), channel_id=1, source_target_pairs={{0,1},{1,2},{2,3},{3,0},{4,5},{5,6},{6,7},{7,4},{8,9},{9,10},{10,1... | collective-permute-start | bytes 98312 | tf_op jit(solution)/shard_map/ppermute | solution.py:636
  160.5 1.0 copy.38
  161.5 0.8 tile.8
  162.3 1.2 tile.9.weights
  164.4 0.8 pad.9.sum_xs
  165.2 1.0 copy-done.2
  166.3 1.0 copy-done.4
  167.3 1.0 copy-done.6
  168.4 1.0 copy-done.8
  169.4 1.0 copy-done.18
  170.4 3.9 %shard_map.111 = (f32[8,12,16,512]{3,2,1,0:T(8,128)}, f32[8,256]{1,0:T(8,128)S(1)}) custom-call(f32[264,512]{1,0:T(8,128)S(1)} %get-tuple-element.140.refs_0_, f32[264,512]{1,0:T(8,128)S(1)} %copy-done.2, f32[264,512]{1,0:T(8,128)S(1)} %copy-done.4, f32[264,512]{1,0:T(8,128)S(1)} %copy-done.6, ...), custom_call_target="tpu_custom_call", output_to_operand_aliasing={{0}: (12, {})} | custom-call | tf_op jit(solution)/shard_map/pallas_call | solution.py:387
  174.4 2.1 %shard_map.116 = (f32[512,128]{1,0:T(8,128)S(1)}, f32[64,128]{1,0:T(8,128)S(1)}, f32[64,128]{1,0:T(8,128)S(1)}, f32[64,128]{1,0:T(8,128)S(1)}, f32[64,128]{1,0:T(8,128)S(1)}) custom-call(f32[640,128]{1,0:T(8,128)S(1)} %copy-done.22, f32[64,128]{1,0:T(8,128)S(1)} %collective-permute-done.36.from_xlow, f32[64,128]{1,0:T(8,128)S(1)} %collective-permute-done.37.from_xup, ...), custom_call_target="tpu_custom_call" | custom-call | tf_op jit(solution)/shard_map/pallas_call | solution.py:576
  176.6 2.9 %collective-permute-start.41 = (f32[64,128]{1,0:T(8,128)S(1)}, f32[64,128]{1,0:T(8,128)S(1)}, u32[]{:S(2)}, u32[]{:S(2)}) collective-permute-start(f32[64,128]{1,0:T(8,128)S(1)} %get-tuple-element.176.xup), channel_id=1, source_target_pairs={{0,4},{4,8},{8,12},{12,16},{16,20},{20,24},{24,28},{28,0},{1,5},{5... | collective-permute-start | bytes 98312 | tf_op jit(solution)/shard_map/ppermute | solution.py:636
  179.5 1.2 collective-permute-done.40.from_x_up
  180.8 1.5 collective-permute-start.42
  182.3 1.1 collective-permute-start.43
  184.6 0.9 collective-permute-done.42.from_s_up
  185.5 1.1 shard_map.117
  186.6 5.1 %shard_map.115 = f32[8,12,16,512]{3,2,1,0:T(8,128)} custom-call(f32[320,512]{1,0:T(8,128)S(1)} %get-tuple-element.162.refs_0_, f32[320,512]{1,0:T(8,128)S(1)} %collective-permute-done.30.refs_1_, f32[320,512]{1,0:T(8,128)S(1)} %collective-permute-done.31.refs_2_, f32[320,512]{1,0:T(8,128)S(1)} %collective-permute-done.32.refs_3_, ...), custom_call_target="tpu_custom_call", output_to_operand_aliasing={{}: (8, {})} | custom-call | tf_op jit(solution)/shard_map/pallas_call | solution.py:387
  (123 shorter events, 8.2 us)
Async XLA Ops:
  0.6 2.8 %copy-start = (f32[256,12,512]{2,0,1:T(8,128)S(1)}, f32[256,12,512]{2,0,1:T(8,128)}, u32[]{:S(2)}) copy-start(f32[256,12,512]{2,0,1:T(8,128)} %param.11) | copy-start | bytes 18874372
  4.1 7.4 %slice-start = ((s8[6291456]{0:T(1024)(128)(4,1)}), s8[4194304]{0:T(1024)(128)(4,1)S(1)}, s32[]{:S(2)}) async-start(s8[6291456]{0:T(1024)(128)(4,1)} %bitcast.43), calls=%async_computation | async-start | bytes 8388608
  5.9 5.6 %slice-start.1 = ((s8[6291456]{0:T(1024)(128)(4,1)}), s8[2097152]{0:T(1024)(128)(4,1)S(1)}, s32[]{:S(2)}) async-start(s8[6291456]{0:T(1024)(128)(4,1)} %bitcast.43), calls=%async_computation.1 | async-start | bytes 4194304
  5.9 2.8 %collective-permute-start.14 = (f32[392,512]{1,0:T(8,128)S(1)}, f32[392,512]{1,0:T(8,128)S(1)}, u32[]{:S(2)}, u32[]{:S(2)}) collective-permute-start(f32[392,512]{1,0:T(8,128)S(1)} %get-tuple-element.125), channel_id=1, source_target_pairs={{0,1},{1,0},{2,3},{3,2},{4,5},{5,4},{6,7},{7,6},{8,9},{9,8},{10,11... | collective-permute-start | bytes 2408456 | tf_op jit(solution)/shard_map/ppermute | solution.py:632
  8.6 26.3 %collective-permute-start.18 = (f32[512,512]{1,0:T(8,128)S(1)}, f32[512,512]{1,0:T(8,128)S(1)}, u32[]{:S(2)}, u32[]{:S(2)}) collective-permute-start(f32[512,512]{1,0:T(8,128)S(1)} %get-tuple-element.135), channel_id=1, source_target_pairs={{0,1},{1,0},{2,3},{3,2},{4,5},{5,4},{6,7},{7,6},{8,9},{9,8},{10,11... | collective-permute-start | bytes 3145736 | tf_op jit(solution)/shard_map/ppermute | solution.py:632
  8.8 20.3 %copy-start.9 = (f32[200,512]{1,0:T(8,128)}, f32[200,512]{1,0:T(8,128)S(1)}, u32[]{:S(2)}) copy-start(f32[200,512]{1,0:T(8,128)S(1)} %get-tuple-element.126.refs_0_) | copy-start | bytes 1228804
  8.8 10.6 %collective-permute-start.15 = (f32[200,512]{1,0:T(8,128)S(1)}, f32[200,512]{1,0:T(8,128)S(1)}, u32[]{:S(2)}, u32[]{:S(2)}) collective-permute-start(f32[200,512]{1,0:T(8,128)S(1)} %get-tuple-element.127), channel_id=1, source_target_pairs={{0,2},{1,3},{2,0},{3,1},{4,6},{5,7},{6,4},{7,5},{8,10},{9,11},{10,... | collective-permute-start | bytes 1228808 | tf_op jit(solution)/shard_map/ppermute | solution.py:632
  10.1 10.2 %collective-permute-start.16 = (f32[200,512]{1,0:T(8,128)S(1)}, f32[200,512]{1,0:T(8,128)S(1)}, u32[]{:S(2)}, u32[]{:S(2)}) collective-permute-start(f32[200,512]{1,0:T(8,128)S(1)} %get-tuple-element.128), channel_id=1, source_target_pairs={{0,4},{1,5},{2,6},{3,7},{4,0},{5,1},{6,2},{7,3},{8,12},{9,13},{10,... | collective-permute-start | bytes 1228808 | tf_op jit(solution)/shard_map/ppermute | solution.py:632
  10.4 22.2 %copy-start.34 = (f32[10,10]{1,0:T(8,128)S(1)}, f32[10,10]{1,0:T(8,128)}, u32[]{:S(2)}) copy-start(f32[10,10]{1,0:T(8,128)} %param.14) | copy-start | bytes 1204
  10.4 18.7 %collective-permute-start.17 = (f32[200,512]{1,0:T(8,128)S(1)}, f32[200,512]{1,0:T(8,128)S(1)}, u32[]{:S(2)}, u32[]{:S(2)}) collective-permute-start(f32[200,512]{1,0:T(8,128)S(1)} %get-tuple-element.129), channel_id=1, source_target_pairs={{0,6},{1,7},{2,4},{3,5},{4,2},{5,3},{6,0},{7,1},{8,14},{9,15},{10,... | collective-permute-start | bytes 1228808 | tf_op jit(solution)/shard_map/ppermute | solution.py:632
  13.9 54.9 %collective-permute-start.29 = (f32[640,512]{1,0:T(8,128)S(1)}, f32[640,512]{1,0:T(8,128)S(1)}, u32[]{:S(2)}, u32[]{:S(2)}) collective-permute-start(f32[640,512]{1,0:T(8,128)S(1)} %get-tuple-element.160), channel_id=1, source_target_pairs={{0,1},{1,0},{2,3},{3,2},{4,5},{5,4},{6,7},{7,6},{8,9},{9,8},{10,11... | collective-permute-start | bytes 3932168 | tf_op jit(solution)/shard_map/ppermute | solution.py:632
  19.4 15.5 %copy-start.11 = (f32[200,512]{1,0:T(8,128)}, f32[200,512]{1,0:T(8,128)S(1)}, u32[]{:S(2)}) copy-start(f32[200,512]{1,0:T(8,128)S(1)} %collective-permute-done.15.refs_1_) | copy-start | bytes 1228804
  20.3 14.6 %copy-start.13 = (f32[200,512]{1,0:T(8,128)}, f32[200,512]{1,0:T(8,128)S(1)}, u32[]{:S(2)}) copy-start(f32[200,512]{1,0:T(8,128)S(1)} %collective-permute-done.16.refs_2_) | copy-start | bytes 1228804
  29.1 5.9 %copy-start.15 = (f32[200,512]{1,0:T(8,128)}, f32[200,512]{1,0:T(8,128)S(1)}, u32[]{:S(2)}) copy-start(f32[200,512]{1,0:T(8,128)S(1)} %collective-permute-done.17.refs_3_) | copy-start | bytes 1228804
  30.9 4.0 %collective-permute-start.19 = (f32[8,256]{1,0:T(8,128)S(1)}, f32[8,256]{1,0:T(8,128)S(1)}, u32[]{:S(2)}, u32[]{:S(2)}) collective-permute-start(f32[8,256]{1,0:T(8,128)S(1)} %get-tuple-element.136.refs_5_), channel_id=1, source_target_pairs={{0,1},{1,0},{2,3},{3,2},{4,5},{5,4},{6,7},{7,6},{8,9},{9,8},{10,11... | collective-permute-start | bytes 24584 | tf_op jit(solution)/shard_map/ppermute | solution.py:632
  32.6 16.0 %collective-permute-start.20 = (f32[152,512]{1,0:T(8,128)S(1)}, f32[152,512]{1,0:T(8,128)S(1)}, u32[]{:S(2)}, u32[]{:S(2)}) collective-permute-start(f32[152,512]{1,0:T(8,128)S(1)} %get-tuple-element.138), channel_id=1, source_target_pairs={{0,16},{1,17},{2,18},{3,19},{4,20},{5,21},{6,22},{7,23},{8,24},{9,... | collective-permute-start | bytes 933896 | tf_op jit(solution)/shard_map/ppermute | solution.py:632
  34.9 13.7 %copy-start.33 = (f32[10,10]{1,0:T(8,128)S(1)}, f32[10,10]{1,0:T(8,128)}, u32[]{:S(2)}) copy-start(f32[10,10]{1,0:T(8,128)} %param.13) | copy-start | bytes 1204
  35.1 29.4 %collective-permute-start.22 = (f32[264,512]{1,0:T(8,128)S(1)}, f32[264,512]{1,0:T(8,128)S(1)}, u32[]{:S(2)}, u32[]{:S(2)}) collective-permute-start(f32[264,512]{1,0:T(8,128)S(1)} %get-tuple-element.141), channel_id=1, source_target_pairs={{0,2},{1,3},{2,0},{3,1},{4,6},{5,7},{6,4},{7,5},{8,10},{9,11},{10,... | collective-permute-start | bytes 1622024 | tf_op jit(solution)/shard_map/ppermute | solution.py:632
  36.4 28.1 %collective-permute-start.23 = (f32[264,512]{1,0:T(8,128)S(1)}, f32[264,512]{1,0:T(8,128)S(1)}, u32[]{:S(2)}, u32[]{:S(2)}) collective-permute-start(f32[264,512]{1,0:T(8,128)S(1)} %get-tuple-element.142), channel_id=1, source_target_pairs={{0,4},{1,5},{2,6},{3,7},{4,0},{5,1},{6,2},{7,3},{8,12},{9,13},{10,... | collective-permute-start | bytes 1622024 | tf_op jit(solution)/shard_map/ppermute | solution.py:632
  36.6 27.9 %collective-permute-start.24 = (f32[264,512]{1,0:T(8,128)S(1)}, f32[264,512]{1,0:T(8,128)S(1)}, u32[]{:S(2)}, u32[]{:S(2)}) collective-permute-start(f32[264,512]{1,0:T(8,128)S(1)} %get-tuple-element.143), channel_id=1, source_target_pairs={{0,6},{1,7},{2,4},{3,5},{4,2},{5,3},{6,0},{7,1},{8,14},{9,15},{10,... | collective-permute-start | bytes 1622024 | tf_op jit(solution)/shard_map/ppermute | solution.py:632
  48.6 15.1 %collective-permute-start.21 = (f32[152,512]{1,0:T(8,128)S(1)}, f32[152,512]{1,0:T(8,128)S(1)}, u32[]{:S(2)}, u32[]{:S(2)}) collective-permute-start(f32[152,512]{1,0:T(8,128)S(1)} %get-tuple-element.139), channel_id=1, source_target_pairs={{0,24},{1,25},{2,26},{3,27},{4,28},{5,29},{6,30},{7,31},{8,16},{9,... | collective-permute-start | bytes 933896 | tf_op jit(solution)/shard_map/ppermute | solution.py:632
  64.5 12.9 %collective-permute-start.25 = (f32[200,512]{1,0:T(8,128)}, f32[200,512]{1,0:T(8,128)}, u32[]{:S(2)}, u32[]{:S(2)}) collective-permute-start(f32[200,512]{1,0:T(8,128)} %get-tuple-element.146), channel_id=1, source_target_pairs={{0,8},{1,9},{2,10},{3,11},{4,12},{5,13},{6,14},{7,15},{8,0},{9,1},... | collective-permute-start | bytes 1228808 | tf_op jit(solution)/shard_map/ppermute | solution.py:632
  64.5 4.2 %copy-start.1 = (f32[264,512]{1,0:T(8,128)}, f32[264,512]{1,0:T(8,128)S(1)}, u32[]{:S(2)}) copy-start(f32[264,512]{1,0:T(8,128)S(1)} %collective-permute-done.22.refs_1_) | copy-start | bytes 1622020
  64.5 4.2 %copy-start.3 = (f32[264,512]{1,0:T(8,128)}, f32[264,512]{1,0:T(8,128)S(1)}, u32[]{:S(2)}) copy-start(f32[264,512]{1,0:T(8,128)S(1)} %collective-permute-done.23.refs_2_) | copy-start | bytes 1622020
  64.5 4.2 %copy-start.5 = (f32[264,512]{1,0:T(8,128)}, f32[264,512]{1,0:T(8,128)S(1)}, u32[]{:S(2)}) copy-start(f32[264,512]{1,0:T(8,128)S(1)} %collective-permute-done.24.refs_3_) | copy-start | bytes 1622020
  66.4 0.8 copy-start.24
  67.2 3.0 %copy-start.25 = (f32[200,512]{1,0:T(8,128)}, f32[200,512]{1,0:T(8,128)S(1)}, u32[]{:S(2)}) copy-start(f32[200,512]{1,0:T(8,128)S(1)} %get-tuple-element.149) | copy-start | bytes 1228804
  67.2 17.2 %collective-permute-start.27 = (f32[200,512]{1,0:T(8,128)}, f32[200,512]{1,0:T(8,128)}, u32[]{:S(2)}, u32[]{:S(2)}) collective-permute-start(f32[200,512]{1,0:T(8,128)} %get-tuple-element.148), channel_id=1, source_target_pairs={{0,16},{1,17},{2,18},{3,19},{4,20},{5,21},{6,22},{7,23},{8,24},{9,... | collective-permute-start | bytes 1228808 | tf_op jit(solution)/shard_map/ppermute | solution.py:632
  70.2 25.5 %collective-permute-start.30 = (f32[320,512]{1,0:T(8,128)}, f32[320,512]{1,0:T(8,128)S(1)}, u32[]{:S(2)}, u32[]{:S(2)}) collective-permute-start(f32[320,512]{1,0:T(8,128)} %get-tuple-element.163), channel_id=1, source_target_pairs={{0,2},{1,3},{2,0},{3,1},{4,6},{5,7},{6,4},{7,5},{8,10},{9,11},{10,... | collective-permute-start | bytes 1966088 | tf_op jit(solution)/shard_map/ppermute | solution.py:632
  71.4 24.3 %collective-permute-start.31 = (f32[320,512]{1,0:T(8,128)}, f32[320,512]{1,0:T(8,128)S(1)}, u32[]{:S(2)}, u32[]{:S(2)}) collective-permute-start(f32[320,512]{1,0:T(8,128)} %get-tuple-element.164), channel_id=1, source_target_pairs={{0,4},{1,5},{2,6},{3,7},{4,0},{5,1},{6,2},{7,3},{8,12},{9,13},{10,... | collective-permute-start | bytes 1966088 | tf_op jit(solution)/shard_map/ppermute | solution.py:632
  71.7 28.3 %collective-permute-start.32 = (f32[320,512]{1,0:T(8,128)}, f32[320,512]{1,0:T(8,128)S(1)}, u32[]{:S(2)}, u32[]{:S(2)}) collective-permute-start(f32[320,512]{1,0:T(8,128)} %get-tuple-element.165), channel_id=1, source_target_pairs={{0,6},{1,7},{2,4},{3,5},{4,2},{5,3},{6,0},{7,1},{8,14},{9,15},{10,... | collective-permute-start | bytes 1966088 | tf_op jit(solution)/shard_map/ppermute | solution.py:632
  73.2 36.7 %copy-start.10 = (f32[200,512]{1,0:T(8,128)S(1)}, f32[200,512]{1,0:T(8,128)}, u32[]{:S(2)}) copy-start(f32[200,512]{1,0:T(8,128)} %copy-done.9) | copy-start | bytes 1228804
  73.2 36.7 %copy-start.12 = (f32[200,512]{1,0:T(8,128)S(1)}, f32[200,512]{1,0:T(8,128)}, u32[]{:S(2)}) copy-start(f32[200,512]{1,0:T(8,128)} %copy-done.11) | copy-start | bytes 1228804
  73.2 36.7 %copy-start.14 = (f32[200,512]{1,0:T(8,128)S(1)}, f32[200,512]{1,0:T(8,128)}, u32[]{:S(2)}) copy-start(f32[200,512]{1,0:T(8,128)} %copy-done.13) | copy-start | bytes 1228804
  73.2 36.7 %copy-start.16 = (f32[200,512]{1,0:T(8,128)S(1)}, f32[200,512]{1,0:T(8,128)}, u32[]{:S(2)}) copy-start(f32[200,512]{1,0:T(8,128)} %copy-done.15) | copy-start | bytes 1228804
  73.2 36.7 %copy-start.20 = (f32[152,512]{1,0:T(8,128)S(1)}, f32[152,512]{1,0:T(8,128)}, u32[]{:S(2)}) copy-start(f32[152,512]{1,0:T(8,128)} %copy-done.19) | copy-start | bytes 933892
  73.2 36.7 %copy-start.26 = (bf16[640,512]{1,0:T(8,128)(2,1)S(1)}, bf16[640,512]{1,0:T(8,128)(2,1)}, u32[]{:S(2)}) copy-start(bf16[640,512]{1,0:T(8,128)(2,1)} %constant.21.clone.refs_11_) | copy-start | bytes 1966084
  77.3 25.2 %collective-permute-start.26 = (f32[264,512]{1,0:T(8,128)}, f32[264,512]{1,0:T(8,128)S(1)}, u32[]{:S(2)}, u32[]{:S(2)}) collective-permute-start(f32[264,512]{1,0:T(8,128)} %copy-done.24), channel_id=1, source_target_pairs={{0,8},{1,9},{2,10},{3,11},{4,12},{5,13},{6,14},{7,15},{8,0},{9,1},... | collective-permute-start | bytes 1622024 | tf_op jit(solution)/shard_map/ppermute | solution.py:632
  84.4 10.5 %collective-permute-start.28 = (f32[200,512]{1,0:T(8,128)}, f32[200,512]{1,0:T(8,128)S(1)}, u32[]{:S(2)}, u32[]{:S(2)}) collective-permute-start(f32[200,512]{1,0:T(8,128)} %copy-done.25), channel_id=1, source_target_pairs={{0,24},{1,25},{2,26},{3,27},{4,28},{5,29},{6,30},{7,31},{8,16},{9,... | collective-permute-start | bytes 1228808 | tf_op jit(solution)/shard_map/ppermute | solution.py:632
  94.9 0.8 copy-start.17
  95.7 22.2 %copy-start.35 = (f32[10]{0:T(128)S(1)}, f32[10]{0:T(128)}, u32[]{:S(2)}) copy-start(f32[10]{0:T(128)} %param.17) | copy-start | bytes 124
  95.7 22.2 %copy-start.36 = (f32[10]{0:T(128)S(1)}, f32[10]{0:T(128)}, u32[]{:S(2)}) copy-start(f32[10]{0:T(128)} %param.16) | copy-start | bytes 124
  103.3 83.4 %collective-permute-start.33 = (f32[320,512]{1,0:T(8,128)}, f32[320,512]{1,0:T(8,128)}, u32[]{:S(2)}, u32[]{:S(2)}) collective-permute-start(f32[320,512]{1,0:T(8,128)} %get-tuple-element.167), channel_id=1, source_target_pairs={{0,8},{1,9},{2,10},{3,11},{4,12},{5,13},{6,14},{7,15},{8,0},{9,1},... | collective-permute-start | bytes 1966088 | tf_op jit(solution)/shard_map/ppermute | solution.py:632
  109.9 54.4 %copy-start.32 = (f32[16,10]{1,0:T(8,128)S(1)}, f32[16,10]{1,0:T(8,128)}, u32[]{:S(2)}) copy-start(f32[16,10]{1,0:T(8,128)} %param.18) | copy-start | bytes 1924
  113.9 72.7 %collective-permute-start.34 = (f32[240,512]{1,0:T(8,128)}, f32[240,512]{1,0:T(8,128)}, u32[]{:S(2)}, u32[]{:S(2)}) collective-permute-start(f32[240,512]{1,0:T(8,128)} %get-tuple-element.168), channel_id=1, source_target_pairs={{0,16},{1,17},{2,18},{3,19},{4,20},{5,21},{6,22},{7,23},{8,24},{9,... | collective-permute-start | bytes 1474568 | tf_op jit(solution)/shard_map/ppermute | solution.py:632
  114.5 72.1 %collective-permute-start.35 = (f32[240,512]{1,0:T(8,128)}, f32[240,512]{1,0:T(8,128)}, u32[]{:S(2)}, u32[]{:S(2)}) collective-permute-start(f32[240,512]{1,0:T(8,128)} %get-tuple-element.169), channel_id=1, source_target_pairs={{0,24},{1,25},{2,26},{3,27},{4,28},{5,29},{6,30},{7,31},{8,16},{9,... | collective-permute-start | bytes 1474568 | tf_op jit(solution)/shard_map/ppermute | solution.py:632
  116.5 38.1 %collective-permute-start.36 = (f32[64,128]{1,0:T(8,128)S(1)}, f32[64,128]{1,0:T(8,128)S(1)}, u32[]{:S(2)}, u32[]{:S(2)}) collective-permute-start(f32[64,128]{1,0:T(8,128)S(1)} %get-tuple-element.236), channel_id=1, source_target_pairs={{0,4},{4,8},{8,12},{12,16},{16,20},{20,24},{24,28},{28,0},{1,5},{5... | collective-permute-start | bytes 98312 | tf_op jit(solution)/shard_map/ppermute | solution.py:636
  117.2 42.3 %collective-permute-start.37 = (f32[64,128]{1,0:T(8,128)S(1)}, f32[64,128]{1,0:T(8,128)S(1)}, u32[]{:S(2)}, u32[]{:S(2)}) collective-permute-start(f32[64,128]{1,0:T(8,128)S(1)} %get-tuple-element.235), channel_id=1, source_target_pairs={{0,28},{4,0},{8,4},{12,8},{16,12},{20,16},{24,20},{28,24},{1,29},{... | collective-permute-start | bytes 98312 | tf_op jit(solution)/shard_map/ppermute | solution.py:636
  154.5 19.8 %collective-permute-start.38 = (f32[64,128]{1,0:T(8,128)}, f32[64,128]{1,0:T(8,128)S(1)}, u32[]{:S(2)}, u32[]{:S(2)}) collective-permute-start(f32[64,128]{1,0:T(8,128)} %get-tuple-element.234), channel_id=1, source_target_pairs={{0,1},{1,2},{2,3},{3,0},{4,5},{5,6},{6,7},{7,4},{8,9},{9,10},{10,1... | collective-permute-start | bytes 98312 | tf_op jit(solution)/shard_map/ppermute | solution.py:636
  159.6 14.8 %collective-permute-start.39 = (f32[64,128]{1,0:T(8,128)}, f32[64,128]{1,0:T(8,128)S(1)}, u32[]{:S(2)}, u32[]{:S(2)}) collective-permute-start(f32[64,128]{1,0:T(8,128)} %get-tuple-element.233), channel_id=1, source_target_pairs={{0,3},{1,0},{2,1},{3,2},{4,7},{5,4},{6,5},{7,6},{8,11},{9,8},{10,9... | collective-permute-start | bytes 98312 | tf_op jit(solution)/shard_map/ppermute | solution.py:636
  165.2 1.0 copy-start.2
  166.3 1.0 copy-start.4
  167.3 1.0 copy-start.6
  168.4 1.0 copy-start.8
  169.4 1.0 copy-start.18
  170.4 3.9 %copy-start.22 = (f32[640,128]{1,0:T(8,128)S(1)}, f32[640,128]{1,0:T(8,128)}, u32[]{:S(2)}) copy-start(f32[640,128]{1,0:T(8,128)} %copy-done.21) | copy-start | bytes 983044
  170.4 4.0 %copy-start.28 = (f32[96,104]{1,0:T(8,128)S(1)}, f32[96,104]{1,0:T(8,128)}, u32[]{:S(2)}) copy-start(f32[96,104]{1,0:T(8,128)} %get-tuple-element.237.mix_t) | copy-start | bytes 119812
  176.5 4.2 %collective-permute-start.40 = (f32[64,128]{1,0:T(8,128)S(1)}, f32[64,128]{1,0:T(8,128)S(1)}, u32[]{:S(2)}, u32[]{:S(2)}) collective-permute-start(f32[64,128]{1,0:T(8,128)S(1)} %get-tuple-element.175.xlow), channel_id=1, source_target_pairs={{0,28},{4,0},{8,4},{12,8},{16,12},{20,16},{24,20},{28,24},{1,29},{... | collective-permute-start | bytes 98312 | tf_op jit(solution)/shard_map/ppermute | solution.py:636
  176.6 5.7 %collective-permute-start.41 = (f32[64,128]{1,0:T(8,128)S(1)}, f32[64,128]{1,0:T(8,128)S(1)}, u32[]{:S(2)}, u32[]{:S(2)}) collective-permute-start(f32[64,128]{1,0:T(8,128)S(1)} %get-tuple-element.176.xup), channel_id=1, source_target_pairs={{0,4},{4,8},{8,12},{12,16},{16,20},{20,24},{24,28},{28,0},{1,5},{5... | collective-permute-start | bytes 98312 | tf_op jit(solution)/shard_map/ppermute | solution.py:636
  180.8 4.7 %collective-permute-start.42 = (f32[64,128]{1,0:T(8,128)S(1)}, f32[64,128]{1,0:T(8,128)S(1)}, u32[]{:S(2)}, u32[]{:S(2)}) collective-permute-start(f32[64,128]{1,0:T(8,128)S(1)} %get-tuple-element.177.slow), channel_id=1, source_target_pairs={{0,3},{1,0},{2,1},{3,2},{4,7},{5,4},{6,5},{7,6},{8,11},{9,8},{10,9... | collective-permute-start | bytes 98312 | tf_op jit(solution)/shard_map/ppermute | solution.py:636
  182.3 3.2 %collective-permute-start.43 = (f32[64,128]{1,0:T(8,128)S(1)}, f32[64,128]{1,0:T(8,128)S(1)}, u32[]{:S(2)}, u32[]{:S(2)}) collective-permute-start(f32[64,128]{1,0:T(8,128)S(1)} %get-tuple-element.178.sup), channel_id=1, source_target_pairs={{0,1},{1,2},{2,3},{3,0},{4,5},{5,6},{6,7},{7,4},{8,9},{9,10},{10,1... | collective-permute-start | bytes 98312 | tf_op jit(solution)/shard_map/ppermute | solution.py:636
  186.6 5.2 %copy-start.37 = (f32[80,512]{1,0:T(8,128)S(1)}, f32[80,512]{1,0:T(8,128)}, u32[]{:S(2)}) copy-start(f32[80,512]{1,0:T(8,128)} %get-tuple-element.179) | copy-start | bytes 491524
  186.6 5.2 %copy-start.38 = (f32[80,512]{1,0:T(8,128)S(1)}, f32[80,512]{1,0:T(8,128)}, u32[]{:S(2)}) copy-start(f32[80,512]{1,0:T(8,128)} %get-tuple-element.180) | copy-start | bytes 491524
  186.6 5.2 %copy-start.39 = (f32[48,512]{1,0:T(8,128)S(1)}, f32[48,512]{1,0:T(8,128)}, u32[]{:S(2)}) copy-start(f32[48,512]{1,0:T(8,128)} %get-tuple-element.183) | copy-start | bytes 294916
  (5 other events, 3.6 us)

commit v4 on v3

--- a/solution.py
+++ b/solution.py
@@ -168,7 +168,7 @@
         if flagged:
             base = fields * plan.pair_rows
             out[base : base + 8, :] = jnp.zeros((8, plan.points), F32)
-            out[base : base + 8, : plan.rows] = jnp.maximum(refs[1][...], refs[2][...])
+            out[base : base + 8, : plan.rows] = refs[1][...]
 
 
 def merge(plan, group, near, aside, marked, flags, cost):
@@ -453,8 +453,10 @@
     return pltpu.roll(value, steps % value.shape[1], 1)
 
 
-def solve_kernel(plan, cells, from_xlow, from_xup, from_slow, from_sup, mix, mix_t, weights, sum_xs, values_w, *refs):
-    total, out_xlow, out_xup, out_slow, out_sup, box, section, modal = refs
+def solve_kernel(plan, cells, from_xlow, from_xup, from_slow, from_sup, *refs):
+    tables, refs = refs[:10], refs[10:]
+    total, out_xlow, out_xup, out_slow, out_sup, box, section, modal, weights, values_w = refs
+    vectors_x, vectors_s, vectors_w, own_x, own_s, own_w, pick_x, pick_s, spread_x, spread_s = tables
     side, extent = plan.side, plan.extent
     layer, row_s, row_x = lane_steps(plan)
     points = side * side
@@ -491,17 +493,27 @@
         box[i * FACE : (i + 1) * FACE, :] = below
         box[last + i * FACE : last + (i + 1) * FACE, :] = above
 
-    modal_rows = mix.shape[0]
+    def exact(left, right, contract=((1,), (0,))):
+        dims = (contract, ((), ()))
+        return lax.dot_general(left, right, dims, precision=HIGHEST, preferred_element_type=F32)
+
+    mix_t = exact(exact(pick_x[...], vectors_x[...]), spread_x[...], ((1,), (1,)))
+    mix_t = mix_t * exact(exact(pick_s[...], vectors_s[...]), spread_s[...], ((1,), (1,)))
+    modal_rows = spread_x.shape[0]
     lanes = plan.per_dev
+    held_by = (iota((width, lanes), 0) == rest(iota((width, lanes), 1), width)).astype(F32)
+    for w in range(extent):
+        weights[w] = exact(vectors_w[w], held_by, ((0,), (0,)))
+    values_w[...] = exact(own_w[...], held_by, ((0,), (0,)))
+    sum_xs = jnp.sum(spread_x[...] * own_x[...] + spread_s[...] * own_s[...], axis=1, keepdims=True)
+    sum_xs = jnp.where(iota(sum_xs.shape, 0) < extent * extent, sum_xs, 1.0)
     for w in range(extent):
         rows = points if w in (0, extent - 1) else box_rows
-        section[w] = jnp.dot(
-            mix[:, :rows], box[w * box_rows : w * box_rows + rows, :], precision=HIGHEST, preferred_element_type=F32
-        )
+        section[w] = exact(mix_t[:rows], box[w * box_rows : w * box_rows + rows, :], ((0,), (0,)))
     for block in range(0, modal_rows, FACE):
         held = [section[w, block : block + FACE, :] for w in range(extent)]
         out = [None] * extent
-        base = jnp.broadcast_to(sum_xs[block : block + FACE, :], (FACE, lanes))
+        base = jnp.broadcast_to(sum_xs[block : block + FACE], (FACE, lanes))
         for k in range(extent):
             value = None
             for w in range(extent):
@@ -515,9 +527,7 @@
             modal[w, block : block + FACE, :] = out[w]
     for w in range(extent):
         rows = points if w in (0, extent - 1) else box_rows
-        box[w * box_rows : w * box_rows + rows, :] = jnp.dot(
-            mix_t[:rows, :], modal[w], precision=HIGHEST, preferred_element_type=F32
-        )
+        box[w * box_rows : w * box_rows + rows, :] = exact(mix_t[:rows], modal[w])
 
     for k in range(side):
         at = (k + 1) * box_rows
@@ -584,34 +594,22 @@
     )(*operands)
 
 
-def box_tables(plan, vectors_x, vectors_s, vectors_w, values_x, values_s, values_w):
-    extent = plan.extent
-    rim = [0, extent - 1]
-    inside = slice(1, extent - 1)
-
-    def kron(left, right):
-        return (left[:, None, :, None] * right[None, :, None, :]).reshape(
-            left.shape[0] * right.shape[0], extent * extent
-        )
-
-    ends_x = jnp.stack([vectors_x[r] for r in rim])
-    ends_s = jnp.stack([vectors_s[r] for r in rim])
-    mix_t = jnp.concatenate(
-        [
-            kron(vectors_x[inside], vectors_s[inside]),
-            kron(ends_x, vectors_s[inside]),
-            kron(ends_s, vectors_x[inside]).reshape(-1, extent, extent).swapaxes(1, 2).reshape(-1, extent * extent),
-        ]
-    )
-    modal_rows = -(-extent * extent // FACE) * FACE
-    more = modal_rows - extent * extent
-    mix_t = jnp.pad(mix_t, ((0, 0), (0, more)))
-    sum_xs = (values_x[:, None] + values_s[None, :]).reshape(-1, 1)
-    sum_xs = jnp.pad(sum_xs, ((0, more), (0, 0)), constant_values=1.0)
-    columns = BX * BS
-    weights = jnp.tile(jnp.transpose(vectors_w, (1, 2, 0)), (1, 1, columns))
-    lane_values = jnp.tile(values_w.T, (1, columns))
-    return mix_t.T, mix_t, weights, sum_xs, lane_values
+def box_rows_of(extent):
+    inside = range(1, extent - 1)
+    points = [(u, v) for u in inside for v in inside]
+    points += [(u, v) for u in (0, extent - 1) for v in inside]
+    points += [(u, v) for v in (0, extent - 1) for u in inside]
+    modes = [(i, j) for i in range(extent) for j in range(extent)]
+    modal_rows = -(-len(modes) // FACE) * FACE
+
+    def hot(rows, values):
+        table = np.zeros((rows, extent), np.float32)
+        table[np.arange(len(values)), values] = 1.0
+        return jnp.asarray(table)
+
+    us, vs = zip(*points)
+    i_s, j_s = zip(*modes)
+    return hot(len(us), us), hot(len(vs), vs), hot(modal_rows, i_s), hot(modal_rows, j_s)
 
 
 def after(value, earlier):
@@ -636,7 +634,8 @@
         return lax.ppermute(value, axis, [(s, (s + steps) % count) for s in range(count)])
 
     order = jnp.asarray(cell_order(plan.side), BF16)
-    tables = box_tables(plan, vectors_x, vectors_s, vectors_w, values_x, values_s, values_w)
+    tables = [vectors_x, vectors_s, jnp.transpose(vectors_w, (1, 0, 2))]
+    tables += [values_x.reshape(1, -1), values_s.reshape(1, -1), values_w, *box_rows_of(plan.extent)]
 
     side = plan.side
     inner = side * side
@@ -656,12 +655,15 @@
         if earlier is not None:
             cells = after(cells, earlier)
         face = jax.ShapeDtypeStruct((side * FACE, plan.per_dev), F32)
-        sections = (plan.extent, tables[0].shape[0], plan.per_dev)
+        sections = (plan.extent, tables[-1].shape[0], plan.per_dev)
         total, xlow, xup, slow, sup = simple_call(
             functools.partial(solve_kernel, plan),
             [cells, *halo, *tables],
             [jax.ShapeDtypeStruct((side * inner, plan.per_dev), F32)] + [face] * 4,
-            [pltpu.VMEM((plan.extent * (inner + 4 * FACE), plan.per_dev), F32)] + [pltpu.VMEM(sections, F32)] * 2,
+            [pltpu.VMEM((plan.extent * (inner + 4 * FACE), plan.per_dev), F32)]
+            + [pltpu.VMEM(sections, F32)] * 2
+            + [pltpu.VMEM((plan.extent, plan.extent, plan.per_dev), F32)]
+            + [pltpu.VMEM((plan.extent, plan.per_dev), F32)],
         )
         returned = [shifted(xlow, "gx", -1), shifted(xup, "gx", 1), shifted(slow, "gy", -1), shifted(sup, "gy", 1)]
         (correction,) = simple_call(
@@ -691,7 +693,7 @@
         relays, late, more = relay(plan, group, messages, marks, flagged)
         if first:
             marks, own, over = more
-            flags = [over, across(over, 1)]
+            flags = [over]
         if flagged:
             (flag,) = more
         gate = relays[0]
@@ -702,6 +704,7 @@
 
     buffer, row_marks, cells = settle(plan, plan.groups[0], *held[0][:2], None, None, own, order, None)
     buffer, flag = settle(plan, plan.groups[1], *held[1][:2], row_marks, buffer, None, None, flag)
+    flag = jnp.maximum(flag[:1, :1], across(flag, 1)[:1, :1])
     correction = solve(after(cells, gate), buffer)
     for group, (messages, arrived, _) in zip(plan.groups[2:], held[2:]):
         (buffer,) = settle(plan, group, messages, arrived, row_marks, buffer, None, None, None)

time: 194 us -> 168 us (0.87)
  local copies, waits for them, and re-layouts: 22.8 us -> 6.41 us
  Pallas kernels: 30.2 us -> 20.7 us
  other arithmetic: 2.93 us -> 0.01 us
    unnamed x78 -> x34, local copies, waits for them, and re-layouts: 13.3 us -> 5.25 us
    pallas_call x3, Pallas kernels: 13.1 us -> 5.2 us  [settle(): pl.pallas_call(functools.partial(settle_kernel, plan, fields, marked, fla...]
    ppermute x22, waiting for transfers between devices: 60.2 us -> 63.7 us  [across(): lax.ppermute(value, both, [(d, d ^ flip) for d in range(plan.devices)])]
    mul x9 -> x0, local copies, waits for them, and re-layouts: 3.37 us -> none  [kron(): left[:, None, :, None] * right[None, :, None, :]]
    ppermute x8, waiting for transfers between devices: 35.4 us -> 33 us  [shifted(): lax.ppermute(value, axis, [(s, (s + steps) % count) for s in range(count)])]
    mul x3 -> x0, other arithmetic: 2.22 us -> none  [kron(): left[:, None, :, None] * right[None, :, None, :]]
    another operation x4 -> x0, local copies, waits for them, and re-layouts: 2.07 us -> none  [the longest x2 1.98 us: box_tables(): weights = jnp.tile(jnp.transpose(vectors_w, (1, 2, 0)), (1, 1, columns))]
    ppermute x22, starting transfers between devices: 26.9 us -> 28.9 us  [across(): lax.ppermute(value, both, [(d, d ^ flip) for d in range(plan.devices)])]
  transfers between devices with their start and end apart: 30 -> 30, of which waited for: 12 -> 12; matrix products, arithmetic and copies ran while one was open for 6% -> 1% of each run, Pallas kernels for 12% -> 10%
where the time goes in v4:
time: 168 us; the launch traced here: 166 us
  waiting for transfers between devices  96.6 us (58%)
  starting transfers between devices  39.8 us (24%)
  Pallas kernels  20.7 us (12%)
  local copies, waits for them, and re-layouts  6.41 us (4%)
  between operations  2.29 us (1%)
    ppermute x22, waiting for transfers between devices, across(): lax.ppermute(value, both, [(d, d ^ flip) for d in range(plan.devices)])  63.7 us
    ppermute x8, waiting for transfers between devices, shifted(): lax.ppermute(value, axis, [(s, (s + steps) % count) for s in range(count)])  33 us
    ppermute x22, starting transfers between devices, across(): lax.ppermute(value, both, [(d, d ^ flip) for d in range(plan.devices)])  28.9 us
    ppermute x8, starting transfers between devices, shifted(): lax.ppermute(value, axis, [(s, (s + steps) % count) for s in range(count)])  10.9 us
    pallas_call x8, Pallas kernels, simple_call(): pl.pallas_call(kernel, in_specs=[pl.BlockSpec(memory_space=pltpu.VMEM)] *...  9.53 us
    pallas_call x3, Pallas kernels, pack(): pl.pallas_call(functools.partial(pack_kernel, plan, fields, marked), grid...  6 us
    unnamed x34, local copies, waits for them, and re-layouts  5.25 us
    pallas_call x3, Pallas kernels, settle(): pl.pallas_call(functools.partial(settle_kernel, plan, fields, marked, fla...  5.2 us
  transfers between devices with their start and end apart: 30, of which 12 were waited for; matrix products, arithmetic and copies ran while one was open for 1% of the time, Pallas kernels for 10%

profile of v4, /device:TPU:11, one launch (start us, length us, event | category | flops | bytes accessed | tf_op | source)
XLA Modules:
  0.0 166.1 jit_solution(5868188568799027380)
XLA Ops:
  0.6 0.0 copy-start
  0.6 2.8 %copy-done = f32[256,12,512]{2,0,1:T(8,128)S(1)} copy-done((f32[256,12,512]{2,0,1:T(8,128)S(1)}, f32[256,12,512]{2,0,1:T(8,128)}, u32[]{:S(2)}) %copy-start) | copy-done | bytes 6291480
  3.4 0.7 copy-done.1
  4.1 1.8 %shard_map.141 = (f32[104,512]{1,0:T(8,128)S(1)}, f32[104,512]{1,0:T(8,128)S(1)}, f32[104,512]{1,0:T(8,128)S(1)}, f32[104,512]{1,0:T(8,128)S(1)}, f32[392,512]{1,0:T(8,128)S(1)}) custom-call(s32[1]{0:T(128)} %bitcast.5.me_ref, s32[1,256]{1,0:T(1,128)S(1)} %bitcast.35, f32[12,256,512]{2,1,0:T(8,128)S(1)} %bitcast.28), custom_call_target="tpu_custom_call" | custom-call | tf_op jit(solution)/shard_map/pallas_call | solution.py:134
  5.9 0.0 slice-start.1
  5.9 0.7 collective-permute-start.14
  6.6 1.9 %shard_map.140 = (f32[128,512]{1,0:T(8,128)S(1)}, f32[128,512]{1,0:T(8,128)S(1)}, f32[128,512]{1,0:T(8,128)S(1)}, f32[128,512]{1,0:T(8,128)S(1)}, f32[512,512]{1,0:T(8,128)S(1)}) custom-call(s32[1]{0:T(128)} %bitcast.5.me_ref, s32[1,256]{1,0:T(1,128)S(1)} %bitcast.36, f32[12,256,512]{2,1,0:T(8,128)S(1)} %bitcast.29), custom_call_target="tpu_custom_call" | custom-call | tf_op jit(solution)/shard_map/pallas_call | solution.py:134
  8.6 0.1 collective-permute-start.18
  8.7 0.1 shard_map.142
  8.8 1.3 collective-permute-start.15
  10.1 0.3 collective-permute-start.16
  10.3 1.1 collective-permute-start.17
  11.5 2.3 %shard_map.148 = (f32[160,512]{1,0:T(8,128)S(1)}, f32[160,512]{1,0:T(8,128)S(1)}, f32[160,512]{1,0:T(8,128)S(1)}, f32[160,512]{1,0:T(8,128)S(1)}, f32[640,512]{1,0:T(8,128)S(1)}) custom-call(s32[1]{0:T(128)} %bitcast.5.me_ref, s32[1,256]{1,0:T(1,128)S(1)} %bitcast.37, f32[12,256,512]{2,1,0:T(8,128)S(1)} %bitcast.32), custom_call_target="tpu_custom_call" | custom-call | tf_op jit(solution)/shard_map/pallas_call | solution.py:134
  13.8 1.4 collective-permute-start.29
  15.2 4.2 %collective-permute-done.15.refs_1_ = f32[200,512]{1,0:T(8,128)S(1)} collective-permute-done((f32[200,512]{1,0:T(8,128)S(1)}, f32[200,512]{1,0:T(8,128)S(1)}, u32[]{:S(2)}, u32[]{:S(2)}) %collective-permute-start.15) | collective-permute-done | bytes 409632 | tf_op jit(solution)/shard_map/ppermute | solution.py:630
  19.4 0.9 collective-permute-done.16.refs_2_
  20.3 8.7 %collective-permute-done.17.refs_3_ = f32[200,512]{1,0:T(8,128)S(1)} collective-permute-done((f32[200,512]{1,0:T(8,128)S(1)}, f32[200,512]{1,0:T(8,128)S(1)}, u32[]{:S(2)}, u32[]{:S(2)}) %collective-permute-start.17) | collective-permute-done | bytes 409632 | tf_op jit(solution)/shard_map/ppermute | solution.py:630
  29.1 1.7 %shard_map.143 = (f32[200,512]{1,0:T(8,128)S(1)}, f32[152,512]{1,0:T(8,128)S(1)}, f32[152,512]{1,0:T(8,128)S(1)}, f32[48,512]{1,0:T(8,128)}, f32[48,512]{1,0:T(8...) custom-call(f32[200,512]{1,0:T(8,128)S(1)} %get-tuple-element.141.refs_0_, ...), custom_call_target="tpu_custom_call" | custom-call | tf_op jit(solution)/shard_map/pallas_call | solution.py:586
  30.8 2.3 %collective-permute-start.19 = (f32[152,512]{1,0:T(8,128)S(1)}, f32[152,512]{1,0:T(8,128)S(1)}, u32[]{:S(2)}, u32[]{:S(2)}) collective-permute-start(f32[152,512]{1,0:T(8,128)S(1)} %get-tuple-element.153), channel_id=1, source_target_pairs={{0,16},{1,17},{2,18},{3,19},{4,20},{5,21},{6,22},{7,23},{8,24},{9,... | collective-permute-start | bytes 933896 | tf_op jit(solution)/shard_map/ppermute | solution.py:630
  33.1 0.1 shard_map.144
  33.2 1.3 collective-permute-start.21
  34.5 0.2 collective-permute-start.22
  34.8 1.2 collective-permute-start.23
  35.9 10.8 %collective-permute-done.19.refs_5_.refs_8_ = f32[152,512]{1,0:T(8,128)S(1)} collective-permute-done((f32[152,512]{1,0:T(8,128)S(1)}, f32[152,512]{1,0:T(8,128)S(1)}, u32[]{:S(2)}, u32[]{:S(2)}) %collective-permute-start.19) | collective-permute-done | bytes 311328 | tf_op jit(solution)/shard_map/ppermute | solution.py:630
  46.7 15.1 %collective-permute-done.20.refs_6_.refs_9_ = f32[152,512]{1,0:T(8,128)S(1)} collective-permute-done((f32[152,512]{1,0:T(8,128)S(1)}, f32[152,512]{1,0:T(8,128)S(1)}, u32[]{:S(2)}, u32[]{:S(2)}) %collective-permute-start.20) | collective-permute-done | bytes 311328 | tf_op jit(solution)/shard_map/ppermute | solution.py:630
  61.9 1.7 %shard_map.145 = (f32[264,512]{1,0:T(8,128)S(1)}, f32[200,512]{1,0:T(8,128)S(1)}, f32[200,512]{1,0:T(8,128)S(1)}, f32[64,512]{1,0:T(8,128)}, f32[64,512]{1,0:T(8,128)}, /*index=5*/f32[8,256]{1,0:T(8,128)S(1)}) custom-call(f32[264,512]{1,0:T(8,128)S(1)} %get-tuple-element.155.refs_0_, f32[264,512]{1,0:T(8,128)S(1)} %collective-permute-done.21.refs_1_, ...), custom_call_target="tpu_custom_call" | custom-call | tf_op jit(solution)/shard_map/pallas_call | solution.py:586
  63.6 1.5 collective-permute-start.26
  65.1 0.2 shard_map.149
  65.3 1.3 collective-permute-start.30
  66.6 0.3 collective-permute-start.31
  66.8 1.2 collective-permute-start.32
  68.0 7.5 %collective-permute-done.24.refs_4_.refs_7_ = f32[200,512]{1,0:T(8,128)S(1)} collective-permute-done((f32[200,512]{1,0:T(8,128)S(1)}, f32[200,512]{1,0:T(8,128)S(1)}, u32[]{:S(2)}, u32[]{:S(2)}) %collective-permute-start.24) | collective-permute-done | bytes 409632 | tf_op jit(solution)/shard_map/ppermute | solution.py:630
  75.5 2.2 %collective-permute-start.25 = (f32[264,512]{1,0:T(8,128)S(1)}, f32[264,512]{1,0:T(8,128)S(1)}, u32[]{:S(2)}, u32[]{:S(2)}) collective-permute-start(f32[264,512]{1,0:T(8,128)S(1)} %get-tuple-element.162), channel_id=1, source_target_pairs={{0,8},{1,9},{2,10},{3,11},{4,12},{5,13},{6,14},{7,15},{8,0},{9,1},... | collective-permute-start | bytes 1622024 | tf_op jit(solution)/shard_map/ppermute | solution.py:630
  77.7 3.0 %collective-permute-done.26.refs_5_.refs_8_ = f32[200,512]{1,0:T(8,128)S(1)} collective-permute-done((f32[200,512]{1,0:T(8,128)S(1)}, f32[200,512]{1,0:T(8,128)S(1)}, u32[]{:S(2)}, u32[]{:S(2)}) %collective-permute-start.26) | collective-permute-done | bytes 409632 | tf_op jit(solution)/shard_map/ppermute | solution.py:630
  80.6 0.8 collective-permute-start.27
  81.5 9.8 %collective-permute-done.27.refs_6_.refs_9_ = f32[200,512]{1,0:T(8,128)S(1)} collective-permute-done((f32[200,512]{1,0:T(8,128)S(1)}, f32[200,512]{1,0:T(8,128)S(1)}, u32[]{:S(2)}, u32[]{:S(2)}) %collective-permute-start.27) | collective-permute-done | bytes 409632 | tf_op jit(solution)/shard_map/ppermute | solution.py:630
  91.2 3.7 %collective-permute-done.32.refs_3_ = f32[320,512]{1,0:T(8,128)S(1)} collective-permute-done((f32[320,512]{1,0:T(8,128)S(1)}, f32[320,512]{1,0:T(8,128)S(1)}, u32[]{:S(2)}, u32[]{:S(2)}) %collective-permute-start.32) | collective-permute-done | bytes 655392 | tf_op jit(solution)/shard_map/ppermute | solution.py:630
  94.9 1.9 %shard_map.150 = (f32[320,512]{1,0:T(8,128)S(1)}, f32[240,512]{1,0:T(8,128)S(1)}, f32[240,512]{1,0:T(8,128)S(1)}, f32[80,512]{1,0:T(8,128)}, f32[80,512]{1,0:T(8,128)}) custom-call(f32[320,512]{1,0:T(8,128)S(1)} %get-tuple-element.177.refs_0_, f32[320,512]{1,0:T(8,128)S(1)} %collective-permute-done.30.refs_1_, ...), custom_call_target="tpu_custom_call" | custom-call | tf_op jit(solution)/shard_map/pallas_call | solution.py:586
  96.8 7.3 %collective-permute-start.33 = (f32[320,512]{1,0:T(8,128)S(1)}, f32[320,512]{1,0:T(8,128)S(1)}, u32[]{:S(2)}, u32[]{:S(2)}) collective-permute-start(f32[320,512]{1,0:T(8,128)S(1)} %get-tuple-element.182), channel_id=1, source_target_pairs={{0,8},{1,9},{2,10},{3,11},{4,12},{5,13},{6,14},{7,15},{8,0},{9,1},... | collective-permute-start | bytes 1966088 | tf_op jit(solution)/shard_map/ppermute | solution.py:630
  104.2 0.5 collective-permute-start.34
  104.7 0.7 collective-permute-start.35
  105.4 1.9 %shard_map.146 = (f32[8,12,16,512]{3,2,1,0:T(8,128)S(1)}, f32[8,256]{1,0:T(8,128)S(1)}, f32[640,128]{1,0:T(8,128)S(1)}) custom-call(f32[200,512]{1,0:T(8,128)S(1)} %get-tuple-element.141.refs_0_, f32[200,512]{1,0:T(8,128)S(1)} %collective-permute-done.15.refs_1_, f32[200,512]{1,0:T(8,128)S(1)} %collective-permute-done.16.refs_2_, ...), custom_call_target="tpu_custom_call" | custom-call | tf_op jit(solution)/shard_map/pallas_call | solution.py:387
  107.3 2.6 %collective-permute-start.39 = (f32[64,128]{1,0:T(8,128)S(1)}, f32[64,128]{1,0:T(8,128)S(1)}, u32[]{:S(2)}, u32[]{:S(2)}) collective-permute-start(f32[64,128]{1,0:T(8,128)S(1)} %get-tuple-element.206), channel_id=1, source_target_pairs={{0,3},{1,0},{2,1},{3,2},{4,7},{5,4},{6,5},{7,6},{8,11},{9,8},{10,9... | collective-permute-start | bytes 98312 | tf_op jit(solution)/shard_map/ppermute | solution.py:634
  109.9 1.2 collective-permute-start.38
  111.1 2.2 %collective-permute-done.39.from_sup = f32[64,128]{1,0:T(8,128)S(1)} collective-permute-done((f32[64,128]{1,0:T(8,128)S(1)}, f32[64,128]{1,0:T(8,128)S(1)}, u32[]{:S(2)}, u32[]{:S(2)}) %collective-permute-start.39) | collective-permute-done | bytes 32800 | tf_op jit(solution)/shard_map/ppermute | solution.py:634
  113.3 0.2 collective-permute-start.37
  113.5 2.2 %collective-permute-start.36 = (f32[64,128]{1,0:T(8,128)S(1)}, f32[64,128]{1,0:T(8,128)S(1)}, u32[]{:S(2)}, u32[]{:S(2)}) collective-permute-start(f32[64,128]{1,0:T(8,128)S(1)} %get-tuple-element.209), channel_id=1, source_target_pairs={{0,4},{4,8},{8,12},{12,16},{16,20},{20,24},{24,28},{28,0},{1,5},{5... | collective-permute-start | bytes 98312 | tf_op jit(solution)/shard_map/ppermute | solution.py:634
  115.6 0.0 copy-start.12
  115.7 1.5 shard_map.147
  117.2 29.5 %collective-permute-done.37.from_xup = f32[64,128]{1,0:T(8,128)S(1)} collective-permute-done((f32[64,128]{1,0:T(8,128)S(1)}, f32[64,128]{1,0:T(8,128)S(1)}, u32[]{:S(2)}, u32[]{:S(2)}) %collective-permute-start.37) | collective-permute-done | bytes 32800 | tf_op jit(solution)/shard_map/ppermute | solution.py:634
  146.7 3.1 %collective-permute-start.28 = (f32[8,256]{1,0:T(8,128)S(1)}, f32[8,256]{1,0:T(8,128)S(1)}, u32[]{:S(2)}, u32[]{:S(2)}) collective-permute-start(f32[8,256]{1,0:T(8,128)S(1)} %get-tuple-element.169), channel_id=1, source_target_pairs={{0,1},{1,0},{2,3},{3,2},{4,5},{5,4},{6,7},{7,6},{8,9},{9,8},{10,11... | collective-permute-start | bytes 24584 | tf_op jit(solution)/shard_map/ppermute | solution.py:630
  149.9 2.7 %shard_map.152 = (f32[512,128]{1,0:T(8,128)S(1)}, f32[64,128]{1,0:T(8,128)S(1)}, f32[64,128]{1,0:T(8,128)S(1)}, f32[64,128]{1,0:T(8,128)S(1)}, f32[64,128]{1,0:T(8,128)S(1)}) custom-call(f32[640,128]{1,0:T(8,128)S(1)} %get-tuple-element.188.cells, f32[64,128]{1,0:T(8,128)S(1)} %collective-permute-done.36.from_xlow, ...), custom_call_target="tpu_custom_call" | custom-call | tf_op jit(solution)/shard_map/pallas_call | solution.py:586
  152.6 0.1 collective-permute-start.40
  152.7 2.3 %collective-permute-start.41 = (f32[64,128]{1,0:T(8,128)S(1)}, f32[64,128]{1,0:T(8,128)S(1)}, u32[]{:S(2)}, u32[]{:S(2)}) collective-permute-start(f32[64,128]{1,0:T(8,128)S(1)} %get-tuple-element.191.xup), channel_id=1, source_target_pairs={{0,4},{4,8},{8,12},{12,16},{16,20},{20,24},{24,28},{28,0},{1,5},{5... | collective-permute-start | bytes 98312 | tf_op jit(solution)/shard_map/ppermute | solution.py:634
  155.1 1.3 collective-permute-done.40.from_x_up
  156.4 1.2 collective-permute-start.42
  157.5 1.2 collective-permute-start.43
  158.7 0.6 slice.30
  159.3 0.6 slice.40
  161.2 1.1 shard_map.153
  162.3 1.8 %shard_map.151 = f32[8,12,16,512]{3,2,1,0:T(8,128)S(1)} custom-call(f32[320,512]{1,0:T(8,128)S(1)} %get-tuple-element.177.refs_0_, f32[320,512]{1,0:T(8,128)S(1)} %collective-permute-done.30.refs_1_, f32[320,512]{1,0:T(8,128)S(1)} %collective-permute-done.31.refs_2_, f32[320,512]{1,0:T(8,128)S(1)} %collective-permute-done.32.refs_3_, ...), custom_call_target="tpu_custom_call", output_to_operand_aliasing={{}: (8, {})} | custom-call | tf_op jit(solution)/shard_map/pallas_call | solution.py:387
  164.1 0.2 conditional.1
  164.4 1.6 copy-done.2
  166.0 0.1 copy-done.6
  (49 shorter events, 0.1 us)
Async XLA Ops:
  0.6 2.8 %copy-start = (f32[256,12,512]{2,0,1:T(8,128)S(1)}, f32[256,12,512]{2,0,1:T(8,128)}, u32[]{:S(2)}) copy-start(f32[256,12,512]{2,0,1:T(8,128)} %param.15) | copy-start | bytes 18874372
  3.4 0.7 copy-start.1
  4.1 7.4 %slice-start = ((s8[6291456]{0:T(1024)(128)(4,1)}), s8[4194304]{0:T(1024)(128)(4,1)S(1)}, s32[]{:S(2)}) async-start(s8[6291456]{0:T(1024)(128)(4,1)} %bitcast.30), calls=%async_computation | async-start | bytes 8388608
  5.9 5.6 %slice-start.1 = ((s8[6291456]{0:T(1024)(128)(4,1)}), s8[2097152]{0:T(1024)(128)(4,1)S(1)}, s32[]{:S(2)}) async-start(s8[6291456]{0:T(1024)(128)(4,1)} %bitcast.30), calls=%async_computation.1 | async-start | bytes 4194304
  5.9 2.8 %collective-permute-start.14 = (f32[392,512]{1,0:T(8,128)S(1)}, f32[392,512]{1,0:T(8,128)S(1)}, u32[]{:S(2)}, u32[]{:S(2)}) collective-permute-start(f32[392,512]{1,0:T(8,128)S(1)} %get-tuple-element.140), channel_id=1, source_target_pairs={{0,1},{1,0},{2,3},{3,2},{4,5},{5,4},{6,7},{7,6},{8,9},{9,8},{10,11... | collective-permute-start | bytes 2408456 | tf_op jit(solution)/shard_map/ppermute | solution.py:630
  8.6 24.5 %collective-permute-start.18 = (f32[512,512]{1,0:T(8,128)S(1)}, f32[512,512]{1,0:T(8,128)S(1)}, u32[]{:S(2)}, u32[]{:S(2)}) collective-permute-start(f32[512,512]{1,0:T(8,128)S(1)} %get-tuple-element.150), channel_id=1, source_target_pairs={{0,1},{1,0},{2,3},{3,2},{4,5},{5,4},{6,7},{7,6},{8,9},{9,8},{10,11... | collective-permute-start | bytes 3145736 | tf_op jit(solution)/shard_map/ppermute | solution.py:630
  8.8 10.6 %collective-permute-start.15 = (f32[200,512]{1,0:T(8,128)S(1)}, f32[200,512]{1,0:T(8,128)S(1)}, u32[]{:S(2)}, u32[]{:S(2)}) collective-permute-start(f32[200,512]{1,0:T(8,128)S(1)} %get-tuple-element.142), channel_id=1, source_target_pairs={{0,2},{1,3},{2,0},{3,1},{4,6},{5,7},{6,4},{7,5},{8,10},{9,11},{10,... | collective-permute-start | bytes 1228808 | tf_op jit(solution)/shard_map/ppermute | solution.py:630
  10.1 10.2 %collective-permute-start.16 = (f32[200,512]{1,0:T(8,128)S(1)}, f32[200,512]{1,0:T(8,128)S(1)}, u32[]{:S(2)}, u32[]{:S(2)}) collective-permute-start(f32[200,512]{1,0:T(8,128)S(1)} %get-tuple-element.143), channel_id=1, source_target_pairs={{0,4},{1,5},{2,6},{3,7},{4,0},{5,1},{6,2},{7,3},{8,12},{9,13},{10,... | collective-permute-start | bytes 1228808 | tf_op jit(solution)/shard_map/ppermute | solution.py:630
  10.3 18.7 %collective-permute-start.17 = (f32[200,512]{1,0:T(8,128)S(1)}, f32[200,512]{1,0:T(8,128)S(1)}, u32[]{:S(2)}, u32[]{:S(2)}) collective-permute-start(f32[200,512]{1,0:T(8,128)S(1)} %get-tuple-element.144), channel_id=1, source_target_pairs={{0,6},{1,7},{2,4},{3,5},{4,2},{5,3},{6,0},{7,1},{8,14},{9,15},{10,... | collective-permute-start | bytes 1228808 | tf_op jit(solution)/shard_map/ppermute | solution.py:630
  13.8 51.3 %collective-permute-start.29 = (f32[640,512]{1,0:T(8,128)S(1)}, f32[640,512]{1,0:T(8,128)S(1)}, u32[]{:S(2)}, u32[]{:S(2)}) collective-permute-start(f32[640,512]{1,0:T(8,128)S(1)} %get-tuple-element.175), channel_id=1, source_target_pairs={{0,1},{1,0},{2,3},{3,2},{4,5},{5,4},{6,7},{7,6},{8,9},{9,8},{10,11... | collective-permute-start | bytes 3932168 | tf_op jit(solution)/shard_map/ppermute | solution.py:630
  30.8 16.0 %collective-permute-start.19 = (f32[152,512]{1,0:T(8,128)S(1)}, f32[152,512]{1,0:T(8,128)S(1)}, u32[]{:S(2)}, u32[]{:S(2)}) collective-permute-start(f32[152,512]{1,0:T(8,128)S(1)} %get-tuple-element.153), channel_id=1, source_target_pairs={{0,16},{1,17},{2,18},{3,19},{4,20},{5,21},{6,22},{7,23},{8,24},{9,... | collective-permute-start | bytes 933896 | tf_op jit(solution)/shard_map/ppermute | solution.py:630
  33.2 28.6 %collective-permute-start.21 = (f32[264,512]{1,0:T(8,128)S(1)}, f32[264,512]{1,0:T(8,128)S(1)}, u32[]{:S(2)}, u32[]{:S(2)}) collective-permute-start(f32[264,512]{1,0:T(8,128)S(1)} %get-tuple-element.156), channel_id=1, source_target_pairs={{0,2},{1,3},{2,0},{3,1},{4,6},{5,7},{6,4},{7,5},{8,10},{9,11},{10,... | collective-permute-start | bytes 1622024 | tf_op jit(solution)/shard_map/ppermute | solution.py:630
  34.5 27.3 %collective-permute-start.22 = (f32[264,512]{1,0:T(8,128)S(1)}, f32[264,512]{1,0:T(8,128)S(1)}, u32[]{:S(2)}, u32[]{:S(2)}) collective-permute-start(f32[264,512]{1,0:T(8,128)S(1)} %get-tuple-element.157), channel_id=1, source_target_pairs={{0,4},{1,5},{2,6},{3,7},{4,0},{5,1},{6,2},{7,3},{8,12},{9,13},{10,... | collective-permute-start | bytes 1622024 | tf_op jit(solution)/shard_map/ppermute | solution.py:630
  34.8 27.1 %collective-permute-start.23 = (f32[264,512]{1,0:T(8,128)S(1)}, f32[264,512]{1,0:T(8,128)S(1)}, u32[]{:S(2)}, u32[]{:S(2)}) collective-permute-start(f32[264,512]{1,0:T(8,128)S(1)} %get-tuple-element.158), channel_id=1, source_target_pairs={{0,6},{1,7},{2,4},{3,5},{4,2},{5,3},{6,0},{7,1},{8,14},{9,15},{10,... | collective-permute-start | bytes 1622024 | tf_op jit(solution)/shard_map/ppermute | solution.py:630
  46.7 15.1 %collective-permute-start.20 = (f32[152,512]{1,0:T(8,128)S(1)}, f32[152,512]{1,0:T(8,128)S(1)}, u32[]{:S(2)}, u32[]{:S(2)}) collective-permute-start(f32[152,512]{1,0:T(8,128)S(1)} %get-tuple-element.154), channel_id=1, source_target_pairs={{0,24},{1,25},{2,26},{3,27},{4,28},{5,29},{6,30},{7,31},{8,16},{9,... | collective-permute-start | bytes 933896 | tf_op jit(solution)/shard_map/ppermute | solution.py:630
  61.8 13.6 %collective-permute-start.24 = (f32[200,512]{1,0:T(8,128)S(1)}, f32[200,512]{1,0:T(8,128)S(1)}, u32[]{:S(2)}, u32[]{:S(2)}) collective-permute-start(f32[200,512]{1,0:T(8,128)S(1)} %get-tuple-element.161), channel_id=1, source_target_pairs={{0,8},{1,9},{2,10},{3,11},{4,12},{5,13},{6,14},{7,15},{8,0},{9,1},... | collective-permute-start | bytes 1228808 | tf_op jit(solution)/shard_map/ppermute | solution.py:630
  63.6 17.0 %collective-permute-start.26 = (f32[200,512]{1,0:T(8,128)S(1)}, f32[200,512]{1,0:T(8,128)S(1)}, u32[]{:S(2)}, u32[]{:S(2)}) collective-permute-start(f32[200,512]{1,0:T(8,128)S(1)} %get-tuple-element.163), channel_id=1, source_target_pairs={{0,16},{1,17},{2,18},{3,19},{4,20},{5,21},{6,22},{7,23},{8,24},{9,... | collective-permute-start | bytes 1228808 | tf_op jit(solution)/shard_map/ppermute | solution.py:630
  65.1 40.3 %copy-start.3 = (bf16[640,512]{1,0:T(8,128)(2,1)S(1)}, bf16[640,512]{1,0:T(8,128)(2,1)}, u32[]{:S(2)}) copy-start(bf16[640,512]{1,0:T(8,128)(2,1)} %constant.24.clone.refs_11_) | copy-start | bytes 1966084
  65.3 26.0 %collective-permute-start.30 = (f32[320,512]{1,0:T(8,128)S(1)}, f32[320,512]{1,0:T(8,128)S(1)}, u32[]{:S(2)}, u32[]{:S(2)}) collective-permute-start(f32[320,512]{1,0:T(8,128)S(1)} %get-tuple-element.178), channel_id=1, source_target_pairs={{0,2},{1,3},{2,0},{3,1},{4,6},{5,7},{6,4},{7,5},{8,10},{9,11},{10,... | collective-permute-start | bytes 1966088 | tf_op jit(solution)/shard_map/ppermute | solution.py:630
  66.6 24.7 %collective-permute-start.31 = (f32[320,512]{1,0:T(8,128)S(1)}, f32[320,512]{1,0:T(8,128)S(1)}, u32[]{:S(2)}, u32[]{:S(2)}) collective-permute-start(f32[320,512]{1,0:T(8,128)S(1)} %get-tuple-element.179), channel_id=1, source_target_pairs={{0,4},{1,5},{2,6},{3,7},{4,0},{5,1},{6,2},{7,3},{8,12},{9,13},{10,... | collective-permute-start | bytes 1966088 | tf_op jit(solution)/shard_map/ppermute | solution.py:630
  66.8 28.1 %collective-permute-start.32 = (f32[320,512]{1,0:T(8,128)S(1)}, f32[320,512]{1,0:T(8,128)S(1)}, u32[]{:S(2)}, u32[]{:S(2)}) collective-permute-start(f32[320,512]{1,0:T(8,128)S(1)} %get-tuple-element.180), channel_id=1, source_target_pairs={{0,6},{1,7},{2,4},{3,5},{4,2},{5,3},{6,0},{7,1},{8,14},{9,15},{10,... | collective-permute-start | bytes 1966088 | tf_op jit(solution)/shard_map/ppermute | solution.py:630
  75.5 21.4 %collective-permute-start.25 = (f32[264,512]{1,0:T(8,128)S(1)}, f32[264,512]{1,0:T(8,128)S(1)}, u32[]{:S(2)}, u32[]{:S(2)}) collective-permute-start(f32[264,512]{1,0:T(8,128)S(1)} %get-tuple-element.162), channel_id=1, source_target_pairs={{0,8},{1,9},{2,10},{3,11},{4,12},{5,13},{6,14},{7,15},{8,0},{9,1},... | collective-permute-start | bytes 1622024 | tf_op jit(solution)/shard_map/ppermute | solution.py:630
  80.6 10.6 %collective-permute-start.27 = (f32[200,512]{1,0:T(8,128)S(1)}, f32[200,512]{1,0:T(8,128)S(1)}, u32[]{:S(2)}, u32[]{:S(2)}) collective-permute-start(f32[200,512]{1,0:T(8,128)S(1)} %get-tuple-element.164), channel_id=1, source_target_pairs={{0,24},{1,25},{2,26},{3,27},{4,28},{5,29},{6,30},{7,31},{8,16},{9,... | collective-permute-start | bytes 1228808 | tf_op jit(solution)/shard_map/ppermute | solution.py:630
  96.8 65.4 %collective-permute-start.33 = (f32[320,512]{1,0:T(8,128)S(1)}, f32[320,512]{1,0:T(8,128)S(1)}, u32[]{:S(2)}, u32[]{:S(2)}) collective-permute-start(f32[320,512]{1,0:T(8,128)S(1)} %get-tuple-element.182), channel_id=1, source_target_pairs={{0,8},{1,9},{2,10},{3,11},{4,12},{5,13},{6,14},{7,15},{8,0},{9,1},... | collective-permute-start | bytes 1966088 | tf_op jit(solution)/shard_map/ppermute | solution.py:630
  104.2 58.1 %collective-permute-start.34 = (f32[240,512]{1,0:T(8,128)S(1)}, f32[240,512]{1,0:T(8,128)S(1)}, u32[]{:S(2)}, u32[]{:S(2)}) collective-permute-start(f32[240,512]{1,0:T(8,128)S(1)} %get-tuple-element.183), channel_id=1, source_target_pairs={{0,16},{1,17},{2,18},{3,19},{4,20},{5,21},{6,22},{7,23},{8,24},{9,... | collective-permute-start | bytes 1474568 | tf_op jit(solution)/shard_map/ppermute | solution.py:630
  104.7 57.5 %collective-permute-start.35 = (f32[240,512]{1,0:T(8,128)S(1)}, f32[240,512]{1,0:T(8,128)S(1)}, u32[]{:S(2)}, u32[]{:S(2)}) collective-permute-start(f32[240,512]{1,0:T(8,128)S(1)} %get-tuple-element.184), channel_id=1, source_target_pairs={{0,24},{1,25},{2,26},{3,27},{4,28},{5,29},{6,30},{7,31},{8,16},{9,... | collective-permute-start | bytes 1474568 | tf_op jit(solution)/shard_map/ppermute | solution.py:630
  107.3 6.0 %collective-permute-start.39 = (f32[64,128]{1,0:T(8,128)S(1)}, f32[64,128]{1,0:T(8,128)S(1)}, u32[]{:S(2)}, u32[]{:S(2)}) collective-permute-start(f32[64,128]{1,0:T(8,128)S(1)} %get-tuple-element.206), channel_id=1, source_target_pairs={{0,3},{1,0},{2,1},{3,2},{4,7},{5,4},{6,5},{7,6},{8,11},{9,8},{10,9... | collective-permute-start | bytes 98312 | tf_op jit(solution)/shard_map/ppermute | solution.py:634
  109.9 3.6 %collective-permute-start.38 = (f32[64,128]{1,0:T(8,128)S(1)}, f32[64,128]{1,0:T(8,128)S(1)}, u32[]{:S(2)}, u32[]{:S(2)}) collective-permute-start(f32[64,128]{1,0:T(8,128)S(1)} %get-tuple-element.207), channel_id=1, source_target_pairs={{0,1},{1,2},{2,3},{3,0},{4,5},{5,6},{6,7},{7,4},{8,9},{9,10},{10,1... | collective-permute-start | bytes 98312 | tf_op jit(solution)/shard_map/ppermute | solution.py:634
  113.3 33.5 %collective-permute-start.37 = (f32[64,128]{1,0:T(8,128)S(1)}, f32[64,128]{1,0:T(8,128)S(1)}, u32[]{:S(2)}, u32[]{:S(2)}) collective-permute-start(f32[64,128]{1,0:T(8,128)S(1)} %get-tuple-element.208), channel_id=1, source_target_pairs={{0,28},{4,0},{8,4},{12,8},{16,12},{20,16},{24,20},{28,24},{1,29},{... | collective-permute-start | bytes 98312 | tf_op jit(solution)/shard_map/ppermute | solution.py:634
  113.5 36.4 %collective-permute-start.36 = (f32[64,128]{1,0:T(8,128)S(1)}, f32[64,128]{1,0:T(8,128)S(1)}, u32[]{:S(2)}, u32[]{:S(2)}) collective-permute-start(f32[64,128]{1,0:T(8,128)S(1)} %get-tuple-element.209), channel_id=1, source_target_pairs={{0,4},{4,8},{8,12},{12,16},{16,20},{20,24},{24,28},{28,0},{1,5},{5... | collective-permute-start | bytes 98312 | tf_op jit(solution)/shard_map/ppermute | solution.py:634
  115.6 34.2 %copy-start.5 = (f32[16,10,10]{2,0,1:T(8,128)S(1)}, f32[16,10,10]{2,0,1:T(8,128)}, u32[]{:S(2)}) copy-start(f32[16,10,10]{2,0,1:T(8,128)} %param.19) | copy-start | bytes 19204
  115.6 34.2 %copy-start.7 = (f32[104,10]{1,0:T(8,128)S(1)}, f32[104,10]{1,0:T(8,128)}, u32[]{:S(2)}) copy-start(f32[104,10]{1,0:T(8,128)} %constant.28.clone.refs_9_) | copy-start | bytes 12484
  115.6 34.2 %copy-start.8 = (f32[104,10]{1,0:T(8,128)S(1)}, f32[104,10]{1,0:T(8,128)}, u32[]{:S(2)}) copy-start(f32[104,10]{1,0:T(8,128)} %constant.27.clone.refs_8_) | copy-start | bytes 12484
  115.6 34.2 %copy-start.11 = (f32[96,10]{1,0:T(8,128)S(1)}, f32[96,10]{1,0:T(8,128)}, u32[]{:S(2)}) copy-start(f32[96,10]{1,0:T(8,128)} %constant.26.clone.refs_7_) | copy-start | bytes 11524
  115.6 34.3 %copy-start.12 = (f32[96,10]{1,0:T(8,128)S(1)}, f32[96,10]{1,0:T(8,128)}, u32[]{:S(2)}) copy-start(f32[96,10]{1,0:T(8,128)} %constant.25.clone.refs_6_) | copy-start | bytes 11524
  115.6 34.3 %copy-start.13 = (f32[10,10]{1,0:T(8,128)S(1)}, f32[10,10]{1,0:T(8,128)}, u32[]{:S(2)}) copy-start(f32[10,10]{1,0:T(8,128)} %refs_0_.1) | copy-start | bytes 1204
  115.7 34.2 %copy-start.14 = (f32[10,10]{1,0:T(8,128)S(1)}, f32[10,10]{1,0:T(8,128)}, u32[]{:S(2)}) copy-start(f32[10,10]{1,0:T(8,128)} %refs_1_.1) | copy-start | bytes 1204
  115.7 34.2 %copy-start.15 = (f32[16,10]{1,0:T(8,128)S(1)}, f32[16,10]{1,0:T(8,128)}, u32[]{:S(2)}) copy-start(f32[16,10]{1,0:T(8,128)} %refs_5_.1) | copy-start | bytes 1924
  115.7 34.2 %copy-start.17 = (f32[10]{0:T(128)S(1)}, f32[10]{0:T(128)}, u32[]{:S(2)}) copy-start(f32[10]{0:T(128)} %param.20) | copy-start | bytes 124
  115.7 34.2 %copy-start.18 = (f32[10]{0:T(128)S(1)}, f32[10]{0:T(128)}, u32[]{:S(2)}) copy-start(f32[10]{0:T(128)} %param.21) | copy-start | bytes 124
  146.7 6.0 %collective-permute-start.28 = (f32[8,256]{1,0:T(8,128)S(1)}, f32[8,256]{1,0:T(8,128)S(1)}, u32[]{:S(2)}, u32[]{:S(2)}) collective-permute-start(f32[8,256]{1,0:T(8,128)S(1)} %get-tuple-element.169), channel_id=1, source_target_pairs={{0,1},{1,0},{2,3},{3,2},{4,5},{5,4},{6,7},{7,6},{8,9},{9,8},{10,11... | collective-permute-start | bytes 24584 | tf_op jit(solution)/shard_map/ppermute | solution.py:630
  152.6 3.7 %collective-permute-start.40 = (f32[64,128]{1,0:T(8,128)S(1)}, f32[64,128]{1,0:T(8,128)S(1)}, u32[]{:S(2)}, u32[]{:S(2)}) collective-permute-start(f32[64,128]{1,0:T(8,128)S(1)} %get-tuple-element.190.xlow), channel_id=1, source_target_pairs={{0,28},{4,0},{8,4},{12,8},{16,12},{20,16},{24,20},{28,24},{1,29},{... | collective-permute-start | bytes 98312 | tf_op jit(solution)/shard_map/ppermute | solution.py:634
  152.7 4.8 %collective-permute-start.41 = (f32[64,128]{1,0:T(8,128)S(1)}, f32[64,128]{1,0:T(8,128)S(1)}, u32[]{:S(2)}, u32[]{:S(2)}) collective-permute-start(f32[64,128]{1,0:T(8,128)S(1)} %get-tuple-element.191.xup), channel_id=1, source_target_pairs={{0,4},{4,8},{8,12},{12,16},{16,20},{20,24},{24,28},{28,0},{1,5},{5... | collective-permute-start | bytes 98312 | tf_op jit(solution)/shard_map/ppermute | solution.py:634
  156.4 4.8 %collective-permute-start.42 = (f32[64,128]{1,0:T(8,128)S(1)}, f32[64,128]{1,0:T(8,128)S(1)}, u32[]{:S(2)}, u32[]{:S(2)}) collective-permute-start(f32[64,128]{1,0:T(8,128)S(1)} %get-tuple-element.192.slow), channel_id=1, source_target_pairs={{0,3},{1,0},{2,1},{3,2},{4,7},{5,4},{6,5},{7,6},{8,11},{9,8},{10,9... | collective-permute-start | bytes 98312 | tf_op jit(solution)/shard_map/ppermute | solution.py:634
  157.5 3.6 %collective-permute-start.43 = (f32[64,128]{1,0:T(8,128)S(1)}, f32[64,128]{1,0:T(8,128)S(1)}, u32[]{:S(2)}, u32[]{:S(2)}) collective-permute-start(f32[64,128]{1,0:T(8,128)S(1)} %get-tuple-element.193.sup), channel_id=1, source_target_pairs={{0,1},{1,2},{2,3},{3,0},{4,5},{5,6},{6,7},{7,4},{8,9},{9,10},{10,1... | collective-permute-start | bytes 98312 | tf_op jit(solution)/shard_map/ppermute | solution.py:634
  164.3 1.7 %copy-start.2 = (f32[8,12,16,512]{3,2,1,0:T(8,128)}, f32[8,12,16,512]{3,2,1,0:T(8,128)S(1)}, u32[]{:S(2)}) copy-start(f32[8,12,16,512]{3,2,1,0:T(8,128)S(1)} %get-tuple-element.200) | copy-start | bytes 9437188
  164.4 1.7 %copy-start.6 = (f32[32,16,128]{2,1,0:T(8,128)}, f32[32,16,128]{2,1,0:T(8,128)S(1)}, u32[]{:S(2)}) copy-start(f32[32,16,128]{2,1,0:T(8,128)S(1)} %get-tuple-element.134) | copy-start | bytes 786436

commit v5 on v4

--- a/solution.py
+++ b/solution.py
@@ -455,7 +455,7 @@
 
 def solve_kernel(plan, cells, from_xlow, from_xup, from_slow, from_sup, *refs):
     tables, refs = refs[:10], refs[10:]
-    total, out_xlow, out_xup, out_slow, out_sup, box, section, modal, weights, values_w = refs
+    total, out_xlow, out_xup, out_slow, out_sup, box, section, modal, weights, values_w, sums = refs
     vectors_x, vectors_s, vectors_w, own_x, own_s, own_w, pick_x, pick_s, spread_x, spread_s = tables
     side, extent = plan.side, plan.extent
     layer, row_s, row_x = lane_steps(plan)
@@ -510,10 +510,14 @@
     for w in range(extent):
         rows = points if w in (0, extent - 1) else box_rows
         section[w] = exact(mix_t[:rows], box[w * box_rows : w * box_rows + rows, :], ((0,), (0,)))
-    for block in range(0, modal_rows, FACE):
-        held = [section[w, block : block + FACE, :] for w in range(extent)]
+    sums[...] = jnp.broadcast_to(sum_xs, sums.shape)
+
+    @pl.loop(0, modal_rows // FACE)
+    def _(block):
+        part = pl.ds(pl.multiple_of(block * FACE, FACE), FACE)
+        held = [section[w, part, :] for w in range(extent)]
         out = [None] * extent
-        base = jnp.broadcast_to(sum_xs[block : block + FACE], (FACE, lanes))
+        base = sums[part, :]
         for k in range(extent):
             value = None
             for w in range(extent):
@@ -524,7 +528,8 @@
                 term = weights[w, k : k + 1, :] * value
                 out[w] = term if out[w] is None else out[w] + term
         for w in range(extent):
-            modal[w, block : block + FACE, :] = out[w]
+            modal[w, part, :] = out[w]
+
     for w in range(extent):
         rows = points if w in (0, extent - 1) else box_rows
         box[w * box_rows : w * box_rows + rows, :] = exact(mix_t[:rows], modal[w])
@@ -640,20 +645,17 @@
     side = plan.side
     inner = side * side
 
-    def solve(cells, earlier):
+    def faces(cells):
         layered = cells.reshape(side, inner + 2 * FACE, plan.per_dev)
 
         def rows(start):
             return layered[:, start : start + FACE].reshape(side * FACE, plan.per_dev)
 
-        halo = [
-            shifted(rows(inner - FACE), "gx", 1),
-            shifted(rows(0), "gx", -1),
-            shifted(rows(inner), "gy", 1),
-            shifted(rows(inner + FACE), "gy", -1),
-        ]
-        if earlier is not None:
-            cells = after(cells, earlier)
+        ends = [rows(inner - FACE), rows(0)]
+        side_faces = [shifted(rows(inner), "gy", 1), shifted(rows(inner + FACE), "gy", -1)]
+        return [shifted(ends[0], "gx", 1), shifted(ends[1], "gx", -1)] + side_faces
+
+    def solve(cells, halo):
         face = jax.ShapeDtypeStruct((side * FACE, plan.per_dev), F32)
         sections = (plan.extent, tables[-1].shape[0], plan.per_dev)
         total, xlow, xup, slow, sup = simple_call(
@@ -663,7 +665,7 @@
             [pltpu.VMEM((plan.extent * (inner + 4 * FACE), plan.per_dev), F32)]
             + [pltpu.VMEM(sections, F32)] * 2
             + [pltpu.VMEM((plan.extent, plan.extent, plan.per_dev), F32)]
-            + [pltpu.VMEM((plan.extent, plan.per_dev), F32)],
+            + [pltpu.VMEM((plan.extent, plan.per_dev), F32), pltpu.VMEM(sections[1:], F32)],
         )
         returned = [shifted(xlow, "gx", -1), shifted(xup, "gx", 1), shifted(slow, "gy", -1), shifted(sup, "gy", 1)]
         (correction,) = simple_call(
@@ -679,8 +681,9 @@
         *near, aside = pack(plan, group, me, place_row, states, g == 0)
         packed.append((near, across(aside, 1)))
 
-    marks = gate = None
-    flags, arrived, held = [], [], []
+    marks = gate = waiting = None
+    flags, held, late = [], [], []
+    last = len(plan.groups) - 1
     for g, (group, (near, aside)) in enumerate(zip(plan.groups, packed)):
         first, flagged = g == 0, g == 1
         if not first:
@@ -689,36 +692,55 @@
         sent = merge(plan, group, near, aside, first, flags if flagged else [], cost)
         messages = [sent[0]] + [across(sent[b], 2 * b) for b in range(1, plan.pairs)]
         if not first:
-            messages[0] = after(messages[0], arrived[1:])
-        relays, late, more = relay(plan, group, messages, marks, flagged)
+            before_it = held[-1][1]
+            messages[0] = after(messages[0], before_it[1:])
+            if flagged:
+                before_it[0] = across(after(waiting, messages[1]), plan.plane)
+        if g == last:
+            buffer, row_marks, cells = settle(plan, plan.groups[0], *held[0], None, None, own, order, None)
+            messages[0] = after(messages[0], cells)
+            halo = faces(cells)
+        relays, rows_left, more = relay(plan, group, messages, marks, flagged)
+        late.append(rows_left)
         if first:
             marks, own, over = more
             flags = [over]
         if flagged:
             (flag,) = more
-        gate = relays[0]
+        gate = waiting = relays[0]
         ready = list(relays)
-        ready[0] = after(ready[0], messages[1:] if first else [messages[1], arrived[0]])
-        arrived = [across(r, m * plan.plane) for m, r in enumerate(ready, 1)]
-        held.append((messages, arrived, late))
-
-    buffer, row_marks, cells = settle(plan, plan.groups[0], *held[0][:2], None, None, own, order, None)
-    buffer, flag = settle(plan, plan.groups[1], *held[1][:2], row_marks, buffer, None, None, flag)
+        if g == last:
+            ready[1:] = [after(r, halo[:2]) for r in ready[1:]]
+            waiting = after(waiting, halo[:2])
+        if not first:
+            ready[1:] = [after(r, held[-1][1][1:]) for r in ready[1:]]
+        arrived = [None]
+        for m in range(2, plan.lines):
+            value = ready[m - 1]
+            if m > 2 and g != last:
+                value = after(value, arrived[-1])
+            if m > 2 and first:
+                value = after(value, packed[-1][1])
+            arrived.append(across(value, m * plan.plane))
+        if not first:
+            arrived[0] = across(after(waiting, [messages[1], held[-1][1][0]]), plan.plane)
+        held.append((messages, arrived))
+
+    buffer, flag = settle(plan, plan.groups[1], *held[1], row_marks, buffer, None, None, flag)
     flag = jnp.maximum(flag[:1, :1], across(flag, 1)[:1, :1])
-    correction = solve(after(cells, gate), buffer)
-    for group, (messages, arrived, _) in zip(plan.groups[2:], held[2:]):
-        (buffer,) = settle(plan, group, messages, arrived, row_marks, buffer, None, None, None)
+    correction = solve(cells, halo)
+    (buffer,) = settle(plan, plan.groups[last], *held[last], row_marks, buffer, None, None, None)
 
     def send_rest(buffer, correction, late):
         for group, parts in zip(plan.groups, late):
             parts = [across(part, m * plan.plane) for m, part in zip(plan.spill, parts)]
             buffer = add_late(plan, group, parts, row_marks, buffer)
-        return buffer, solve(cells_of(plan, buffer, order), None)
+        cells = cells_of(plan, buffer, order)
+        return buffer, solve(cells, faces(cells))
 
     def keep(buffer, correction, late):
         return buffer, correction
 
-    late = [rows_left for _, _, rows_left in held]
     if plan.spill:
         buffer, correction = lax.cond(flag[0, 0] > 0.0, send_rest, keep, buffer, correction, late)
     new_states = buffer.reshape(BX, BS, fields, plan.layers, points).transpose(0, 1, 3, 2, 4)

time: 168 us -> 159 us (0.946); the launches traced: 166 us -> 159 us
  waiting for transfers between devices: 96.6 us -> 89.6 us
    ppermute x22, starting transfers between devices: 28.9 us -> 23.5 us  [across(): lax.ppermute(value, both, [(d, d ^ flip) for d in range(plan.devices)])]
    ppermute x8, starting transfers between devices: 10.9 us -> 16 us  [shifted(): lax.ppermute(value, axis, [(s, (s + steps) % count) for s in range(count)])]
    ppermute x8, waiting for transfers between devices: 33 us -> 28.1 us  [shifted(): lax.ppermute(value, axis, [(s, (s + steps) % count) for s in range(count)])]
    ppermute x22, waiting for transfers between devices: 63.7 us -> 61.5 us  [across(): lax.ppermute(value, both, [(d, d ^ flip) for d in range(plan.devices)])]
  transfers between devices with their start and end apart: 30 -> 30, of which waited for: 12 -> 11; matrix products, arithmetic and copies ran while one was open for 1% -> 1% of each run, Pallas kernels for 10% -> 11%
where the time goes in v5:
time: 159 us
  waiting for transfers between devices  89.6 us (56%)
  starting transfers between devices  39.4 us (25%)
  Pallas kernels  21.2 us (13%)
  local copies, waits for them, and re-layouts  6.41 us (4%)
  between operations  2.28 us (1%)
    ppermute x22, waiting for transfers between devices, across(): lax.ppermute(value, both, [(d, d ^ flip) for d in range(plan.devices)])  61.5 us
    ppermute x8, waiting for transfers between devices, shifted(): lax.ppermute(value, axis, [(s, (s + steps) % count) for s in range(count)])  28.1 us
    ppermute x22, starting transfers between devices, across(): lax.ppermute(value, both, [(d, d ^ flip) for d in range(plan.devices)])  23.5 us
    ppermute x8, starting transfers between devices, shifted(): lax.ppermute(value, axis, [(s, (s + steps) % count) for s in range(count)])  16 us
    pallas_call x8, Pallas kernels, simple_call(): pl.pallas_call(kernel, in_specs=[pl.BlockSpec(memory_space=pltpu.VMEM)] *...  10 us
    pallas_call x3, Pallas kernels, pack(): pl.pallas_call(functools.partial(pack_kernel, plan, fields, marked), grid...  6 us
    unnamed x34, local copies, waits for them, and re-layouts  5.25 us
    pallas_call x3, Pallas kernels, settle(): pl.pallas_call(functools.partial(settle_kernel, plan, fields, marked, fla...  5.2 us
  transfers between devices with their start and end apart: 30, of which 11 were waited for; matrix products, arithmetic and copies ran while one was open for 1% of the time, Pallas kernels for 11%

profile of v5, /device:TPU:11, one launch (start us, length us, event | category | flops | bytes accessed | tf_op | source)
XLA Modules:
  0.0 159.2 jit_solution(278028027326756875)
XLA Ops:
  0.6 0.0 copy-start
  0.6 2.8 %copy-done = f32[256,12,512]{2,0,1:T(8,128)S(1)} copy-done((f32[256,12,512]{2,0,1:T(8,128)S(1)}, f32[256,12,512]{2,0,1:T(8,128)}, u32[]{:S(2)}) %copy-start) | copy-done | bytes 6291480
  3.4 0.7 copy-done.1
  4.1 1.8 %shard_map.141 = (f32[104,512]{1,0:T(8,128)S(1)}, f32[104,512]{1,0:T(8,128)S(1)}, f32[104,512]{1,0:T(8,128)S(1)}, f32[104,512]{1,0:T(8,128)S(1)}, f32[392,512]{1,0:T(8,128)S(1)}) custom-call(s32[1]{0:T(128)} %bitcast.5.me_ref, s32[1,256]{1,0:T(1,128)S(1)} %bitcast.35, f32[12,256,512]{2,1,0:T(8,128)S(1)} %bitcast.28), custom_call_target="tpu_custom_call" | custom-call | tf_op jit(solution)/shard_map/pallas_call | solution.py:134
  5.9 0.0 slice-start.1
  5.9 0.7 collective-permute-start.14
  6.6 1.9 %shard_map.140 = (f32[128,512]{1,0:T(8,128)S(1)}, f32[128,512]{1,0:T(8,128)S(1)}, f32[128,512]{1,0:T(8,128)S(1)}, f32[128,512]{1,0:T(8,128)S(1)}, f32[512,512]{1,0:T(8,128)S(1)}) custom-call(s32[1]{0:T(128)} %bitcast.5.me_ref, s32[1,256]{1,0:T(1,128)S(1)} %bitcast.36, f32[12,256,512]{2,1,0:T(8,128)S(1)} %bitcast.29), custom_call_target="tpu_custom_call" | custom-call | tf_op jit(solution)/shard_map/pallas_call | solution.py:134
  8.6 0.1 collective-permute-start.18
  8.7 0.1 shard_map.142
  8.8 1.3 collective-permute-start.15
  10.1 0.3 collective-permute-start.16
  10.3 1.1 collective-permute-start.17
  11.5 2.3 %shard_map.145 = (f32[160,512]{1,0:T(8,128)S(1)}, f32[160,512]{1,0:T(8,128)S(1)}, f32[160,512]{1,0:T(8,128)S(1)}, f32[160,512]{1,0:T(8,128)S(1)}, f32[640,512]{1,0:T(8,128)S(1)}) custom-call(s32[1]{0:T(128)} %bitcast.5.me_ref, s32[1,256]{1,0:T(1,128)S(1)} %bitcast.37, f32[12,256,512]{2,1,0:T(8,128)S(1)} %bitcast.32), custom_call_target="tpu_custom_call" | custom-call | tf_op jit(solution)/shard_map/pallas_call | solution.py:134
  13.8 1.4 collective-permute-start.20
  15.2 4.2 %collective-permute-done.15.refs_1_ = f32[200,512]{1,0:T(8,128)S(1)} collective-permute-done((f32[200,512]{1,0:T(8,128)S(1)}, f32[200,512]{1,0:T(8,128)S(1)}, u32[]{:S(2)}, u32[]{:S(2)}) %collective-permute-start.15) | collective-permute-done | bytes 409632 | tf_op jit(solution)/shard_map/ppermute | solution.py:635
  19.4 0.9 collective-permute-done.16.refs_2_
  20.3 8.7 %collective-permute-done.17.refs_3_ = f32[200,512]{1,0:T(8,128)S(1)} collective-permute-done((f32[200,512]{1,0:T(8,128)S(1)}, f32[200,512]{1,0:T(8,128)S(1)}, u32[]{:S(2)}, u32[]{:S(2)}) %collective-permute-start.17) | collective-permute-done | bytes 409632 | tf_op jit(solution)/shard_map/ppermute | solution.py:635
  29.1 1.7 %shard_map.143 = (f32[200,512]{1,0:T(8,128)S(1)}, f32[152,512]{1,0:T(8,128)S(1)}, f32[152,512]{1,0:T(8,128)S(1)}, f32[48,512]{1,0:T(8,128)}, f32[48,512]{1,0:T(8...) custom-call(f32[200,512]{1,0:T(8,128)S(1)} %get-tuple-element.150.refs_0_, ...), custom_call_target="tpu_custom_call" | custom-call | tf_op jit(solution)/shard_map/pallas_call | solution.py:591
  30.8 2.3 %collective-permute-start.19 = (f32[152,512]{1,0:T(8,128)S(1)}, f32[152,512]{1,0:T(8,128)S(1)}, u32[]{:S(2)}, u32[]{:S(2)}) collective-permute-start(f32[152,512]{1,0:T(8,128)S(1)} %get-tuple-element.162), channel_id=1, source_target_pairs={{0,16},{1,17},{2,18},{3,19},{4,20},{5,21},{6,22},{7,23},{8,24},{9,... | collective-permute-start | bytes 933896 | tf_op jit(solution)/shard_map/ppermute | solution.py:635
  33.1 0.1 shard_map.144
  33.2 1.3 collective-permute-start.22
  34.5 0.2 collective-permute-start.23
  34.8 1.2 collective-permute-start.24
  35.9 10.8 %collective-permute-done.19.refs_5_.refs_8_ = f32[152,512]{1,0:T(8,128)S(1)} collective-permute-done((f32[152,512]{1,0:T(8,128)S(1)}, f32[152,512]{1,0:T(8,128)S(1)}, u32[]{:S(2)}, u32[]{:S(2)}) %collective-permute-start.19) | collective-permute-done | bytes 311328 | tf_op jit(solution)/shard_map/ppermute | solution.py:635
  46.7 4.3 %collective-permute-start.25 = (f32[200,512]{1,0:T(8,128)S(1)}, f32[200,512]{1,0:T(8,128)S(1)}, u32[]{:S(2)}, u32[]{:S(2)}) collective-permute-start(f32[200,512]{1,0:T(8,128)S(1)} %get-tuple-element.173), channel_id=1, source_target_pairs={{0,8},{1,9},{2,10},{3,11},{4,12},{5,13},{6,14},{7,15},{8,0},{9,1},... | collective-permute-start | bytes 1228808 | tf_op jit(solution)/shard_map/ppermute | solution.py:635
  51.0 10.8 %collective-permute-done.21.refs_6_.refs_9_ = f32[152,512]{1,0:T(8,128)S(1)} collective-permute-done((f32[152,512]{1,0:T(8,128)S(1)}, f32[152,512]{1,0:T(8,128)S(1)}, u32[]{:S(2)}, u32[]{:S(2)}) %collective-permute-start.21) | collective-permute-done | bytes 311328 | tf_op jit(solution)/shard_map/ppermute | solution.py:635
  61.8 1.8 %shard_map.146 = (f32[264,512]{1,0:T(8,128)S(1)}, f32[200,512]{1,0:T(8,128)S(1)}, f32[200,512]{1,0:T(8,128)S(1)}, f32[64,512]{1,0:T(8,128)}, f32[64,512]{1,0:T(8,128)}, /*index=5*/f32[8,256]{1,0:T(8,128)S(1)}) custom-call(f32[264,512]{1,0:T(8,128)S(1)} %get-tuple-element.167.refs_0_, f32[264,512]{1,0:T(8,128)S(1)} %collective-permute-done.22.refs_1_, ...), custom_call_target="tpu_custom_call" | custom-call | tf_op jit(solution)/shard_map/pallas_call | solution.py:591
  63.6 0.2 shard_map.149
  63.8 1.3 collective-permute-start.30
  65.1 0.3 collective-permute-start.31
  65.4 1.2 collective-permute-start.32
  66.5 1.1 collective-permute-done.25.refs_4_.refs_7_
  67.6 2.2 %collective-permute-start.26 = (f32[264,512]{1,0:T(8,128)S(1)}, f32[264,512]{1,0:T(8,128)S(1)}, u32[]{:S(2)}, u32[]{:S(2)}) collective-permute-start(f32[264,512]{1,0:T(8,128)S(1)} %get-tuple-element.174), channel_id=1, source_target_pairs={{0,8},{1,9},{2,10},{3,11},{4,12},{5,13},{6,14},{7,15},{8,0},{9,1},... | collective-permute-start | bytes 1622024 | tf_op jit(solution)/shard_map/ppermute | solution.py:635
  69.8 10.4 %collective-permute-done.27.refs_5_.refs_8_ = f32[200,512]{1,0:T(8,128)S(1)} collective-permute-done((f32[200,512]{1,0:T(8,128)S(1)}, f32[200,512]{1,0:T(8,128)S(1)}, u32[]{:S(2)}, u32[]{:S(2)}) %collective-permute-start.27) | collective-permute-done | bytes 409632 | tf_op jit(solution)/shard_map/ppermute | solution.py:635
  80.2 0.7 collective-permute-start.28
  80.9 0.0 copy-start.8
  81.0 0.0 copy-start.9
  81.0 0.0 copy-start.11
  81.0 1.9 %shard_map.147 = (f32[8,12,16,512]{3,2,1,0:T(8,128)S(1)}, f32[8,256]{1,0:T(8,128)S(1)}, f32[640,128]{1,0:T(8,128)S(1)}) custom-call(f32[200,512]{1,0:T(8,128)S(1)} %get-tuple-element.150.refs_0_, f32[200,512]{1,0:T(8,128)S(1)} %collective-permute-done.15.refs_1_, f32[200,512]{1,0:T(8,128)S(1)} %collective-permute-done.16.refs_2_, ...), custom_call_target="tpu_custom_call" | custom-call | tf_op jit(solution)/shard_map/pallas_call | solution.py:387
  83.0 0.3 collective-permute-start.34
  83.3 14.5 %collective-permute-done.28.refs_6_.refs_9_ = f32[200,512]{1,0:T(8,128)S(1)} collective-permute-done((f32[200,512]{1,0:T(8,128)S(1)}, f32[200,512]{1,0:T(8,128)S(1)}, u32[]{:S(2)}, u32[]{:S(2)}) %collective-permute-start.28) | collective-permute-done | bytes 409632 | tf_op jit(solution)/shard_map/ppermute | solution.py:635
  97.8 2.7 %collective-permute-start.33 = (f32[64,128]{1,0:T(8,128)S(1)}, f32[64,128]{1,0:T(8,128)S(1)}, u32[]{:S(2)}, u32[]{:S(2)}) collective-permute-start(f32[64,128]{1,0:T(8,128)S(1)} %get-tuple-element.227), channel_id=1, source_target_pairs={{0,4},{4,8},{8,12},{12,16},{16,20},{20,24},{24,28},{28,0},{1,5},{5... | collective-permute-start | bytes 98312 | tf_op jit(solution)/shard_map/ppermute | solution.py:639
  100.4 2.0 %shard_map.150 = (f32[320,512]{1,0:T(8,128)S(1)}, f32[240,512]{1,0:T(8,128)S(1)}, f32[240,512]{1,0:T(8,128)S(1)}, f32[80,512]{1,0:T(8,128)}, f32[80,512]{1,0:T(8,128)}) custom-call(f32[320,512]{1,0:T(8,128)S(1)} %get-tuple-element.193.refs_0_, f32[320,512]{1,0:T(8,128)S(1)} %collective-permute-done.30.refs_1_, ...), custom_call_target="tpu_custom_call" | custom-call | tf_op jit(solution)/shard_map/pallas_call | solution.py:591
  102.4 0.1 collective-permute-start.35
  102.5 0.1 collective-permute-start.37
  102.6 3.5 %collective-permute-start.36 = (f32[240,512]{1,0:T(8,128)S(1)}, f32[240,512]{1,0:T(8,128)S(1)}, u32[]{:S(2)}, u32[]{:S(2)}) collective-permute-start(f32[240,512]{1,0:T(8,128)S(1)} %get-tuple-element.202), channel_id=1, source_target_pairs={{0,16},{1,17},{2,18},{3,19},{4,20},{5,21},{6,22},{7,23},{8,24},{9,... | collective-permute-start | bytes 1474568 | tf_op jit(solution)/shard_map/ppermute | solution.py:635
  106.0 3.5 %collective-permute-start.39 = (f32[64,128]{1,0:T(8,128)S(1)}, f32[64,128]{1,0:T(8,128)S(1)}, u32[]{:S(2)}, u32[]{:S(2)}) collective-permute-start(f32[64,128]{1,0:T(8,128)S(1)} %get-tuple-element.224), channel_id=1, source_target_pairs={{0,3},{1,0},{2,1},{3,2},{4,7},{5,4},{6,5},{7,6},{8,11},{9,8},{10,9... | collective-permute-start | bytes 98312 | tf_op jit(solution)/shard_map/ppermute | solution.py:639
  109.6 1.1 collective-permute-start.38
  110.7 2.2 %collective-permute-done.39.from_sup = f32[64,128]{1,0:T(8,128)S(1)} collective-permute-done((f32[64,128]{1,0:T(8,128)S(1)}, f32[64,128]{1,0:T(8,128)S(1)}, u32[]{:S(2)}, u32[]{:S(2)}) %collective-permute-start.39) | collective-permute-done | bytes 32800 | tf_op jit(solution)/shard_map/ppermute | solution.py:639
  113.0 3.1 %shard_map.152 = (f32[512,128]{1,0:T(8,128)S(1)}, f32[64,128]{1,0:T(8,128)S(1)}, f32[64,128]{1,0:T(8,128)S(1)}, f32[64,128]{1,0:T(8,128)S(1)}, f32[64,128]{1,0:T(8,128)S(1)}) custom-call(f32[640,128]{1,0:T(8,128)S(1)} %get-tuple-element.192.cells, f32[64,128]{1,0:T(8,128)S(1)} %collective-permute-done.33.from_xlow, ...), custom_call_target="tpu_custom_call" | custom-call | tf_op jit(solution)/shard_map/pallas_call | solution.py:591
  116.1 1.2 collective-permute-start.40
  117.2 1.4 collective-permute-start.41
  118.7 25.3 %collective-permute-done.40.from_x_up = f32[64,128]{1,0:T(8,128)S(1)} collective-permute-done((f32[64,128]{1,0:T(8,128)S(1)}, f32[64,128]{1,0:T(8,128)S(1)}, u32[]{:S(2)}, u32[]{:S(2)}) %collective-permute-start.40) | collective-permute-done | bytes 32800 | tf_op jit(solution)/shard_map/ppermute | solution.py:639
  144.0 4.6 %collective-permute-start.42 = (f32[64,128]{1,0:T(8,128)S(1)}, f32[64,128]{1,0:T(8,128)S(1)}, u32[]{:S(2)}, u32[]{:S(2)}) collective-permute-start(f32[64,128]{1,0:T(8,128)S(1)} %get-tuple-element.210.slow), channel_id=1, source_target_pairs={{0,3},{1,0},{2,1},{3,2},{4,7},{5,4},{6,5},{7,6},{8,11},{9,8},{10,9... | collective-permute-start | bytes 98312 | tf_op jit(solution)/shard_map/ppermute | solution.py:639
  148.6 1.2 collective-permute-start.43
  149.7 1.5 shard_map.148
  151.2 0.6 collective-permute-done.42.from_s_up
  151.8 1.1 shard_map.153
  152.9 0.5 slice.30
  153.4 0.6 slice.40
  155.3 1.8 %shard_map.151 = f32[8,12,16,512]{3,2,1,0:T(8,128)S(1)} custom-call(f32[320,512]{1,0:T(8,128)S(1)} %get-tuple-element.193.refs_0_, f32[320,512]{1,0:T(8,128)S(1)} %collective-permute-done.30.refs_1_, f32[320,512]{1,0:T(8,128)S(1)} %collective-permute-done.31.refs_2_, f32[320,512]{1,0:T(8,128)S(1)} %collective-permute-done.32.refs_3_, ...), custom_call_target="tpu_custom_call", output_to_operand_aliasing={{}: (8, {})} | custom-call | tf_op jit(solution)/shard_map/pallas_call | solution.py:387
  157.2 0.2 conditional.1
  157.4 1.6 %copy-done.2 = f32[8,12,16,512]{3,2,1,0:T(8,128)} copy-done((f32[8,12,16,512]{3,2,1,0:T(8,128)}, f32[8,12,16,512]{3,2,1,0:T(8,128)S(1)}, u32[]{:S(2)}) %copy-start.2) | copy-done | bytes 3145752
  159.1 0.1 copy-done.5
  (49 shorter events, 0.1 us)
Async XLA Ops:
  0.6 2.8 %copy-start = (f32[256,12,512]{2,0,1:T(8,128)S(1)}, f32[256,12,512]{2,0,1:T(8,128)}, u32[]{:S(2)}) copy-start(f32[256,12,512]{2,0,1:T(8,128)} %param.15) | copy-start | bytes 18874372
  3.4 0.7 copy-start.1
  4.1 7.4 %slice-start = ((s8[6291456]{0:T(1024)(128)(4,1)}), s8[4194304]{0:T(1024)(128)(4,1)S(1)}, s32[]{:S(2)}) async-start(s8[6291456]{0:T(1024)(128)(4,1)} %bitcast.30), calls=%async_computation | async-start | bytes 8388608
  5.9 5.6 %slice-start.1 = ((s8[6291456]{0:T(1024)(128)(4,1)}), s8[2097152]{0:T(1024)(128)(4,1)S(1)}, s32[]{:S(2)}) async-start(s8[6291456]{0:T(1024)(128)(4,1)} %bitcast.30), calls=%async_computation.1 | async-start | bytes 4194304
  5.9 2.8 %collective-permute-start.14 = (f32[392,512]{1,0:T(8,128)S(1)}, f32[392,512]{1,0:T(8,128)S(1)}, u32[]{:S(2)}, u32[]{:S(2)}) collective-permute-start(f32[392,512]{1,0:T(8,128)S(1)} %get-tuple-element.149), channel_id=1, source_target_pairs={{0,1},{1,0},{2,3},{3,2},{4,5},{5,4},{6,7},{7,6},{8,9},{9,8},{10,11... | collective-permute-start | bytes 2408456 | tf_op jit(solution)/shard_map/ppermute | solution.py:635
  8.6 24.5 %collective-permute-start.18 = (f32[512,512]{1,0:T(8,128)S(1)}, f32[512,512]{1,0:T(8,128)S(1)}, u32[]{:S(2)}, u32[]{:S(2)}) collective-permute-start(f32[512,512]{1,0:T(8,128)S(1)} %get-tuple-element.159), channel_id=1, source_target_pairs={{0,1},{1,0},{2,3},{3,2},{4,5},{5,4},{6,7},{7,6},{8,9},{9,8},{10,11... | collective-permute-start | bytes 3145736 | tf_op jit(solution)/shard_map/ppermute | solution.py:635
  8.8 10.6 %collective-permute-start.15 = (f32[200,512]{1,0:T(8,128)S(1)}, f32[200,512]{1,0:T(8,128)S(1)}, u32[]{:S(2)}, u32[]{:S(2)}) collective-permute-start(f32[200,512]{1,0:T(8,128)S(1)} %get-tuple-element.151), channel_id=1, source_target_pairs={{0,2},{1,3},{2,0},{3,1},{4,6},{5,7},{6,4},{7,5},{8,10},{9,11},{10,... | collective-permute-start | bytes 1228808 | tf_op jit(solution)/shard_map/ppermute | solution.py:635
  10.1 10.2 %collective-permute-start.16 = (f32[200,512]{1,0:T(8,128)S(1)}, f32[200,512]{1,0:T(8,128)S(1)}, u32[]{:S(2)}, u32[]{:S(2)}) collective-permute-start(f32[200,512]{1,0:T(8,128)S(1)} %get-tuple-element.152), channel_id=1, source_target_pairs={{0,4},{1,5},{2,6},{3,7},{4,0},{5,1},{6,2},{7,3},{8,12},{9,13},{10,... | collective-permute-start | bytes 1228808 | tf_op jit(solution)/shard_map/ppermute | solution.py:635
  10.3 18.7 %collective-permute-start.17 = (f32[200,512]{1,0:T(8,128)S(1)}, f32[200,512]{1,0:T(8,128)S(1)}, u32[]{:S(2)}, u32[]{:S(2)}) collective-permute-start(f32[200,512]{1,0:T(8,128)S(1)} %get-tuple-element.153), channel_id=1, source_target_pairs={{0,6},{1,7},{2,4},{3,5},{4,2},{5,3},{6,0},{7,1},{8,14},{9,15},{10,... | collective-permute-start | bytes 1228808 | tf_op jit(solution)/shard_map/ppermute | solution.py:635
  13.8 32.9 %collective-permute-start.20 = (f32[640,512]{1,0:T(8,128)S(1)}, f32[640,512]{1,0:T(8,128)S(1)}, u32[]{:S(2)}, u32[]{:S(2)}) collective-permute-start(f32[640,512]{1,0:T(8,128)S(1)} %get-tuple-element.165), channel_id=1, source_target_pairs={{0,1},{1,0},{2,3},{3,2},{4,5},{5,4},{6,7},{7,6},{8,9},{9,8},{10,11... | collective-permute-start | bytes 3932168 | tf_op jit(solution)/shard_map/ppermute | solution.py:635
  30.8 16.0 %collective-permute-start.19 = (f32[152,512]{1,0:T(8,128)S(1)}, f32[152,512]{1,0:T(8,128)S(1)}, u32[]{:S(2)}, u32[]{:S(2)}) collective-permute-start(f32[152,512]{1,0:T(8,128)S(1)} %get-tuple-element.162), channel_id=1, source_target_pairs={{0,16},{1,17},{2,18},{3,19},{4,20},{5,21},{6,22},{7,23},{8,24},{9,... | collective-permute-start | bytes 933896 | tf_op jit(solution)/shard_map/ppermute | solution.py:635
  33.2 13.5 %collective-permute-start.22 = (f32[264,512]{1,0:T(8,128)S(1)}, f32[264,512]{1,0:T(8,128)S(1)}, u32[]{:S(2)}, u32[]{:S(2)}) collective-permute-start(f32[264,512]{1,0:T(8,128)S(1)} %get-tuple-element.168), channel_id=1, source_target_pairs={{0,2},{1,3},{2,0},{3,1},{4,6},{5,7},{6,4},{7,5},{8,10},{9,11},{10,... | collective-permute-start | bytes 1622024 | tf_op jit(solution)/shard_map/ppermute | solution.py:635
  34.5 27.3 %collective-permute-start.23 = (f32[264,512]{1,0:T(8,128)S(1)}, f32[264,512]{1,0:T(8,128)S(1)}, u32[]{:S(2)}, u32[]{:S(2)}) collective-permute-start(f32[264,512]{1,0:T(8,128)S(1)} %get-tuple-element.169), channel_id=1, source_target_pairs={{0,4},{1,5},{2,6},{3,7},{4,0},{5,1},{6,2},{7,3},{8,12},{9,13},{10,... | collective-permute-start | bytes 1622024 | tf_op jit(solution)/shard_map/ppermute | solution.py:635
  34.8 27.1 %collective-permute-start.24 = (f32[264,512]{1,0:T(8,128)S(1)}, f32[264,512]{1,0:T(8,128)S(1)}, u32[]{:S(2)}, u32[]{:S(2)}) collective-permute-start(f32[264,512]{1,0:T(8,128)S(1)} %get-tuple-element.170), channel_id=1, source_target_pairs={{0,6},{1,7},{2,4},{3,5},{4,2},{5,3},{6,0},{7,1},{8,14},{9,15},{10,... | collective-permute-start | bytes 1622024 | tf_op jit(solution)/shard_map/ppermute | solution.py:635
  46.7 15.1 %collective-permute-start.21 = (f32[152,512]{1,0:T(8,128)S(1)}, f32[152,512]{1,0:T(8,128)S(1)}, u32[]{:S(2)}, u32[]{:S(2)}) collective-permute-start(f32[152,512]{1,0:T(8,128)S(1)} %get-tuple-element.166), channel_id=1, source_target_pairs={{0,24},{1,25},{2,26},{3,27},{4,28},{5,29},{6,30},{7,31},{8,16},{9,... | collective-permute-start | bytes 933896 | tf_op jit(solution)/shard_map/ppermute | solution.py:635
  46.7 20.9 %collective-permute-start.25 = (f32[200,512]{1,0:T(8,128)S(1)}, f32[200,512]{1,0:T(8,128)S(1)}, u32[]{:S(2)}, u32[]{:S(2)}) collective-permute-start(f32[200,512]{1,0:T(8,128)S(1)} %get-tuple-element.173), channel_id=1, source_target_pairs={{0,8},{1,9},{2,10},{3,11},{4,12},{5,13},{6,14},{7,15},{8,0},{9,1},... | collective-permute-start | bytes 1228808 | tf_op jit(solution)/shard_map/ppermute | solution.py:635
  63.6 16.6 %collective-permute-start.27 = (f32[200,512]{1,0:T(8,128)S(1)}, f32[200,512]{1,0:T(8,128)S(1)}, u32[]{:S(2)}, u32[]{:S(2)}) collective-permute-start(f32[200,512]{1,0:T(8,128)S(1)} %get-tuple-element.176), channel_id=1, source_target_pairs={{0,16},{1,17},{2,18},{3,19},{4,20},{5,21},{6,22},{7,23},{8,24},{9,... | collective-permute-start | bytes 1228808 | tf_op jit(solution)/shard_map/ppermute | solution.py:635
  63.6 17.3 %copy-start.3 = (bf16[640,512]{1,0:T(8,128)(2,1)S(1)}, bf16[640,512]{1,0:T(8,128)(2,1)}, u32[]{:S(2)}) copy-start(bf16[640,512]{1,0:T(8,128)(2,1)} %constant.24.clone.refs_11_) | copy-start | bytes 1966084
  63.8 19.2 %collective-permute-start.30 = (f32[320,512]{1,0:T(8,128)S(1)}, f32[320,512]{1,0:T(8,128)S(1)}, u32[]{:S(2)}, u32[]{:S(2)}) collective-permute-start(f32[320,512]{1,0:T(8,128)S(1)} %get-tuple-element.194), channel_id=1, source_target_pairs={{0,2},{1,3},{2,0},{3,1},{4,6},{5,7},{6,4},{7,5},{8,10},{9,11},{10,... | collective-permute-start | bytes 1966088 | tf_op jit(solution)/shard_map/ppermute | solution.py:635
  65.1 35.3 %collective-permute-start.31 = (f32[320,512]{1,0:T(8,128)S(1)}, f32[320,512]{1,0:T(8,128)S(1)}, u32[]{:S(2)}, u32[]{:S(2)}) collective-permute-start(f32[320,512]{1,0:T(8,128)S(1)} %get-tuple-element.195), channel_id=1, source_target_pairs={{0,4},{1,5},{2,6},{3,7},{4,0},{5,1},{6,2},{7,3},{8,12},{9,13},{10,... | collective-permute-start | bytes 1966088 | tf_op jit(solution)/shard_map/ppermute | solution.py:635
  65.4 35.1 %collective-permute-start.32 = (f32[320,512]{1,0:T(8,128)S(1)}, f32[320,512]{1,0:T(8,128)S(1)}, u32[]{:S(2)}, u32[]{:S(2)}) collective-permute-start(f32[320,512]{1,0:T(8,128)S(1)} %get-tuple-element.196), channel_id=1, source_target_pairs={{0,6},{1,7},{2,4},{3,5},{4,2},{5,3},{6,0},{7,1},{8,14},{9,15},{10,... | collective-permute-start | bytes 1966088 | tf_op jit(solution)/shard_map/ppermute | solution.py:635
  67.6 34.8 %collective-permute-start.26 = (f32[264,512]{1,0:T(8,128)S(1)}, f32[264,512]{1,0:T(8,128)S(1)}, u32[]{:S(2)}, u32[]{:S(2)}) collective-permute-start(f32[264,512]{1,0:T(8,128)S(1)} %get-tuple-element.174), channel_id=1, source_target_pairs={{0,8},{1,9},{2,10},{3,11},{4,12},{5,13},{6,14},{7,15},{8,0},{9,1},... | collective-permute-start | bytes 1622024 | tf_op jit(solution)/shard_map/ppermute | solution.py:635
  80.2 17.5 %collective-permute-start.28 = (f32[200,512]{1,0:T(8,128)S(1)}, f32[200,512]{1,0:T(8,128)S(1)}, u32[]{:S(2)}, u32[]{:S(2)}) collective-permute-start(f32[200,512]{1,0:T(8,128)S(1)} %get-tuple-element.179), channel_id=1, source_target_pairs={{0,24},{1,25},{2,26},{3,27},{4,28},{5,29},{6,30},{7,31},{8,16},{9,... | collective-permute-start | bytes 1228808 | tf_op jit(solution)/shard_map/ppermute | solution.py:635
  80.9 31.9 %copy-start.4 = (f32[16,10,10]{2,0,1:T(8,128)S(1)}, f32[16,10,10]{2,0,1:T(8,128)}, u32[]{:S(2)}) copy-start(f32[16,10,10]{2,0,1:T(8,128)} %param.19) | copy-start | bytes 19204
  80.9 31.9 %copy-start.6 = (f32[104,10]{1,0:T(8,128)S(1)}, f32[104,10]{1,0:T(8,128)}, u32[]{:S(2)}) copy-start(f32[104,10]{1,0:T(8,128)} %constant.28.clone.refs_9_) | copy-start | bytes 12484
  80.9 31.9 %copy-start.7 = (f32[104,10]{1,0:T(8,128)S(1)}, f32[104,10]{1,0:T(8,128)}, u32[]{:S(2)}) copy-start(f32[104,10]{1,0:T(8,128)} %constant.27.clone.refs_8_) | copy-start | bytes 12484
  80.9 31.9 %copy-start.8 = (f32[96,10]{1,0:T(8,128)S(1)}, f32[96,10]{1,0:T(8,128)}, u32[]{:S(2)}) copy-start(f32[96,10]{1,0:T(8,128)} %constant.26.clone.refs_7_) | copy-start | bytes 11524
  81.0 31.9 %copy-start.9 = (f32[96,10]{1,0:T(8,128)S(1)}, f32[96,10]{1,0:T(8,128)}, u32[]{:S(2)}) copy-start(f32[96,10]{1,0:T(8,128)} %constant.25.clone.refs_6_) | copy-start | bytes 11524
  81.0 31.9 %copy-start.10 = (f32[10,10]{1,0:T(8,128)S(1)}, f32[10,10]{1,0:T(8,128)}, u32[]{:S(2)}) copy-start(f32[10,10]{1,0:T(8,128)} %refs_0_.1) | copy-start | bytes 1204
  81.0 31.9 %copy-start.11 = (f32[10,10]{1,0:T(8,128)S(1)}, f32[10,10]{1,0:T(8,128)}, u32[]{:S(2)}) copy-start(f32[10,10]{1,0:T(8,128)} %refs_1_.1) | copy-start | bytes 1204
  81.0 31.9 %copy-start.12 = (f32[16,10]{1,0:T(8,128)S(1)}, f32[16,10]{1,0:T(8,128)}, u32[]{:S(2)}) copy-start(f32[16,10]{1,0:T(8,128)} %refs_5_.1) | copy-start | bytes 1924
  81.0 31.9 %copy-start.13 = (f32[10]{0:T(128)S(1)}, f32[10]{0:T(128)}, u32[]{:S(2)}) copy-start(f32[10]{0:T(128)} %param.20) | copy-start | bytes 124
  81.0 31.9 %copy-start.14 = (f32[10]{0:T(128)S(1)}, f32[10]{0:T(128)}, u32[]{:S(2)}) copy-start(f32[10]{0:T(128)} %param.21) | copy-start | bytes 124
  83.0 19.4 %collective-permute-start.34 = (f32[64,128]{1,0:T(8,128)S(1)}, f32[64,128]{1,0:T(8,128)S(1)}, u32[]{:S(2)}, u32[]{:S(2)}) collective-permute-start(f32[64,128]{1,0:T(8,128)S(1)} %get-tuple-element.226), channel_id=1, source_target_pairs={{0,28},{4,0},{8,4},{12,8},{16,12},{20,16},{24,20},{28,24},{1,29},{... | collective-permute-start | bytes 98312 | tf_op jit(solution)/shard_map/ppermute | solution.py:639
  97.8 4.6 %collective-permute-start.33 = (f32[64,128]{1,0:T(8,128)S(1)}, f32[64,128]{1,0:T(8,128)S(1)}, u32[]{:S(2)}, u32[]{:S(2)}) collective-permute-start(f32[64,128]{1,0:T(8,128)S(1)} %get-tuple-element.227), channel_id=1, source_target_pairs={{0,4},{4,8},{8,12},{12,16},{16,20},{20,24},{24,28},{28,0},{1,5},{5... | collective-permute-start | bytes 98312 | tf_op jit(solution)/shard_map/ppermute | solution.py:639
  102.4 52.9 %collective-permute-start.35 = (f32[320,512]{1,0:T(8,128)S(1)}, f32[320,512]{1,0:T(8,128)S(1)}, u32[]{:S(2)}, u32[]{:S(2)}) collective-permute-start(f32[320,512]{1,0:T(8,128)S(1)} %get-tuple-element.199), channel_id=1, source_target_pairs={{0,8},{1,9},{2,10},{3,11},{4,12},{5,13},{6,14},{7,15},{8,0},{9,1},... | collective-permute-start | bytes 1966088 | tf_op jit(solution)/shard_map/ppermute | solution.py:635
  102.5 52.8 %collective-permute-start.37 = (f32[240,512]{1,0:T(8,128)S(1)}, f32[240,512]{1,0:T(8,128)S(1)}, u32[]{:S(2)}, u32[]{:S(2)}) collective-permute-start(f32[240,512]{1,0:T(8,128)S(1)} %get-tuple-element.205), channel_id=1, source_target_pairs={{0,24},{1,25},{2,26},{3,27},{4,28},{5,29},{6,30},{7,31},{8,16},{9,... | collective-permute-start | bytes 1474568 | tf_op jit(solution)/shard_map/ppermute | solution.py:635
  102.6 52.8 %collective-permute-start.36 = (f32[240,512]{1,0:T(8,128)S(1)}, f32[240,512]{1,0:T(8,128)S(1)}, u32[]{:S(2)}, u32[]{:S(2)}) collective-permute-start(f32[240,512]{1,0:T(8,128)S(1)} %get-tuple-element.202), channel_id=1, source_target_pairs={{0,16},{1,17},{2,18},{3,19},{4,20},{5,21},{6,22},{7,23},{8,24},{9,... | collective-permute-start | bytes 1474568 | tf_op jit(solution)/shard_map/ppermute | solution.py:635
  106.0 6.8 %collective-permute-start.39 = (f32[64,128]{1,0:T(8,128)S(1)}, f32[64,128]{1,0:T(8,128)S(1)}, u32[]{:S(2)}, u32[]{:S(2)}) collective-permute-start(f32[64,128]{1,0:T(8,128)S(1)} %get-tuple-element.224), channel_id=1, source_target_pairs={{0,3},{1,0},{2,1},{3,2},{4,7},{5,4},{6,5},{7,6},{8,11},{9,8},{10,9... | collective-permute-start | bytes 98312 | tf_op jit(solution)/shard_map/ppermute | solution.py:639
  109.6 3.3 %collective-permute-start.38 = (f32[64,128]{1,0:T(8,128)S(1)}, f32[64,128]{1,0:T(8,128)S(1)}, u32[]{:S(2)}, u32[]{:S(2)}) collective-permute-start(f32[64,128]{1,0:T(8,128)S(1)} %get-tuple-element.225), channel_id=1, source_target_pairs={{0,1},{1,2},{2,3},{3,0},{4,5},{5,6},{6,7},{7,4},{8,9},{9,10},{10,1... | collective-permute-start | bytes 98312 | tf_op jit(solution)/shard_map/ppermute | solution.py:639
  116.1 27.9 %collective-permute-start.40 = (f32[64,128]{1,0:T(8,128)S(1)}, f32[64,128]{1,0:T(8,128)S(1)}, u32[]{:S(2)}, u32[]{:S(2)}) collective-permute-start(f32[64,128]{1,0:T(8,128)S(1)} %get-tuple-element.208.xlow), channel_id=1, source_target_pairs={{0,28},{4,0},{8,4},{12,8},{16,12},{20,16},{24,20},{28,24},{1,29},{... | collective-permute-start | bytes 98312 | tf_op jit(solution)/shard_map/ppermute | solution.py:639
  117.2 31.3 %collective-permute-start.41 = (f32[64,128]{1,0:T(8,128)S(1)}, f32[64,128]{1,0:T(8,128)S(1)}, u32[]{:S(2)}, u32[]{:S(2)}) collective-permute-start(f32[64,128]{1,0:T(8,128)S(1)} %get-tuple-element.209.xup), channel_id=1, source_target_pairs={{0,4},{4,8},{8,12},{12,16},{16,20},{20,24},{24,28},{28,0},{1,5},{5... | collective-permute-start | bytes 98312 | tf_op jit(solution)/shard_map/ppermute | solution.py:639
  144.0 7.8 %collective-permute-start.42 = (f32[64,128]{1,0:T(8,128)S(1)}, f32[64,128]{1,0:T(8,128)S(1)}, u32[]{:S(2)}, u32[]{:S(2)}) collective-permute-start(f32[64,128]{1,0:T(8,128)S(1)} %get-tuple-element.210.slow), channel_id=1, source_target_pairs={{0,3},{1,0},{2,1},{3,2},{4,7},{5,4},{6,5},{7,6},{8,11},{9,8},{10,9... | collective-permute-start | bytes 98312 | tf_op jit(solution)/shard_map/ppermute | solution.py:639
  148.6 3.2 %collective-permute-start.43 = (f32[64,128]{1,0:T(8,128)S(1)}, f32[64,128]{1,0:T(8,128)S(1)}, u32[]{:S(2)}, u32[]{:S(2)}) collective-permute-start(f32[64,128]{1,0:T(8,128)S(1)} %get-tuple-element.211.sup), channel_id=1, source_target_pairs={{0,1},{1,2},{2,3},{3,0},{4,5},{5,6},{6,7},{7,4},{8,9},{9,10},{10,1... | collective-permute-start | bytes 98312 | tf_op jit(solution)/shard_map/ppermute | solution.py:639
  151.8 1.6 %collective-permute-start.29 = (f32[8,256]{1,0:T(8,128)S(1)}, f32[8,256]{1,0:T(8,128)S(1)}, u32[]{:S(2)}, u32[]{:S(2)}) collective-permute-start(f32[8,256]{1,0:T(8,128)S(1)} %get-tuple-element.184), channel_id=1, source_target_pairs={{0,1},{1,0},{2,3},{3,2},{4,5},{5,4},{6,7},{7,6},{8,9},{9,8},{10,11... | collective-permute-start | bytes 24584 | tf_op jit(solution)/shard_map/ppermute | solution.py:635
  157.4 1.7 %copy-start.2 = (f32[8,12,16,512]{3,2,1,0:T(8,128)}, f32[8,12,16,512]{3,2,1,0:T(8,128)S(1)}, u32[]{:S(2)}) copy-start(f32[8,12,16,512]{3,2,1,0:T(8,128)S(1)} %get-tuple-element.218) | copy-start | bytes 9437188
  157.4 1.7 %copy-start.5 = (f32[32,16,128]{2,1,0:T(8,128)}, f32[32,16,128]{2,1,0:T(8,128)S(1)}, u32[]{:S(2)}) copy-start(f32[32,16,128]{2,1,0:T(8,128)S(1)} %get-tuple-element.143) | copy-start | bytes 786436

commit v6 on v5

--- a/solution.py
+++ b/solution.py
@@ -728,7 +728,7 @@
 
     buffer, flag = settle(plan, plan.groups[1], *held[1], row_marks, buffer, None, None, flag)
     flag = jnp.maximum(flag[:1, :1], across(flag, 1)[:1, :1])
-    correction = solve(cells, halo)
+    correction = solve(after(cells, [buffer, flag]), halo)
     (buffer,) = settle(plan, plan.groups[last], *held[last], row_marks, buffer, None, None, None)
 
     def send_rest(buffer, correction, late):

time: 159 us -> 157 us (0.987)
  waiting for transfers between devices: 89.6 us -> 86.7 us
    ppermute x8, waiting for transfers between devices: 28.1 us -> 24.3 us  [shifted(): lax.ppermute(value, axis, [(s, (s + steps) % count) for s in range(count)])]
    ppermute x22, starting transfers between devices: 23.5 us -> 27.1 us  [across(): lax.ppermute(value, both, [(d, d ^ flip) for d in range(plan.devices)])]
    ppermute x8, starting transfers between devices: 16 us -> 12.9 us  [shifted(): lax.ppermute(value, axis, [(s, (s + steps) % count) for s in range(count)])]
where the time goes in v6:
time: 157 us
  waiting for transfers between devices  86.7 us (55%)
  starting transfers between devices  39.9 us (25%)
  Pallas kernels  21.2 us (14%)
  local copies, waits for them, and re-layouts  6.38 us (4%)
  between operations  2.3 us (1%)
    ppermute x22, waiting for transfers between devices, across(): lax.ppermute(value, both, [(d, d ^ flip) for d in range(plan.devices)])  62.4 us
    ppermute x22, starting transfers between devices, across(): lax.ppermute(value, both, [(d, d ^ flip) for d in range(plan.devices)])  27.1 us
    ppermute x8, waiting for transfers between devices, shifted(): lax.ppermute(value, axis, [(s, (s + steps) % count) for s in range(count)])  24.3 us
    ppermute x8, starting transfers between devices, shifted(): lax.ppermute(value, axis, [(s, (s + steps) % count) for s in range(count)])  12.9 us
    pallas_call x8, Pallas kernels, simple_call(): pl.pallas_call(kernel, in_specs=[pl.BlockSpec(memory_space=pltpu.VMEM)] *...  9.94 us
    pallas_call x3, Pallas kernels, pack(): pl.pallas_call(functools.partial(pack_kernel, plan, fields, marked), grid...  6 us
    unnamed x34, local copies, waits for them, and re-layouts  5.25 us
    pallas_call x3, Pallas kernels, settle(): pl.pallas_call(functools.partial(settle_kernel, plan, fields, marked, fla...  5.21 us
  transfers between devices with their start and end apart: 30, of which 11 were waited for; matrix products, arithmetic and copies ran while one was open for 1% of the time, Pallas kernels for 11%

profile of v6, /device:TPU:11, one launch (start us, length us, event | category | flops | bytes accessed | tf_op | source)
XLA Modules:
  0.0 156.7 jit_solution(4381387933739351459)
XLA Ops:
  0.6 2.8 %copy-done = f32[256,12,512]{2,0,1:T(8,128)S(1)} copy-done((f32[256,12,512]{2,0,1:T(8,128)S(1)}, f32[256,12,512]{2,0,1:T(8,128)}, u32[]{:S(2)}) %copy-start) | copy-done | bytes 6291480
  3.4 0.7 copy-done.1
  4.1 1.8 %shard_map.141 = (f32[104,512]{1,0:T(8,128)S(1)}, f32[104,512]{1,0:T(8,128)S(1)}, f32[104,512]{1,0:T(8,128)S(1)}, f32[104,512]{1,0:T(8,128)S(1)}, f32[392,512]{1,0:T(8,128)S(1)}) custom-call(s32[1]{0:T(128)} %bitcast.5.me_ref, s32[1,256]{1,0:T(1,128)S(1)} %bitcast.35, f32[12,256,512]{2,1,0:T(8,128)S(1)} %bitcast.28), custom_call_target="tpu_custom_call" | custom-call | tf_op jit(solution)/shard_map/pallas_call | solution.py:134
  5.9 0.0 slice-start.1
  5.9 0.7 collective-permute-start.14
  6.6 1.9 %shard_map.140 = (f32[128,512]{1,0:T(8,128)S(1)}, f32[128,512]{1,0:T(8,128)S(1)}, f32[128,512]{1,0:T(8,128)S(1)}, f32[128,512]{1,0:T(8,128)S(1)}, f32[512,512]{1,0:T(8,128)S(1)}) custom-call(s32[1]{0:T(128)} %bitcast.5.me_ref, s32[1,256]{1,0:T(1,128)S(1)} %bitcast.36, f32[12,256,512]{2,1,0:T(8,128)S(1)} %bitcast.29), custom_call_target="tpu_custom_call" | custom-call | tf_op jit(solution)/shard_map/pallas_call | solution.py:134
  8.6 0.1 collective-permute-start.18
  8.7 0.1 shard_map.142
  8.8 1.3 collective-permute-start.15
  10.1 0.3 collective-permute-start.16
  10.3 1.1 collective-permute-start.17
  11.5 2.3 %shard_map.145 = (f32[160,512]{1,0:T(8,128)S(1)}, f32[160,512]{1,0:T(8,128)S(1)}, f32[160,512]{1,0:T(8,128)S(1)}, f32[160,512]{1,0:T(8,128)S(1)}, f32[640,512]{1,0:T(8,128)S(1)}) custom-call(s32[1]{0:T(128)} %bitcast.5.me_ref, s32[1,256]{1,0:T(1,128)S(1)} %bitcast.37, f32[12,256,512]{2,1,0:T(8,128)S(1)} %bitcast.32), custom_call_target="tpu_custom_call" | custom-call | tf_op jit(solution)/shard_map/pallas_call | solution.py:134
  13.8 1.4 collective-permute-start.20
  15.2 4.2 %collective-permute-done.15.refs_1_ = f32[200,512]{1,0:T(8,128)S(1)} collective-permute-done((f32[200,512]{1,0:T(8,128)S(1)}, f32[200,512]{1,0:T(8,128)S(1)}, u32[]{:S(2)}, u32[]{:S(2)}) %collective-permute-start.15) | collective-permute-done | bytes 409632 | tf_op jit(solution)/shard_map/ppermute | solution.py:635
  19.4 0.9 collective-permute-done.16.refs_2_
  20.3 8.7 %collective-permute-done.17.refs_3_ = f32[200,512]{1,0:T(8,128)S(1)} collective-permute-done((f32[200,512]{1,0:T(8,128)S(1)}, f32[200,512]{1,0:T(8,128)S(1)}, u32[]{:S(2)}, u32[]{:S(2)}) %collective-permute-start.17) | collective-permute-done | bytes 409632 | tf_op jit(solution)/shard_map/ppermute | solution.py:635
  29.1 1.7 %shard_map.143 = (f32[200,512]{1,0:T(8,128)S(1)}, f32[152,512]{1,0:T(8,128)S(1)}, f32[152,512]{1,0:T(8,128)S(1)}, f32[48,512]{1,0:T(8,128)}, f32[48,512]{1,0:T(8...) custom-call(f32[200,512]{1,0:T(8,128)S(1)} %get-tuple-element.151.refs_0_, ...), custom_call_target="tpu_custom_call" | custom-call | tf_op jit(solution)/shard_map/pallas_call | solution.py:591
  30.8 2.3 %collective-permute-start.19 = (f32[152,512]{1,0:T(8,128)S(1)}, f32[152,512]{1,0:T(8,128)S(1)}, u32[]{:S(2)}, u32[]{:S(2)}) collective-permute-start(f32[152,512]{1,0:T(8,128)S(1)} %get-tuple-element.163), channel_id=1, source_target_pairs={{0,16},{1,17},{2,18},{3,19},{4,20},{5,21},{6,22},{7,23},{8,24},{9,... | collective-permute-start | bytes 933896 | tf_op jit(solution)/shard_map/ppermute | solution.py:635
  33.1 0.1 shard_map.144
  33.2 1.3 collective-permute-start.22
  34.5 0.2 collective-permute-start.23
  34.7 1.2 collective-permute-start.24
  35.9 10.8 %collective-permute-done.19.refs_5_.refs_8_ = f32[152,512]{1,0:T(8,128)S(1)} collective-permute-done((f32[152,512]{1,0:T(8,128)S(1)}, f32[152,512]{1,0:T(8,128)S(1)}, u32[]{:S(2)}, u32[]{:S(2)}) %collective-permute-start.19) | collective-permute-done | bytes 311328 | tf_op jit(solution)/shard_map/ppermute | solution.py:635
  46.7 4.3 %collective-permute-start.25 = (f32[200,512]{1,0:T(8,128)S(1)}, f32[200,512]{1,0:T(8,128)S(1)}, u32[]{:S(2)}, u32[]{:S(2)}) collective-permute-start(f32[200,512]{1,0:T(8,128)S(1)} %get-tuple-element.174), channel_id=1, source_target_pairs={{0,8},{1,9},{2,10},{3,11},{4,12},{5,13},{6,14},{7,15},{8,0},{9,1},... | collective-permute-start | bytes 1228808 | tf_op jit(solution)/shard_map/ppermute | solution.py:635
  51.0 10.8 %collective-permute-done.21.refs_6_.refs_9_ = f32[152,512]{1,0:T(8,128)S(1)} collective-permute-done((f32[152,512]{1,0:T(8,128)S(1)}, f32[152,512]{1,0:T(8,128)S(1)}, u32[]{:S(2)}, u32[]{:S(2)}) %collective-permute-start.21) | collective-permute-done | bytes 311328 | tf_op jit(solution)/shard_map/ppermute | solution.py:635
  61.8 1.7 %shard_map.146 = (f32[264,512]{1,0:T(8,128)S(1)}, f32[200,512]{1,0:T(8,128)S(1)}, f32[200,512]{1,0:T(8,128)S(1)}, f32[64,512]{1,0:T(8,128)S(1)}, f32[64,512]{1,0:T(8,128)}, /*index=5*/f32[8,256]{1,0:T(8,128)S(1)}) custom-call(f32[264,512]{1,0:T(8,128)S(1)} %get-tuple-element.168.refs_0_, f32[264,512]{1,0:T(8,128)S(1)} %collective-permute-done.22.refs_1_, ...), custom_call_target="tpu_custom_call" | custom-call | tf_op jit(solution)/shard_map/pallas_call | solution.py:591
  63.6 0.2 shard_map.149
  63.7 1.3 collective-permute-start.30
  65.0 0.3 collective-permute-start.31
  65.3 1.2 collective-permute-start.32
  66.5 1.1 collective-permute-done.25.refs_4_.refs_7_
  67.6 2.2 %collective-permute-start.26 = (f32[264,512]{1,0:T(8,128)S(1)}, f32[264,512]{1,0:T(8,128)S(1)}, u32[]{:S(2)}, u32[]{:S(2)}) collective-permute-start(f32[264,512]{1,0:T(8,128)S(1)} %get-tuple-element.175), channel_id=1, source_target_pairs={{0,8},{1,9},{2,10},{3,11},{4,12},{5,13},{6,14},{7,15},{8,0},{9,1},... | collective-permute-start | bytes 1622024 | tf_op jit(solution)/shard_map/ppermute | solution.py:635
  69.8 10.4 %collective-permute-done.27.refs_5_.refs_8_ = f32[200,512]{1,0:T(8,128)S(1)} collective-permute-done((f32[200,512]{1,0:T(8,128)S(1)}, f32[200,512]{1,0:T(8,128)S(1)}, u32[]{:S(2)}, u32[]{:S(2)}) %collective-permute-start.27) | collective-permute-done | bytes 409632 | tf_op jit(solution)/shard_map/ppermute | solution.py:635
  80.2 0.7 collective-permute-start.28
  80.9 1.9 %shard_map.147 = (f32[8,12,16,512]{3,2,1,0:T(8,128)S(1)}, f32[8,256]{1,0:T(8,128)S(1)}, f32[640,128]{1,0:T(8,128)S(1)}) custom-call(f32[200,512]{1,0:T(8,128)S(1)} %get-tuple-element.151.refs_0_, f32[200,512]{1,0:T(8,128)S(1)} %collective-permute-done.15.refs_1_, f32[200,512]{1,0:T(8,128)S(1)} %collective-permute-done.16.refs_2_, ...), custom_call_target="tpu_custom_call" | custom-call | tf_op jit(solution)/shard_map/pallas_call | solution.py:387
  82.8 0.3 collective-permute-start.34
  83.0 14.7 %collective-permute-done.28.refs_6_.refs_9_ = f32[200,512]{1,0:T(8,128)S(1)} collective-permute-done((f32[200,512]{1,0:T(8,128)S(1)}, f32[200,512]{1,0:T(8,128)S(1)}, u32[]{:S(2)}, u32[]{:S(2)}) %collective-permute-start.28) | collective-permute-done | bytes 409632 | tf_op jit(solution)/shard_map/ppermute | solution.py:635
  97.7 2.7 %collective-permute-start.33 = (f32[64,128]{1,0:T(8,128)S(1)}, f32[64,128]{1,0:T(8,128)S(1)}, u32[]{:S(2)}, u32[]{:S(2)}) collective-permute-start(f32[64,128]{1,0:T(8,128)S(1)} %get-tuple-element.229), channel_id=1, source_target_pairs={{0,4},{4,8},{8,12},{12,16},{16,20},{20,24},{24,28},{28,0},{1,5},{5... | collective-permute-start | bytes 98312 | tf_op jit(solution)/shard_map/ppermute | solution.py:639
  100.4 1.9 %shard_map.150 = (f32[320,512]{1,0:T(8,128)S(1)}, f32[240,512]{1,0:T(8,128)S(1)}, f32[240,512]{1,0:T(8,128)S(1)}, f32[80,512]{1,0:T(8,128)}, f32[80,512]{1,0:T(8,128)}) custom-call(f32[320,512]{1,0:T(8,128)S(1)} %get-tuple-element.194.refs_0_, f32[320,512]{1,0:T(8,128)S(1)} %collective-permute-done.30.refs_1_, ...), custom_call_target="tpu_custom_call" | custom-call | tf_op jit(solution)/shard_map/pallas_call | solution.py:591
  102.3 0.1 collective-permute-start.35
  102.4 0.1 collective-permute-start.37
  102.5 3.4 %collective-permute-start.36 = (f32[240,512]{1,0:T(8,128)S(1)}, f32[240,512]{1,0:T(8,128)S(1)}, u32[]{:S(2)}, u32[]{:S(2)}) collective-permute-start(f32[240,512]{1,0:T(8,128)S(1)} %get-tuple-element.203), channel_id=1, source_target_pairs={{0,16},{1,17},{2,18},{3,19},{4,20},{5,21},{6,22},{7,23},{8,24},{9,... | collective-permute-start | bytes 1474568 | tf_op jit(solution)/shard_map/ppermute | solution.py:635
  105.9 0.0 copy-start.9
  106.0 0.0 copy-start.10
  106.0 0.0 copy-start.11
  106.0 1.5 shard_map.148
  107.5 3.6 %collective-permute-start.29 = (f32[8,256]{1,0:T(8,128)S(1)}, f32[8,256]{1,0:T(8,128)S(1)}, u32[]{:S(2)}, u32[]{:S(2)}) collective-permute-start(f32[8,256]{1,0:T(8,128)S(1)} %get-tuple-element.185), channel_id=1, source_target_pairs={{0,1},{1,0},{2,3},{3,2},{4,5},{5,4},{6,7},{7,6},{8,9},{9,8},{10,11... | collective-permute-start | bytes 24584 | tf_op jit(solution)/shard_map/ppermute | solution.py:635
  111.1 0.1 collective-permute-start.39
  111.2 0.8 collective-permute-done.29
  112.0 1.5 collective-permute-start.38
  113.4 0.6 slice.30
  114.0 0.5 slice.40
  116.0 3.1 %shard_map.152 = (f32[512,128]{1,0:T(8,128)S(1)}, f32[64,128]{1,0:T(8,128)S(1)}, f32[64,128]{1,0:T(8,128)S(1)}, f32[64,128]{1,0:T(8,128)S(1)}, f32[64,128]{1,0:T(8,128)S(1)}) custom-call(f32[640,128]{1,0:T(8,128)S(1)} %get-tuple-element.208.cells, f32[64,128]{1,0:T(8,128)S(1)} %collective-permute-done.33.from_xlow, ...), custom_call_target="tpu_custom_call" | custom-call | tf_op jit(solution)/shard_map/pallas_call | solution.py:591
  119.1 1.2 collective-permute-start.40
  120.3 1.4 collective-permute-start.41
  121.8 22.2 %collective-permute-done.40.from_x_up = f32[64,128]{1,0:T(8,128)S(1)} collective-permute-done((f32[64,128]{1,0:T(8,128)S(1)}, f32[64,128]{1,0:T(8,128)S(1)}, u32[]{:S(2)}, u32[]{:S(2)}) %collective-permute-start.40) | collective-permute-done | bytes 32800 | tf_op jit(solution)/shard_map/ppermute | solution.py:639
  143.9 4.6 %collective-permute-start.42 = (f32[64,128]{1,0:T(8,128)S(1)}, f32[64,128]{1,0:T(8,128)S(1)}, u32[]{:S(2)}, u32[]{:S(2)}) collective-permute-start(f32[64,128]{1,0:T(8,128)S(1)} %get-tuple-element.212.slow), channel_id=1, source_target_pairs={{0,3},{1,0},{2,1},{3,2},{4,7},{5,4},{6,5},{7,6},{8,11},{9,8},{10,9... | collective-permute-start | bytes 98312 | tf_op jit(solution)/shard_map/ppermute | solution.py:639
  148.5 1.1 collective-permute-start.43
  149.7 2.1 %collective-permute-done.42.from_s_up = f32[64,128]{1,0:T(8,128)S(1)} collective-permute-done((f32[64,128]{1,0:T(8,128)S(1)}, f32[64,128]{1,0:T(8,128)S(1)}, u32[]{:S(2)}, u32[]{:S(2)}) %collective-permute-start.42) | collective-permute-done | bytes 32800 | tf_op jit(solution)/shard_map/ppermute | solution.py:639
  151.7 1.1 shard_map.153
  152.8 1.8 %shard_map.151 = f32[8,12,16,512]{3,2,1,0:T(8,128)S(1)} custom-call(f32[320,512]{1,0:T(8,128)S(1)} %get-tuple-element.194.refs_0_, f32[320,512]{1,0:T(8,128)S(1)} %collective-permute-done.30.refs_1_, f32[320,512]{1,0:T(8,128)S(1)} %collective-permute-done.31.refs_2_, f32[320,512]{1,0:T(8,128)S(1)} %collective-permute-done.32.refs_3_, ...), custom_call_target="tpu_custom_call", output_to_operand_aliasing={{}: (8, {})} | custom-call | tf_op jit(solution)/shard_map/pallas_call | solution.py:387
  154.7 0.2 conditional.1
  154.9 1.6 %copy-done.2 = f32[8,12,16,512]{3,2,1,0:T(8,128)} copy-done((f32[8,12,16,512]{3,2,1,0:T(8,128)}, f32[8,12,16,512]{3,2,1,0:T(8,128)S(1)}, u32[]{:S(2)}) %copy-start.2) | copy-done | bytes 3145752
  156.6 0.1 copy-done.5
  (49 shorter events, 0.1 us)
Async XLA Ops:
  0.6 2.8 %copy-start = (f32[256,12,512]{2,0,1:T(8,128)S(1)}, f32[256,12,512]{2,0,1:T(8,128)}, u32[]{:S(2)}) copy-start(f32[256,12,512]{2,0,1:T(8,128)} %param.15) | copy-start | bytes 18874372
  3.4 0.7 copy-start.1
  4.1 7.4 %slice-start = ((s8[6291456]{0:T(1024)(128)(4,1)}), s8[4194304]{0:T(1024)(128)(4,1)S(1)}, s32[]{:S(2)}) async-start(s8[6291456]{0:T(1024)(128)(4,1)} %bitcast.30), calls=%async_computation | async-start | bytes 8388608
  5.9 5.6 %slice-start.1 = ((s8[6291456]{0:T(1024)(128)(4,1)}), s8[2097152]{0:T(1024)(128)(4,1)S(1)}, s32[]{:S(2)}) async-start(s8[6291456]{0:T(1024)(128)(4,1)} %bitcast.30), calls=%async_computation.1 | async-start | bytes 4194304
  5.9 2.8 %collective-permute-start.14 = (f32[392,512]{1,0:T(8,128)S(1)}, f32[392,512]{1,0:T(8,128)S(1)}, u32[]{:S(2)}, u32[]{:S(2)}) collective-permute-start(f32[392,512]{1,0:T(8,128)S(1)} %get-tuple-element.150), channel_id=1, source_target_pairs={{0,1},{1,0},{2,3},{3,2},{4,5},{5,4},{6,7},{7,6},{8,9},{9,8},{10,11... | collective-permute-start | bytes 2408456 | tf_op jit(solution)/shard_map/ppermute | solution.py:635
  8.6 24.5 %collective-permute-start.18 = (f32[512,512]{1,0:T(8,128)S(1)}, f32[512,512]{1,0:T(8,128)S(1)}, u32[]{:S(2)}, u32[]{:S(2)}) collective-permute-start(f32[512,512]{1,0:T(8,128)S(1)} %get-tuple-element.160), channel_id=1, source_target_pairs={{0,1},{1,0},{2,3},{3,2},{4,5},{5,4},{6,7},{7,6},{8,9},{9,8},{10,11... | collective-permute-start | bytes 3145736 | tf_op jit(solution)/shard_map/ppermute | solution.py:635
  8.8 10.6 %collective-permute-start.15 = (f32[200,512]{1,0:T(8,128)S(1)}, f32[200,512]{1,0:T(8,128)S(1)}, u32[]{:S(2)}, u32[]{:S(2)}) collective-permute-start(f32[200,512]{1,0:T(8,128)S(1)} %get-tuple-element.152), channel_id=1, source_target_pairs={{0,2},{1,3},{2,0},{3,1},{4,6},{5,7},{6,4},{7,5},{8,10},{9,11},{10,... | collective-permute-start | bytes 1228808 | tf_op jit(solution)/shard_map/ppermute | solution.py:635
  10.1 10.2 %collective-permute-start.16 = (f32[200,512]{1,0:T(8,128)S(1)}, f32[200,512]{1,0:T(8,128)S(1)}, u32[]{:S(2)}, u32[]{:S(2)}) collective-permute-start(f32[200,512]{1,0:T(8,128)S(1)} %get-tuple-element.153), channel_id=1, source_target_pairs={{0,4},{1,5},{2,6},{3,7},{4,0},{5,1},{6,2},{7,3},{8,12},{9,13},{10,... | collective-permute-start | bytes 1228808 | tf_op jit(solution)/shard_map/ppermute | solution.py:635
  10.3 18.7 %collective-permute-start.17 = (f32[200,512]{1,0:T(8,128)S(1)}, f32[200,512]{1,0:T(8,128)S(1)}, u32[]{:S(2)}, u32[]{:S(2)}) collective-permute-start(f32[200,512]{1,0:T(8,128)S(1)} %get-tuple-element.154), channel_id=1, source_target_pairs={{0,6},{1,7},{2,4},{3,5},{4,2},{5,3},{6,0},{7,1},{8,14},{9,15},{10,... | collective-permute-start | bytes 1228808 | tf_op jit(solution)/shard_map/ppermute | solution.py:635
  13.8 32.9 %collective-permute-start.20 = (f32[640,512]{1,0:T(8,128)S(1)}, f32[640,512]{1,0:T(8,128)S(1)}, u32[]{:S(2)}, u32[]{:S(2)}) collective-permute-start(f32[640,512]{1,0:T(8,128)S(1)} %get-tuple-element.166), channel_id=1, source_target_pairs={{0,1},{1,0},{2,3},{3,2},{4,5},{5,4},{6,7},{7,6},{8,9},{9,8},{10,11... | collective-permute-start | bytes 3932168 | tf_op jit(solution)/shard_map/ppermute | solution.py:635
  30.8 16.0 %collective-permute-start.19 = (f32[152,512]{1,0:T(8,128)S(1)}, f32[152,512]{1,0:T(8,128)S(1)}, u32[]{:S(2)}, u32[]{:S(2)}) collective-permute-start(f32[152,512]{1,0:T(8,128)S(1)} %get-tuple-element.163), channel_id=1, source_target_pairs={{0,16},{1,17},{2,18},{3,19},{4,20},{5,21},{6,22},{7,23},{8,24},{9,... | collective-permute-start | bytes 933896 | tf_op jit(solution)/shard_map/ppermute | solution.py:635
  33.2 13.5 %collective-permute-start.22 = (f32[264,512]{1,0:T(8,128)S(1)}, f32[264,512]{1,0:T(8,128)S(1)}, u32[]{:S(2)}, u32[]{:S(2)}) collective-permute-start(f32[264,512]{1,0:T(8,128)S(1)} %get-tuple-element.169), channel_id=1, source_target_pairs={{0,2},{1,3},{2,0},{3,1},{4,6},{5,7},{6,4},{7,5},{8,10},{9,11},{10,... | collective-permute-start | bytes 1622024 | tf_op jit(solution)/shard_map/ppermute | solution.py:635
  34.5 27.3 %collective-permute-start.23 = (f32[264,512]{1,0:T(8,128)S(1)}, f32[264,512]{1,0:T(8,128)S(1)}, u32[]{:S(2)}, u32[]{:S(2)}) collective-permute-start(f32[264,512]{1,0:T(8,128)S(1)} %get-tuple-element.170), channel_id=1, source_target_pairs={{0,4},{1,5},{2,6},{3,7},{4,0},{5,1},{6,2},{7,3},{8,12},{9,13},{10,... | collective-permute-start | bytes 1622024 | tf_op jit(solution)/shard_map/ppermute | solution.py:635
  34.7 27.1 %collective-permute-start.24 = (f32[264,512]{1,0:T(8,128)S(1)}, f32[264,512]{1,0:T(8,128)S(1)}, u32[]{:S(2)}, u32[]{:S(2)}) collective-permute-start(f32[264,512]{1,0:T(8,128)S(1)} %get-tuple-element.171), channel_id=1, source_target_pairs={{0,6},{1,7},{2,4},{3,5},{4,2},{5,3},{6,0},{7,1},{8,14},{9,15},{10,... | collective-permute-start | bytes 1622024 | tf_op jit(solution)/shard_map/ppermute | solution.py:635
  46.7 15.1 %collective-permute-start.21 = (f32[152,512]{1,0:T(8,128)S(1)}, f32[152,512]{1,0:T(8,128)S(1)}, u32[]{:S(2)}, u32[]{:S(2)}) collective-permute-start(f32[152,512]{1,0:T(8,128)S(1)} %get-tuple-element.167), channel_id=1, source_target_pairs={{0,24},{1,25},{2,26},{3,27},{4,28},{5,29},{6,30},{7,31},{8,16},{9,... | collective-permute-start | bytes 933896 | tf_op jit(solution)/shard_map/ppermute | solution.py:635
  46.7 20.9 %collective-permute-start.25 = (f32[200,512]{1,0:T(8,128)S(1)}, f32[200,512]{1,0:T(8,128)S(1)}, u32[]{:S(2)}, u32[]{:S(2)}) collective-permute-start(f32[200,512]{1,0:T(8,128)S(1)} %get-tuple-element.174), channel_id=1, source_target_pairs={{0,8},{1,9},{2,10},{3,11},{4,12},{5,13},{6,14},{7,15},{8,0},{9,1},... | collective-permute-start | bytes 1228808 | tf_op jit(solution)/shard_map/ppermute | solution.py:635
  63.6 16.6 %collective-permute-start.27 = (f32[200,512]{1,0:T(8,128)S(1)}, f32[200,512]{1,0:T(8,128)S(1)}, u32[]{:S(2)}, u32[]{:S(2)}) collective-permute-start(f32[200,512]{1,0:T(8,128)S(1)} %get-tuple-element.177), channel_id=1, source_target_pairs={{0,16},{1,17},{2,18},{3,19},{4,20},{5,21},{6,22},{7,23},{8,24},{9,... | collective-permute-start | bytes 1228808 | tf_op jit(solution)/shard_map/ppermute | solution.py:635
  63.6 17.3 %copy-start.3 = (bf16[640,512]{1,0:T(8,128)(2,1)S(1)}, bf16[640,512]{1,0:T(8,128)(2,1)}, u32[]{:S(2)}) copy-start(bf16[640,512]{1,0:T(8,128)(2,1)} %constant.24.clone.refs_11_) | copy-start | bytes 1966084
  63.7 19.0 %collective-permute-start.30 = (f32[320,512]{1,0:T(8,128)S(1)}, f32[320,512]{1,0:T(8,128)S(1)}, u32[]{:S(2)}, u32[]{:S(2)}) collective-permute-start(f32[320,512]{1,0:T(8,128)S(1)} %get-tuple-element.195), channel_id=1, source_target_pairs={{0,2},{1,3},{2,0},{3,1},{4,6},{5,7},{6,4},{7,5},{8,10},{9,11},{10,... | collective-permute-start | bytes 1966088 | tf_op jit(solution)/shard_map/ppermute | solution.py:635
  65.0 35.3 %collective-permute-start.31 = (f32[320,512]{1,0:T(8,128)S(1)}, f32[320,512]{1,0:T(8,128)S(1)}, u32[]{:S(2)}, u32[]{:S(2)}) collective-permute-start(f32[320,512]{1,0:T(8,128)S(1)} %get-tuple-element.196), channel_id=1, source_target_pairs={{0,4},{1,5},{2,6},{3,7},{4,0},{5,1},{6,2},{7,3},{8,12},{9,13},{10,... | collective-permute-start | bytes 1966088 | tf_op jit(solution)/shard_map/ppermute | solution.py:635
  65.3 35.1 %collective-permute-start.32 = (f32[320,512]{1,0:T(8,128)S(1)}, f32[320,512]{1,0:T(8,128)S(1)}, u32[]{:S(2)}, u32[]{:S(2)}) collective-permute-start(f32[320,512]{1,0:T(8,128)S(1)} %get-tuple-element.197), channel_id=1, source_target_pairs={{0,6},{1,7},{2,4},{3,5},{4,2},{5,3},{6,0},{7,1},{8,14},{9,15},{10,... | collective-permute-start | bytes 1966088 | tf_op jit(solution)/shard_map/ppermute | solution.py:635
  67.6 34.7 %collective-permute-start.26 = (f32[264,512]{1,0:T(8,128)S(1)}, f32[264,512]{1,0:T(8,128)S(1)}, u32[]{:S(2)}, u32[]{:S(2)}) collective-permute-start(f32[264,512]{1,0:T(8,128)S(1)} %get-tuple-element.175), channel_id=1, source_target_pairs={{0,8},{1,9},{2,10},{3,11},{4,12},{5,13},{6,14},{7,15},{8,0},{9,1},... | collective-permute-start | bytes 1622024 | tf_op jit(solution)/shard_map/ppermute | solution.py:635
  80.2 17.5 %collective-permute-start.28 = (f32[200,512]{1,0:T(8,128)S(1)}, f32[200,512]{1,0:T(8,128)S(1)}, u32[]{:S(2)}, u32[]{:S(2)}) collective-permute-start(f32[200,512]{1,0:T(8,128)S(1)} %get-tuple-element.180), channel_id=1, source_target_pairs={{0,24},{1,25},{2,26},{3,27},{4,28},{5,29},{6,30},{7,31},{8,16},{9,... | collective-permute-start | bytes 1228808 | tf_op jit(solution)/shard_map/ppermute | solution.py:635
  82.8 19.5 %collective-permute-start.34 = (f32[64,128]{1,0:T(8,128)S(1)}, f32[64,128]{1,0:T(8,128)S(1)}, u32[]{:S(2)}, u32[]{:S(2)}) collective-permute-start(f32[64,128]{1,0:T(8,128)S(1)} %get-tuple-element.228), channel_id=1, source_target_pairs={{0,28},{4,0},{8,4},{12,8},{16,12},{20,16},{24,20},{28,24},{1,29},{... | collective-permute-start | bytes 98312 | tf_op jit(solution)/shard_map/ppermute | solution.py:639
  97.7 4.6 %collective-permute-start.33 = (f32[64,128]{1,0:T(8,128)S(1)}, f32[64,128]{1,0:T(8,128)S(1)}, u32[]{:S(2)}, u32[]{:S(2)}) collective-permute-start(f32[64,128]{1,0:T(8,128)S(1)} %get-tuple-element.229), channel_id=1, source_target_pairs={{0,4},{4,8},{8,12},{12,16},{16,20},{20,24},{24,28},{28,0},{1,5},{5... | collective-permute-start | bytes 98312 | tf_op jit(solution)/shard_map/ppermute | solution.py:639
  102.3 50.5 %collective-permute-start.35 = (f32[320,512]{1,0:T(8,128)S(1)}, f32[320,512]{1,0:T(8,128)S(1)}, u32[]{:S(2)}, u32[]{:S(2)}) collective-permute-start(f32[320,512]{1,0:T(8,128)S(1)} %get-tuple-element.200), channel_id=1, source_target_pairs={{0,8},{1,9},{2,10},{3,11},{4,12},{5,13},{6,14},{7,15},{8,0},{9,1},... | collective-permute-start | bytes 1966088 | tf_op jit(solution)/shard_map/ppermute | solution.py:635
  102.4 50.4 %collective-permute-start.37 = (f32[240,512]{1,0:T(8,128)S(1)}, f32[240,512]{1,0:T(8,128)S(1)}, u32[]{:S(2)}, u32[]{:S(2)}) collective-permute-start(f32[240,512]{1,0:T(8,128)S(1)} %get-tuple-element.206), channel_id=1, source_target_pairs={{0,24},{1,25},{2,26},{3,27},{4,28},{5,29},{6,30},{7,31},{8,16},{9,... | collective-permute-start | bytes 1474568 | tf_op jit(solution)/shard_map/ppermute | solution.py:635
  102.5 50.3 %collective-permute-start.36 = (f32[240,512]{1,0:T(8,128)S(1)}, f32[240,512]{1,0:T(8,128)S(1)}, u32[]{:S(2)}, u32[]{:S(2)}) collective-permute-start(f32[240,512]{1,0:T(8,128)S(1)} %get-tuple-element.203), channel_id=1, source_target_pairs={{0,16},{1,17},{2,18},{3,19},{4,20},{5,21},{6,22},{7,23},{8,24},{9,... | collective-permute-start | bytes 1474568 | tf_op jit(solution)/shard_map/ppermute | solution.py:635
  105.9 10.0 %copy-start.4 = (f32[16,10,10]{2,0,1:T(8,128)S(1)}, f32[16,10,10]{2,0,1:T(8,128)}, u32[]{:S(2)}) copy-start(f32[16,10,10]{2,0,1:T(8,128)} %param.19) | copy-start | bytes 19204
  105.9 10.0 %copy-start.6 = (f32[104,10]{1,0:T(8,128)S(1)}, f32[104,10]{1,0:T(8,128)}, u32[]{:S(2)}) copy-start(f32[104,10]{1,0:T(8,128)} %constant.28.clone.refs_9_) | copy-start | bytes 12484
  105.9 10.0 %copy-start.7 = (f32[104,10]{1,0:T(8,128)S(1)}, f32[104,10]{1,0:T(8,128)}, u32[]{:S(2)}) copy-start(f32[104,10]{1,0:T(8,128)} %constant.27.clone.refs_8_) | copy-start | bytes 12484
  105.9 10.0 %copy-start.8 = (f32[96,10]{1,0:T(8,128)S(1)}, f32[96,10]{1,0:T(8,128)}, u32[]{:S(2)}) copy-start(f32[96,10]{1,0:T(8,128)} %constant.26.clone.refs_7_) | copy-start | bytes 11524
  105.9 10.0 %copy-start.9 = (f32[96,10]{1,0:T(8,128)S(1)}, f32[96,10]{1,0:T(8,128)}, u32[]{:S(2)}) copy-start(f32[96,10]{1,0:T(8,128)} %constant.25.clone.refs_6_) | copy-start | bytes 11524
  106.0 10.0 %copy-start.10 = (f32[10,10]{1,0:T(8,128)S(1)}, f32[10,10]{1,0:T(8,128)}, u32[]{:S(2)}) copy-start(f32[10,10]{1,0:T(8,128)} %refs_0_.1) | copy-start | bytes 1204
  106.0 10.0 %copy-start.11 = (f32[10,10]{1,0:T(8,128)S(1)}, f32[10,10]{1,0:T(8,128)}, u32[]{:S(2)}) copy-start(f32[10,10]{1,0:T(8,128)} %refs_1_.1) | copy-start | bytes 1204
  106.0 10.0 %copy-start.12 = (f32[16,10]{1,0:T(8,128)S(1)}, f32[16,10]{1,0:T(8,128)}, u32[]{:S(2)}) copy-start(f32[16,10]{1,0:T(8,128)} %refs_5_.1) | copy-start | bytes 1924
  106.0 10.0 %copy-start.13 = (f32[10]{0:T(128)S(1)}, f32[10]{0:T(128)}, u32[]{:S(2)}) copy-start(f32[10]{0:T(128)} %param.20) | copy-start | bytes 124
  106.0 10.0 %copy-start.14 = (f32[10]{0:T(128)S(1)}, f32[10]{0:T(128)}, u32[]{:S(2)}) copy-start(f32[10]{0:T(128)} %param.21) | copy-start | bytes 124
  107.5 4.4 %collective-permute-start.29 = (f32[8,256]{1,0:T(8,128)S(1)}, f32[8,256]{1,0:T(8,128)S(1)}, u32[]{:S(2)}, u32[]{:S(2)}) collective-permute-start(f32[8,256]{1,0:T(8,128)S(1)} %get-tuple-element.185), channel_id=1, source_target_pairs={{0,1},{1,0},{2,3},{3,2},{4,5},{5,4},{6,7},{7,6},{8,9},{9,8},{10,11... | collective-permute-start | bytes 24584 | tf_op jit(solution)/shard_map/ppermute | solution.py:635
  111.1 4.7 %collective-permute-start.39 = (f32[64,128]{1,0:T(8,128)S(1)}, f32[64,128]{1,0:T(8,128)S(1)}, u32[]{:S(2)}, u32[]{:S(2)}) collective-permute-start(f32[64,128]{1,0:T(8,128)S(1)} %get-tuple-element.226), channel_id=1, source_target_pairs={{0,3},{1,0},{2,1},{3,2},{4,7},{5,4},{6,5},{7,6},{8,11},{9,8},{10,9... | collective-permute-start | bytes 98312 | tf_op jit(solution)/shard_map/ppermute | solution.py:639
  112.0 3.9 %collective-permute-start.38 = (f32[64,128]{1,0:T(8,128)S(1)}, f32[64,128]{1,0:T(8,128)S(1)}, u32[]{:S(2)}, u32[]{:S(2)}) collective-permute-start(f32[64,128]{1,0:T(8,128)S(1)} %get-tuple-element.227), channel_id=1, source_target_pairs={{0,1},{1,2},{2,3},{3,0},{4,5},{5,6},{6,7},{7,4},{8,9},{9,10},{10,1... | collective-permute-start | bytes 98312 | tf_op jit(solution)/shard_map/ppermute | solution.py:639
  119.1 24.8 %collective-permute-start.40 = (f32[64,128]{1,0:T(8,128)S(1)}, f32[64,128]{1,0:T(8,128)S(1)}, u32[]{:S(2)}, u32[]{:S(2)}) collective-permute-start(f32[64,128]{1,0:T(8,128)S(1)} %get-tuple-element.210.xlow), channel_id=1, source_target_pairs={{0,28},{4,0},{8,4},{12,8},{16,12},{20,16},{24,20},{28,24},{1,29},{... | collective-permute-start | bytes 98312 | tf_op jit(solution)/shard_map/ppermute | solution.py:639
  120.3 28.2 %collective-permute-start.41 = (f32[64,128]{1,0:T(8,128)S(1)}, f32[64,128]{1,0:T(8,128)S(1)}, u32[]{:S(2)}, u32[]{:S(2)}) collective-permute-start(f32[64,128]{1,0:T(8,128)S(1)} %get-tuple-element.211.xup), channel_id=1, source_target_pairs={{0,4},{4,8},{8,12},{12,16},{16,20},{20,24},{24,28},{28,0},{1,5},{5... | collective-permute-start | bytes 98312 | tf_op jit(solution)/shard_map/ppermute | solution.py:639
  143.9 7.8 %collective-permute-start.42 = (f32[64,128]{1,0:T(8,128)S(1)}, f32[64,128]{1,0:T(8,128)S(1)}, u32[]{:S(2)}, u32[]{:S(2)}) collective-permute-start(f32[64,128]{1,0:T(8,128)S(1)} %get-tuple-element.212.slow), channel_id=1, source_target_pairs={{0,3},{1,0},{2,1},{3,2},{4,7},{5,4},{6,5},{7,6},{8,11},{9,8},{10,9... | collective-permute-start | bytes 98312 | tf_op jit(solution)/shard_map/ppermute | solution.py:639
  148.5 3.2 %collective-permute-start.43 = (f32[64,128]{1,0:T(8,128)S(1)}, f32[64,128]{1,0:T(8,128)S(1)}, u32[]{:S(2)}, u32[]{:S(2)}) collective-permute-start(f32[64,128]{1,0:T(8,128)S(1)} %get-tuple-element.213.sup), channel_id=1, source_target_pairs={{0,1},{1,2},{2,3},{3,0},{4,5},{5,6},{6,7},{7,4},{8,9},{9,10},{10,1... | collective-permute-start | bytes 98312 | tf_op jit(solution)/shard_map/ppermute | solution.py:639
  154.9 1.7 %copy-start.2 = (f32[8,12,16,512]{3,2,1,0:T(8,128)}, f32[8,12,16,512]{3,2,1,0:T(8,128)S(1)}, u32[]{:S(2)}) copy-start(f32[8,12,16,512]{3,2,1,0:T(8,128)S(1)} %get-tuple-element.220) | copy-start | bytes 9437188
  154.9 1.7 %copy-start.5 = (f32[32,16,128]{2,1,0:T(8,128)}, f32[32,16,128]{2,1,0:T(8,128)S(1)}, u32[]{:S(2)}) copy-start(f32[32,16,128]{2,1,0:T(8,128)S(1)} %get-tuple-element.144) | copy-start | bytes 786436

commit v7 on v6

--- a/solution.py
+++ b/solution.py
@@ -695,7 +695,7 @@
             before_it = held[-1][1]
             messages[0] = after(messages[0], before_it[1:])
             if flagged:
-                before_it[0] = across(after(waiting, messages[1]), plan.plane)
+                before_it[0] = across(after(waiting, messages[2]), plan.plane)
         if g == last:
             buffer, row_marks, cells = settle(plan, plan.groups[0], *held[0], None, None, own, order, None)
             messages[0] = after(messages[0], cells)
@@ -723,7 +723,7 @@
                 value = after(value, packed[-1][1])
             arrived.append(across(value, m * plan.plane))
         if not first:
-            arrived[0] = across(after(waiting, [messages[1], held[-1][1][0]]), plan.plane)
+            arrived[0] = across(after(waiting, [messages[2], held[-1][1][0]]), plan.plane)
         held.append((messages, arrived))
 
     buffer, flag = settle(plan, plan.groups[1], *held[1], row_marks, buffer, None, None, flag)

time: 157 us -> 157 us (level)
  no operation moved by 1% of the time
where the time goes in v7:
time: 157 us
  waiting for transfers between devices  86.7 us (55%)
  starting transfers between devices  39.9 us (25%)
  Pallas kernels  21.2 us (14%)
  local copies, waits for them, and re-layouts  6.38 us (4%)
  between operations  2.3 us (1%)
    ppermute x22, waiting for transfers between devices, across(): lax.ppermute(value, both, [(d, d ^ flip) for d in range(plan.devices)])  62.4 us
    ppermute x22, starting transfers between devices, across(): lax.ppermute(value, both, [(d, d ^ flip) for d in range(plan.devices)])  27.1 us
    ppermute x8, waiting for transfers between devices, shifted(): lax.ppermute(value, axis, [(s, (s + steps) % count) for s in range(count)])  24.3 us
    ppermute x8, starting transfers between devices, shifted(): lax.ppermute(value, axis, [(s, (s + steps) % count) for s in range(count)])  12.9 us
    pallas_call x8, Pallas kernels, simple_call(): pl.pallas_call(kernel, in_specs=[pl.BlockSpec(memory_space=pltpu.VMEM)] *...  9.94 us
    pallas_call x3, Pallas kernels, pack(): pl.pallas_call(functools.partial(pack_kernel, plan, fields, marked), grid...  6 us
    unnamed x34, local copies, waits for them, and re-layouts  5.25 us
    pallas_call x3, Pallas kernels, settle(): pl.pallas_call(functools.partial(settle_kernel, plan, fields, marked, fla...  5.21 us
  transfers between devices with their start and end apart: 30, of which 11 were waited for; matrix products, arithmetic and copies ran while one was open for 1% of the time, Pallas kernels for 11%

profile of v7, /device:TPU:11, one launch (start us, length us, event | category | flops | bytes accessed | tf_op | source)
XLA Modules:
  0.0 156.7 jit_solution(5208160687784773568)
XLA Ops:
  0.6 2.8 %copy-done = f32[256,12,512]{2,0,1:T(8,128)S(1)} copy-done((f32[256,12,512]{2,0,1:T(8,128)S(1)}, f32[256,12,512]{2,0,1:T(8,128)}, u32[]{:S(2)}) %copy-start) | copy-done | bytes 6291480
  3.4 0.7 copy-done.1
  4.1 1.8 %shard_map.141 = (f32[104,512]{1,0:T(8,128)S(1)}, f32[104,512]{1,0:T(8,128)S(1)}, f32[104,512]{1,0:T(8,128)S(1)}, f32[104,512]{1,0:T(8,128)S(1)}, f32[392,512]{1,0:T(8,128)S(1)}) custom-call(s32[1]{0:T(128)} %bitcast.5.me_ref, s32[1,256]{1,0:T(1,128)S(1)} %bitcast.35, f32[12,256,512]{2,1,0:T(8,128)S(1)} %bitcast.28), custom_call_target="tpu_custom_call" | custom-call | tf_op jit(solution)/shard_map/pallas_call | solution.py:134
  5.9 0.0 slice-start.1
  5.9 0.7 collective-permute-start.14
  6.6 1.9 %shard_map.140 = (f32[128,512]{1,0:T(8,128)S(1)}, f32[128,512]{1,0:T(8,128)S(1)}, f32[128,512]{1,0:T(8,128)S(1)}, f32[128,512]{1,0:T(8,128)S(1)}, f32[512,512]{1,0:T(8,128)S(1)}) custom-call(s32[1]{0:T(128)} %bitcast.5.me_ref, s32[1,256]{1,0:T(1,128)S(1)} %bitcast.36, f32[12,256,512]{2,1,0:T(8,128)S(1)} %bitcast.29), custom_call_target="tpu_custom_call" | custom-call | tf_op jit(solution)/shard_map/pallas_call | solution.py:134
  8.6 0.1 collective-permute-start.18
  8.7 0.1 shard_map.142
  8.8 1.3 collective-permute-start.15
  10.1 0.3 collective-permute-start.16
  10.3 1.1 collective-permute-start.17
  11.5 2.3 %shard_map.145 = (f32[160,512]{1,0:T(8,128)S(1)}, f32[160,512]{1,0:T(8,128)S(1)}, f32[160,512]{1,0:T(8,128)S(1)}, f32[160,512]{1,0:T(8,128)S(1)}, f32[640,512]{1,0:T(8,128)S(1)}) custom-call(s32[1]{0:T(128)} %bitcast.5.me_ref, s32[1,256]{1,0:T(1,128)S(1)} %bitcast.37, f32[12,256,512]{2,1,0:T(8,128)S(1)} %bitcast.32), custom_call_target="tpu_custom_call" | custom-call | tf_op jit(solution)/shard_map/pallas_call | solution.py:134
  13.8 1.4 collective-permute-start.20
  15.2 4.2 %collective-permute-done.15.refs_1_ = f32[200,512]{1,0:T(8,128)S(1)} collective-permute-done((f32[200,512]{1,0:T(8,128)S(1)}, f32[200,512]{1,0:T(8,128)S(1)}, u32[]{:S(2)}, u32[]{:S(2)}) %collective-permute-start.15) | collective-permute-done | bytes 409632 | tf_op jit(solution)/shard_map/ppermute | solution.py:635
  19.4 0.9 collective-permute-done.16.refs_2_
  20.3 8.7 %collective-permute-done.17.refs_3_ = f32[200,512]{1,0:T(8,128)S(1)} collective-permute-done((f32[200,512]{1,0:T(8,128)S(1)}, f32[200,512]{1,0:T(8,128)S(1)}, u32[]{:S(2)}, u32[]{:S(2)}) %collective-permute-start.17) | collective-permute-done | bytes 409632 | tf_op jit(solution)/shard_map/ppermute | solution.py:635
  29.1 1.7 %shard_map.143 = (f32[200,512]{1,0:T(8,128)S(1)}, f32[152,512]{1,0:T(8,128)S(1)}, f32[152,512]{1,0:T(8,128)S(1)}, f32[48,512]{1,0:T(8,128)}, f32[48,512]{1,0:T(8...) custom-call(f32[200,512]{1,0:T(8,128)S(1)} %get-tuple-element.151.refs_0_, ...), custom_call_target="tpu_custom_call" | custom-call | tf_op jit(solution)/shard_map/pallas_call | solution.py:591
  30.8 2.3 %collective-permute-start.19 = (f32[152,512]{1,0:T(8,128)S(1)}, f32[152,512]{1,0:T(8,128)S(1)}, u32[]{:S(2)}, u32[]{:S(2)}) collective-permute-start(f32[152,512]{1,0:T(8,128)S(1)} %get-tuple-element.163), channel_id=1, source_target_pairs={{0,16},{1,17},{2,18},{3,19},{4,20},{5,21},{6,22},{7,23},{8,24},{9,... | collective-permute-start | bytes 933896 | tf_op jit(solution)/shard_map/ppermute | solution.py:635
  33.1 0.1 shard_map.144
  33.2 0.3 collective-permute-start.23
  33.5 1.2 collective-permute-start.22
  34.7 1.2 collective-permute-start.24
  35.9 10.8 %collective-permute-done.19.refs_5_.refs_8_ = f32[152,512]{1,0:T(8,128)S(1)} collective-permute-done((f32[152,512]{1,0:T(8,128)S(1)}, f32[152,512]{1,0:T(8,128)S(1)}, u32[]{:S(2)}, u32[]{:S(2)}) %collective-permute-start.19) | collective-permute-done | bytes 311328 | tf_op jit(solution)/shard_map/ppermute | solution.py:635
  46.7 4.3 %collective-permute-start.25 = (f32[200,512]{1,0:T(8,128)S(1)}, f32[200,512]{1,0:T(8,128)S(1)}, u32[]{:S(2)}, u32[]{:S(2)}) collective-permute-start(f32[200,512]{1,0:T(8,128)S(1)} %get-tuple-element.174), channel_id=1, source_target_pairs={{0,8},{1,9},{2,10},{3,11},{4,12},{5,13},{6,14},{7,15},{8,0},{9,1},... | collective-permute-start | bytes 1228808 | tf_op jit(solution)/shard_map/ppermute | solution.py:635
  51.0 10.8 %collective-permute-done.21.refs_6_.refs_9_ = f32[152,512]{1,0:T(8,128)S(1)} collective-permute-done((f32[152,512]{1,0:T(8,128)S(1)}, f32[152,512]{1,0:T(8,128)S(1)}, u32[]{:S(2)}, u32[]{:S(2)}) %collective-permute-start.21) | collective-permute-done | bytes 311328 | tf_op jit(solution)/shard_map/ppermute | solution.py:635
  61.8 1.7 %shard_map.146 = (f32[264,512]{1,0:T(8,128)S(1)}, f32[200,512]{1,0:T(8,128)S(1)}, f32[200,512]{1,0:T(8,128)S(1)}, f32[64,512]{1,0:T(8,128)S(1)}, f32[64,512]{1,0:T(8,128)}, /*index=5*/f32[8,256]{1,0:T(8,128)S(1)}) custom-call(f32[264,512]{1,0:T(8,128)S(1)} %get-tuple-element.168.refs_0_, f32[264,512]{1,0:T(8,128)S(1)} %collective-permute-done.22.refs_1_, ...), custom_call_target="tpu_custom_call" | custom-call | tf_op jit(solution)/shard_map/pallas_call | solution.py:591
  63.6 0.2 shard_map.149
  63.7 1.3 collective-permute-start.30
  65.0 0.3 collective-permute-start.31
  65.3 1.2 collective-permute-start.32
  66.5 1.1 collective-permute-done.25.refs_4_.refs_7_
  67.6 2.2 %collective-permute-start.26 = (f32[264,512]{1,0:T(8,128)S(1)}, f32[264,512]{1,0:T(8,128)S(1)}, u32[]{:S(2)}, u32[]{:S(2)}) collective-permute-start(f32[264,512]{1,0:T(8,128)S(1)} %get-tuple-element.175), channel_id=1, source_target_pairs={{0,8},{1,9},{2,10},{3,11},{4,12},{5,13},{6,14},{7,15},{8,0},{9,1},... | collective-permute-start | bytes 1622024 | tf_op jit(solution)/shard_map/ppermute | solution.py:635
  69.8 10.4 %collective-permute-done.27.refs_5_.refs_8_ = f32[200,512]{1,0:T(8,128)S(1)} collective-permute-done((f32[200,512]{1,0:T(8,128)S(1)}, f32[200,512]{1,0:T(8,128)S(1)}, u32[]{:S(2)}, u32[]{:S(2)}) %collective-permute-start.27) | collective-permute-done | bytes 409632 | tf_op jit(solution)/shard_map/ppermute | solution.py:635
  80.2 0.7 collective-permute-start.28
  80.9 1.9 %shard_map.147 = (f32[8,12,16,512]{3,2,1,0:T(8,128)S(1)}, f32[8,256]{1,0:T(8,128)S(1)}, f32[640,128]{1,0:T(8,128)S(1)}) custom-call(f32[200,512]{1,0:T(8,128)S(1)} %get-tuple-element.151.refs_0_, f32[200,512]{1,0:T(8,128)S(1)} %collective-permute-done.15.refs_1_, f32[200,512]{1,0:T(8,128)S(1)} %collective-permute-done.16.refs_2_, ...), custom_call_target="tpu_custom_call" | custom-call | tf_op jit(solution)/shard_map/pallas_call | solution.py:387
  82.8 0.3 collective-permute-start.34
  83.0 14.7 %collective-permute-done.28.refs_6_.refs_9_ = f32[200,512]{1,0:T(8,128)S(1)} collective-permute-done((f32[200,512]{1,0:T(8,128)S(1)}, f32[200,512]{1,0:T(8,128)S(1)}, u32[]{:S(2)}, u32[]{:S(2)}) %collective-permute-start.28) | collective-permute-done | bytes 409632 | tf_op jit(solution)/shard_map/ppermute | solution.py:635
  97.7 2.7 %collective-permute-start.33 = (f32[64,128]{1,0:T(8,128)S(1)}, f32[64,128]{1,0:T(8,128)S(1)}, u32[]{:S(2)}, u32[]{:S(2)}) collective-permute-start(f32[64,128]{1,0:T(8,128)S(1)} %get-tuple-element.229), channel_id=1, source_target_pairs={{0,4},{4,8},{8,12},{12,16},{16,20},{20,24},{24,28},{28,0},{1,5},{5... | collective-permute-start | bytes 98312 | tf_op jit(solution)/shard_map/ppermute | solution.py:639
  100.4 1.9 %shard_map.150 = (f32[320,512]{1,0:T(8,128)S(1)}, f32[240,512]{1,0:T(8,128)S(1)}, f32[240,512]{1,0:T(8,128)S(1)}, f32[80,512]{1,0:T(8,128)}, f32[80,512]{1,0:T(8,128)}) custom-call(f32[320,512]{1,0:T(8,128)S(1)} %get-tuple-element.194.refs_0_, f32[320,512]{1,0:T(8,128)S(1)} %collective-permute-done.30.refs_1_, ...), custom_call_target="tpu_custom_call" | custom-call | tf_op jit(solution)/shard_map/pallas_call | solution.py:591
  102.3 0.1 collective-permute-start.35
  102.4 0.1 collective-permute-start.37
  102.5 3.4 %collective-permute-start.36 = (f32[240,512]{1,0:T(8,128)S(1)}, f32[240,512]{1,0:T(8,128)S(1)}, u32[]{:S(2)}, u32[]{:S(2)}) collective-permute-start(f32[240,512]{1,0:T(8,128)S(1)} %get-tuple-element.203), channel_id=1, source_target_pairs={{0,16},{1,17},{2,18},{3,19},{4,20},{5,21},{6,22},{7,23},{8,24},{9,... | collective-permute-start | bytes 1474568 | tf_op jit(solution)/shard_map/ppermute | solution.py:635
  105.9 0.0 copy-start.9
  106.0 0.0 copy-start.10
  106.0 0.0 copy-start.11
  106.0 1.5 shard_map.148
  107.5 3.6 %collective-permute-start.29 = (f32[8,256]{1,0:T(8,128)S(1)}, f32[8,256]{1,0:T(8,128)S(1)}, u32[]{:S(2)}, u32[]{:S(2)}) collective-permute-start(f32[8,256]{1,0:T(8,128)S(1)} %get-tuple-element.185), channel_id=1, source_target_pairs={{0,1},{1,0},{2,3},{3,2},{4,5},{5,4},{6,7},{7,6},{8,9},{9,8},{10,11... | collective-permute-start | bytes 24584 | tf_op jit(solution)/shard_map/ppermute | solution.py:635
  111.1 0.1 collective-permute-start.39
  111.2 0.8 collective-permute-done.29
  112.0 1.5 collective-permute-start.38
  113.4 0.6 slice.30
  114.0 0.5 slice.40
  116.0 3.1 %shard_map.152 = (f32[512,128]{1,0:T(8,128)S(1)}, f32[64,128]{1,0:T(8,128)S(1)}, f32[64,128]{1,0:T(8,128)S(1)}, f32[64,128]{1,0:T(8,128)S(1)}, f32[64,128]{1,0:T(8,128)S(1)}) custom-call(f32[640,128]{1,0:T(8,128)S(1)} %get-tuple-element.208.cells, f32[64,128]{1,0:T(8,128)S(1)} %collective-permute-done.33.from_xlow, ...), custom_call_target="tpu_custom_call" | custom-call | tf_op jit(solution)/shard_map/pallas_call | solution.py:591
  119.1 1.2 collective-permute-start.40
  120.3 1.4 collective-permute-start.41
  121.8 22.2 %collective-permute-done.40.from_x_up = f32[64,128]{1,0:T(8,128)S(1)} collective-permute-done((f32[64,128]{1,0:T(8,128)S(1)}, f32[64,128]{1,0:T(8,128)S(1)}, u32[]{:S(2)}, u32[]{:S(2)}) %collective-permute-start.40) | collective-permute-done | bytes 32800 | tf_op jit(solution)/shard_map/ppermute | solution.py:639
  143.9 4.6 %collective-permute-start.42 = (f32[64,128]{1,0:T(8,128)S(1)}, f32[64,128]{1,0:T(8,128)S(1)}, u32[]{:S(2)}, u32[]{:S(2)}) collective-permute-start(f32[64,128]{1,0:T(8,128)S(1)} %get-tuple-element.212.slow), channel_id=1, source_target_pairs={{0,3},{1,0},{2,1},{3,2},{4,7},{5,4},{6,5},{7,6},{8,11},{9,8},{10,9... | collective-permute-start | bytes 98312 | tf_op jit(solution)/shard_map/ppermute | solution.py:639
  148.5 1.1 collective-permute-start.43
  149.7 2.1 %collective-permute-done.42.from_s_up = f32[64,128]{1,0:T(8,128)S(1)} collective-permute-done((f32[64,128]{1,0:T(8,128)S(1)}, f32[64,128]{1,0:T(8,128)S(1)}, u32[]{:S(2)}, u32[]{:S(2)}) %collective-permute-start.42) | collective-permute-done | bytes 32800 | tf_op jit(solution)/shard_map/ppermute | solution.py:639
  151.7 1.1 shard_map.153
  152.8 1.8 %shard_map.151 = f32[8,12,16,512]{3,2,1,0:T(8,128)S(1)} custom-call(f32[320,512]{1,0:T(8,128)S(1)} %get-tuple-element.194.refs_0_, f32[320,512]{1,0:T(8,128)S(1)} %collective-permute-done.30.refs_1_, f32[320,512]{1,0:T(8,128)S(1)} %collective-permute-done.31.refs_2_, f32[320,512]{1,0:T(8,128)S(1)} %collective-permute-done.32.refs_3_, ...), custom_call_target="tpu_custom_call", output_to_operand_aliasing={{}: (8, {})} | custom-call | tf_op jit(solution)/shard_map/pallas_call | solution.py:387
  154.7 0.2 conditional.1
  154.9 1.6 %copy-done.2 = f32[8,12,16,512]{3,2,1,0:T(8,128)} copy-done((f32[8,12,16,512]{3,2,1,0:T(8,128)}, f32[8,12,16,512]{3,2,1,0:T(8,128)S(1)}, u32[]{:S(2)}) %copy-start.2) | copy-done | bytes 3145752
  156.6 0.1 copy-done.5
  (49 shorter events, 0.1 us)
Async XLA Ops:
  0.6 2.8 %copy-start = (f32[256,12,512]{2,0,1:T(8,128)S(1)}, f32[256,12,512]{2,0,1:T(8,128)}, u32[]{:S(2)}) copy-start(f32[256,12,512]{2,0,1:T(8,128)} %param.15) | copy-start | bytes 18874372
  3.4 0.7 copy-start.1
  4.1 7.4 %slice-start = ((s8[6291456]{0:T(1024)(128)(4,1)}), s8[4194304]{0:T(1024)(128)(4,1)S(1)}, s32[]{:S(2)}) async-start(s8[6291456]{0:T(1024)(128)(4,1)} %bitcast.30), calls=%async_computation | async-start | bytes 8388608
  5.9 5.6 %slice-start.1 = ((s8[6291456]{0:T(1024)(128)(4,1)}), s8[2097152]{0:T(1024)(128)(4,1)S(1)}, s32[]{:S(2)}) async-start(s8[6291456]{0:T(1024)(128)(4,1)} %bitcast.30), calls=%async_computation.1 | async-start | bytes 4194304
  5.9 2.8 %collective-permute-start.14 = (f32[392,512]{1,0:T(8,128)S(1)}, f32[392,512]{1,0:T(8,128)S(1)}, u32[]{:S(2)}, u32[]{:S(2)}) collective-permute-start(f32[392,512]{1,0:T(8,128)S(1)} %get-tuple-element.150), channel_id=1, source_target_pairs={{0,1},{1,0},{2,3},{3,2},{4,5},{5,4},{6,7},{7,6},{8,9},{9,8},{10,11... | collective-permute-start | bytes 2408456 | tf_op jit(solution)/shard_map/ppermute | solution.py:635
  8.6 24.5 %collective-permute-start.18 = (f32[512,512]{1,0:T(8,128)S(1)}, f32[512,512]{1,0:T(8,128)S(1)}, u32[]{:S(2)}, u32[]{:S(2)}) collective-permute-start(f32[512,512]{1,0:T(8,128)S(1)} %get-tuple-element.160), channel_id=1, source_target_pairs={{0,1},{1,0},{2,3},{3,2},{4,5},{5,4},{6,7},{7,6},{8,9},{9,8},{10,11... | collective-permute-start | bytes 3145736 | tf_op jit(solution)/shard_map/ppermute | solution.py:635
  8.8 10.6 %collective-permute-start.15 = (f32[200,512]{1,0:T(8,128)S(1)}, f32[200,512]{1,0:T(8,128)S(1)}, u32[]{:S(2)}, u32[]{:S(2)}) collective-permute-start(f32[200,512]{1,0:T(8,128)S(1)} %get-tuple-element.152), channel_id=1, source_target_pairs={{0,2},{1,3},{2,0},{3,1},{4,6},{5,7},{6,4},{7,5},{8,10},{9,11},{10,... | collective-permute-start | bytes 1228808 | tf_op jit(solution)/shard_map/ppermute | solution.py:635
  10.1 10.2 %collective-permute-start.16 = (f32[200,512]{1,0:T(8,128)S(1)}, f32[200,512]{1,0:T(8,128)S(1)}, u32[]{:S(2)}, u32[]{:S(2)}) collective-permute-start(f32[200,512]{1,0:T(8,128)S(1)} %get-tuple-element.153), channel_id=1, source_target_pairs={{0,4},{1,5},{2,6},{3,7},{4,0},{5,1},{6,2},{7,3},{8,12},{9,13},{10,... | collective-permute-start | bytes 1228808 | tf_op jit(solution)/shard_map/ppermute | solution.py:635
  10.3 18.7 %collective-permute-start.17 = (f32[200,512]{1,0:T(8,128)S(1)}, f32[200,512]{1,0:T(8,128)S(1)}, u32[]{:S(2)}, u32[]{:S(2)}) collective-permute-start(f32[200,512]{1,0:T(8,128)S(1)} %get-tuple-element.154), channel_id=1, source_target_pairs={{0,6},{1,7},{2,4},{3,5},{4,2},{5,3},{6,0},{7,1},{8,14},{9,15},{10,... | collective-permute-start | bytes 1228808 | tf_op jit(solution)/shard_map/ppermute | solution.py:635
  13.8 32.9 %collective-permute-start.20 = (f32[640,512]{1,0:T(8,128)S(1)}, f32[640,512]{1,0:T(8,128)S(1)}, u32[]{:S(2)}, u32[]{:S(2)}) collective-permute-start(f32[640,512]{1,0:T(8,128)S(1)} %get-tuple-element.166), channel_id=1, source_target_pairs={{0,1},{1,0},{2,3},{3,2},{4,5},{5,4},{6,7},{7,6},{8,9},{9,8},{10,11... | collective-permute-start | bytes 3932168 | tf_op jit(solution)/shard_map/ppermute | solution.py:635
  30.8 16.0 %collective-permute-start.19 = (f32[152,512]{1,0:T(8,128)S(1)}, f32[152,512]{1,0:T(8,128)S(1)}, u32[]{:S(2)}, u32[]{:S(2)}) collective-permute-start(f32[152,512]{1,0:T(8,128)S(1)} %get-tuple-element.163), channel_id=1, source_target_pairs={{0,16},{1,17},{2,18},{3,19},{4,20},{5,21},{6,22},{7,23},{8,24},{9,... | collective-permute-start | bytes 933896 | tf_op jit(solution)/shard_map/ppermute | solution.py:635
  33.2 13.5 %collective-permute-start.23 = (f32[264,512]{1,0:T(8,128)S(1)}, f32[264,512]{1,0:T(8,128)S(1)}, u32[]{:S(2)}, u32[]{:S(2)}) collective-permute-start(f32[264,512]{1,0:T(8,128)S(1)} %get-tuple-element.170), channel_id=1, source_target_pairs={{0,4},{1,5},{2,6},{3,7},{4,0},{5,1},{6,2},{7,3},{8,12},{9,13},{10,... | collective-permute-start | bytes 1622024 | tf_op jit(solution)/shard_map/ppermute | solution.py:635
  33.5 28.3 %collective-permute-start.22 = (f32[264,512]{1,0:T(8,128)S(1)}, f32[264,512]{1,0:T(8,128)S(1)}, u32[]{:S(2)}, u32[]{:S(2)}) collective-permute-start(f32[264,512]{1,0:T(8,128)S(1)} %get-tuple-element.169), channel_id=1, source_target_pairs={{0,2},{1,3},{2,0},{3,1},{4,6},{5,7},{6,4},{7,5},{8,10},{9,11},{10,... | collective-permute-start | bytes 1622024 | tf_op jit(solution)/shard_map/ppermute | solution.py:635
  34.7 27.1 %collective-permute-start.24 = (f32[264,512]{1,0:T(8,128)S(1)}, f32[264,512]{1,0:T(8,128)S(1)}, u32[]{:S(2)}, u32[]{:S(2)}) collective-permute-start(f32[264,512]{1,0:T(8,128)S(1)} %get-tuple-element.171), channel_id=1, source_target_pairs={{0,6},{1,7},{2,4},{3,5},{4,2},{5,3},{6,0},{7,1},{8,14},{9,15},{10,... | collective-permute-start | bytes 1622024 | tf_op jit(solution)/shard_map/ppermute | solution.py:635
  46.7 15.1 %collective-permute-start.21 = (f32[152,512]{1,0:T(8,128)S(1)}, f32[152,512]{1,0:T(8,128)S(1)}, u32[]{:S(2)}, u32[]{:S(2)}) collective-permute-start(f32[152,512]{1,0:T(8,128)S(1)} %get-tuple-element.167), channel_id=1, source_target_pairs={{0,24},{1,25},{2,26},{3,27},{4,28},{5,29},{6,30},{7,31},{8,16},{9,... | collective-permute-start | bytes 933896 | tf_op jit(solution)/shard_map/ppermute | solution.py:635
  46.7 20.9 %collective-permute-start.25 = (f32[200,512]{1,0:T(8,128)S(1)}, f32[200,512]{1,0:T(8,128)S(1)}, u32[]{:S(2)}, u32[]{:S(2)}) collective-permute-start(f32[200,512]{1,0:T(8,128)S(1)} %get-tuple-element.174), channel_id=1, source_target_pairs={{0,8},{1,9},{2,10},{3,11},{4,12},{5,13},{6,14},{7,15},{8,0},{9,1},... | collective-permute-start | bytes 1228808 | tf_op jit(solution)/shard_map/ppermute | solution.py:635
  63.6 16.6 %collective-permute-start.27 = (f32[200,512]{1,0:T(8,128)S(1)}, f32[200,512]{1,0:T(8,128)S(1)}, u32[]{:S(2)}, u32[]{:S(2)}) collective-permute-start(f32[200,512]{1,0:T(8,128)S(1)} %get-tuple-element.177), channel_id=1, source_target_pairs={{0,16},{1,17},{2,18},{3,19},{4,20},{5,21},{6,22},{7,23},{8,24},{9,... | collective-permute-start | bytes 1228808 | tf_op jit(solution)/shard_map/ppermute | solution.py:635
  63.6 17.3 %copy-start.3 = (bf16[640,512]{1,0:T(8,128)(2,1)S(1)}, bf16[640,512]{1,0:T(8,128)(2,1)}, u32[]{:S(2)}) copy-start(bf16[640,512]{1,0:T(8,128)(2,1)} %constant.24.clone.refs_11_) | copy-start | bytes 1966084
  63.7 19.0 %collective-permute-start.30 = (f32[320,512]{1,0:T(8,128)S(1)}, f32[320,512]{1,0:T(8,128)S(1)}, u32[]{:S(2)}, u32[]{:S(2)}) collective-permute-start(f32[320,512]{1,0:T(8,128)S(1)} %get-tuple-element.195), channel_id=1, source_target_pairs={{0,2},{1,3},{2,0},{3,1},{4,6},{5,7},{6,4},{7,5},{8,10},{9,11},{10,... | collective-permute-start | bytes 1966088 | tf_op jit(solution)/shard_map/ppermute | solution.py:635
  65.0 35.3 %collective-permute-start.31 = (f32[320,512]{1,0:T(8,128)S(1)}, f32[320,512]{1,0:T(8,128)S(1)}, u32[]{:S(2)}, u32[]{:S(2)}) collective-permute-start(f32[320,512]{1,0:T(8,128)S(1)} %get-tuple-element.196), channel_id=1, source_target_pairs={{0,4},{1,5},{2,6},{3,7},{4,0},{5,1},{6,2},{7,3},{8,12},{9,13},{10,... | collective-permute-start | bytes 1966088 | tf_op jit(solution)/shard_map/ppermute | solution.py:635
  65.3 35.1 %collective-permute-start.32 = (f32[320,512]{1,0:T(8,128)S(1)}, f32[320,512]{1,0:T(8,128)S(1)}, u32[]{:S(2)}, u32[]{:S(2)}) collective-permute-start(f32[320,512]{1,0:T(8,128)S(1)} %get-tuple-element.197), channel_id=1, source_target_pairs={{0,6},{1,7},{2,4},{3,5},{4,2},{5,3},{6,0},{7,1},{8,14},{9,15},{10,... | collective-permute-start | bytes 1966088 | tf_op jit(solution)/shard_map/ppermute | solution.py:635
  67.6 34.7 %collective-permute-start.26 = (f32[264,512]{1,0:T(8,128)S(1)}, f32[264,512]{1,0:T(8,128)S(1)}, u32[]{:S(2)}, u32[]{:S(2)}) collective-permute-start(f32[264,512]{1,0:T(8,128)S(1)} %get-tuple-element.175), channel_id=1, source_target_pairs={{0,8},{1,9},{2,10},{3,11},{4,12},{5,13},{6,14},{7,15},{8,0},{9,1},... | collective-permute-start | bytes 1622024 | tf_op jit(solution)/shard_map/ppermute | solution.py:635
  80.2 17.5 %collective-permute-start.28 = (f32[200,512]{1,0:T(8,128)S(1)}, f32[200,512]{1,0:T(8,128)S(1)}, u32[]{:S(2)}, u32[]{:S(2)}) collective-permute-start(f32[200,512]{1,0:T(8,128)S(1)} %get-tuple-element.180), channel_id=1, source_target_pairs={{0,24},{1,25},{2,26},{3,27},{4,28},{5,29},{6,30},{7,31},{8,16},{9,... | collective-permute-start | bytes 1228808 | tf_op jit(solution)/shard_map/ppermute | solution.py:635
  82.8 19.5 %collective-permute-start.34 = (f32[64,128]{1,0:T(8,128)S(1)}, f32[64,128]{1,0:T(8,128)S(1)}, u32[]{:S(2)}, u32[]{:S(2)}) collective-permute-start(f32[64,128]{1,0:T(8,128)S(1)} %get-tuple-element.228), channel_id=1, source_target_pairs={{0,28},{4,0},{8,4},{12,8},{16,12},{20,16},{24,20},{28,24},{1,29},{... | collective-permute-start | bytes 98312 | tf_op jit(solution)/shard_map/ppermute | solution.py:639
  97.7 4.6 %collective-permute-start.33 = (f32[64,128]{1,0:T(8,128)S(1)}, f32[64,128]{1,0:T(8,128)S(1)}, u32[]{:S(2)}, u32[]{:S(2)}) collective-permute-start(f32[64,128]{1,0:T(8,128)S(1)} %get-tuple-element.229), channel_id=1, source_target_pairs={{0,4},{4,8},{8,12},{12,16},{16,20},{20,24},{24,28},{28,0},{1,5},{5... | collective-permute-start | bytes 98312 | tf_op jit(solution)/shard_map/ppermute | solution.py:639
  102.3 50.5 %collective-permute-start.35 = (f32[320,512]{1,0:T(8,128)S(1)}, f32[320,512]{1,0:T(8,128)S(1)}, u32[]{:S(2)}, u32[]{:S(2)}) collective-permute-start(f32[320,512]{1,0:T(8,128)S(1)} %get-tuple-element.200), channel_id=1, source_target_pairs={{0,8},{1,9},{2,10},{3,11},{4,12},{5,13},{6,14},{7,15},{8,0},{9,1},... | collective-permute-start | bytes 1966088 | tf_op jit(solution)/shard_map/ppermute | solution.py:635
  102.4 50.4 %collective-permute-start.37 = (f32[240,512]{1,0:T(8,128)S(1)}, f32[240,512]{1,0:T(8,128)S(1)}, u32[]{:S(2)}, u32[]{:S(2)}) collective-permute-start(f32[240,512]{1,0:T(8,128)S(1)} %get-tuple-element.206), channel_id=1, source_target_pairs={{0,24},{1,25},{2,26},{3,27},{4,28},{5,29},{6,30},{7,31},{8,16},{9,... | collective-permute-start | bytes 1474568 | tf_op jit(solution)/shard_map/ppermute | solution.py:635
  102.5 50.3 %collective-permute-start.36 = (f32[240,512]{1,0:T(8,128)S(1)}, f32[240,512]{1,0:T(8,128)S(1)}, u32[]{:S(2)}, u32[]{:S(2)}) collective-permute-start(f32[240,512]{1,0:T(8,128)S(1)} %get-tuple-element.203), channel_id=1, source_target_pairs={{0,16},{1,17},{2,18},{3,19},{4,20},{5,21},{6,22},{7,23},{8,24},{9,... | collective-permute-start | bytes 1474568 | tf_op jit(solution)/shard_map/ppermute | solution.py:635
  105.9 10.0 %copy-start.4 = (f32[16,10,10]{2,0,1:T(8,128)S(1)}, f32[16,10,10]{2,0,1:T(8,128)}, u32[]{:S(2)}) copy-start(f32[16,10,10]{2,0,1:T(8,128)} %param.19) | copy-start | bytes 19204
  105.9 10.0 %copy-start.6 = (f32[104,10]{1,0:T(8,128)S(1)}, f32[104,10]{1,0:T(8,128)}, u32[]{:S(2)}) copy-start(f32[104,10]{1,0:T(8,128)} %constant.28.clone.refs_9_) | copy-start | bytes 12484
  105.9 10.0 %copy-start.7 = (f32[104,10]{1,0:T(8,128)S(1)}, f32[104,10]{1,0:T(8,128)}, u32[]{:S(2)}) copy-start(f32[104,10]{1,0:T(8,128)} %constant.27.clone.refs_8_) | copy-start | bytes 12484
  105.9 10.0 %copy-start.8 = (f32[96,10]{1,0:T(8,128)S(1)}, f32[96,10]{1,0:T(8,128)}, u32[]{:S(2)}) copy-start(f32[96,10]{1,0:T(8,128)} %constant.26.clone.refs_7_) | copy-start | bytes 11524
  105.9 10.0 %copy-start.9 = (f32[96,10]{1,0:T(8,128)S(1)}, f32[96,10]{1,0:T(8,128)}, u32[]{:S(2)}) copy-start(f32[96,10]{1,0:T(8,128)} %constant.25.clone.refs_6_) | copy-start | bytes 11524
  106.0 10.0 %copy-start.10 = (f32[10,10]{1,0:T(8,128)S(1)}, f32[10,10]{1,0:T(8,128)}, u32[]{:S(2)}) copy-start(f32[10,10]{1,0:T(8,128)} %refs_0_.1) | copy-start | bytes 1204
  106.0 10.0 %copy-start.11 = (f32[10,10]{1,0:T(8,128)S(1)}, f32[10,10]{1,0:T(8,128)}, u32[]{:S(2)}) copy-start(f32[10,10]{1,0:T(8,128)} %refs_1_.1) | copy-start | bytes 1204
  106.0 10.0 %copy-start.12 = (f32[16,10]{1,0:T(8,128)S(1)}, f32[16,10]{1,0:T(8,128)}, u32[]{:S(2)}) copy-start(f32[16,10]{1,0:T(8,128)} %refs_5_.1) | copy-start | bytes 1924
  106.0 10.0 %copy-start.13 = (f32[10]{0:T(128)S(1)}, f32[10]{0:T(128)}, u32[]{:S(2)}) copy-start(f32[10]{0:T(128)} %param.20) | copy-start | bytes 124
  106.0 10.0 %copy-start.14 = (f32[10]{0:T(128)S(1)}, f32[10]{0:T(128)}, u32[]{:S(2)}) copy-start(f32[10]{0:T(128)} %param.21) | copy-start | bytes 124
  107.5 4.4 %collective-permute-start.29 = (f32[8,256]{1,0:T(8,128)S(1)}, f32[8,256]{1,0:T(8,128)S(1)}, u32[]{:S(2)}, u32[]{:S(2)}) collective-permute-start(f32[8,256]{1,0:T(8,128)S(1)} %get-tuple-element.185), channel_id=1, source_target_pairs={{0,1},{1,0},{2,3},{3,2},{4,5},{5,4},{6,7},{7,6},{8,9},{9,8},{10,11... | collective-permute-start | bytes 24584 | tf_op jit(solution)/shard_map/ppermute | solution.py:635
  111.1 4.7 %collective-permute-start.39 = (f32[64,128]{1,0:T(8,128)S(1)}, f32[64,128]{1,0:T(8,128)S(1)}, u32[]{:S(2)}, u32[]{:S(2)}) collective-permute-start(f32[64,128]{1,0:T(8,128)S(1)} %get-tuple-element.226), channel_id=1, source_target_pairs={{0,3},{1,0},{2,1},{3,2},{4,7},{5,4},{6,5},{7,6},{8,11},{9,8},{10,9... | collective-permute-start | bytes 98312 | tf_op jit(solution)/shard_map/ppermute | solution.py:639
  112.0 3.9 %collective-permute-start.38 = (f32[64,128]{1,0:T(8,128)S(1)}, f32[64,128]{1,0:T(8,128)S(1)}, u32[]{:S(2)}, u32[]{:S(2)}) collective-permute-start(f32[64,128]{1,0:T(8,128)S(1)} %get-tuple-element.227), channel_id=1, source_target_pairs={{0,1},{1,2},{2,3},{3,0},{4,5},{5,6},{6,7},{7,4},{8,9},{9,10},{10,1... | collective-permute-start | bytes 98312 | tf_op jit(solution)/shard_map/ppermute | solution.py:639
  119.1 24.8 %collective-permute-start.40 = (f32[64,128]{1,0:T(8,128)S(1)}, f32[64,128]{1,0:T(8,128)S(1)}, u32[]{:S(2)}, u32[]{:S(2)}) collective-permute-start(f32[64,128]{1,0:T(8,128)S(1)} %get-tuple-element.210.xlow), channel_id=1, source_target_pairs={{0,28},{4,0},{8,4},{12,8},{16,12},{20,16},{24,20},{28,24},{1,29},{... | collective-permute-start | bytes 98312 | tf_op jit(solution)/shard_map/ppermute | solution.py:639
  120.3 28.2 %collective-permute-start.41 = (f32[64,128]{1,0:T(8,128)S(1)}, f32[64,128]{1,0:T(8,128)S(1)}, u32[]{:S(2)}, u32[]{:S(2)}) collective-permute-start(f32[64,128]{1,0:T(8,128)S(1)} %get-tuple-element.211.xup), channel_id=1, source_target_pairs={{0,4},{4,8},{8,12},{12,16},{16,20},{20,24},{24,28},{28,0},{1,5},{5... | collective-permute-start | bytes 98312 | tf_op jit(solution)/shard_map/ppermute | solution.py:639
  143.9 7.8 %collective-permute-start.42 = (f32[64,128]{1,0:T(8,128)S(1)}, f32[64,128]{1,0:T(8,128)S(1)}, u32[]{:S(2)}, u32[]{:S(2)}) collective-permute-start(f32[64,128]{1,0:T(8,128)S(1)} %get-tuple-element.212.slow), channel_id=1, source_target_pairs={{0,3},{1,0},{2,1},{3,2},{4,7},{5,4},{6,5},{7,6},{8,11},{9,8},{10,9... | collective-permute-start | bytes 98312 | tf_op jit(solution)/shard_map/ppermute | solution.py:639
  148.5 3.2 %collective-permute-start.43 = (f32[64,128]{1,0:T(8,128)S(1)}, f32[64,128]{1,0:T(8,128)S(1)}, u32[]{:S(2)}, u32[]{:S(2)}) collective-permute-start(f32[64,128]{1,0:T(8,128)S(1)} %get-tuple-element.213.sup), channel_id=1, source_target_pairs={{0,1},{1,2},{2,3},{3,0},{4,5},{5,6},{6,7},{7,4},{8,9},{9,10},{10,1... | collective-permute-start | bytes 98312 | tf_op jit(solution)/shard_map/ppermute | solution.py:639
  154.9 1.7 %copy-start.2 = (f32[8,12,16,512]{3,2,1,0:T(8,128)}, f32[8,12,16,512]{3,2,1,0:T(8,128)S(1)}, u32[]{:S(2)}) copy-start(f32[8,12,16,512]{3,2,1,0:T(8,128)S(1)} %get-tuple-element.220) | copy-start | bytes 9437188
  154.9 1.7 %copy-start.5 = (f32[32,16,128]{2,1,0:T(8,128)}, f32[32,16,128]{2,1,0:T(8,128)S(1)}, u32[]{:S(2)}) copy-start(f32[32,16,128]{2,1,0:T(8,128)S(1)} %get-tuple-element.144) | copy-start | bytes 786436
